TPU v7x, 32 devices: a whole 2x2x4 slice. The times are simulated.
32 devices in a mesh: dp: 4 (over y, x), fsdp: 8 (over z, core).
Axes of the slice: x: 2, y: 2, z: 4, core: 2. Of those that a mesh axis runs over, the one named last changes fastest.
Arguments:
- samples: bfloat16 [32, 64, 64, 128], P(('dp', 'fsdp')), may hold values from -6 to 6
- cotangent: bfloat16 [32, 32, 32, 256], P(('dp', 'fsdp')), may hold values from -6 to 6
- class_ids: int32 [32], P(('dp', 'fsdp')), may hold values from 0 to 15
- conv_state: float32 [4, 4, 147456], P(None, None, ('dp', 'fsdp')), as said below
- mlp_state: float32 [4, 401408], P(None, ('dp', 'fsdp')), as said below
- small_state: float32 [4, 1792], P(None, ('dp', 'fsdp')), as said below
Outputs:
- block_out: bfloat16 [32, 32, 32, 256], P(('dp', 'fsdp'))
- input_grad: bfloat16 [32, 64, 64, 128], P(('dp', 'fsdp'))
- conv_new: float32 [4, 4, 147456], P(None, None, ('dp', 'fsdp'))
- mlp_new: float32 [4, 401408], P(None, ('dp', 'fsdp'))
- small_new: float32 [4, 1792], P(None, ('dp', 'fsdp'))
- conv_copy: bfloat16 [4, 147456], P(None, ('dp', 'fsdp'))
- mlp_copy: bfloat16 [401408], P(('dp', 'fsdp'))
- small_copy: bfloat16 [1792], P(('dp', 'fsdp'))
Inputs may be any that keep to these rules, and one draw needn't show every extreme that they name: `conv_state`: slot 2 (second moments) of each state is positive. `mlp_state`: slot 2 (second moments) of each state is positive. `small_state`: slot 2 (second moments) of each state is positive.
All inputs are finite; a program needn't handle non-finite values.
Results may differ from a plain program's by a relative error of at most 0.0066.
Values may be sent and summed in bfloat16 or wider, within the bound.
No kernel may reach another device: no remote copies, remote signals or barrier semaphores. Data moves between devices by JAX's collectives and lax.ppermute only.
A program may use at most 192 MiB of HBM per device.

v0:
```python
import jax
import jax.numpy as jnp
from jax import lax
from jax.sharding import PartitionSpec as P

C = 128
EMB = 512
GROUPS = 8
H = 64
W = 64
NCLASS = 16
STEP = 10


beta_one = 0.9
beta_two = 0.999
adam_eps = 1e-08
ema_decay = 0.99
norm_eps = 1e-05
rate_conv = 0.08
rate_table = 0.6
rate_dense = 0.1
rate_small = 0.15
decay_weights = 0.01


def group_norm(values, offset_gain, offset_bias):
    grouped = values.reshape(values.shape[:3] + (GROUPS, C // GROUPS))
    centre = jnp.mean(grouped, axis=(1, 2, 4), keepdims=True)
    spread = jnp.mean(jnp.square(grouped - centre), axis=(1, 2, 4), keepdims=True)
    scaled = ((grouped - centre) * lax.rsqrt(spread + norm_eps)).reshape(values.shape)
    return scaled * (1.0 + offset_gain) + offset_bias


def front_part(values, offset_gain, offset_bias):
    return jax.nn.gelu(group_norm(values, offset_gain, offset_bias), approximate=False)


def conv_taps(activation, kernel, stride):
    padded = jnp.pad(activation, ((0, 0), (1, 1), (1, 1), (0, 0)))
    summed = None
    for tap_row in range(3):
        for tap_col in range(3):
            window = padded[:, tap_row : tap_row + H : stride, tap_col : tap_col + W : stride]
            contrib = jnp.einsum(
                "bhwi,io->bhwo",
                window,
                kernel[tap_row, tap_col],
                preferred_element_type=jnp.float32,
            )
            summed = contrib if summed is None else summed + contrib
    return summed


def conv_back_taps(activation, upstream, kernel, stride):
    padded = jnp.pad(activation, ((0, 0), (1, 1), (1, 1), (0, 0)))
    grad_pad = jnp.zeros(padded.shape, jnp.float32)
    kernel_rows = []
    for tap_row in range(3):
        row_grads = []
        for tap_col in range(3):
            window = padded[:, tap_row : tap_row + H : stride, tap_col : tap_col + W : stride]
            row_grads.append(
                jnp.einsum("bhwi,bhwo->io", window, upstream, preferred_element_type=jnp.float32)
            )
            contrib = jnp.einsum(
                "bhwo,io->bhwi",
                upstream,
                kernel[tap_row, tap_col],
                preferred_element_type=jnp.float32,
            )
            grad_pad = grad_pad.at[
                :, tap_row : tap_row + H : stride, tap_col : tap_col + W : stride
            ].add(contrib)
        kernel_rows.append(jnp.stack(row_grads))
    return (jnp.stack(kernel_rows), grad_pad[:, 1:-1, 1:-1])


def split_kernels(conv_all):
    kernel_one = conv_all[0].reshape(3, 3, C, C)
    kernel_two = conv_all[1].reshape(3, 3, C, C)
    kernel_down = jnp.concatenate(
        [conv_all[2].reshape(3, 3, C, C), conv_all[3].reshape(3, 3, C, C)], axis=3
    )
    return (kernel_one, kernel_two, kernel_down)


def split_dense(dense_all):
    table_len = NCLASS * EMB
    class_embed = dense_all[:table_len].reshape(NCLASS, EMB)
    dense_one = dense_all[table_len : table_len + EMB * EMB].reshape(EMB, EMB)
    dense_two = dense_all[table_len + EMB * EMB :].reshape(EMB, 2 * C)
    return (class_embed, dense_one, dense_two)


def split_small(small_all):
    widths = [C, C, C, C, C, C, 2 * C, EMB, 2 * C]
    pieces = []
    offset = 0
    for extent in widths:
        pieces.append(small_all[offset : offset + extent])
        offset = offset + extent
    return pieces


def class_table(class_embed, dense_one, bias_hidden, dense_two, bias_out):
    hidden = jax.nn.gelu(
        jnp.dot(
            class_embed,
            dense_one,
            preferred_element_type=jnp.float32,
            precision=lax.Precision.HIGHEST,
        )
        + bias_hidden,
        approximate=False,
    )
    return (
        jnp.dot(
            hidden, dense_two, preferred_element_type=jnp.float32, precision=lax.Precision.HIGHEST
        )
        + bias_out
    )


def adam_update(state_stack, gradient, step_rate, weight_decay):
    weight = state_stack[0]
    first_moment = beta_one * state_stack[1] + (1.0 - beta_one) * gradient
    second = beta_two * state_stack[2] + (1.0 - beta_two) * gradient * gradient
    first_hat = first_moment / (1.0 - beta_one**STEP)
    second_hat = second / (1.0 - beta_two**STEP)
    weight_new = weight - step_rate * (
        first_hat / (jnp.sqrt(second_hat) + adam_eps) + weight_decay * weight
    )
    average = ema_decay * state_stack[3] + (1.0 - ema_decay) * weight_new
    return (jnp.stack([weight_new, first_moment, second, average]), weight_new.astype(jnp.bfloat16))


def per_device(samples, cotangent, class_ids, conv_state, mlp_state, small_state):
    conv_own = conv_state[0].astype(jnp.bfloat16)
    dense_own = mlp_state[0].astype(jnp.bfloat16)
    small_own = small_state[0].astype(jnp.bfloat16)
    dense_len = dense_own.shape[0]
    small_len = small_own.shape[0]
    position = lax.axis_index(("dp", "fsdp"))
    conv_all, dense_all, small_all = (
        lax.all_gather(conv_own, ("dp", "fsdp"), axis=1, tiled=True),
        lax.all_gather(dense_own, ("dp", "fsdp"), axis=0, tiled=True),
        lax.all_gather(small_own, ("dp", "fsdp"), axis=0, tiled=True),
    )
    kernel_one, kernel_two, kernel_down = split_kernels(conv_all)
    class_embed, dense_one, dense_two = split_dense(dense_all.astype(jnp.float32))
    (
        gain_one,
        shift_one,
        conv_bias_one,
        gain_two,
        shift_two,
        conv_bias_two,
        bias_down,
        bias_hidden,
        bias_out,
    ) = split_small(small_all.astype(jnp.float32))
    class_values, class_pull = jax.vjp(
        class_table, class_embed, dense_one, bias_hidden, dense_two, bias_out
    )
    one_hot = (class_ids[:, None] == jnp.arange(NCLASS, dtype=jnp.int32)[None, :]).astype(
        jnp.float32
    )
    chosen = jnp.dot(
        one_hot, class_values, preferred_element_type=jnp.float32, precision=lax.Precision.HIGHEST
    )
    film_scale = chosen[:, None, None, :C]
    film_shift = chosen[:, None, None, C:]
    source_field = samples.astype(jnp.float32)
    act_one, pull_one = jax.vjp(front_part, source_field, gain_one, shift_one)
    act_one_low = act_one.astype(jnp.bfloat16)
    conv_one_out = conv_taps(act_one_low, kernel_one, 1) + conv_bias_one
    modulated = conv_one_out * (1.0 + film_scale) + film_shift
    act_two, pull_two = jax.vjp(front_part, modulated, gain_two, shift_two)
    act_two_low = act_two.astype(jnp.bfloat16)
    conv_two_out = conv_taps(act_two_low, kernel_two, 1) + conv_bias_two
    residual_low = (source_field + conv_two_out).astype(jnp.bfloat16)
    block_out = (conv_taps(residual_low, kernel_down, 2) + bias_down).astype(jnp.bfloat16)
    conv_again = lax.all_gather(conv_own, ("dp", "fsdp"), axis=1, tiled=True)
    kernel_one, kernel_two, kernel_down = split_kernels(conv_again)
    grad_down, grad_resid = conv_back_taps(residual_low, cotangent, kernel_down, 2)
    grad_bias_down = jnp.sum(cotangent.astype(jnp.float32), axis=(0, 1, 2))
    grad_bias_two = jnp.sum(grad_resid, axis=(0, 1, 2))
    resid_low = grad_resid.astype(jnp.bfloat16)
    grad_two, grad_act_two = conv_back_taps(act_two_low, resid_low, kernel_two, 1)
    grad_mod, grad_gain_two, grad_shift_two = pull_two(grad_act_two)
    grad_scale = jnp.sum(grad_mod * conv_one_out, axis=(1, 2))
    grad_film_shift = jnp.sum(grad_mod, axis=(1, 2))
    grad_conv_one = grad_mod * (1.0 + film_scale)
    grad_bias_one = jnp.sum(grad_conv_one, axis=(0, 1, 2))
    grad_one, grad_act_one = conv_back_taps(
        act_one_low, grad_conv_one.astype(jnp.bfloat16), kernel_one, 1
    )
    grad_source, grad_gain_one, grad_shift_one = pull_one(grad_act_one)
    input_grad = (grad_resid + grad_source).astype(jnp.bfloat16)
    class_terms = jnp.dot(
        one_hot.T,
        jnp.concatenate([grad_scale, grad_film_shift], axis=1),
        preferred_element_type=jnp.float32,
        precision=lax.Precision.HIGHEST,
    )
    conv_grad = jnp.stack(
        [
            grad_one.reshape(-1),
            grad_two.reshape(-1),
            grad_down[..., :C].reshape(-1),
            grad_down[..., C:].reshape(-1),
        ]
    )
    norm_grads = [
        grad_gain_one,
        grad_shift_one,
        grad_bias_one,
        grad_gain_two,
        grad_shift_two,
        grad_bias_two,
        grad_bias_down,
    ]
    class_total = lax.psum(class_terms, ("dp", "fsdp"))
    grad_embed, grad_dense_one, grad_hidden, grad_dense_two, grad_out = class_pull(class_total)
    dense_grad = jnp.concatenate(
        [grad_embed.reshape(-1), grad_dense_one.reshape(-1), grad_dense_two.reshape(-1)]
    )
    small_local = jnp.concatenate(
        norm_grads + [jnp.zeros((EMB,), jnp.float32), jnp.zeros((2 * C,), jnp.float32)]
    )
    conv_red, small_red = (
        lax.psum_scatter(conv_grad, ("dp", "fsdp"), scatter_dimension=1, tiled=True),
        lax.psum_scatter(small_local, ("dp", "fsdp"), scatter_dimension=0, tiled=True),
    )
    dense_red = lax.dynamic_slice_in_dim(dense_grad, position * dense_len, dense_len)
    bias_tail = jnp.concatenate([jnp.zeros((8 * C,), jnp.float32), grad_hidden, grad_out])
    small_red = small_red + lax.dynamic_slice_in_dim(bias_tail, position * small_len, small_len)
    flat_index = position * dense_len + jnp.arange(dense_len, dtype=jnp.int32)
    dense_rate = jnp.where(flat_index < NCLASS * EMB, rate_table, rate_dense)
    conv_new, conv_copy = adam_update(conv_state, conv_red, rate_conv, decay_weights)
    mlp_new, mlp_copy = adam_update(mlp_state, dense_red, dense_rate, decay_weights)
    small_new, small_copy = adam_update(small_state, small_red, rate_small, 0.0)
    return (block_out, input_grad, conv_new, mlp_new, small_new, conv_copy, mlp_copy, small_copy)


def solution(mesh):
    return jax.shard_map(
        per_device,
        mesh=mesh,
        in_specs=(
            P(("dp", "fsdp"), None, None, None),
            P(("dp", "fsdp"), None, None, None),
            P(("dp", "fsdp")),
            P(None, None, ("dp", "fsdp")),
            P(None, ("dp", "fsdp")),
            P(None, ("dp", "fsdp")),
        ),
        out_specs=(
            P(("dp", "fsdp"), None, None, None),
            P(("dp", "fsdp"), None, None, None),
            P(None, None, ("dp", "fsdp")),
            P(None, ("dp", "fsdp")),
            P(None, ("dp", "fsdp")),
            P(None, ("dp", "fsdp")),
            P(("dp", "fsdp")),
            P(("dp", "fsdp")),
        ),
        check_vma=False,
    )
```

profile of v0, /device:TPU:0, one launch (start us, length us, event | category | flops | bytes accessed | tf_op | source)
XLA Modules:
  0.0 1378.3 jit_solution(16158578225000293441)
XLA Ops:
  9.7 42.1 %all-reduce.5 = bf16[1792]{0:T(1024)(128)(2,1)S(1)} all-reduce(bf16[1792]{0:T(1024)(128)(2,1)S(1)} %dynamic-update-slice.54), channel_id=1, replica_groups=mesh['dp'=4,'fsdp'=8] {'dp','fsdp'}, use_global_device_ids=true, to_apply=%add.5 | all-reduce | flops 1792 | bytes 7168
  55.6 48.8 %all-gather = bf16[32,1,12544]{2,1,0:T(2,128)(2,1)S(1)} all-gather(bf16[1,1,12544]{2,1,0:T(2,128)(2,1)S(1)} %reshape.1849), channel_id=1, replica_groups=mesh['dp'=4,'fsdp'=8] {'dp','fsdp'}, dimensions={0}, use_global_device_ids=true | all-gather | bytes 827904 | tf_op jit(solution)/shard_map/all_gather | solution.py:147
  129.5 10.1 slice_reduce_fusion.1
  170.8 7.2 scatter_fusion
  178.0 7.2 scatter_fusion.1
  185.2 7.2 scatter_fusion.2
  192.4 7.4 scatter_fusion.3
  199.8 7.2 scatter_fusion.4
  206.9 7.2 scatter_fusion.5
  238.6 12.8 scatter-add.163
  256.7 12.3 scatter-add.164
  275.9 11.1 scatter-add.166
  290.4 11.1 scatter-add.167
  308.4 11.1 scatter-add.169
  323.0 11.1 scatter-add.170
  334.0 9.2 fusion.48
  356.4 9.7 fusion.25
  417.0 12.4 scatter-add.172
  435.0 12.3 scatter-add.173
  454.5 11.1 scatter-add.175
  469.4 11.1 scatter-add.176
  487.7 11.1 scatter-add.178
  502.5 11.1 scatter-add.179
  544.6 37.6 %all-reduce.7 = (f32[16,256]{1,0:T(8,128)S(1)}, f32[1792]{0:T(1024)}) all-reduce(f32[16,256]{1,0:T(8,128)S(1)} %broadcast_multiply_fusion, f32[1792]{0:T(1024)} %constant_dynamic-update-slice_fusion), channel_id=1, replica_groups=mesh['dp'=4,'fsdp'=8] {'dp','fsdp'}, use_global_device_ids=true, to_apply=%region_33.34 | all-reduce | flops 5888 | bytes 47104 | tf_op jit(solution)/shard_map/psum | solution.py:224
  597.1 9.8 slice.1020
  606.9 9.7 slice.1018
  616.6 9.7 slice.1016
  626.3 9.7 slice.1014
  636.1 9.7 slice.1012
  645.8 9.7 slice.1010
  674.9 34.5 %copy.17 = f32[4,147456]{0,1:T(8,128)} copy(f32[4,147456]{1,0:T(4,128)S(1)} %pad_maximum_fusion) | data formatting | bytes 4718592
  718.1 648.9 %reduce-scatter.4.cloned.1.call-done = f32[4608,4]{1,0:T(8,128)} async-done(((f32[147456,4]{1,0:T(8,128)}), f32[4608,4]{1,0:T(8,128)}) %reduce-scatter.4.cloned.1.call-update) | async-done | bytes 73744
  (447 shorter events, 280.7 us)
Async XLA Ops:
  7.2 122.3 %all-gather.3.cloned.1.call-start = ((), (), s32[]{:S(2)}) async-start(), calls=%async_computation.1 | async-start | bytes 1216512 | tf_op jit(solution)/shard_map/all_gather | solution.py:146
  8.8 1358.3 %reduce-scatter.4.cloned.1.call-start = ((), (), s32[]{:S(2)}) async-start(), calls=%async_computation.2 | async-start | bytes 77856768
  110.2 6.0 copy-start.1
  113.1 4.8 copy-start.16
  113.1 5.9 copy-start.89
  116.2 4.8 copy-start.92
  117.3 6.2 copy-start.73
  118.8 10.6 copy-start.77
  120.5 8.9 copy-start.50
  123.0 6.5 copy-start.83
  123.5 5.9 copy-start.79
  129.4 31.5 %copy-start.4 = (bf16[1,64,64,128]{3,2,1,0:T(8,128)(2,1)}, bf16[1,64,64,128]{3,2,1,0:T(8,128)(2,1)S(1)}, u32[]{:S(2)}) copy-start(bf16[1,64,64,128]{3,2,1,0:T(8,128)(2,1)S(1)} %get-tuple-element.277) | copy-start | bytes 3145732
  139.6 21.4 %copy-start.18 = (bf16[147456]{0:T(1024)(128)(2,1)}, bf16[147456]{0:T(1024)(128)(2,1)S(1)}, u32[]{:S(2)}) copy-start(bf16[147456]{0:T(1024)(128)(2,1)S(1)} %get-tuple-element.237) | copy-start | bytes 884740
  139.6 23.1 %copy-start.35 = (bf16[128,256,1]{1,0,2:T(8,128)(2,1)}, bf16[128,256,1]{1,0,2:T(8,128)(2,1)S(1)}, u32[]{:S(2)}) copy-start(bf16[128,256,1]{1,0,2:T(8,128)(2,1)S(1)} %fusion.227) | copy-start | bytes 196612
  388.1 9.8 copy-start.2
  400.3 11.3 copy-start.6
  502.5 11.1 copy-start.74
  502.5 11.1 copy-start.78
  535.5 5.2 copy-start.85
  535.5 9.0 copy-start.86
  535.5 9.0 copy-start.87
  535.5 9.0 copy-start.90
  539.2 48.6 %copy-start.51 = (bf16[16,512]{1,0:T(8,128)(2,1)S(1)}, bf16[16,512]{1,0:T(8,128)(2,1)}, u32[]{:S(2)}) copy-start(bf16[16,512]{1,0:T(8,128)(2,1)} %copy-done.50) | copy-start | bytes 49156
  539.2 50.3 %copy-start.3 = (bf16[64,64,128]{2,1,0:T(8,128)(2,1)S(1)}, bf16[64,64,128]{2,1,0:T(8,128)(2,1)}, u32[]{:S(2)}) copy-start(bf16[64,64,128]{2,1,0:T(8,128)(2,1)} %copy-done.2) | copy-start | bytes 3145732
  539.2 50.3 %copy-start.17 = (bf16[147456]{0:T(1024)(128)(2,1)S(1)}, bf16[147456]{0:T(1024)(128)(2,1)}, u32[]{:S(2)}) copy-start(bf16[147456]{0:T(1024)(128)(2,1)} %get-tuple-element.236) | copy-start | bytes 884740
  596.2 71.0 %copy-start.19 = (bf16[1,32,32,128]{3,2,1,0:T(8,128)(2,1)}, bf16[1,32,32,128]{3,2,1,0:T(8,128)(2,1)S(1)}, u32[]{:S(2)}) copy-start(bf16[1,32,32,128]{3,2,1,0:T(8,128)(2,1)S(1)} %slice.1024) | copy-start | bytes 786436
  597.1 70.4 %copy-start.21 = (bf16[1,32,32,128]{3,2,1,0:T(8,128)(2,1)}, bf16[1,32,32,128]{3,2,1,0:T(8,128)(2,1)S(1)}, u32[]{:S(2)}) copy-start(bf16[1,32,32,128]{3,2,1,0:T(8,128)(2,1)S(1)} %slice.1022) | copy-start | bytes 786436
  636.1 22.4 %copy-start.52 = (f32[2,4,8,128]{3,2,1,0:T(8,128)S(1)}, f32[2,4,8,128]{3,2,1,0:T(8,128)}, u32[]{:S(2)}) copy-start(f32[2,4,8,128]{3,2,1,0:T(8,128)} %convolution_bitcast_fusion.31) | copy-start | bytes 98308
  659.6 4.2 copy-start.39
  659.6 4.2 copy-start.44
  659.6 4.2 copy-start.45
  716.2 653.2 %copy-start.40 = (f32[4,4,4608]{2,1,0:T(4,128)S(1)}, f32[4,4,4608]{2,1,0:T(4,128)}, u32[]{:S(2)}) copy-start(f32[4,4,4608]{2,1,0:T(4,128)} %param.45) | copy-start | bytes 884740
  (64 other events, 132.4 us)
Sparse Core Ops, SparseCore 0:
  11.6 57.0 all-gather.2
  709.6 657.4 reduce-scatter.3
where the time goes:
time: 1390 us; the launch traced here: 1380 us
  waiting for transfers between devices  649 us (47%)
  local copies, waits for them, and re-layouts  309 us (22%)
  matrix products  139 us (10%)
  other arithmetic  137 us (10%)
  blocking collectives  129 us (9%)
  between operations  16.5 us (1%)
    unnamed x3, waiting for transfers between devices  649 us
    scatter-add x15, local copies, waits for them, and re-layouts, conv_back_taps(): grad_pad = grad_pad.at[:, tap_row:tap_row + H:stride, tap_col:tap_col + W...  143 us
    dot_general x27, matrix products, conv_back_taps(): jnp.einsum('bhwo,io->bhwi', upstream, kernel[tap_row, tap_col], preferred...  74.4 us
    unnamed x21, other arithmetic  64.8 us
    unnamed x212, local copies, waits for them, and re-layouts  63.5 us
    slice x9, local copies, waits for them, and re-layouts, conv_taps(): window = padded[:, tap_row:tap_row + H:stride, tap_col:tap_col + W:stride]  60.9 us
    all_gather x1, blocking collectives, per_device(): lax.all_gather(dense_own, ('dp', 'fsdp'), axis=0, tiled=True)  48.8 us
    unnamed x1, blocking collectives  42.1 us
  transfers between devices with their start and end apart: 2, of which 1 were waited for; matrix products, arithmetic and copies ran while one was open for 2% of the time, Pallas kernels for 0%

commit v1 on v0

v1 whole, which is shorter than its diff:
```python
import jax
import jax.numpy as jnp
from jax import lax
from jax.experimental import pallas as pl
from jax.experimental.pallas import tpu as pltpu
from jax.sharding import PartitionSpec as P

C = 128
EMB = 512
GROUPS = 8
H = 64
W = 64
NCLASS = 16
STEP = 10
TAPS = 9
CELLS = H * W
PER_GROUP = CELLS * (C // GROUPS)
TABLE_ROWS = NCLASS * EMB // C
M1_ROWS = EMB * EMB // C
M2_ROWS = EMB * 2
MLP_ROWS = TABLE_ROWS + M1_ROWS + M2_ROWS
KERNEL_ROWS = TAPS * C
AXES = ("dp", "fsdp")

beta_one = 0.9
beta_two = 0.999
adam_eps = 1e-08
ema_decay = 0.99
norm_eps = 1e-05
rate_conv = 0.08
rate_table = 0.6
rate_dense = 0.1
rate_small = 0.15
decay_weights = 0.01

f32 = jnp.float32
bf16 = jnp.bfloat16
NN = (((1,), (0,)), ((), ()))
NT = (((1,), (1,)), ((), ()))
TN = (((0,), (0,)), ((), ()))
VMEM_LIMIT = 58 << 20
R = 8
Q = 8


def mm(a, b, dims=NN):
    return lax.dot_general(a, b, dims, preferred_element_type=f32)


def three(v):
    high = v.astype(bf16)
    rest = v - high.astype(f32)
    mid = rest.astype(bf16)
    return high, mid, (rest - mid.astype(f32)).astype(bf16)


def group_sum(rows):
    lane = lax.broadcasted_iota(jnp.int32, rows.shape, 1)
    for step in (1, 2, 4, 8):
        up = pltpu.roll(rows, C - step, 1)
        down = pltpu.roll(rows, step, 1)
        rows = rows + jnp.where((lane & step) == 0, up, down)
    return rows


def fold(values):
    return jnp.sum(values.reshape(-1, 8, values.shape[-1]), axis=0)


def total_of(partial):
    return jnp.broadcast_to(jnp.sum(partial, axis=0, keepdims=True), partial.shape)


def one(rows):
    return rows[0:1].reshape(1, 1, C)


def normal_cdf(v):
    return 0.5 * (1.0 + lax.erf(v * 0.7071067811865476))


def gelu_slope(v, prob):
    return prob + v * (jnp.exp(-0.5 * v * v) * 0.3989422804014327)


def put_windows(win_ref, row, values):
    rows = values.shape[0]
    place = lax.broadcasted_iota(jnp.int32, values.shape, 1)
    left = jnp.where(place == 0, 0.0, pltpu.roll(values, 1, 1))
    right = jnp.where(place == W - 1, 0.0, pltpu.roll(values, W - 1, 1))
    win_ref[pl.ds(row + 1, rows), :, 0:C] = left.astype(bf16)
    win_ref[pl.ds(row + 1, rows), :, C : 2 * C] = values.astype(bf16)
    win_ref[pl.ds(row + 1, rows), :, 2 * C : 3 * C] = right.astype(bf16)


def clear_edges(win_ref):
    edge = jnp.zeros((1,) + tuple(win_ref.shape[1:]), win_ref.dtype)
    win_ref[0:1] = edge
    win_ref[H + 1 : H + 2] = edge


def pair_forward(pair_ref, kernel_ref):
    zero = jnp.zeros((3 * C, C), bf16)
    pair_ref[0 : TAPS * C, 0:C] = kernel_ref[...]
    pair_ref[TAPS * C :, 0:C] = zero
    pair_ref[0 : 3 * C, C:] = zero
    pair_ref[3 * C :, C:] = kernel_ref[...]


def flip(block):
    return jnp.transpose(block.astype(f32)).astype(bf16)


def pair_backward(pair_ref, kernel_ref):
    zero = jnp.zeros((3 * C, C), bf16)
    pair_ref[TAPS * C :, 0:C] = zero
    pair_ref[0 : 3 * C, C:] = zero
    for tap in range(TAPS):
        block = flip(kernel_ref[(TAPS - 1 - tap) * C : (TAPS - tap) * C, :])
        pair_ref[tap * C : (tap + 1) * C, 0:C] = block
        pair_ref[(tap + 3) * C : (tap + 4) * C, C:] = block


def pair_conv(win_ref, pair_ref, first):
    view = win_ref.reshape(H // 2 + 1, 2, W, 3 * C)
    taken = [view[pl.ds(first + t // 2, Q), t % 2] for t in range(4)]
    stacked = jnp.concatenate(taken, axis=-1).reshape(Q * W, 12 * C)
    return mm(stacked, pair_ref[...]).reshape(Q, W, 2 * C)


def pairs_of(ref, first):
    view = ref.reshape(H // 2, 2, W, C)
    return [view.at[pl.ds(first, Q), parity] for parity in range(2)]


def kernel_grad(act_ref, win_ref, out_ref):
    left = act_ref[1 : H + 1, :, C : 2 * C].reshape(CELLS, C)
    right = jnp.concatenate([win_ref[t : t + H] for t in range(3)], axis=-1)
    got = mm(left, right.reshape(CELLS, TAPS * C), TN)
    for t in range(TAPS):
        out_ref[t * C : (t + 1) * C, :] = got[:, (TAPS - 1 - t) * C : (TAPS - t) * C]


def block_body(
    cls_ref, x_ref, cot_ref, k1_ref, k2_ref, kd0_ref, kd1_ref, small_ref, table_ref, m1_ref, m2_ref,
    out_ref, dx_ref, gk1_ref, gk2_ref, gkd0_ref, gkd1_ref, gsmall_ref, gclass_ref,
    a1w, a2w, tw, rw, cw, c1, g1p, g2p, drf, pair,
):
    def small_row(index):
        return jnp.broadcast_to(small_ref[index : index + 1, :].astype(f32), (8, C))

    def small_run(first, count):
        return jnp.concatenate([small_ref[first + i : first + i + 1, :].astype(f32) for i in range(count)], axis=1)

    gain1, bias1, cb1, gain2, bias2, cb2 = [small_row(i) for i in range(6)]
    zero8 = jnp.zeros((8, C), f32)

    hidden = mm(table_ref[...], m1_ref[...]) + small_run(8, 4)
    act = hidden * normal_cdf(hidden)
    ss = sum(mm(part, m2_ref[...]) for part in three(act)) + small_run(12, 2)
    mine = lax.broadcasted_iota(jnp.int32, (NCLASS, 2 * C), 0) == cls_ref[0]
    chosen = jnp.sum(jnp.where(mine, ss, 0.0), axis=0, keepdims=True)
    scale = jnp.broadcast_to(1.0 + chosen[:, :C], (8, C))
    shift = jnp.broadcast_to(chosen[:, C:], (8, C))

    def read_x(i):
        return x_ref[pl.ds(i * R, R)].astype(f32)

    total = lax.fori_loop(0, H // R, lambda i, s: s + fold(read_x(i)), zero8)
    mean1 = group_sum(total_of(total)) * (1.0 / PER_GROUP)

    def square_x(i, s):
        d = read_x(i) - one(mean1)
        return s + fold(d * d)

    var1 = group_sum(total_of(lax.fori_loop(0, H // R, square_x, zero8))) * (1.0 / PER_GROUP)
    rs1 = lax.rsqrt(var1 + norm_eps)
    slope1 = rs1 * (1.0 + gain1)
    clear_edges(a1w)

    def front1(i, carry):
        v = (read_x(i) - one(mean1)) * one(slope1) + one(bias1)
        prob = normal_cdf(v)
        put_windows(a1w, i * R, v * prob)
        g1p[pl.ds(i * R, R)] = gelu_slope(v, prob)
        return carry

    lax.fori_loop(0, H // R, front1, 0)

    pair_forward(pair, k1_ref)

    def conv1(i, s):
        got = pair_conv(a1w, pair, i * Q)
        for parity, place in enumerate(pairs_of(c1, i * Q)):
            value = got[..., parity * C : (parity + 1) * C] + one(cb1)
            place[...] = value
            s = s + fold(value)
        return s

    centre = total_of(lax.fori_loop(0, H // 2 // Q, conv1, zero8)) * (1.0 / CELLS)

    def square_c(i, s):
        d = c1[pl.ds(i * R, R)] - one(centre)
        return s + fold(d * d)

    spread = total_of(lax.fori_loop(0, H // R, square_c, zero8)) * (1.0 / CELLS)

    centre_s = centre * scale + shift
    mean2 = group_sum(centre_s) * (GROUPS / C)
    off = centre_s - mean2
    var2 = group_sum(spread * scale * scale + off * off) * (GROUPS / C)
    rs2 = lax.rsqrt(var2 + norm_eps)

    def unit2(values):
        return (values * one(scale) + one(shift - mean2)) * one(rs2)

    clear_edges(a2w)

    def front2(i, carry):
        v = unit2(c1[pl.ds(i * R, R)]) * one(1.0 + gain2) + one(bias2)
        prob = normal_cdf(v)
        put_windows(a2w, i * R, v * prob)
        g2p[pl.ds(i * R, R)] = gelu_slope(v, prob)
        return carry

    lax.fori_loop(0, H // R, front2, 0)

    pair_forward(pair, k2_ref)

    def conv2(i, carry):
        got = pair_conv(a2w, pair, i * Q)
        for parity, (place, source) in enumerate(zip(pairs_of(drf, i * Q), pairs_of(x_ref, i * Q))):
            r = source[...].astype(f32) + (got[..., parity * C : (parity + 1) * C] + one(cb2))
            place[...] = r.astype(bf16).astype(f32)
        return carry

    lax.fori_loop(0, H // 2 // Q, conv2, 0)
    rw[0:1] = jnp.zeros((1, W // 2, 3 * C), bf16)

    def split(i, carry):
        even = drf[pl.ds(i * R, R), pl.ds(0, W // 2, 2), :]
        odd = drf[pl.ds(i * R, R), pl.ds(1, W // 2, 2), :]
        place = lax.broadcasted_iota(jnp.int32, odd.shape, 1)
        before = jnp.where(place == 0, 0.0, pltpu.roll(odd, 1, 1))
        rw[pl.ds(i * R + 1, R), :, 0:C] = before.astype(bf16)
        rw[pl.ds(i * R + 1, R), :, C : 2 * C] = even.astype(bf16)
        rw[pl.ds(i * R + 1, R), :, 2 * C :] = odd.astype(bf16)
        return carry

    lax.fori_loop(0, H // R, split, 0)

    def down_rows(first, rows):
        view = rw.reshape(H // 2 + 1, 2, W // 2, 3 * C)
        taken = [view[pl.ds(first + t // 2, rows), t % 2] for t in range(3)]
        return jnp.concatenate(taken, axis=-1).reshape(rows * W // 2, TAPS * C)

    kd = jnp.concatenate([kd0_ref[...], kd1_ref[...]], axis=1)
    bias_down = small_run(6, 2)

    def down(i, carry):
        got = mm(down_rows(i * Q, Q), kd) + bias_down
        out_ref[pl.ds(i * Q, Q)] = got.reshape(Q, W // 2, 2 * C).astype(bf16)
        return carry

    lax.fori_loop(0, H // 2 // Q, down, 0)
    @pl.when(cls_ref[0] >= 0)
    def _():
        gkd = mm(down_rows(0, H // 2), cot_ref[...].reshape(CELLS // 4, 2 * C), TN)
        gkd0_ref[...] = gkd[:, :C]
        gkd1_ref[...] = gkd[:, C:]


    cw[H // 2 : H // 2 + 1] = jnp.zeros((1, W // 2, 4 * C), bf16)

    def cot_windows(i, s):
        values = cot_ref[pl.ds(i * Q, Q)].astype(f32)
        place = lax.broadcasted_iota(jnp.int32, values.shape, 1)
        after = jnp.where(place == W // 2 - 1, 0.0, pltpu.roll(values, W // 2 - 1, 1))
        cw[pl.ds(i * Q, Q), :, 0 : 2 * C] = values.astype(bf16)
        cw[pl.ds(i * Q, Q), :, 2 * C :] = after.astype(bf16)
        return s + fold(values)

    gdb = total_of(lax.fori_loop(0, H // 2 // Q, cot_windows, jnp.zeros((8, 2 * C), f32)))

    def tap(i, j):
        return flip(kd[(3 * i + j) * C : (3 * i + j + 1) * C, :])

    none = jnp.zeros((2 * C, C), bf16)
    even_rows = jnp.concatenate([
        jnp.concatenate([tap(1, 1), none], axis=0),
        jnp.concatenate([tap(1, 2), tap(1, 0)], axis=0),
    ], axis=1)
    odd_rows = jnp.concatenate([
        jnp.concatenate([tap(2, 1), none, tap(0, 1), none], axis=0),
        jnp.concatenate([tap(2, 2), tap(2, 0), tap(0, 2), tap(0, 0)], axis=0),
    ], axis=1)

    def back_down(i, s):
        rows = jnp.concatenate([cw[pl.ds(i * Q, Q)], cw[pl.ds(i * Q + 1, Q)]], axis=-1)
        rows = rows.reshape(Q * W // 2, 8 * C)
        view = drf.reshape(H // 2, 2, W, C)
        for parity, got in enumerate((mm(rows[:, : 4 * C], even_rows), mm(rows, odd_rows))):
            got = got.reshape(Q, W // 2, 2 * C)
            view[pl.ds(i * Q, Q), parity, pl.ds(0, W // 2, 2), :] = got[..., :C]
            view[pl.ds(i * Q, Q), parity, pl.ds(1, W // 2, 2), :] = got[..., C:]
        return s

    lax.fori_loop(0, H // 2 // Q, back_down, 0)

    def pull(kernel_ref, slope_ref, units):
        pair_backward(pair, kernel_ref)

        def step(i, s):
            got = pair_conv(tw, pair, i * Q)
            for parity, (place, unit) in enumerate(zip(pairs_of(slope_ref, i * Q), units(i))):
                dn = got[..., parity * C : (parity + 1) * C] * place[...]
                place[...] = dn
                s = s[0] + fold(dn), s[1] + fold(dn * unit)
            return s

        got = lax.fori_loop(0, H // 2 // Q, step, (zero8, zero8))
        return total_of(got[0]), total_of(got[1])

    clear_edges(tw)

    def t2_windows(i, s):
        values = drf[pl.ds(i * R, R)]
        put_windows(tw, i * R, values)
        return s + fold(values)

    gcb2 = total_of(lax.fori_loop(0, H // R, t2_windows, zero8))
    pl.when(cls_ref[0] >= 0)(lambda: kernel_grad(a2w, tw, gk2_ref))
    gb2, gg2 = pull(k2_ref, g2p, lambda i: [unit2(ref[...]) for ref in pairs_of(c1, i * Q)])
    mean_du2 = group_sum(gb2 * (1.0 + gain2)) * (1.0 / PER_GROUP)
    mean_duu2 = group_sum(gg2 * (1.0 + gain2)) * (1.0 / PER_GROUP)

    def t1_windows(i, s):
        values = c1[pl.ds(i * R, R)]
        du = g2p[pl.ds(i * R, R)] * one(1.0 + gain2)
        ds = (du - one(mean_du2) - unit2(values) * one(mean_duu2)) * one(rs2)
        put_windows(tw, i * R, ds * one(scale))
        return s[0] + fold(ds * values), s[1] + fold(ds)

    gsc, gsh = lax.fori_loop(0, H // R, t1_windows, (zero8, zero8))
    gsc, gsh = total_of(gsc), total_of(gsh)
    pl.when(cls_ref[0] >= 0)(lambda: kernel_grad(a1w, tw, gk1_ref))

    def unit1(ref):
        return (ref[...].astype(f32) - one(mean1)) * one(rs1)

    gb1, gg1 = pull(k1_ref, g1p, lambda i: [unit1(ref) for ref in pairs_of(x_ref, i * Q)])
    mean_du1 = group_sum(gb1 * (1.0 + gain1)) * (1.0 / PER_GROUP)
    mean_duu1 = group_sum(gg1 * (1.0 + gain1)) * (1.0 / PER_GROUP)

    def finish(i, carry):
        du = g1p[pl.ds(i * R, R)] * one(1.0 + gain1)
        unit = unit1(x_ref.at[pl.ds(i * R, R)])
        dx = (du - one(mean_du1) - unit * one(mean_duu1)) * one(rs1)
        dx_ref[pl.ds(i * R, R)] = (drf[pl.ds(i * R, R)] + dx).astype(bf16)
        return carry

    lax.fori_loop(0, H // R, finish, 0)

    rows = [gg1, gb1, gsh * scale, gg2, gb2, gcb2, gdb[:, :C], gdb[:, C:]]
    for index, row in enumerate(rows):
        gsmall_ref[index : index + 1, :] = row[0:1]
    both = jnp.concatenate([gsc[0:1], gsh[0:1]], axis=1)
    gclass_ref[...] = jnp.where(mine, both, 0.0)


def vmem_specs(count):
    return [pl.BlockSpec(memory_space=pltpu.VMEM)] * count


def run_block(class_ids, x, cot, kernels, small, mlp):
    shapes = (
        [jax.ShapeDtypeStruct((H // 2, W // 2, 2 * C), bf16), jax.ShapeDtypeStruct((H, W, C), bf16)]
        + [jax.ShapeDtypeStruct((KERNEL_ROWS, C), f32)] * 4
        + [jax.ShapeDtypeStruct((8, C), f32), jax.ShapeDtypeStruct((NCLASS, 2 * C), f32)]
    )
    windows = pltpu.VMEM((H + 2, W, 3 * C), bf16)
    plane = pltpu.VMEM((H, W, C), f32)
    return pl.pallas_call(
        block_body,
        out_shape=shapes,
        in_specs=[pl.BlockSpec(memory_space=pltpu.SMEM)] + vmem_specs(10),
        out_specs=vmem_specs(8),
        scratch_shapes=[
            windows,
            windows,
            windows,
            pltpu.VMEM((H + 2, W // 2, 3 * C), bf16),
            pltpu.VMEM((H // 2 + 1, W // 2, 4 * C), bf16),
            plane,
            plane,
            plane,
            plane,
            pltpu.VMEM((12 * C, 2 * C), bf16),
        ],
        compiler_params=pltpu.CompilerParams(vmem_limit_bytes=VMEM_LIMIT),
        name="block",
    )(class_ids, x, cot, *kernels, small, *mlp)


def mlp_body(table_ref, m1_ref, m2_ref, small_ref, dss_ref, out_ref, tail_ref):
    def small_run(first, count):
        return jnp.concatenate([small_ref[first + i : first + i + 1, :].astype(f32) for i in range(count)], axis=1)

    table = table_ref[...]
    hidden = mm(table, m1_ref[...]) + small_run(8, 4)
    prob = normal_cdf(hidden)
    dss = dss_ref[...]

    def put(first, values):
        parts = values.shape[1] // C
        for part in range(parts):
            out_ref[pl.ds(first + part, values.shape[0], parts), :] = values[:, part * C : (part + 1) * C]

    def outer(left, right):
        lefts = [a for k, a in enumerate(left) for b in right[: 3 - k]]
        rights = [b for k, a in enumerate(left) for b in right[: 3 - k]]
        return mm(jnp.concatenate(lefts, axis=0), jnp.concatenate(rights, axis=0), TN)

    def back(values, weights):
        return sum(mm(part, weights, NT) for part in three(values))

    dp = back(dss, m2_ref[...]) * gelu_slope(hidden, prob)
    put(0, back(dp, m1_ref[...]))
    put(TABLE_ROWS, outer([table], three(dp)))
    put(TABLE_ROWS + M1_ROWS, outer(three(hidden * prob), three(dss)))
    ge1 = jnp.sum(dp, axis=0, keepdims=True)
    ge2 = jnp.sum(dss, axis=0, keepdims=True)
    for i in range(4):
        tail_ref[i : i + 1, :] = ge1[:, i * C : (i + 1) * C]
    for i in range(2):
        tail_ref[4 + i : 5 + i, :] = ge2[:, i * C : (i + 1) * C]
    tail_ref[6:8, :] = jnp.zeros((2, C), f32)


def run_mlp(mlp, small, dss):
    return pl.pallas_call(
        mlp_body,
        out_shape=[jax.ShapeDtypeStruct((MLP_ROWS, C), f32), jax.ShapeDtypeStruct((8, C), f32)],
        in_specs=vmem_specs(5),
        out_specs=vmem_specs(2),
        compiler_params=pltpu.CompilerParams(vmem_limit_bytes=VMEM_LIMIT),
        name="mlp_grad",
    )(*mlp, small, dss)


def adam_update(state_stack, gradient, step_rate, weight_decay):
    weight = state_stack[0]
    first_moment = beta_one * state_stack[1] + (1.0 - beta_one) * gradient
    second = beta_two * state_stack[2] + (1.0 - beta_two) * gradient * gradient
    first_hat = first_moment / (1.0 - beta_one**STEP)
    second_hat = second / (1.0 - beta_two**STEP)
    weight_new = weight - step_rate * (
        first_hat / (jnp.sqrt(second_hat) + adam_eps) + weight_decay * weight
    )
    average = ema_decay * state_stack[3] + (1.0 - ema_decay) * weight_new
    return (jnp.stack([weight_new, first_moment, second, average]), weight_new.astype(bf16))


def exchange(values, axis, size, bit):
    return lax.ppermute(values, axis, [(i, i ^ bit) for i in range(size)])


def stage_list(sizes):
    (outer, outer_size), (inner, inner_size) = sizes
    inner_bits = [1 << k for k in reversed(range(inner_size.bit_length() - 1))]
    outer_bits = [1 << k for k in range(outer_size.bit_length() - 1)]
    inner_stages = [(inner, inner_size, bit, bit) for bit in inner_bits]
    outer_stages = [(outer, outer_size, bit, bit * inner_size) for bit in outer_bits]
    return inner_stages[:-1] + outer_stages + inner_stages[-1:]


def relative(sizes, position):
    order = [0]
    for _, _, _, bit in stage_list(sizes):
        order = order + [k ^ bit for k in order]
    return jnp.asarray(order, jnp.int32) ^ position


def inverse(sizes, position):
    order = [0]
    for _, _, _, bit in stage_list(sizes):
        order = order + [k ^ bit for k in order]
    place = [order.index(k) for k in range(len(order))]
    return jnp.asarray(place, jnp.int32)[jnp.arange(len(order), dtype=jnp.int32) ^ position]


def gather_ring(own, sizes):
    parts = own[None]
    for axis, size, bit, _ in stage_list(sizes):
        parts = jnp.concatenate([parts, exchange(parts, axis, size, bit)])
    return parts


def reduce_ring(blocks, extra, sizes):
    rows = extra.shape[0]
    for axis, size, bit, _ in reversed(stage_list(sizes)):
        half = blocks.shape[0] // 2
        high = extra.astype(bf16)
        low = (extra - high.astype(f32)).astype(bf16)
        width = blocks.shape[1]
        sent = jnp.concatenate([blocks[half:].astype(bf16).reshape(-1, C), high, low])
        got = exchange(sent, axis, size, bit)
        blocks = blocks[:half] + got[: half * width].reshape(half, width, C).astype(f32)
        extra = (
            extra
            + got[half * width : half * width + rows].astype(f32)
            + got[half * width + rows :].astype(f32)
        )
    return blocks[0], extra


def split_mlp(dense):
    return [
        dense[:TABLE_ROWS].reshape(NCLASS, EMB),
        dense[TABLE_ROWS : TABLE_ROWS + M1_ROWS].reshape(EMB, EMB),
        dense[TABLE_ROWS + M1_ROWS :].reshape(EMB, 2 * C),
    ]


def gather_all(sizes, position, conv_own, dense_own, small_own):
    conv_len, dense_len, small_len = conv_own.shape[1], dense_own.shape[0], small_own.shape[0]
    if not whole_rows(sizes, conv_len, dense_len):
        conv = lax.all_gather(conv_own, AXES, axis=1, tiled=True)
        dense = lax.all_gather(dense_own, AXES, axis=0, tiled=True)
        small = lax.all_gather(small_own, AXES, axis=0, tiled=True)
        return [conv[k].reshape(KERNEL_ROWS, C) for k in range(4)], dense.reshape(MLP_ROWS, C), small.reshape(-1, C)
    conv_rows, dense_rows = conv_len // C, dense_len // C
    own_rows = 4 * conv_rows + dense_rows
    own = jnp.concatenate(
        [
            conv_own.reshape(4 * conv_rows, C),
            dense_own.reshape(dense_rows, C),
            jnp.pad(small_own, (0, C - small_len)).reshape(1, C),
        ]
    )
    gathered = gather_ring(own, sizes)[inverse(sizes, position)]
    kernels = [
        gathered[:, k * conv_rows : (k + 1) * conv_rows].reshape(KERNEL_ROWS, C) for k in range(4)
    ]
    dense = gathered[:, 4 * conv_rows : own_rows].reshape(MLP_ROWS, C)
    return kernels, dense, gathered[:, own_rows, :small_len].reshape(-1, C)


def reduce_all(sizes, position, grads, extra, conv_len, dense_len):
    if not whole_rows(sizes, conv_len, dense_len):
        flat = jnp.stack([g.reshape(-1) for g in grads])
        return lax.psum_scatter(flat, AXES, scatter_dimension=1, tiled=True), lax.psum(extra, AXES)
    conv_rows = conv_len // C
    blocks = jnp.concatenate([g.reshape(-1, conv_rows, C) for g in grads], axis=1)
    red, extra = reduce_ring(blocks[relative(sizes, position)], extra, sizes)
    return red.reshape(4, conv_len), extra


def whole_rows(sizes, conv_len, dense_len):
    return conv_len % C == 0 and dense_len % C == 0 and all(n & (n - 1) == 0 for _, n in sizes)


def per_device(sizes, samples, cotangent, class_ids, conv_state, mlp_state, small_state):
    position = lax.axis_index(AXES)
    conv_len, dense_len, small_len = conv_state.shape[2], mlp_state.shape[1], small_state.shape[1]
    kernels, dense, small = gather_all(
        sizes, position, conv_state[0].astype(bf16), mlp_state[0].astype(bf16), small_state[0].astype(bf16)
    )
    mlp = split_mlp(dense)
    out, dx, gk1, gk2, gkd0, gkd1, gsmall, gclass = run_block(
        class_ids, samples[0], cotangent[0], kernels, small, mlp
    )
    extra = jnp.concatenate([gsmall, gclass.reshape(2 * NCLASS, C)])
    conv_red, extra = reduce_all(sizes, position, (gk1, gk2, gkd0, gkd1), extra, conv_len, dense_len)
    dense_grad, tail = run_mlp(mlp, small, extra[8:].reshape(NCLASS, 2 * C))
    dense_red = lax.dynamic_slice_in_dim(dense_grad.reshape(-1), position * dense_len, dense_len)
    small_red = lax.dynamic_slice_in_dim(
        jnp.concatenate([extra[:8], tail]).reshape(-1), position * small_len, small_len
    )
    flat_index = position * dense_len + jnp.arange(dense_len, dtype=jnp.int32)
    dense_rate = jnp.where(flat_index < NCLASS * EMB, rate_table, rate_dense)
    conv_new, conv_copy = adam_update(conv_state, conv_red, rate_conv, decay_weights)
    mlp_new, mlp_copy = adam_update(mlp_state, dense_red, dense_rate, decay_weights)
    small_new, small_copy = adam_update(small_state, small_red, rate_small, 0.0)
    return (out[None], dx[None], conv_new, mlp_new, small_new, conv_copy, mlp_copy, small_copy)


def solution(mesh):
    sizes = tuple((axis, mesh.shape[axis]) for axis in AXES)

    def body(*args):
        return per_device(sizes, *args)

    return jax.shard_map(
        body,
        mesh=mesh,
        in_specs=(
            P(AXES, None, None, None),
            P(AXES, None, None, None),
            P(AXES),
            P(None, None, AXES),
            P(None, AXES),
            P(None, AXES),
        ),
        out_specs=(
            P(AXES, None, None, None),
            P(AXES, None, None, None),
            P(None, None, AXES),
            P(None, AXES),
            P(None, AXES),
            P(None, AXES),
            P(AXES),
            P(AXES),
        ),
        check_vma=False,
    )
```

time: 1390 us -> 133 us (0.10)
  waiting for transfers between devices: 649 us -> 37 us
  local copies, waits for them, and re-layouts: 309 us -> 30 us
  matrix products: 139 us -> 0 us
  blocking collectives: 129 us -> 0 us
  other arithmetic: 137 us -> 8.77 us
  Pallas kernels: 0 us -> 35.6 us
  starting transfers between devices: 0.08 us -> 19.4 us
  between operations: 16.5 us -> 1.75 us
    unnamed x3 -> x0, waiting for transfers between devices: 649 us -> none
    scatter-add x15 -> x0, local copies, waits for them, and re-layouts: 143 us -> none  [conv_back_taps(): grad_pad = grad_pad.at[:, tap_row:tap_row + H:stride, tap_col:tap_col + W...]
    dot_general x88 -> x0, matrix products: 139 us -> none  [the longest x27 74.4 us: conv_back_taps(): jnp.einsum('bhwo,io->bhwi', upstream, kernel[tap_row, tap_col], preferred...]
    slice x21 -> x20, local copies, waits for them, and re-layouts: 72.8 us -> 3.73 us  [the longest x4 1.57 us: reduce_ring(): blocks[half:].astype(bf16).reshape(-1, C)]
    unnamed x21 -> x1, other arithmetic: 64.8 us -> 0.01 us
    unnamed x212 -> x27, local copies, waits for them, and re-layouts: 63.5 us -> 2.75 us
    all_gather x1 -> x0, blocking collectives: 48.8 us -> none  [per_device(): lax.all_gather(dense_own, ('dp', 'fsdp'), axis=0, tiled=True)]
    reduce_sum x22 -> x0, other arithmetic: 43.5 us -> none  [the longest x2 16 us: group_norm(): return scaled * (1.0 + offset_gain) + offset_bias]
  transfers between devices with their start and end apart: 2 -> 10, of which waited for: 1 -> 10; matrix products, arithmetic and copies ran while one was open for 2% -> 3% of each run, Pallas kernels for 0% -> 0%
where the time goes in v1:
time: 133 us; the launch traced here: 132 us
  waiting for transfers between devices  37 us (28%)
  Pallas kernels  35.6 us (27%)
  local copies, waits for them, and re-layouts  30 us (23%)
  starting transfers between devices  19.4 us (15%)
  other arithmetic  8.77 us (7%)
  between operations  1.75 us (1%)
    ppermute x10, waiting for transfers between devices, exchange(): return lax.ppermute(values, axis, [(i, i ^ bit) for i in range(size)])  37 us
    pallas_call x1, Pallas kernels, run_block(): pl.pallas_call(block_body, out_shape=shapes, in_specs=[pl.BlockSpec(memor...  32.1 us
    ppermute x10, starting transfers between devices, exchange(): return lax.ppermute(values, axis, [(i, i ^ bit) for i in range(size)])  19.4 us
    reshape x4, local copies, waits for them, and re-layouts, reduce_all(): g.reshape(-1, conv_rows, C)  4.91 us
    reshape x4, local copies, waits for them, and re-layouts, gather_all(): gathered[:, k * conv_rows:(k + 1) * conv_rows].reshape(KERNEL_ROWS, C)  4.07 us
    pallas_call x1, Pallas kernels, run_mlp(): pl.pallas_call(mlp_body, out_shape=[jax.ShapeDtypeStruct((MLP_ROWS, C), f...  3.45 us
    convert_element_type x3, other arithmetic, adam_update(): weight_new.astype(bf16)  2.91 us
    unnamed x27, local copies, waits for them, and re-layouts  2.75 us
  transfers between devices with their start and end apart: 10, of which 10 were waited for; matrix products, arithmetic and copies ran while one was open for 3% of the time, Pallas kernels for 0%

profile of v1, /device:TPU:0, one launch (start us, length us, event | category | flops | bytes accessed | tf_op | source)
XLA Modules:
  0.0 132.4 jit_solution(13484634983281949274)
XLA Ops:
  1.6 1.1 convert_reduce_fusion
  3.3 4.1 %collective-permute-start = (bf16[1,243,128]{2,1,0:T(8,128)(2,1)S(1)}, bf16[1,243,128]{2,1,0:T(8,128)(2,1)S(1)}, u32[]{:S(2)}, u32[]{:S(2)}) collective-permute-start(bf16[1,243,128]{2,1,0:T(8,128)(2,1)S(1)} %get-tuple-element.57), channel_id=1, source_target_pairs={{0,4},{1,5},{2,6},{3,7},{4,0},{5,1},{6,2},{7,3},{8,12},{9,13},{10,... | collective-permute-start | bytes 186632 | tf_op jit(solution)/shard_map/ppermute | solution.py:465
  7.4 3.6 %collective-permute-done = bf16[1,243,128]{2,1,0:T(8,128)(2,1)S(1)} collective-permute-done((bf16[1,243,128]{2,1,0:T(8,128)(2,1)S(1)}, bf16[1,243,128]{2,1,0:T(8,128)(2,1)S(1)}, u32[]{:S(2)}, u32[]{:S(2)}) %collective-permute-start) | collective-permute-done | bytes 62240 | tf_op jit(solution)/shard_map/ppermute | solution.py:465
  11.7 4.4 %collective-permute-done.1 = bf16[2,243,128]{2,1,0:T(8,128)(2,1)S(1)} collective-permute-done((bf16[2,243,128]{2,1,0:T(8,128)(2,1)S(1)}, bf16[2,243,128]{2,1,0:T(8,128)(2,1)S(1)}, u32[]{:S(2)}, u32[]{:S(2)}) %collective-permute-start.1) | collective-permute-done | bytes 124448 | tf_op jit(solution)/shard_map/ppermute | solution.py:465
  16.1 1.8 %collective-permute-start.2 = (bf16[4,243,128]{2,1,0:T(8,128)(2,1)S(1)}, bf16[4,243,128]{2,1,0:T(8,128)(2,1)S(1)}, u32[]{:S(2)}, u32[]{:S(2)}) collective-permute-start(bf16[4,243,128]{2,1,0:T(8,128)(2,1)S(1)} %pad_maximum_fusion.5), channel_id=1, source_target_pairs={{0,8},{8,0},{16,24},{24,16},{1,9},{9,1},{17,25},{25,17},{2,10},{10... | collective-permute-start | bytes 746504 | tf_op jit(solution)/shard_map/ppermute | solution.py:465
  17.8 4.6 %collective-permute-done.2 = bf16[4,243,128]{2,1,0:T(8,128)(2,1)S(1)} collective-permute-done((bf16[4,243,128]{2,1,0:T(8,128)(2,1)S(1)}, bf16[4,243,128]{2,1,0:T(8,128)(2,1)S(1)}, u32[]{:S(2)}, u32[]{:S(2)}) %collective-permute-start.2) | collective-permute-done | bytes 248864 | tf_op jit(solution)/shard_map/ppermute | solution.py:465
  22.5 1.8 %collective-permute-start.3 = (bf16[8,243,128]{2,1,0:T(8,128)(2,1)S(1)}, bf16[8,243,128]{2,1,0:T(8,128)(2,1)S(1)}, u32[]{:S(2)}, u32[]{:S(2)}) collective-permute-start(bf16[8,243,128]{2,1,0:T(8,128)(2,1)S(1)} %pad_maximum_fusion.2), channel_id=1, source_target_pairs={{0,16},{8,24},{16,0},{24,8},{1,17},{9,25},{17,1},{25,9},{2,18},{10... | collective-permute-start | bytes 1493000 | tf_op jit(solution)/shard_map/ppermute | solution.py:465
  27.0 5.1 %collective-permute-done.3 = bf16[8,243,128]{2,1,0:T(8,128)(2,1)S(1)} collective-permute-done((bf16[8,243,128]{2,1,0:T(8,128)(2,1)S(1)}, bf16[8,243,128]{2,1,0:T(8,128)(2,1)S(1)}, u32[]{:S(2)}, u32[]{:S(2)}) %collective-permute-start.3) | collective-permute-done | bytes 497696 | tf_op jit(solution)/shard_map/ppermute | solution.py:465
  34.6 1.1 collective-permute-done.4
  35.7 1.2 copy_dynamic-update-slice_fusion
  37.0 2.5 %gather_fusion.1 = bf16[32,243,128]{2,1,0:T(8,128)(2,1)S(1)} fusion(bf16[32,243,128]{2,1,0:T(8,128)(2,1)} %copy_dynamic-update-slice_fusion, s32[1024]{0:T(1024)S(1)} %pad_clamp_fusion.1), kind=kCustom, calls=%fused_computation.1 | custom fusion | bytes 3981440 | tf_op jit(solution)/shard_map/gather | solution.py:541
  39.5 1.1 reshape.184
  40.6 1.0 fusion.27
  41.8 1.1 reshape.186.m1_ref
  44.3 1.7 %reshape.180.k1_ref = bf16[1152,128]{1,0:T(8,128)(2,1)} reshape(bf16[32,36,128]{2,1,0:T(8,128)(2,1)} %get-tuple-element.61) | data formatting | bytes 589824 | tf_op jit(solution)/shard_map/reshape | solution.py:543
  49.1 32.1 %block.1 = (bf16[32,32,256]{2,1,0:T(8,128)(2,1)}, bf16[64,64,128]{2,1,0:T(8,128)(2,1)}, f32[1152,128]{1,0:T(8,128)}, f32[1152,128]{1,0:T(8,128)}, f32[1152,128]{...) custom-call(s32[1]{0:T(128)S(6)} %copy.33.cls_ref, bf16[64,64,128]{2,1,0:T(8,128)(2,1)} %bitcast.91, ...), custom_call_target="tpu_custom_call" | custom-call | tf_op jit(solution)/shard_map/block/pallas_call | solution.py:383
  81.2 1.2 reshape.188
  82.4 1.9 %reshape.189 = f32[32,36,128]{2,1,0:T(8,128)} reshape(f32[1152,128]{1,0:T(8,128)} %get-tuple-element.21) | data formatting | bytes 1179648 | tf_op jit(solution)/shard_map/reshape | solution.py:554
  86.1 1.7 %pad_maximum_fusion = f32[32,144,128]{2,1,0:T(8,128)S(1)} fusion(f32[32,36,128]{2,1,0:T(8,128)} %reshape.191, f32[32,36,128]{2,1,0:T(8,128)} %reshape.190, f32[32,36,128]{2,1,0:T(8,128)} %reshape.189, f32[32,36,128]{2,1,0:T(8,128)S(1)} %reshape.188), kind=kLoop, calls=%fused_computation.3 | loop fusion | flops 1769472 | bytes 4718592 | tf_op jit(solution)/shard_map/concatenate | solution.py:554
  87.8 2.1 %gather_fusion.2 = f32[32,144,128]{2,1,0:T(8,128)} fusion(f32[32,144,128]{2,1,0:T(8,128)S(1)} %pad_maximum_fusion, s32[1024]{0:T(1024)S(1)} %get-tuple-element.70), kind=kCustom, calls=%fused_computation.2 | custom fusion | bytes 4718720 | tf_op jit(solution)/shard_map/gather | solution.py:555
  89.9 1.5 %slice.316 = bf16[16,144,128]{2,1,0:T(8,128)(2,1)S(1)} slice(f32[32,144,128]{2,1,0:T(8,128)} %gather_fusion.2), slice={[16:32], [0:144], [0:128]} | slice | bytes 1179648 | tf_op jit(solution)/shard_map/slice | solution.py:506
  91.7 1.9 %collective-permute-done.5 = bf16[2384,128]{1,0:T(8,128)(2,1)S(1)} collective-permute-done((bf16[2384,128]{1,0:T(8,128)(2,1)S(1)}, bf16[2384,128]{1,0:T(8,128)(2,1)S(1)}, u32[]{:S(2)}, u32[]{:S(2)}) %collective-permute-start.5) | collective-permute-done | bytes 610336 | tf_op jit(solution)/shard_map/ppermute | solution.py:465
  93.9 1.6 %collective-permute-start.6 = (bf16[1232,128]{1,0:T(8,128)(2,1)S(1)}, bf16[1232,128]{1,0:T(8,128)(2,1)S(1)}, u32[]{:S(2)}, u32[]{:S(2)}) collective-permute-start(bf16[1232,128]{1,0:T(8,128)(2,1)S(1)} %pad_maximum_fusion.3), channel_id=1, source_target_pairs={{0,16},{8,24},{16,0},{24,8},{1,17},{9,25},{17,1},{25,9},{2,18},{10... | collective-permute-start | bytes 946184 | tf_op jit(solution)/shard_map/ppermute | solution.py:465
  95.5 8.0 %collective-permute-done.6 = bf16[1232,128]{1,0:T(8,128)(2,1)S(1)} collective-permute-done((bf16[1232,128]{1,0:T(8,128)(2,1)S(1)}, bf16[1232,128]{1,0:T(8,128)(2,1)S(1)}, u32[]{:S(2)}, u32[]{:S(2)}) %collective-permute-start.6) | collective-permute-done | bytes 315424 | tf_op jit(solution)/shard_map/ppermute | solution.py:465
  103.6 1.6 %collective-permute-start.7 = (bf16[656,128]{1,0:T(8,128)(2,1)S(1)}, bf16[656,128]{1,0:T(8,128)(2,1)S(1)}, u32[]{:S(2)}, u32[]{:S(2)}) collective-permute-start(bf16[656,128]{1,0:T(8,128)(2,1)S(1)} %pad_maximum_fusion.7), channel_id=1, source_target_pairs={{0,8},{8,0},{16,24},{24,16},{1,9},{9,1},{17,25},{25,17},{2,10},{10... | collective-permute-start | bytes 503816 | tf_op jit(solution)/shard_map/ppermute | solution.py:465
  105.2 4.0 %collective-permute-done.7 = bf16[656,128]{1,0:T(8,128)(2,1)S(1)} collective-permute-done((bf16[656,128]{1,0:T(8,128)(2,1)S(1)}, bf16[656,128]{1,0:T(8,128)(2,1)S(1)}, u32[]{:S(2)}, u32[]{:S(2)}) %collective-permute-start.7) | collective-permute-done | bytes 167968 | tf_op jit(solution)/shard_map/ppermute | solution.py:465
  109.3 2.1 %collective-permute-start.8 = (bf16[368,128]{1,0:T(8,128)(2,1)S(1)}, bf16[368,128]{1,0:T(8,128)(2,1)S(1)}, u32[]{:S(2)}, u32[]{:S(2)}) collective-permute-start(bf16[368,128]{1,0:T(8,128)(2,1)S(1)} %pad_maximum_fusion.9), channel_id=1, source_target_pairs={{0,2},{1,3},{2,0},{3,1},{4,6},{5,7},{6,4},{7,5},{8,10},{9,11},{10,... | collective-permute-start | bytes 282632 | tf_op jit(solution)/shard_map/ppermute | solution.py:465
  111.4 2.6 %collective-permute-done.8 = bf16[368,128]{1,0:T(8,128)(2,1)S(1)} collective-permute-done((bf16[368,128]{1,0:T(8,128)(2,1)S(1)}, bf16[368,128]{1,0:T(8,128)(2,1)S(1)}, u32[]{:S(2)}, u32[]{:S(2)}) %collective-permute-start.8) | collective-permute-done | bytes 94240 | tf_op jit(solution)/shard_map/ppermute | solution.py:465
  114.1 5.6 %collective-permute-start.9 = (bf16[224,128]{1,0:T(8,128)(2,1)S(1)}, bf16[224,128]{1,0:T(8,128)(2,1)S(1)}, u32[]{:S(2)}, u32[]{:S(2)}) collective-permute-start(bf16[224,128]{1,0:T(8,128)(2,1)S(1)} %pad_maximum_fusion.10), channel_id=1, source_target_pairs={{0,4},{1,5},{2,6},{3,7},{4,0},{5,1},{6,2},{7,3},{8,12},{9,13},{10,... | collective-permute-start | bytes 172040 | tf_op jit(solution)/shard_map/ppermute | solution.py:465
  120.2 1.8 %collective-permute-done.9 = bf16[224,128]{1,0:T(8,128)(2,1)S(1)} collective-permute-done((bf16[224,128]{1,0:T(8,128)(2,1)S(1)}, bf16[224,128]{1,0:T(8,128)(2,1)S(1)}, u32[]{:S(2)}, u32[]{:S(2)}) %collective-permute-start.9) | collective-permute-done | bytes 57376 | tf_op jit(solution)/shard_map/ppermute | solution.py:465
  122.7 3.5 %mlp_grad.1 = (f32[3136,128]{1,0:T(8,128)}, f32[8,128]{1,0:T(8,128)}) custom-call(bf16[16,512]{1,0:T(8,128)(2,1)} %reshape.185.table_ref, bf16[512,512]{1,0:T(8,128)(2,1)} %reshape.186.m1_ref, bf16[512,256]{1,0:T(8,128)(2,1)} %reshape.187.m2_ref, bf16[14,128]{1,0:T(8,128)(2,1)} %reshape_squeeze.8.small_ref, f32[16,256]{1,0:T(8,128)} %reshape.198.dss_ref), custom_call_target="tpu_custom_call" | custom-call | tf_op jit(solution)/shard_map/mlp_grad/pallas_call | solution.py:441
  127.5 1.6 %fusion.22 = (bf16[12544]{0:T(1024)(128)(2,1)}, f32[12544]{0:T(1024)S(1)}, f32[12544]{0:T(1024)S(1)}, f32[12544]{0:T(1024)S(1)}) fusion(f32[12544]{0:T(1024)S(1)} %get-tuple-element.29, s32[]{:T(128)S(6)} %mul.241, f32[12544]{0:T(1024)S(1)} %get-tuple-element.28, f32[401408]{0:T(1024)} %bitcast.101, s32[]{:T(128)S(6)} %select_n.37, ...), kind=kLoop, calls=%fused_computation.107 | loop fusion | flops 213248 | bytes 376328 | tf_op jit(solution)/shard_map/convert_element_type | solution.py:461
  (107 shorter events, 19.9 us)
Async XLA Ops:
  3.3 7.7 %collective-permute-start = (bf16[1,243,128]{2,1,0:T(8,128)(2,1)S(1)}, bf16[1,243,128]{2,1,0:T(8,128)(2,1)S(1)}, u32[]{:S(2)}, u32[]{:S(2)}) collective-permute-start(bf16[1,243,128]{2,1,0:T(8,128)(2,1)S(1)} %get-tuple-element.57), channel_id=1, source_target_pairs={{0,4},{1,5},{2,6},{3,7},{4,0},{5,1},{6,2},{7,3},{8,12},{9,13},{10,... | collective-permute-start | bytes 186632 | tf_op jit(solution)/shard_map/ppermute | solution.py:465
  11.0 5.0 %collective-permute-start.1 = (bf16[2,243,128]{2,1,0:T(8,128)(2,1)S(1)}, bf16[2,243,128]{2,1,0:T(8,128)(2,1)S(1)}, u32[]{:S(2)}, u32[]{:S(2)}) collective-permute-start(bf16[2,243,128]{2,1,0:T(8,128)(2,1)S(1)} %pad_maximum_fusion.8), channel_id=1, source_target_pairs={{0,2},{1,3},{2,0},{3,1},{4,6},{5,7},{6,4},{7,5},{8,10},{9,11},{10,... | collective-permute-start | bytes 373256 | tf_op jit(solution)/shard_map/ppermute | solution.py:465
  16.1 6.3 %collective-permute-start.2 = (bf16[4,243,128]{2,1,0:T(8,128)(2,1)S(1)}, bf16[4,243,128]{2,1,0:T(8,128)(2,1)S(1)}, u32[]{:S(2)}, u32[]{:S(2)}) collective-permute-start(bf16[4,243,128]{2,1,0:T(8,128)(2,1)S(1)} %pad_maximum_fusion.5), channel_id=1, source_target_pairs={{0,8},{8,0},{16,24},{24,16},{1,9},{9,1},{17,25},{25,17},{2,10},{10... | collective-permute-start | bytes 746504 | tf_op jit(solution)/shard_map/ppermute | solution.py:465
  22.5 9.6 %collective-permute-start.3 = (bf16[8,243,128]{2,1,0:T(8,128)(2,1)S(1)}, bf16[8,243,128]{2,1,0:T(8,128)(2,1)S(1)}, u32[]{:S(2)}, u32[]{:S(2)}) collective-permute-start(bf16[8,243,128]{2,1,0:T(8,128)(2,1)S(1)} %pad_maximum_fusion.2), channel_id=1, source_target_pairs={{0,16},{8,24},{16,0},{24,8},{1,17},{9,25},{17,1},{25,9},{2,18},{10... | collective-permute-start | bytes 1493000 | tf_op jit(solution)/shard_map/ppermute | solution.py:465
  26.2 7.6 %copy-start.10 = (s32[32]{0:T(128)S(1)}, s32[32]{0:T(128)}, u32[]{:S(2)}) copy-start(s32[32]{0:T(128)} %constant.17.clone) | copy-start | bytes 388
  26.2 7.7 %copy-start = (s32[32]{0:T(128)S(1)}, s32[32]{0:T(128)}, u32[]{:S(2)}) copy-start(s32[32]{0:T(128)} %constant.16.clone) | copy-start | bytes 388
  33.1 2.6 %collective-permute-start.4 = (bf16[16,243,128]{2,0,1:T(8,128)(2,1)S(1)}, bf16[16,243,128]{2,0,1:T(8,128)(2,1)S(1)}, u32[]{:S(2)}, u32[]{:S(2)}) collective-permute-start(bf16[16,243,128]{2,0,1:T(8,128)(2,1)S(1)} %copy.20), channel_id=1, source_target_pairs={{0,1},{1,0},{2,3},{3,2},{4,5},{5,4},{6,7},{7,6},{8,9},{9,8},{10,11... | collective-permute-start | bytes 2985992 | tf_op jit(solution)/shard_map/ppermute | solution.py:465
  40.6 1.1 slice-start
  40.6 2.3 %slice-start.1 = ((bf16[3136,128]{1,0:T(8,128)(2,1)}), bf16[1024,128]{1,0:T(8,128)(2,1)S(1)}, s32[]{:S(2)}) async-start(bf16[3136,128]{1,0:T(8,128)(2,1)} %reshape.184), calls=%async_computation.1 | async-start | bytes 524288 | tf_op jit(solution)/shard_map/slice | solution.py:521
  40.6 3.0 %slice-start.2 = ((bf16[3136,128]{1,0:T(8,128)(2,1)}), bf16[64,128]{1,0:T(8,128)(2,1)S(1)}, s32[]{:S(2)}) async-start(bf16[3136,128]{1,0:T(8,128)(2,1)} %reshape.184), calls=%async_computation.2 | async-start | bytes 32768 | tf_op jit(solution)/shard_map/slice | solution.py:519
  41.8 4.3 %copy-start.2 = (bf16[32,36,128]{2,1,0:T(8,128)(2,1)S(1)}, bf16[32,36,128]{2,1,0:T(8,128)(2,1)}, u32[]{:S(2)}) copy-start(bf16[32,36,128]{2,1,0:T(8,128)(2,1)} %get-tuple-element.60) | copy-start | bytes 884740
  81.2 3.2 %copy-start.5 = (f32[1152,128]{1,0:T(8,128)S(1)}, f32[1152,128]{1,0:T(8,128)}, u32[]{:S(2)}) copy-start(f32[1152,128]{1,0:T(8,128)} %get-tuple-element.22) | copy-start | bytes 1769476
  81.2 4.1 %copy-start.4 = (f32[1152,128]{1,0:T(8,128)S(1)}, f32[1152,128]{1,0:T(8,128)}, u32[]{:S(2)}) copy-start(f32[1152,128]{1,0:T(8,128)} %get-tuple-element.23) | copy-start | bytes 1769476
  87.8 3.6 %copy-start.8 = (f32[8,128]{1,0:T(8,128)S(1)}, f32[8,128]{1,0:T(8,128)}, u32[]{:S(2)}) copy-start(f32[8,128]{1,0:T(8,128)} %get-tuple-element.24) | copy-start | bytes 12292
  87.8 3.6 %copy-start.7 = (f32[16,256]{1,0:T(8,128)S(1)}, f32[16,256]{1,0:T(8,128)}, u32[]{:S(2)}) copy-start(f32[16,256]{1,0:T(8,128)} %get-tuple-element.25) | copy-start | bytes 49156
  89.9 3.8 %copy-start.1 = (f32[32,144,128]{2,1,0:T(8,128)S(1)}, f32[32,144,128]{2,1,0:T(8,128)}, u32[]{:S(2)}) copy-start(f32[32,144,128]{2,1,0:T(8,128)} %gather_fusion.2) | copy-start | bytes 7077892
  91.5 2.1 %collective-permute-start.5 = (bf16[2384,128]{1,0:T(8,128)(2,1)S(1)}, bf16[2384,128]{1,0:T(8,128)(2,1)S(1)}, u32[]{:S(2)}, u32[]{:S(2)}) collective-permute-start(bf16[2384,128]{1,0:T(8,128)(2,1)S(1)} %pad_maximum_fusion.1), channel_id=1, source_target_pairs={{0,1},{1,0},{2,3},{3,2},{4,5},{5,4},{6,7},{7,6},{8,9},{9,8},{10,11... | collective-permute-start | bytes 1830920 | tf_op jit(solution)/shard_map/ppermute | solution.py:465
  93.9 9.6 %collective-permute-start.6 = (bf16[1232,128]{1,0:T(8,128)(2,1)S(1)}, bf16[1232,128]{1,0:T(8,128)(2,1)S(1)}, u32[]{:S(2)}, u32[]{:S(2)}) collective-permute-start(bf16[1232,128]{1,0:T(8,128)(2,1)S(1)} %pad_maximum_fusion.3), channel_id=1, source_target_pairs={{0,16},{8,24},{16,0},{24,8},{1,17},{9,25},{17,1},{25,9},{2,18},{10... | collective-permute-start | bytes 946184 | tf_op jit(solution)/shard_map/ppermute | solution.py:465
  103.5 16.2 %copy-start.6 = (f32[4,12544]{1,0:T(4,128)S(1)}, f32[4,12544]{1,0:T(4,128)}, u32[]{:S(2)}) copy-start(f32[4,12544]{1,0:T(4,128)} %param.12) | copy-start | bytes 602116
  103.6 23.3 %copy-start.9 = (f32[4,56]{1,0:T(4,128)S(1)}, f32[4,56]{1,0:T(4,128)}, u32[]{:S(2)}) copy-start(f32[4,56]{1,0:T(4,128)} %param.13) | copy-start | bytes 2692
  103.6 5.6 %collective-permute-start.7 = (bf16[656,128]{1,0:T(8,128)(2,1)S(1)}, bf16[656,128]{1,0:T(8,128)(2,1)S(1)}, u32[]{:S(2)}, u32[]{:S(2)}) collective-permute-start(bf16[656,128]{1,0:T(8,128)(2,1)S(1)} %pad_maximum_fusion.7), channel_id=1, source_target_pairs={{0,8},{8,0},{16,24},{24,16},{1,9},{9,1},{17,25},{25,17},{2,10},{10... | collective-permute-start | bytes 503816 | tf_op jit(solution)/shard_map/ppermute | solution.py:465
  109.2 20.0 %copy-start.3 = (f32[4,4,4608]{2,1,0:T(4,128)S(1)}, f32[4,4,4608]{2,1,0:T(4,128)}, u32[]{:S(2)}) copy-start(f32[4,4,4608]{2,1,0:T(4,128)} %param.11) | copy-start | bytes 884740
  109.3 4.7 %collective-permute-start.8 = (bf16[368,128]{1,0:T(8,128)(2,1)S(1)}, bf16[368,128]{1,0:T(8,128)(2,1)S(1)}, u32[]{:S(2)}, u32[]{:S(2)}) collective-permute-start(bf16[368,128]{1,0:T(8,128)(2,1)S(1)} %pad_maximum_fusion.9), channel_id=1, source_target_pairs={{0,2},{1,3},{2,0},{3,1},{4,6},{5,7},{6,4},{7,5},{8,10},{9,11},{10,... | collective-permute-start | bytes 282632 | tf_op jit(solution)/shard_map/ppermute | solution.py:465
  114.1 7.9 %collective-permute-start.9 = (bf16[224,128]{1,0:T(8,128)(2,1)S(1)}, bf16[224,128]{1,0:T(8,128)(2,1)S(1)}, u32[]{:S(2)}, u32[]{:S(2)}) collective-permute-start(bf16[224,128]{1,0:T(8,128)(2,1)S(1)} %pad_maximum_fusion.10), channel_id=1, source_target_pairs={{0,4},{1,5},{2,6},{3,7},{4,0},{5,1},{6,2},{7,3},{8,12},{9,13},{10,... | collective-permute-start | bytes 172040 | tf_op jit(solution)/shard_map/ppermute | solution.py:465

commit v2 on v1

--- a/solution.py
+++ b/solution.py
@@ -1,3 +1,5 @@
+import functools
+
 import jax
 import jax.numpy as jnp
 from jax import lax
@@ -38,7 +40,7 @@
 NN = (((1,), (0,)), ((), ()))
 NT = (((1,), (1,)), ((), ()))
 TN = (((0,), (0,)), ((), ()))
-VMEM_LIMIT = 58 << 20
+EXTRA = 8 + 2 * NCLASS
 R = 8
 Q = 8
 
@@ -141,21 +143,68 @@
         out_ref[t * C : (t + 1) * C, :] = got[:, (TAPS - 1 - t) * C : (TAPS - t) * C]
 
 
-def block_body(
-    cls_ref, x_ref, cot_ref, k1_ref, k2_ref, kd0_ref, kd1_ref, small_ref, table_ref, m1_ref, m2_ref,
-    out_ref, dx_ref, gk1_ref, gk2_ref, gkd0_ref, gkd1_ref, gsmall_ref, gclass_ref,
-    a1w, a2w, tw, rw, cw, c1, g1p, g2p, drf, pair,
-):
+def position_of(sizes):
+    (outer, _), (inner, inner_size) = sizes
+    return lax.axis_index(outer) * inner_size + lax.axis_index(inner)
+
+
+def take_shards(plan, me, parts, conv, dense):
+    conv[...] = jnp.zeros(conv.shape, f32)
+    dense[...] = jnp.zeros(dense.shape, f32)
+    small = jnp.zeros((16, C), f32)
+    for (near, turn), part_ref in zip(plan.sources, parts):
+        values = part_ref[near].astype(f32)
+        owner = me ^ turn
+        first = plan.tile_of(owner * plan.conv_rows)
+        for k in range(4):
+            conv[k, pl.ds(first, plan.conv_pad), :] += values[k * plan.conv_pad : (k + 1) * plan.conv_pad]
+        first = plan.tile_of(owner * plan.dense_rows)
+        dense[pl.ds(first, plan.dense_pad), :] += values[plan.dense_at : plan.dense_at + plan.dense_pad]
+        small = small + values[plan.small_at : plan.small_at + 16]
+    return small
+
+
+def block_body(plan, *refs):
+    refs = list(refs)
+    cls_ref, x_ref, cot_ref = refs[:3]
+    inputs = refs[3 : 3 + plan.inputs]
+    out_ref, dx_ref, table_ref, m1_ref, m2_ref, hidden_ref = refs[3 + plan.inputs : 9 + plan.inputs]
+    results = refs[9 + plan.inputs : 11 + plan.inputs]
+    a1w, a2w, tw, rw, cw, c1, g1p, g2p, drf, pair, conv, dense, kernels, smalls = refs[11 + plan.inputs :]
+    me = position_of(plan.sizes)
+    if plan.rings:
+        parts = [ref for ref in inputs for _ in range(plan.line)]
+        smalls[...] = take_shards(plan, me, parts, conv, dense)
+        kernels[...] = conv[:, 0:KERNEL_ROWS].astype(bf16)
+    else:
+        kernels[...] = inputs[0][...]
+        dense[0:MLP_ROWS] = inputs[1][...].astype(f32)
+        smalls[0:14] = inputs[2][...].astype(f32)
+
+    def lanes(first, rows, parts):
+        pieces = [dense[pl.ds(first + part, rows, parts), :] for part in range(parts)]
+        return jnp.concatenate(pieces, axis=1).astype(bf16)
+
+    table_ref[...] = lanes(0, NCLASS, EMB // C)
+    m1_ref[...] = lanes(TABLE_ROWS, EMB, EMB // C)
+    m2_ref[...] = lanes(TABLE_ROWS + M1_ROWS, EMB, 2)
+    k1_ref, k2_ref, kd0_ref, kd1_ref = [kernels.at[k] for k in range(4)]
+    gk1_ref, gk2_ref, gkd0_ref, gkd1_ref = [conv.at[k] for k in range(4)]
+
     def small_row(index):
-        return jnp.broadcast_to(small_ref[index : index + 1, :].astype(f32), (8, C))
+        return jnp.broadcast_to(smalls[index : index + 1, :], (8, C))
 
     def small_run(first, count):
-        return jnp.concatenate([small_ref[first + i : first + i + 1, :].astype(f32) for i in range(count)], axis=1)
+        return jnp.concatenate([smalls[first + i : first + i + 1, :] for i in range(count)], axis=1)
+
+    def alone(step):
+        pl.when(me >= 0)(step)
 
     gain1, bias1, cb1, gain2, bias2, cb2 = [small_row(i) for i in range(6)]
     zero8 = jnp.zeros((8, C), f32)
 
     hidden = mm(table_ref[...], m1_ref[...]) + small_run(8, 4)
+    hidden_ref[...] = hidden
     act = hidden * normal_cdf(hidden)
     ss = sum(mm(part, m2_ref[...]) for part in three(act)) + small_run(12, 2)
     mine = lax.broadcasted_iota(jnp.int32, (NCLASS, 2 * C), 0) == cls_ref[0]
@@ -263,11 +312,11 @@
         return carry
 
     lax.fori_loop(0, H // 2 // Q, down, 0)
-    @pl.when(cls_ref[0] >= 0)
+    @alone
     def _():
         gkd = mm(down_rows(0, H // 2), cot_ref[...].reshape(CELLS // 4, 2 * C), TN)
-        gkd0_ref[...] = gkd[:, :C]
-        gkd1_ref[...] = gkd[:, C:]
+        gkd0_ref[0:KERNEL_ROWS] = gkd[:, :C]
+        gkd1_ref[0:KERNEL_ROWS] = gkd[:, C:]
 
 
     cw[H // 2 : H // 2 + 1] = jnp.zeros((1, W // 2, 4 * C), bf16)
@@ -329,7 +378,7 @@
         return s + fold(values)
 
     gcb2 = total_of(lax.fori_loop(0, H // R, t2_windows, zero8))
-    pl.when(cls_ref[0] >= 0)(lambda: kernel_grad(a2w, tw, gk2_ref))
+    alone(lambda: kernel_grad(a2w, tw, gk2_ref))
     gb2, gg2 = pull(k2_ref, g2p, lambda i: [unit2(ref[...]) for ref in pairs_of(c1, i * Q)])
     mean_du2 = group_sum(gb2 * (1.0 + gain2)) * (1.0 / PER_GROUP)
     mean_duu2 = group_sum(gg2 * (1.0 + gain2)) * (1.0 / PER_GROUP)
@@ -343,7 +392,7 @@
 
     gsc, gsh = lax.fori_loop(0, H // R, t1_windows, (zero8, zero8))
     gsc, gsh = total_of(gsc), total_of(gsh)
-    pl.when(cls_ref[0] >= 0)(lambda: kernel_grad(a1w, tw, gk1_ref))
+    alone(lambda: kernel_grad(a1w, tw, gk1_ref))
 
     def unit1(ref):
         return (ref[...].astype(f32) - one(mean1)) * one(rs1)
@@ -362,28 +411,88 @@
     lax.fori_loop(0, H // R, finish, 0)
 
     rows = [gg1, gb1, gsh * scale, gg2, gb2, gcb2, gdb[:, :C], gdb[:, C:]]
-    for index, row in enumerate(rows):
-        gsmall_ref[index : index + 1, :] = row[0:1]
-    both = jnp.concatenate([gsc[0:1], gsh[0:1]], axis=1)
-    gclass_ref[...] = jnp.where(mine, both, 0.0)
+    rows = [row[0:1] for row in rows]
+    rows = rows + [jnp.where(mine[:, :C], row[0:1], 0.0) for row in (gsc, gsh)]
+    extra = jnp.concatenate(rows, axis=0)
+    if not plan.rings:
+        results[0][...] = conv[:, 0:KERNEL_ROWS]
+        results[1][...] = extra
+        return
+    keep_ref, send_ref = results
+    for place, (core, turn) in enumerate(plan.targets):
+        first = plan.tile_of((me ^ turn) * plan.conv_rows)
+        block = jnp.concatenate([conv[k, pl.ds(first, plan.conv_pad), :] for k in range(4)], axis=0)
+        at = place % plan.half * plan.width
+        if core:
+            send_ref[at : at + plan.width] = block.astype(bf16)
+        else:
+            keep_ref[at : at + plan.width] = block
+    keep_ref[plan.half * plan.width :] = extra
+    send_ref[plan.half * plan.width :] = two_terms(extra)
+
+
+def two_terms(extra):
+    high = extra.astype(bf16)
+    return jnp.concatenate([high.astype(f32), extra - high.astype(f32)], axis=0).astype(bf16)
 
 
 def vmem_specs(count):
     return [pl.BlockSpec(memory_space=pltpu.VMEM)] * count
 
 
-def run_block(class_ids, x, cot, kernels, small, mlp):
-    shapes = (
-        [jax.ShapeDtypeStruct((H // 2, W // 2, 2 * C), bf16), jax.ShapeDtypeStruct((H, W, C), bf16)]
-        + [jax.ShapeDtypeStruct((KERNEL_ROWS, C), f32)] * 4
-        + [jax.ShapeDtypeStruct((8, C), f32), jax.ShapeDtypeStruct((NCLASS, 2 * C), f32)]
-    )
+def limit(size):
+    return pltpu.CompilerParams(vmem_limit_bytes=size << 20)
+
+
+class Plan:
+    def __init__(self, sizes, conv_len, dense_len, small_len):
+        (_, outer_size), (_, inner_size) = sizes
+        count = outer_size * inner_size
+        self.sizes, self.line = sizes, inner_size // 2
+        self.conv_len, self.dense_len, self.small_len = conv_len, dense_len, small_len
+        self.conv_rows, self.dense_rows = conv_len // C, dense_len // C
+        powers = all(n & (n - 1) == 0 for _, n in sizes) and inner_size > 1
+        self.rings = powers and conv_len % C == 0 and dense_len % C == 0 and small_len <= C
+        self.inputs = 2 * outer_size if self.rings else 3
+        self.conv_pad = self.padded(self.conv_rows, count)
+        self.dense_pad = self.padded(self.dense_rows, count)
+        self.dense_at = 4 * self.conv_pad
+        self.small_at = self.dense_at + self.dense_pad
+        self.own_rows = -(-(self.small_at + 16) // 16) * 16
+        turns = [(core, plane * inner_size + 2 * near + core) for core in (0, 1) for plane in range(outer_size) for near in range(self.line)]
+        self.targets = turns
+        self.sources = [(place % self.line, turn) for place, (_, turn) in enumerate(turns)]
+        self.half = count // 2
+        self.width = 4 * self.conv_pad
+
+    def padded(self, rows, count):
+        return max(-(-(rows * k % 8 + rows) // 8) * 8 for k in range(count))
+
+    def tile_of(self, row):
+        return pl.multiple_of(row // 8 * 8, 8)
+
+
+def run_block(plan, class_ids, x, cot, inputs):
+    struct = jax.ShapeDtypeStruct
+    shapes = [
+        struct((H // 2, W // 2, 2 * C), bf16),
+        struct((H, W, C), bf16),
+        struct((NCLASS, EMB), bf16),
+        struct((EMB, EMB), bf16),
+        struct((EMB, 2 * C), bf16),
+        struct((NCLASS, EMB), f32),
+    ]
+    if plan.rings:
+        rows = plan.half * plan.width
+        shapes += [struct((rows + EXTRA, C), f32), struct((rows + 2 * EXTRA, C), bf16)]
+    else:
+        shapes += [struct((4, KERNEL_ROWS, C), f32), struct((EXTRA, C), f32)]
     windows = pltpu.VMEM((H + 2, W, 3 * C), bf16)
     plane = pltpu.VMEM((H, W, C), f32)
     return pl.pallas_call(
-        block_body,
+        functools.partial(block_body, plan),
         out_shape=shapes,
-        in_specs=[pl.BlockSpec(memory_space=pltpu.SMEM)] + vmem_specs(10),
+        in_specs=[pl.BlockSpec(memory_space=pltpu.SMEM)] + vmem_specs(2 + len(inputs)),
         out_specs=vmem_specs(8),
         scratch_shapes=[
             windows,
@@ -396,20 +505,88 @@
             plane,
             plane,
             pltpu.VMEM((12 * C, 2 * C), bf16),
+            pltpu.VMEM((4, KERNEL_ROWS + 2 * plan.conv_pad, C), f32),
+            pltpu.VMEM((MLP_ROWS + 2 * plan.dense_pad, C), f32),
+            pltpu.VMEM((4, KERNEL_ROWS, C), bf16),
+            pltpu.VMEM((16, C), f32),
         ],
-        compiler_params=pltpu.CompilerParams(vmem_limit_bytes=VMEM_LIMIT),
+        compiler_params=limit(48),
         name="block",
-    )(class_ids, x, cot, *kernels, small, *mlp)
-
-
-def mlp_body(table_ref, m1_ref, m2_ref, small_ref, dss_ref, out_ref, tail_ref):
-    def small_run(first, count):
-        return jnp.concatenate([small_ref[first + i : first + i + 1, :].astype(f32) for i in range(count)], axis=1)
-
-    table = table_ref[...]
-    hidden = mm(table, m1_ref[...]) + small_run(8, 4)
+    )(class_ids, x, cot, *inputs)
+
+
+def pack_body(plan, conv_ref, dense_ref, small_ref, out_ref, rows):
+    me = position_of(plan.sizes)
+    rows[...] = jnp.zeros(rows.shape, f32)
+    first = me * plan.conv_rows % 8
+    for r in range(plan.conv_rows):
+        rows[pl.ds(first + r, 4, plan.conv_pad), :] = conv_ref[0, :, r * C : (r + 1) * C]
+    first = plan.dense_at + me * plan.dense_rows % 8
+    for r in range(plan.dense_rows):
+        rows[pl.ds(first + r, 1), :] = dense_ref[0:1, r * C : (r + 1) * C]
+    start = me * plan.small_len
+    own = jnp.concatenate([small_ref[0:1, :], jnp.zeros((1, C - plan.small_len), f32)], axis=1)
+    own = pltpu.roll(jnp.broadcast_to(own, (16, C)), start % C, 1)
+    row = lax.broadcasted_iota(jnp.int32, (16, C), 0)
+    lane = lax.broadcasted_iota(jnp.int32, (16, C), 1)
+    place = row * C + lane
+    mine = (place >= start) & (place < start + plan.small_len)
+    rows[plan.small_at : plan.small_at + 16] = jnp.where(mine, own, 0.0)
+    out_ref[...] = rows[...].astype(bf16)
+
+
+def run_pack(plan, conv_state, mlp_state, small_state):
+    return pl.pallas_call(
+        functools.partial(pack_body, plan),
+        out_shape=jax.ShapeDtypeStruct((plan.own_rows, C), bf16),
+        in_specs=vmem_specs(3),
+        out_specs=pl.BlockSpec(memory_space=pltpu.VMEM),
+        scratch_shapes=[pltpu.VMEM((plan.own_rows, C), f32)],
+        compiler_params=limit(8),
+        name="pack",
+    )(conv_state, mlp_state, small_state)
+
+
+def sum_extra(extra, received, at):
+    for ref in received:
+        extra = extra + ref[at : at + EXTRA].astype(f32) + ref[at + EXTRA : at + 2 * EXTRA].astype(f32)
+    return extra
+
+
+def merge_body(plan, blocks, groups, *refs):
+    keep_ref, received = refs[0], refs[1 : len(refs) - groups]
+    outs = refs[len(refs) - groups :]
+    size = blocks // groups
+    for block in range(blocks):
+        at = block * plan.width
+        total = keep_ref[at : at + plan.width]
+        for ref in received:
+            total = total + ref[at : at + plan.width].astype(f32)
+        group, place = block // size, block % size * plan.width
+        outs[group][place : place + plan.width] = total.astype(outs[group].dtype)
+    at = blocks * plan.width
+    extra = sum_extra(keep_ref[at : at + EXTRA], received, at)
+    outs[0][size * plan.width :] = extra
+    for ref in outs[1:]:
+        ref[size * plan.width :] = two_terms(extra)
+
+
+def run_merge(plan, blocks, groups, keep, received):
+    rows = blocks // groups * plan.width
+    shapes = [jax.ShapeDtypeStruct((rows + EXTRA, C), f32)]
+    shapes += [jax.ShapeDtypeStruct((rows + 2 * EXTRA, C), bf16)] * (groups - 1)
+    return pl.pallas_call(
+        functools.partial(merge_body, plan, blocks, groups),
+        out_shape=shapes,
+        in_specs=vmem_specs(1 + len(received)),
+        out_specs=vmem_specs(groups),
+        compiler_params=limit(16),
+        name="merge",
+    )(keep, *received)
+
+
+def mlp_grads(table, m1_ref, m2_ref, hidden, dss, out_ref):
     prob = normal_cdf(hidden)
-    dss = dss_ref[...]
 
     def put(first, values):
         parts = values.shape[1] // C
@@ -430,159 +607,170 @@
     put(TABLE_ROWS + M1_ROWS, outer(three(hidden * prob), three(dss)))
     ge1 = jnp.sum(dp, axis=0, keepdims=True)
     ge2 = jnp.sum(dss, axis=0, keepdims=True)
-    for i in range(4):
-        tail_ref[i : i + 1, :] = ge1[:, i * C : (i + 1) * C]
-    for i in range(2):
-        tail_ref[4 + i : 5 + i, :] = ge2[:, i * C : (i + 1) * C]
-    tail_ref[6:8, :] = jnp.zeros((2, C), f32)
-
-
-def run_mlp(mlp, small, dss):
+    return [ge1[:, i * C : (i + 1) * C] for i in range(4)] + [ge2[:, i * C : (i + 1) * C] for i in range(2)]
+
+
+def mlp_body(table_ref, m1_ref, m2_ref, hidden_ref, dss_ref, out_ref, tail_ref):
+    tail = mlp_grads(table_ref[...], m1_ref, m2_ref, hidden_ref[...], dss_ref[...], out_ref)
+    for i, row in enumerate(tail):
+        tail_ref[i : i + 1, :] = row
+
+
+def run_mlp(table, m1, m2, hidden, dss):
     return pl.pallas_call(
         mlp_body,
-        out_shape=[jax.ShapeDtypeStruct((MLP_ROWS, C), f32), jax.ShapeDtypeStruct((8, C), f32)],
+        out_shape=[jax.ShapeDtypeStruct((MLP_ROWS, C), f32), jax.ShapeDtypeStruct((6, C), f32)],
         in_specs=vmem_specs(5),
         out_specs=vmem_specs(2),
-        compiler_params=pltpu.CompilerParams(vmem_limit_bytes=VMEM_LIMIT),
+        compiler_params=limit(32),
         name="mlp_grad",
-    )(*mlp, small, dss)
-
-
-def adam_update(state_stack, gradient, step_rate, weight_decay):
-    weight = state_stack[0]
-    first_moment = beta_one * state_stack[1] + (1.0 - beta_one) * gradient
-    second = beta_two * state_stack[2] + (1.0 - beta_two) * gradient * gradient
-    first_hat = first_moment / (1.0 - beta_one**STEP)
-    second_hat = second / (1.0 - beta_two**STEP)
-    weight_new = weight - step_rate * (
-        first_hat / (jnp.sqrt(second_hat) + adam_eps) + weight_decay * weight
+    )(table, m1, m2, hidden, dss)
+
+
+def adam(weight, first, second, average, gradient, rate, decay):
+    first = beta_one * first + (1.0 - beta_one) * gradient
+    second = beta_two * second + (1.0 - beta_two) * gradient * gradient
+    first_hat = first * (1.0 / (1.0 - beta_one**STEP))
+    second_hat = second * (1.0 / (1.0 - beta_two**STEP))
+    weight = weight - rate * (first_hat / (jnp.sqrt(second_hat) + adam_eps) + decay * weight)
+    return weight, first, second, ema_decay * average + (1.0 - ema_decay) * weight
+
+
+def update_body(plan, received_count, *refs):
+    keep_ref, received = refs[0], refs[1 : 1 + received_count]
+    table_ref, m1_ref, m2_ref, hidden_ref, conv_ref, dense_ref, small_ref = refs[1 + received_count : 8 + received_count]
+    conv_new, dense_new, small_new, conv_copy, dense_copy, small_copy = refs[8 + received_count : 14 + received_count]
+    block, grads, rows, smalls = refs[14 + received_count :]
+    me = position_of(plan.sizes)
+    total = keep_ref[0 : plan.width]
+    for ref in received:
+        total = total + ref[0 : plan.width].astype(f32)
+    block[...] = total
+    extra = sum_extra(keep_ref[plan.width : plan.width + EXTRA], received, plan.width)
+    smalls[0:8] = extra[0:8]
+    dss = jnp.concatenate([extra[8 : 8 + NCLASS], extra[8 + NCLASS :]], axis=1)
+    tail = mlp_grads(table_ref[...], m1_ref, m2_ref, hidden_ref[...], dss, grads)
+    for i, row in enumerate(tail):
+        smalls[8 + i : 9 + i, :] = row
+
+    first = me * plan.conv_rows % 8
+    for r in range(plan.conv_rows):
+        at = slice(r * C, (r + 1) * C)
+        gradient = block[pl.ds(first + r, 4, plan.conv_pad), :]
+        new = adam(*[conv_ref[k, :, at] for k in range(4)], gradient, rate_conv, decay_weights)
+        for k in range(4):
+            conv_new[k, :, at] = new[k]
+        conv_copy[:, at] = new[0].astype(bf16)
+
+    start = me * plan.dense_rows
+    for r in range(plan.dense_rows):
+        at = slice(r * C, (r + 1) * C)
+        gradient = grads[pl.ds(start + r, 1), :]
+        rate = jnp.where(start + r < TABLE_ROWS, rate_table, rate_dense)
+        new = adam(*[dense_ref[k : k + 1, at] for k in range(4)], gradient, rate, decay_weights)
+        for k in range(4):
+            dense_new[k : k + 1, at] = new[k]
+        rows[r : r + 1, :] = new[0]
+    dense_copy[...] = rows[...].astype(bf16)
+
+    start = me * plan.small_len
+    lane = lax.broadcasted_iota(jnp.int32, (8, C), 1)
+    near = jnp.broadcast_to(smalls[pl.ds(start // C, 1), :], (8, C))
+    far = jnp.broadcast_to(smalls[pl.ds(start // C + 1, 1), :], (8, C))
+    off = C - start % C
+    gradient = jnp.where(lane < off, pltpu.roll(near, off, 1), pltpu.roll(far, off, 1))
+    gradient = gradient[0:1, 0 : plan.small_len]
+    new = adam(*[small_ref[k : k + 1, :] for k in range(4)], gradient, rate_small, 0.0)
+    for k in range(4):
+        small_new[k : k + 1, :] = new[k]
+    small_copy[...] = new[0].astype(bf16)
+
+
+def run_update(plan, keep, received, mlp, states):
+    struct = jax.ShapeDtypeStruct
+    shapes = [struct(state.shape, f32) for state in states]
+    shapes += [struct((4, plan.conv_len), bf16), struct((plan.dense_rows, C), bf16), struct((1, plan.small_len), bf16)]
+    return pl.pallas_call(
+        functools.partial(update_body, plan, len(received)),
+        out_shape=shapes,
+        in_specs=vmem_specs(1 + len(received) + 4 + 3),
+        out_specs=vmem_specs(6),
+        scratch_shapes=[
+            pltpu.VMEM((plan.width, C), f32),
+            pltpu.VMEM((MLP_ROWS, C), f32),
+            pltpu.VMEM((plan.dense_rows, C), f32),
+            pltpu.VMEM((24, C), f32),
+        ],
+        compiler_params=limit(24),
+        name="update",
+    )(keep, *received, *mlp, *states)
+
+
+def swap(values, axis, size, turn):
+    return lax.ppermute(values, axis, [(i, i ^ turn) for i in range(size)])
+
+
+def gather_ring(plan, own):
+    (outer, outer_size), (inner, inner_size) = plan.sizes
+    line = jnp.stack([own] + [swap(own, inner, inner_size, 2 * k) for k in range(1, plan.line)])
+    planes = [line] + [swap(line, outer, outer_size, k) for k in range(1, outer_size)]
+    return planes + [swap(plane, inner, inner_size, 1) for plane in planes]
+
+
+def reduce_ring(plan, keep, send):
+    (outer, outer_size), (inner, inner_size) = plan.sizes
+    received = [swap(send, inner, inner_size, 1)]
+    keep, *sends = run_merge(plan, plan.half, outer_size, keep, received)
+    received = [swap(part, outer, outer_size, k + 1) for k, part in enumerate(sends)]
+    keep, *sends = run_merge(plan, plan.line, plan.line, keep, received)
+    return keep, [swap(part, inner, inner_size, 2 * (k + 1)) for k, part in enumerate(sends)]
+
+
+def plain_update(plan, position, grads, extra, mlp, states):
+    conv_state, mlp_state, small_state = states
+    conv_red = lax.psum_scatter(grads.reshape(4, -1), AXES, scatter_dimension=1, tiled=True)
+    extra = lax.psum(extra, AXES)
+    dss = jnp.concatenate([extra[8 : 8 + NCLASS], extra[8 + NCLASS :]], axis=1)
+    dense_grad, tail = run_mlp(*mlp, dss)
+    dense_red = lax.dynamic_slice_in_dim(dense_grad.reshape(-1), position * plan.dense_len, plan.dense_len)
+    flat = jnp.concatenate([extra[:8], tail]).reshape(-1)
+    small_red = lax.dynamic_slice_in_dim(flat, position * plan.small_len, plan.small_len)
+    flat_index = position * plan.dense_len + jnp.arange(plan.dense_len, dtype=jnp.int32)
+    dense_rate = jnp.where(flat_index < NCLASS * EMB, rate_table, rate_dense)
+    new = [
+        jnp.stack(adam(*state, red, rate, decay))
+        for state, red, rate, decay in (
+            (conv_state, conv_red, rate_conv, decay_weights),
+            (mlp_state, dense_red, dense_rate, decay_weights),
+            (small_state, small_red, rate_small, 0.0),
+        )
+    ]
+    return new + [state[0].astype(bf16) for state in new]
+
+
+def per_device(sizes, samples, cotangent, class_ids, *states):
+    conv_state, mlp_state, small_state = states
+    plan = Plan(sizes, conv_state.shape[2], mlp_state.shape[1], small_state.shape[1])
+    if plan.rings:
+        inputs = gather_ring(plan, run_pack(plan, *states))
+    else:
+        conv, dense, small = [state[0].astype(bf16) for state in states]
+        inputs = [
+            lax.all_gather(conv, AXES, axis=1, tiled=True).reshape(4, KERNEL_ROWS, C),
+            lax.all_gather(dense, AXES, axis=0, tiled=True).reshape(MLP_ROWS, C),
+            lax.all_gather(small, AXES, axis=0, tiled=True).reshape(-1, C),
+        ]
+    out, dx, table, m1, m2, hidden, first, second = run_block(
+        plan, class_ids, samples[0], cotangent[0], inputs
     )
-    average = ema_decay * state_stack[3] + (1.0 - ema_decay) * weight_new
-    return (jnp.stack([weight_new, first_moment, second, average]), weight_new.astype(bf16))
-
-
-def exchange(values, axis, size, bit):
-    return lax.ppermute(values, axis, [(i, i ^ bit) for i in range(size)])
-
-
-def stage_list(sizes):
-    (outer, outer_size), (inner, inner_size) = sizes
-    inner_bits = [1 << k for k in reversed(range(inner_size.bit_length() - 1))]
-    outer_bits = [1 << k for k in range(outer_size.bit_length() - 1)]
-    inner_stages = [(inner, inner_size, bit, bit) for bit in inner_bits]
-    outer_stages = [(outer, outer_size, bit, bit * inner_size) for bit in outer_bits]
-    return inner_stages[:-1] + outer_stages + inner_stages[-1:]
-
-
-def relative(sizes, position):
-    order = [0]
-    for _, _, _, bit in stage_list(sizes):
-        order = order + [k ^ bit for k in order]
-    return jnp.asarray(order, jnp.int32) ^ position
-
-
-def inverse(sizes, position):
-    order = [0]
-    for _, _, _, bit in stage_list(sizes):
-        order = order + [k ^ bit for k in order]
-    place = [order.index(k) for k in range(len(order))]
-    return jnp.asarray(place, jnp.int32)[jnp.arange(len(order), dtype=jnp.int32) ^ position]
-
-
-def gather_ring(own, sizes):
-    parts = own[None]
-    for axis, size, bit, _ in stage_list(sizes):
-        parts = jnp.concatenate([parts, exchange(parts, axis, size, bit)])
-    return parts
-
-
-def reduce_ring(blocks, extra, sizes):
-    rows = extra.shape[0]
-    for axis, size, bit, _ in reversed(stage_list(sizes)):
-        half = blocks.shape[0] // 2
-        high = extra.astype(bf16)
-        low = (extra - high.astype(f32)).astype(bf16)
-        width = blocks.shape[1]
-        sent = jnp.concatenate([blocks[half:].astype(bf16).reshape(-1, C), high, low])
-        got = exchange(sent, axis, size, bit)
-        blocks = blocks[:half] + got[: half * width].reshape(half, width, C).astype(f32)
-        extra = (
-            extra
-            + got[half * width : half * width + rows].astype(f32)
-            + got[half * width + rows :].astype(f32)
-        )
-    return blocks[0], extra
-
-
-def split_mlp(dense):
-    return [
-        dense[:TABLE_ROWS].reshape(NCLASS, EMB),
-        dense[TABLE_ROWS : TABLE_ROWS + M1_ROWS].reshape(EMB, EMB),
-        dense[TABLE_ROWS + M1_ROWS :].reshape(EMB, 2 * C),
-    ]
-
-
-def gather_all(sizes, position, conv_own, dense_own, small_own):
-    conv_len, dense_len, small_len = conv_own.shape[1], dense_own.shape[0], small_own.shape[0]
-    if not whole_rows(sizes, conv_len, dense_len):
-        conv = lax.all_gather(conv_own, AXES, axis=1, tiled=True)
-        dense = lax.all_gather(dense_own, AXES, axis=0, tiled=True)
-        small = lax.all_gather(small_own, AXES, axis=0, tiled=True)
-        return [conv[k].reshape(KERNEL_ROWS, C) for k in range(4)], dense.reshape(MLP_ROWS, C), small.reshape(-1, C)
-    conv_rows, dense_rows = conv_len // C, dense_len // C
-    own_rows = 4 * conv_rows + dense_rows
-    own = jnp.concatenate(
-        [
-            conv_own.reshape(4 * conv_rows, C),
-            dense_own.reshape(dense_rows, C),
-            jnp.pad(small_own, (0, C - small_len)).reshape(1, C),
-        ]
-    )
-    gathered = gather_ring(own, sizes)[inverse(sizes, position)]
-    kernels = [
-        gathered[:, k * conv_rows : (k + 1) * conv_rows].reshape(KERNEL_ROWS, C) for k in range(4)
-    ]
-    dense = gathered[:, 4 * conv_rows : own_rows].reshape(MLP_ROWS, C)
-    return kernels, dense, gathered[:, own_rows, :small_len].reshape(-1, C)
-
-
-def reduce_all(sizes, position, grads, extra, conv_len, dense_len):
-    if not whole_rows(sizes, conv_len, dense_len):
-        flat = jnp.stack([g.reshape(-1) for g in grads])
-        return lax.psum_scatter(flat, AXES, scatter_dimension=1, tiled=True), lax.psum(extra, AXES)
-    conv_rows = conv_len // C
-    blocks = jnp.concatenate([g.reshape(-1, conv_rows, C) for g in grads], axis=1)
-    red, extra = reduce_ring(blocks[relative(sizes, position)], extra, sizes)
-    return red.reshape(4, conv_len), extra
-
-
-def whole_rows(sizes, conv_len, dense_len):
-    return conv_len % C == 0 and dense_len % C == 0 and all(n & (n - 1) == 0 for _, n in sizes)
-
-
-def per_device(sizes, samples, cotangent, class_ids, conv_state, mlp_state, small_state):
-    position = lax.axis_index(AXES)
-    conv_len, dense_len, small_len = conv_state.shape[2], mlp_state.shape[1], small_state.shape[1]
-    kernels, dense, small = gather_all(
-        sizes, position, conv_state[0].astype(bf16), mlp_state[0].astype(bf16), small_state[0].astype(bf16)
-    )
-    mlp = split_mlp(dense)
-    out, dx, gk1, gk2, gkd0, gkd1, gsmall, gclass = run_block(
-        class_ids, samples[0], cotangent[0], kernels, small, mlp
-    )
-    extra = jnp.concatenate([gsmall, gclass.reshape(2 * NCLASS, C)])
-    conv_red, extra = reduce_all(sizes, position, (gk1, gk2, gkd0, gkd1), extra, conv_len, dense_len)
-    dense_grad, tail = run_mlp(mlp, small, extra[8:].reshape(NCLASS, 2 * C))
-    dense_red = lax.dynamic_slice_in_dim(dense_grad.reshape(-1), position * dense_len, dense_len)
-    small_red = lax.dynamic_slice_in_dim(
-        jnp.concatenate([extra[:8], tail]).reshape(-1), position * small_len, small_len
-    )
-    flat_index = position * dense_len + jnp.arange(dense_len, dtype=jnp.int32)
-    dense_rate = jnp.where(flat_index < NCLASS * EMB, rate_table, rate_dense)
-    conv_new, conv_copy = adam_update(conv_state, conv_red, rate_conv, decay_weights)
-    mlp_new, mlp_copy = adam_update(mlp_state, dense_red, dense_rate, decay_weights)
-    small_new, small_copy = adam_update(small_state, small_red, rate_small, 0.0)
-    return (out[None], dx[None], conv_new, mlp_new, small_new, conv_copy, mlp_copy, small_copy)
+    mlp = (table, m1, m2, hidden)
+    if plan.rings:
+        keep, received = reduce_ring(plan, first, second)
+        results = run_update(plan, keep, received, mlp, states)
+    else:
+        results = plain_update(plan, lax.axis_index(AXES), first, second, mlp, states)
+    conv_new, mlp_new, small_new, conv_copy, mlp_copy, small_copy = results
+    return out[None], dx[None], conv_new, mlp_new, small_new, conv_copy, mlp_copy.reshape(-1), small_copy.reshape(-1)
 
 
 def solution(mesh):

time: 133 us -> 90.9 us (0.68)
  local copies, waits for them, and re-layouts: 30 us -> 4.95 us
  other arithmetic: 8.77 us -> 0.04 us
  waiting for transfers between devices: 37 us -> 33.1 us
  Pallas kernels: 35.6 us -> 33.5 us
  starting transfers between devices: 19.4 us -> 17.7 us
    reshape x16 -> x0, local copies, waits for them, and re-layouts: 13.2 us -> none  [the longest x4 4.91 us: reduce_all(): g.reshape(-1, conv_rows, C)]
    gather x3 -> x0, local copies, waits for them, and re-layouts: 5.3 us -> none  [the longest x1 2.51 us: gather_all(): gathered = gather_ring(own, sizes)[inverse(sizes, position)]]
    ppermute x10 -> x17, waiting for transfers between devices: 37 us -> 33.1 us  [swap(): return lax.ppermute(values, axis, [(i, i ^ turn) for i in range(size)])]
    slice x20 -> x0, local copies, waits for them, and re-layouts: 3.73 us -> none  [the longest x4 1.57 us: reduce_ring(): blocks[half:].astype(bf16).reshape(-1, C)]
    convert_element_type x8 -> x0, other arithmetic: 2.96 us -> none  [the longest x3 2.91 us: adam_update(): weight_new.astype(bf16)]
    concatenate x4 -> x0, local copies, waits for them, and re-layouts: 2.28 us -> none  [the longest x3 2.28 us: gather_ring(): parts = jnp.concatenate([parts, exchange(parts, axis, size, bit)])]
    another operation x4 -> x1, other arithmetic: 2.24 us -> 0.04 us  [gather_ring(): jnp.stack([own] + [swap(own, inner, inner_size, 2 * k) for k in range(1,...]
    unnamed x27 -> x18, local copies, waits for them, and re-layouts: 2.75 us -> 4.95 us
  transfers between devices with their start and end apart: 10 -> 17, of which waited for: 10 -> 12; matrix products, arithmetic and copies ran while one was open for 3% -> 0% of each run, Pallas kernels for 0% -> 0%
where the time goes in v2:
time: 90.9 us; the launch traced here: 90.6 us
  Pallas kernels  33.5 us (37%)
  waiting for transfers between devices  33.1 us (36%)
  starting transfers between devices  17.7 us (19%)
  local copies, waits for them, and re-layouts  4.95 us (5%)
  between operations  1.35 us (1%)
    ppermute x17, waiting for transfers between devices, swap(): return lax.ppermute(values, axis, [(i, i ^ turn) for i in range(size)])  33.1 us
    pallas_call x1, Pallas kernels, run_block(): pl.pallas_call(functools.partial(block_body, plan), out_shape=shapes, in_...  30.7 us
    ppermute x17, starting transfers between devices, swap(): return lax.ppermute(values, axis, [(i, i ^ turn) for i in range(size)])  17.7 us
    unnamed x18, local copies, waits for them, and re-layouts  4.95 us
    pallas_call x1, Pallas kernels, run_update(): pl.pallas_call(functools.partial(update_body, plan, len(received)), out_s...  2.4 us
  transfers between devices with their start and end apart: 17, of which 12 were waited for; matrix products, arithmetic and copies ran while one was open for 0% of the time, Pallas kernels for 0%

profile of v2, /device:TPU:0, one launch (start us, length us, event | category | flops | bytes accessed | tf_op | source)
XLA Modules:
  0.0 90.6 jit_solution(11227585102238680697)
XLA Ops:
  0.6 1.0 %copy-done.1 = f32[4,4,4608]{2,1,0:T(4,128)S(1)} copy-done((f32[4,4,4608]{2,1,0:T(4,128)S(1)}, f32[4,4,4608]{2,1,0:T(4,128)}, u32[]{:S(2)}) %copy-start.1) | copy-done | bytes 294936
  1.6 0.9 %copy-done.4 = f32[4,12544]{1,0:T(4,128)S(1)} copy-done((f32[4,12544]{1,0:T(4,128)S(1)}, f32[4,12544]{1,0:T(4,128)}, u32[]{:S(2)}) %copy-start.4) | copy-done | bytes 200728
  2.5 0.7 copy-done.7
  3.3 5.1 %collective-permute-start.2 = (bf16[288,128]{1,0:T(8,128)(2,1)S(1)}, bf16[288,128]{1,0:T(8,128)(2,1)S(1)}, u32[]{:S(2)}, u32[]{:S(2)}) collective-permute-start(bf16[288,128]{1,0:T(8,128)(2,1)S(1)} %pack.1), channel_id=1, source_target_pairs={{0,6},{1,7},{2,4},{3,5},{4,2},{5,3},{6,0},{7,1},{8,14},{9,15},{10,... | collective-permute-start | bytes 221192 | tf_op jit(solution)/shard_map/ppermute | solution.py:710
  8.4 0.6 collective-permute-start
  9.0 2.1 %collective-permute-done.2 = bf16[288,128]{1,0:T(8,128)(2,1)S(1)} collective-permute-done((bf16[288,128]{1,0:T(8,128)(2,1)S(1)}, bf16[288,128]{1,0:T(8,128)(2,1)S(1)}, u32[]{:S(2)}, u32[]{:S(2)}) %collective-permute-start.2) | collective-permute-done | bytes 73760 | tf_op jit(solution)/shard_map/ppermute | solution.py:710
  11.2 3.5 %collective-permute-done.1 = bf16[288,128]{1,0:T(8,128)(2,1)S(1)} collective-permute-done((bf16[288,128]{1,0:T(8,128)(2,1)S(1)}, bf16[288,128]{1,0:T(8,128)(2,1)S(1)}, u32[]{:S(2)}, u32[]{:S(2)}) %collective-permute-start.1) | collective-permute-done | bytes 73760 | tf_op jit(solution)/shard_map/ppermute | solution.py:710
  14.7 2.5 %collective-permute-start.5 = (bf16[4,288,128]{2,1,0:T(8,128)(2,1)S(1)}, bf16[4,288,128]{2,1,0:T(8,128)(2,1)S(1)}, u32[]{:S(2)}, u32[]{:S(2)}) collective-permute-start(bf16[4,288,128]{2,1,0:T(8,128)(2,1)S(1)} %pad_maximum_fusion.refs_3_), channel_id=1, source_target_pairs={{0,24},{8,16},{16,8},{24,0},{1,25},{9,17},{17,9},{25,1},{2,26},{10... | collective-permute-start | bytes 884744 | tf_op jit(solution)/shard_map/ppermute | solution.py:710
  17.2 0.5 collective-permute-start.4
  17.7 0.5 collective-permute-start.3
  18.2 7.4 %collective-permute-done.5.refs_6_ = bf16[4,288,128]{2,1,0:T(8,128)(2,1)S(1)} collective-permute-done((bf16[4,288,128]{2,1,0:T(8,128)(2,1)S(1)}, bf16[4,288,128]{2,1,0:T(8,128)(2,1)S(1)}, u32[]{:S(2)}, u32[]{:S(2)}) %collective-permute-start.5) | collective-permute-done | bytes 294944 | tf_op jit(solution)/shard_map/ppermute | solution.py:710
  25.6 4.7 %collective-permute-done.4.refs_5_ = bf16[4,288,128]{2,1,0:T(8,128)(2,1)S(1)} collective-permute-done((bf16[4,288,128]{2,1,0:T(8,128)(2,1)S(1)}, bf16[4,288,128]{2,1,0:T(8,128)(2,1)S(1)}, u32[]{:S(2)}, u32[]{:S(2)}) %collective-permute-start.4) | collective-permute-done | bytes 294944 | tf_op jit(solution)/shard_map/ppermute | solution.py:710
  30.3 0.3 collective-permute-done.3.refs_4_
  30.6 0.2 collective-permute-start.7
  31.5 0.4 collective-permute-done.8.refs_9_
  31.9 0.4 collective-permute-done.7.refs_8_
  32.3 1.0 %copy-done.6 = bf16[1,32,32,256]{3,2,1,0:T(8,128)(2,1)S(1)} copy-done((bf16[1,32,32,256]{3,2,1,0:T(8,128)(2,1)S(1)}, bf16[1,32,32,256]{3,2,1,0:T(8,128)(2,1)}, u32[]{:S(2)}) %copy-start.6) | copy-done | bytes 524312
  33.4 30.7 %block.1 = (bf16[32,32,256]{2,1,0:T(8,128)(2,1)}, bf16[64,64,128]{2,1,0:T(8,128)(2,1)}, bf16[16,512]{1,0:T(8,128)(2,1)S(1)}, bf16[512,512]{1,0:T(8,128)(2,1)S(1)...) custom-call(s32[1]{0:T(128)S(6)} %copy.14.refs_0_, ...), custom_call_target="tpu_custom_call" | custom-call | tf_op jit(solution)/shard_map/block/pallas_call | solution.py:492
  64.1 0.2 collective-permute-start.10
  64.3 2.0 %collective-permute-done.10.refs_1_ = bf16[2640,128]{1,0:T(8,128)(2,1)S(1)} collective-permute-done((bf16[2640,128]{1,0:T(8,128)(2,1)S(1)}, bf16[2640,128]{1,0:T(8,128)(2,1)S(1)}, u32[]{:S(2)}, u32[]{:S(2)}) %collective-permute-start.10) | collective-permute-done | bytes 675872 | tf_op jit(solution)/shard_map/ppermute | solution.py:710
  66.2 1.3 %copy-done = f32[2600,128]{1,0:T(8,128)S(1)} copy-done((f32[2600,128]{1,0:T(8,128)S(1)}, f32[2600,128]{1,0:T(8,128)}, u32[]{:S(2)}) %copy-start) | copy-done | bytes 1331224
  67.5 0.2 merge.2
  67.7 1.8 %collective-permute-start.11 = (bf16[720,128]{1,0:T(8,128)(2,1)S(1)}, bf16[720,128]{1,0:T(8,128)(2,1)S(1)}, u32[]{:S(2)}, u32[]{:S(2)}) collective-permute-start(bf16[720,128]{1,0:T(8,128)(2,1)S(1)} %get-tuple-element.35), channel_id=1, source_target_pairs={{0,8},{8,0},{16,24},{24,16},{1,9},{9,1},{17,25},{25,17},{2,10},{10... | collective-permute-start | bytes 552968 | tf_op jit(solution)/shard_map/ppermute | solution.py:710
  69.5 0.7 collective-permute-start.12
  70.2 1.1 %collective-permute-start.13 = (bf16[720,128]{1,0:T(8,128)(2,1)S(1)}, bf16[720,128]{1,0:T(8,128)(2,1)S(1)}, u32[]{:S(2)}, u32[]{:S(2)}) collective-permute-start(bf16[720,128]{1,0:T(8,128)(2,1)S(1)} %get-tuple-element.37), channel_id=1, source_target_pairs={{0,24},{8,16},{16,8},{24,0},{1,25},{9,17},{17,9},{25,1},{2,26},{10... | collective-permute-start | bytes 552968 | tf_op jit(solution)/shard_map/ppermute | solution.py:710
  71.3 4.0 %collective-permute-done.11.refs_1_ = bf16[720,128]{1,0:T(8,128)(2,1)S(1)} collective-permute-done((bf16[720,128]{1,0:T(8,128)(2,1)S(1)}, bf16[720,128]{1,0:T(8,128)(2,1)S(1)}, u32[]{:S(2)}, u32[]{:S(2)}) %collective-permute-start.11) | collective-permute-done | bytes 184352 | tf_op jit(solution)/shard_map/ppermute | solution.py:710
  75.3 4.6 %collective-permute-done.12.refs_2_ = bf16[720,128]{1,0:T(8,128)(2,1)S(1)} collective-permute-done((bf16[720,128]{1,0:T(8,128)(2,1)S(1)}, bf16[720,128]{1,0:T(8,128)(2,1)S(1)}, u32[]{:S(2)}, u32[]{:S(2)}) %collective-permute-start.12) | collective-permute-done | bytes 184352 | tf_op jit(solution)/shard_map/ppermute | solution.py:710
  80.1 2.1 %collective-permute-start.15 = (bf16[240,128]{1,0:T(8,128)(2,1)S(1)}, bf16[240,128]{1,0:T(8,128)(2,1)S(1)}, u32[]{:S(2)}, u32[]{:S(2)}) collective-permute-start(bf16[240,128]{1,0:T(8,128)(2,1)S(1)} %get-tuple-element.40), channel_id=1, source_target_pairs={{0,4},{1,5},{2,6},{3,7},{4,0},{5,1},{6,2},{7,3},{8,12},{9,13},{10,... | collective-permute-start | bytes 184328 | tf_op jit(solution)/shard_map/ppermute | solution.py:710
  82.2 2.2 %collective-permute-start.16 = (bf16[240,128]{1,0:T(8,128)(2,1)S(1)}, bf16[240,128]{1,0:T(8,128)(2,1)S(1)}, u32[]{:S(2)}, u32[]{:S(2)}) collective-permute-start(bf16[240,128]{1,0:T(8,128)(2,1)S(1)} %get-tuple-element.41), channel_id=1, source_target_pairs={{0,6},{1,7},{2,4},{3,5},{4,2},{5,3},{6,0},{7,1},{8,14},{9,15},{10,... | collective-permute-start | bytes 184328 | tf_op jit(solution)/shard_map/ppermute | solution.py:710
  84.4 2.3 %collective-permute-done.15.refs_2_ = bf16[240,128]{1,0:T(8,128)(2,1)S(1)} collective-permute-done((bf16[240,128]{1,0:T(8,128)(2,1)S(1)}, bf16[240,128]{1,0:T(8,128)(2,1)S(1)}, u32[]{:S(2)}, u32[]{:S(2)}) %collective-permute-start.15) | collective-permute-done | bytes 61472 | tf_op jit(solution)/shard_map/ppermute | solution.py:710
  86.7 1.6 %collective-permute-done.16.refs_3_ = bf16[240,128]{1,0:T(8,128)(2,1)S(1)} collective-permute-done((bf16[240,128]{1,0:T(8,128)(2,1)S(1)}, bf16[240,128]{1,0:T(8,128)(2,1)S(1)}, u32[]{:S(2)}, u32[]{:S(2)}) %collective-permute-start.16) | collective-permute-done | bytes 61472 | tf_op jit(solution)/shard_map/ppermute | solution.py:710
  88.2 2.4 %update.1 = (f32[4,4,4608]{2,1,0:T(4,128)}, f32[4,12544]{1,0:T(4,128)}, f32[4,56]{1,0:T(4,128)}, bf16[4,4608]{1,0:T(4,128)(2,1)}, bf16[98,128]{1,0:T(8,128)(2,1)}, /*index=5*/bf16[1,56]{1,0:T(2,128)(2,1)}) custom-call(f32[200,128]{1,0:T(8,128)S(1)} %get-tuple-element.38.refs_0_, bf16[240,128]{1,0:T(8,128)(2,1)S(1)} %collective-permute-done.14.refs_1_, ...), custom_call_target="tpu_custom_call" | custom-call | tf_op jit(solution)/shard_map/update/pallas_call | solution.py:693
  (26 shorter events, 0.5 us)
Async XLA Ops:
  0.6 1.0 %copy-start.1 = (f32[4,4,4608]{2,1,0:T(4,128)S(1)}, f32[4,4,4608]{2,1,0:T(4,128)}, u32[]{:S(2)}) copy-start(f32[4,4,4608]{2,1,0:T(4,128)} %refs_8_.1) | copy-start | bytes 884740
  1.6 0.9 %copy-start.4 = (f32[4,12544]{1,0:T(4,128)S(1)}, f32[4,12544]{1,0:T(4,128)}, u32[]{:S(2)}) copy-start(f32[4,12544]{1,0:T(4,128)} %refs_9_.1) | copy-start | bytes 602116
  2.5 0.7 copy-start.7
  3.2 29.1 %copy-start.3 = (bf16[1,64,64,128]{3,2,1,0:T(8,128)(2,1)S(1)}, bf16[1,64,64,128]{3,2,1,0:T(8,128)(2,1)}, u32[]{:S(2)}) copy-start(bf16[1,64,64,128]{3,2,1,0:T(8,128)(2,1)} %param.6) | copy-start | bytes 3145732
  3.3 7.8 %collective-permute-start.2 = (bf16[288,128]{1,0:T(8,128)(2,1)S(1)}, bf16[288,128]{1,0:T(8,128)(2,1)S(1)}, u32[]{:S(2)}, u32[]{:S(2)}) collective-permute-start(bf16[288,128]{1,0:T(8,128)(2,1)S(1)} %pack.1), channel_id=1, source_target_pairs={{0,6},{1,7},{2,4},{3,5},{4,2},{5,3},{6,0},{7,1},{8,14},{9,15},{10,... | collective-permute-start | bytes 221192 | tf_op jit(solution)/shard_map/ppermute | solution.py:710
  8.4 6.2 %collective-permute-start.1 = (bf16[288,128]{1,0:T(8,128)(2,1)S(1)}, bf16[288,128]{1,0:T(8,128)(2,1)S(1)}, u32[]{:S(2)}, u32[]{:S(2)}) collective-permute-start(bf16[288,128]{1,0:T(8,128)(2,1)S(1)} %pack.1), channel_id=1, source_target_pairs={{0,4},{1,5},{2,6},{3,7},{4,0},{5,1},{6,2},{7,3},{8,12},{9,13},{10,... | collective-permute-start | bytes 221192 | tf_op jit(solution)/shard_map/ppermute | solution.py:710
  8.4 6.2 %collective-permute-start = (bf16[288,128]{1,0:T(8,128)(2,1)S(1)}, bf16[288,128]{1,0:T(8,128)(2,1)S(1)}, u32[]{:S(2)}, u32[]{:S(2)}) collective-permute-start(bf16[288,128]{1,0:T(8,128)(2,1)S(1)} %pack.1), channel_id=1, source_target_pairs={{0,2},{1,3},{2,0},{3,1},{4,6},{5,7},{6,4},{7,5},{8,10},{9,11},{10,... | collective-permute-start | bytes 221192 | tf_op jit(solution)/shard_map/ppermute | solution.py:710
  14.7 11.0 %collective-permute-start.5 = (bf16[4,288,128]{2,1,0:T(8,128)(2,1)S(1)}, bf16[4,288,128]{2,1,0:T(8,128)(2,1)S(1)}, u32[]{:S(2)}, u32[]{:S(2)}) collective-permute-start(bf16[4,288,128]{2,1,0:T(8,128)(2,1)S(1)} %pad_maximum_fusion.refs_3_), channel_id=1, source_target_pairs={{0,24},{8,16},{16,8},{24,0},{1,25},{9,17},{17,9},{25,1},{2,26},{10... | collective-permute-start | bytes 884744 | tf_op jit(solution)/shard_map/ppermute | solution.py:710
  17.2 13.1 %collective-permute-start.4 = (bf16[4,288,128]{2,1,0:T(8,128)(2,1)S(1)}, bf16[4,288,128]{2,1,0:T(8,128)(2,1)S(1)}, u32[]{:S(2)}, u32[]{:S(2)}) collective-permute-start(bf16[4,288,128]{2,1,0:T(8,128)(2,1)S(1)} %pad_maximum_fusion.refs_3_), channel_id=1, source_target_pairs={{0,16},{8,24},{16,0},{24,8},{1,17},{9,25},{17,1},{25,9},{2,18},{10... | collective-permute-start | bytes 884744 | tf_op jit(solution)/shard_map/ppermute | solution.py:710
  17.7 12.9 %collective-permute-start.3 = (bf16[4,288,128]{2,1,0:T(8,128)(2,1)S(1)}, bf16[4,288,128]{2,1,0:T(8,128)(2,1)S(1)}, u32[]{:S(2)}, u32[]{:S(2)}) collective-permute-start(bf16[4,288,128]{2,1,0:T(8,128)(2,1)S(1)} %pad_maximum_fusion.refs_3_), channel_id=1, source_target_pairs={{0,8},{8,0},{16,24},{24,16},{1,9},{9,1},{17,25},{25,17},{2,10},{10... | collective-permute-start | bytes 884744 | tf_op jit(solution)/shard_map/ppermute | solution.py:710
  18.2 13.3 %collective-permute-start.6 = (bf16[4,288,128]{2,1,0:T(8,128)(2,1)S(1)}, bf16[4,288,128]{2,1,0:T(8,128)(2,1)S(1)}, u32[]{:S(2)}, u32[]{:S(2)}) collective-permute-start(bf16[4,288,128]{2,1,0:T(8,128)(2,1)S(1)} %pad_maximum_fusion.refs_3_), channel_id=1, source_target_pairs={{0,1},{1,0},{2,3},{3,2},{4,5},{5,4},{6,7},{7,6},{8,9},{9,8},{10,11... | collective-permute-start | bytes 884744 | tf_op jit(solution)/shard_map/ppermute | solution.py:710
  25.6 5.9 %collective-permute-start.9 = (bf16[4,288,128]{2,1,0:T(8,128)(2,1)S(1)}, bf16[4,288,128]{2,1,0:T(8,128)(2,1)S(1)}, u32[]{:S(2)}, u32[]{:S(2)}) collective-permute-start(bf16[4,288,128]{2,1,0:T(8,128)(2,1)S(1)} %collective-permute-done.5.refs_6_), channel_id=1, source_target_pairs={{0,1},{1,0},{2,3},{3,2},{4,5},{5,4},{6,7},{7,6},{8,9},{9,8},{10,11... | collective-permute-start | bytes 884744 | tf_op jit(solution)/shard_map/ppermute | solution.py:710
  30.3 1.6 %collective-permute-start.8 = (bf16[4,288,128]{2,1,0:T(8,128)(2,1)S(1)}, bf16[4,288,128]{2,1,0:T(8,128)(2,1)S(1)}, u32[]{:S(2)}, u32[]{:S(2)}) collective-permute-start(bf16[4,288,128]{2,1,0:T(8,128)(2,1)S(1)} %collective-permute-done.4.refs_5_), channel_id=1, source_target_pairs={{0,1},{1,0},{2,3},{3,2},{4,5},{5,4},{6,7},{7,6},{8,9},{9,8},{10,11... | collective-permute-start | bytes 884744 | tf_op jit(solution)/shard_map/ppermute | solution.py:710
  30.6 1.7 %collective-permute-start.7 = (bf16[4,288,128]{2,1,0:T(8,128)(2,1)S(1)}, bf16[4,288,128]{2,1,0:T(8,128)(2,1)S(1)}, u32[]{:S(2)}, u32[]{:S(2)}) collective-permute-start(bf16[4,288,128]{2,1,0:T(8,128)(2,1)S(1)} %collective-permute-done.3.refs_4_), channel_id=1, source_target_pairs={{0,1},{1,0},{2,3},{3,2},{4,5},{5,4},{6,7},{7,6},{8,9},{9,8},{10,11... | collective-permute-start | bytes 884744 | tf_op jit(solution)/shard_map/ppermute | solution.py:710
  32.3 1.0 %copy-start.6 = (bf16[1,32,32,256]{3,2,1,0:T(8,128)(2,1)S(1)}, bf16[1,32,32,256]{3,2,1,0:T(8,128)(2,1)}, u32[]{:S(2)}) copy-start(bf16[1,32,32,256]{3,2,1,0:T(8,128)(2,1)} %param.7) | copy-start | bytes 1572868
  64.1 2.1 %collective-permute-start.10 = (bf16[2640,128]{1,0:T(8,128)(2,1)S(1)}, bf16[2640,128]{1,0:T(8,128)(2,1)S(1)}, u32[]{:S(2)}, u32[]{:S(2)}) collective-permute-start(bf16[2640,128]{1,0:T(8,128)(2,1)S(1)} %get-tuple-element.33), channel_id=1, source_target_pairs={{0,1},{1,0},{2,3},{3,2},{4,5},{5,4},{6,7},{7,6},{8,9},{9,8},{10,11... | collective-permute-start | bytes 2027528 | tf_op jit(solution)/shard_map/ppermute | solution.py:710
  66.2 1.3 %copy-start = (f32[2600,128]{1,0:T(8,128)S(1)}, f32[2600,128]{1,0:T(8,128)}, u32[]{:S(2)}) copy-start(f32[2600,128]{1,0:T(8,128)} %get-tuple-element.32.refs_0_) | copy-start | bytes 3993604
  67.5 20.7 %copy-start.2 = (f32[4,4,4608]{2,1,0:T(4,128)S(1)}, f32[4,4,4608]{2,1,0:T(4,128)}, u32[]{:S(2)}) copy-start(f32[4,4,4608]{2,1,0:T(4,128)} %refs_8_.1) | copy-start | bytes 884740
  67.5 20.7 %copy-start.5 = (f32[4,12544]{1,0:T(4,128)S(1)}, f32[4,12544]{1,0:T(4,128)}, u32[]{:S(2)}) copy-start(f32[4,12544]{1,0:T(4,128)} %refs_9_.1) | copy-start | bytes 602116
  67.5 20.7 %copy-start.8 = (f32[4,56]{1,0:T(4,128)S(1)}, f32[4,56]{1,0:T(4,128)}, u32[]{:S(2)}) copy-start(f32[4,56]{1,0:T(4,128)} %refs_10_.1) | copy-start | bytes 2692
  67.7 7.5 %collective-permute-start.11 = (bf16[720,128]{1,0:T(8,128)(2,1)S(1)}, bf16[720,128]{1,0:T(8,128)(2,1)S(1)}, u32[]{:S(2)}, u32[]{:S(2)}) collective-permute-start(bf16[720,128]{1,0:T(8,128)(2,1)S(1)} %get-tuple-element.35), channel_id=1, source_target_pairs={{0,8},{8,0},{16,24},{24,16},{1,9},{9,1},{17,25},{25,17},{2,10},{10... | collective-permute-start | bytes 552968 | tf_op jit(solution)/shard_map/ppermute | solution.py:710
  69.5 10.4 %collective-permute-start.12 = (bf16[720,128]{1,0:T(8,128)(2,1)S(1)}, bf16[720,128]{1,0:T(8,128)(2,1)S(1)}, u32[]{:S(2)}, u32[]{:S(2)}) collective-permute-start(bf16[720,128]{1,0:T(8,128)(2,1)S(1)} %get-tuple-element.36), channel_id=1, source_target_pairs={{0,16},{8,24},{16,0},{24,8},{1,17},{9,25},{17,1},{25,9},{2,18},{10... | collective-permute-start | bytes 552968 | tf_op jit(solution)/shard_map/ppermute | solution.py:710
  70.2 9.7 %collective-permute-start.13 = (bf16[720,128]{1,0:T(8,128)(2,1)S(1)}, bf16[720,128]{1,0:T(8,128)(2,1)S(1)}, u32[]{:S(2)}, u32[]{:S(2)}) collective-permute-start(bf16[720,128]{1,0:T(8,128)(2,1)S(1)} %get-tuple-element.37), channel_id=1, source_target_pairs={{0,24},{8,16},{16,8},{24,0},{1,25},{9,17},{17,9},{25,1},{2,26},{10... | collective-permute-start | bytes 552968 | tf_op jit(solution)/shard_map/ppermute | solution.py:710
  79.9 4.5 %collective-permute-start.14 = (bf16[240,128]{1,0:T(8,128)(2,1)S(1)}, bf16[240,128]{1,0:T(8,128)(2,1)S(1)}, u32[]{:S(2)}, u32[]{:S(2)}) collective-permute-start(bf16[240,128]{1,0:T(8,128)(2,1)S(1)} %get-tuple-element.39), channel_id=1, source_target_pairs={{0,2},{1,3},{2,0},{3,1},{4,6},{5,7},{6,4},{7,5},{8,10},{9,11},{10,... | collective-permute-start | bytes 184328 | tf_op jit(solution)/shard_map/ppermute | solution.py:710
  80.1 6.6 %collective-permute-start.15 = (bf16[240,128]{1,0:T(8,128)(2,1)S(1)}, bf16[240,128]{1,0:T(8,128)(2,1)S(1)}, u32[]{:S(2)}, u32[]{:S(2)}) collective-permute-start(bf16[240,128]{1,0:T(8,128)(2,1)S(1)} %get-tuple-element.40), channel_id=1, source_target_pairs={{0,4},{1,5},{2,6},{3,7},{4,0},{5,1},{6,2},{7,3},{8,12},{9,13},{10,... | collective-permute-start | bytes 184328 | tf_op jit(solution)/shard_map/ppermute | solution.py:710
  82.2 6.0 %collective-permute-start.16 = (bf16[240,128]{1,0:T(8,128)(2,1)S(1)}, bf16[240,128]{1,0:T(8,128)(2,1)S(1)}, u32[]{:S(2)}, u32[]{:S(2)}) collective-permute-start(bf16[240,128]{1,0:T(8,128)(2,1)S(1)} %get-tuple-element.41), channel_id=1, source_target_pairs={{0,6},{1,7},{2,4},{3,5},{4,2},{5,3},{6,0},{7,1},{8,14},{9,15},{10,... | collective-permute-start | bytes 184328 | tf_op jit(solution)/shard_map/ppermute | solution.py:710

commit v3 on v2

--- a/solution.py
+++ b/solution.py
@@ -148,38 +148,154 @@
     return lax.axis_index(outer) * inner_size + lax.axis_index(inner)
 
 
-def take_shards(plan, me, parts, conv, dense):
-    conv[...] = jnp.zeros(conv.shape, f32)
-    dense[...] = jnp.zeros(dense.shape, f32)
-    small = jnp.zeros((16, C), f32)
-    for (near, turn), part_ref in zip(plan.sources, parts):
-        values = part_ref[near].astype(f32)
-        owner = me ^ turn
-        first = plan.tile_of(owner * plan.conv_rows)
-        for k in range(4):
-            conv[k, pl.ds(first, plan.conv_pad), :] += values[k * plan.conv_pad : (k + 1) * plan.conv_pad]
-        first = plan.tile_of(owner * plan.dense_rows)
-        dense[pl.ds(first, plan.dense_pad), :] += values[plan.dense_at : plan.dense_at + plan.dense_pad]
-        small = small + values[plan.small_at : plan.small_at + 16]
-    return small
+def prepare_body(x_ref, cot_ref, stats_ref, cw, gdb_ref):
+    zero8 = jnp.zeros((8, C), f32)
+
+    def read_x(i):
+        return x_ref[pl.ds(i * R, R)].astype(f32)
+
+    total = lax.fori_loop(0, H // R, lambda i, s: s + fold(read_x(i)), zero8)
+    mean = group_sum(total_of(total)) * (1.0 / PER_GROUP)
+
+    def square_x(i, s):
+        d = read_x(i) - one(mean)
+        return s + fold(d * d)
+
+    var = group_sum(total_of(lax.fori_loop(0, H // R, square_x, zero8))) * (1.0 / PER_GROUP)
+    stats_ref[0:8] = mean
+    stats_ref[8:16] = lax.rsqrt(var + norm_eps)
+    cw[H // 2 : H // 2 + 1] = jnp.zeros((1, W // 2, 4 * C), bf16)
+
+    def cot_windows(i, s):
+        values = cot_ref[pl.ds(i * Q, Q)].astype(f32)
+        place = lax.broadcasted_iota(jnp.int32, values.shape, 1)
+        after = jnp.where(place == W // 2 - 1, 0.0, pltpu.roll(values, W // 2 - 1, 1))
+        cw[pl.ds(i * Q, Q), :, 0 : 2 * C] = values.astype(bf16)
+        cw[pl.ds(i * Q, Q), :, 2 * C :] = after.astype(bf16)
+        return s + fold(values)
+
+    gdb_ref[...] = total_of(lax.fori_loop(0, H // 2 // Q, cot_windows, jnp.zeros((8, 2 * C), f32)))
+
+
+def run_prepare(x, cot):
+    struct = jax.ShapeDtypeStruct
+    return pl.pallas_call(
+        prepare_body,
+        out_shape=[struct((16, C), f32), struct((H // 2 + 1, W // 2, 4 * C), bf16), struct((8, 2 * C), f32)],
+        in_specs=vmem_specs(2),
+        out_specs=vmem_specs(3),
+        compiler_params=limit(8),
+        cost_estimate=cost(2, 3 << 20),
+        name="prepare",
+    )(x, cot)
+
+
+def front_body(plan, *refs):
+    count = plan.parts if plan.rings else 2
+    x_ref, stats_ref = refs[:2]
+    inputs = refs[2 : 2 + count]
+    a1w, g1p, c1, moments_ref, k1_ref, smalls, conv, pair = refs[2 + count :]
+    if plan.rings:
+        me = position_of(plan.sizes)
+        conv[...] = jnp.zeros(conv.shape, f32)
+        small = jnp.zeros((16, C), f32)
+        row = lax.broadcasted_iota(jnp.int32, (16, C), 0)
+        lane = lax.broadcasted_iota(jnp.int32, (16, C), 1)
+        for part, place, turn in plan.sources:
+            owner = me ^ turn
+            values = inputs[part][place, 0 : plan.first_rows].astype(f32)
+            first = plan.tile_of(owner * plan.conv_rows)
+            conv[pl.ds(first, plan.conv_pad), :] += values[: plan.conv_pad]
+            at = row * C + lane - owner * plan.small_len
+            own = jnp.broadcast_to(values[plan.conv_pad : plan.conv_pad + 1], (16, C))
+            small = jnp.where((at >= 0) & (at < plan.small_len), own, small)
+        smalls[...] = small
+        k1_ref[...] = conv[0:KERNEL_ROWS].astype(bf16)
+    else:
+        k1_ref[...] = inputs[0][...]
+        smalls[0:14] = inputs[1][...].astype(f32)
+    gain1, bias1, cb1 = [jnp.broadcast_to(smalls[i : i + 1, :], (8, C)) for i in range(3)]
+    mean1 = stats_ref[0:8]
+    slope1 = stats_ref[8:16] * (1.0 + gain1)
+    zero8 = jnp.zeros((8, C), f32)
+    clear_edges(a1w)
+
+    def front1(i, carry):
+        v = (x_ref[pl.ds(i * R, R)].astype(f32) - one(mean1)) * one(slope1) + one(bias1)
+        prob = normal_cdf(v)
+        put_windows(a1w, i * R, v * prob)
+        g1p[pl.ds(i * R, R)] = gelu_slope(v, prob)
+        return carry
+
+    lax.fori_loop(0, H // R, front1, 0)
+    pair_forward(pair, k1_ref)
+
+    def conv1(i, s):
+        got = pair_conv(a1w, pair, i * Q)
+        for parity, place in enumerate(pairs_of(c1, i * Q)):
+            value = got[..., parity * C : (parity + 1) * C] + one(cb1)
+            place[...] = value
+            s = s + fold(value)
+        return s
+
+    centre = total_of(lax.fori_loop(0, H // 2 // Q, conv1, zero8)) * (1.0 / CELLS)
+
+    def square_c(i, s):
+        d = c1[pl.ds(i * R, R)] - one(centre)
+        return s + fold(d * d)
+
+    moments_ref[0:8] = centre
+    moments_ref[8:16] = total_of(lax.fori_loop(0, H // R, square_c, zero8)) * (1.0 / CELLS)
+
+
+def run_front(plan, x, stats, inputs):
+    struct = jax.ShapeDtypeStruct
+    return pl.pallas_call(
+        functools.partial(front_body, plan),
+        out_shape=[
+            struct((H + 2, W, 3 * C), bf16),
+            struct((H, W, C), f32),
+            struct((H, W, C), f32),
+            struct((16, C), f32),
+            struct((KERNEL_ROWS, C), bf16),
+            struct((16, C), f32),
+        ],
+        in_specs=vmem_specs(2 + len(inputs)),
+        out_specs=vmem_specs(6),
+        scratch_shapes=[
+            pltpu.VMEM((KERNEL_ROWS + 2 * plan.conv_pad, C), f32),
+            pltpu.VMEM((12 * C, 2 * C), bf16),
+        ],
+        compiler_params=limit(20),
+        cost_estimate=cost(1300, 8 << 20),
+        name="front",
+    )(x, stats, *inputs)
 
 
 def block_body(plan, *refs):
     refs = list(refs)
-    cls_ref, x_ref, cot_ref = refs[:3]
-    inputs = refs[3 : 3 + plan.inputs]
-    out_ref, dx_ref, table_ref, m1_ref, m2_ref, hidden_ref = refs[3 + plan.inputs : 9 + plan.inputs]
-    results = refs[9 + plan.inputs : 11 + plan.inputs]
-    a1w, a2w, tw, rw, cw, c1, g1p, g2p, drf, pair, conv, dense, kernels, smalls = refs[11 + plan.inputs :]
+    cls_ref, x_ref, cot_ref, stats_ref, cw, gdb_ref, a1w, g1p, c1, moments_ref, k1_ref, smalls = refs[:12]
+    count = plan.parts if plan.rings else 2
+    inputs = refs[12 : 12 + count]
+    out_hbm, dx_hbm, table_ref, m1_ref, m2_ref, hidden_ref = refs[12 + count : 18 + count]
+    results = refs[18 + count : 20 + count]
+    a2w, tw, rw, g2p, drf, pair, conv, dense, kernels, out_ref, dx_ref, out_sem, dx_sem = refs[20 + count :]
     me = position_of(plan.sizes)
     if plan.rings:
-        parts = [ref for ref in inputs for _ in range(plan.line)]
-        smalls[...] = take_shards(plan, me, parts, conv, dense)
-        kernels[...] = conv[:, 0:KERNEL_ROWS].astype(bf16)
+        conv[1:4] = jnp.zeros((3,) + conv.shape[1:], f32)
+        dense[...] = jnp.zeros(dense.shape, f32)
+        for part, place, turn in plan.sources:
+            owner = me ^ turn
+            values = inputs[part][place, plan.first_rows : plan.own_rows].astype(f32)
+            first = plan.tile_of(owner * plan.conv_rows)
+            for k in range(3):
+                conv[k + 1, pl.ds(first, plan.conv_pad), :] += values[k * plan.conv_pad : (k + 1) * plan.conv_pad]
+            first = plan.tile_of(owner * plan.dense_rows)
+            dense[pl.ds(first, plan.dense_pad), :] += values[plan.dense_at : plan.dense_at + plan.dense_pad]
+        kernels[...] = conv[1:4, 0:KERNEL_ROWS].astype(bf16)
     else:
         kernels[...] = inputs[0][...]
         dense[0:MLP_ROWS] = inputs[1][...].astype(f32)
-        smalls[0:14] = inputs[2][...].astype(f32)
 
     def lanes(first, rows, parts):
         pieces = [dense[pl.ds(first + part, rows, parts), :] for part in range(parts)]
@@ -188,7 +304,7 @@
     table_ref[...] = lanes(0, NCLASS, EMB // C)
     m1_ref[...] = lanes(TABLE_ROWS, EMB, EMB // C)
     m2_ref[...] = lanes(TABLE_ROWS + M1_ROWS, EMB, 2)
-    k1_ref, k2_ref, kd0_ref, kd1_ref = [kernels.at[k] for k in range(4)]
+    k2_ref, kd0_ref, kd1_ref = [kernels.at[k] for k in range(3)]
     gk1_ref, gk2_ref, gkd0_ref, gkd1_ref = [conv.at[k] for k in range(4)]
 
     def small_row(index):
@@ -200,7 +316,7 @@
     def alone(step):
         pl.when(me >= 0)(step)
 
-    gain1, bias1, cb1, gain2, bias2, cb2 = [small_row(i) for i in range(6)]
+    gain1, _, _, gain2, bias2, cb2 = [small_row(i) for i in range(6)]
     zero8 = jnp.zeros((8, C), f32)
 
     hidden = mm(table_ref[...], m1_ref[...]) + small_run(8, 4)
@@ -212,47 +328,8 @@
     scale = jnp.broadcast_to(1.0 + chosen[:, :C], (8, C))
     shift = jnp.broadcast_to(chosen[:, C:], (8, C))
 
-    def read_x(i):
-        return x_ref[pl.ds(i * R, R)].astype(f32)
-
-    total = lax.fori_loop(0, H // R, lambda i, s: s + fold(read_x(i)), zero8)
-    mean1 = group_sum(total_of(total)) * (1.0 / PER_GROUP)
-
-    def square_x(i, s):
-        d = read_x(i) - one(mean1)
-        return s + fold(d * d)
-
-    var1 = group_sum(total_of(lax.fori_loop(0, H // R, square_x, zero8))) * (1.0 / PER_GROUP)
-    rs1 = lax.rsqrt(var1 + norm_eps)
-    slope1 = rs1 * (1.0 + gain1)
-    clear_edges(a1w)
-
-    def front1(i, carry):
-        v = (read_x(i) - one(mean1)) * one(slope1) + one(bias1)
-        prob = normal_cdf(v)
-        put_windows(a1w, i * R, v * prob)
-        g1p[pl.ds(i * R, R)] = gelu_slope(v, prob)
-        return carry
-
-    lax.fori_loop(0, H // R, front1, 0)
-
-    pair_forward(pair, k1_ref)
-
-    def conv1(i, s):
-        got = pair_conv(a1w, pair, i * Q)
-        for parity, place in enumerate(pairs_of(c1, i * Q)):
-            value = got[..., parity * C : (parity + 1) * C] + one(cb1)
-            place[...] = value
-            s = s + fold(value)
-        return s
-
-    centre = total_of(lax.fori_loop(0, H // 2 // Q, conv1, zero8)) * (1.0 / CELLS)
-
-    def square_c(i, s):
-        d = c1[pl.ds(i * R, R)] - one(centre)
-        return s + fold(d * d)
-
-    spread = total_of(lax.fori_loop(0, H // R, square_c, zero8)) * (1.0 / CELLS)
+    mean1, rs1 = stats_ref[0:8], stats_ref[8:16]
+    centre, spread = moments_ref[0:8], moments_ref[8:16]
 
     centre_s = centre * scale + shift
     mean2 = group_sum(centre_s) * (GROUPS / C)
@@ -312,6 +389,8 @@
         return carry
 
     lax.fori_loop(0, H // 2 // Q, down, 0)
+    out_copy = pltpu.make_async_copy(out_ref, out_hbm, out_sem)
+    out_copy.start()
     @alone
     def _():
         gkd = mm(down_rows(0, H // 2), cot_ref[...].reshape(CELLS // 4, 2 * C), TN)
@@ -319,17 +398,7 @@
         gkd1_ref[0:KERNEL_ROWS] = gkd[:, C:]
 
 
-    cw[H // 2 : H // 2 + 1] = jnp.zeros((1, W // 2, 4 * C), bf16)
-
-    def cot_windows(i, s):
-        values = cot_ref[pl.ds(i * Q, Q)].astype(f32)
-        place = lax.broadcasted_iota(jnp.int32, values.shape, 1)
-        after = jnp.where(place == W // 2 - 1, 0.0, pltpu.roll(values, W // 2 - 1, 1))
-        cw[pl.ds(i * Q, Q), :, 0 : 2 * C] = values.astype(bf16)
-        cw[pl.ds(i * Q, Q), :, 2 * C :] = after.astype(bf16)
-        return s + fold(values)
-
-    gdb = total_of(lax.fori_loop(0, H // 2 // Q, cot_windows, jnp.zeros((8, 2 * C), f32)))
+    gdb = gdb_ref[...]
 
     def tap(i, j):
         return flip(kd[(3 * i + j) * C : (3 * i + j + 1) * C, :])
@@ -408,17 +477,28 @@
         dx_ref[pl.ds(i * R, R)] = (drf[pl.ds(i * R, R)] + dx).astype(bf16)
         return carry
 
-    lax.fori_loop(0, H // R, finish, 0)
+    dx_copies = []
+    for part in range(4):
+        lax.fori_loop(part * H // R // 4, (part + 1) * H // R // 4, finish, 0)
+        rows = pl.ds(part * H // 4, H // 4)
+        dx_copies.append(pltpu.make_async_copy(dx_ref.at[rows], dx_hbm.at[rows], dx_sem.at[part]))
+        dx_copies[-1].start()
 
     rows = [gg1, gb1, gsh * scale, gg2, gb2, gcb2, gdb[:, :C], gdb[:, C:]]
     rows = [row[0:1] for row in rows]
     rows = rows + [jnp.where(mine[:, :C], row[0:1], 0.0) for row in (gsc, gsh)]
     extra = jnp.concatenate(rows, axis=0)
-    if not plan.rings:
+    if plan.rings:
+        put_results(plan, me, conv, extra, *results)
+    else:
         results[0][...] = conv[:, 0:KERNEL_ROWS]
         results[1][...] = extra
-        return
-    keep_ref, send_ref = results
+    out_copy.wait()
+    for copy in dx_copies:
+        copy.wait()
+
+
+def put_results(plan, me, conv, extra, keep_ref, send_ref):
     for place, (core, turn) in enumerate(plan.targets):
         first = plan.tile_of((me ^ turn) * plan.conv_rows)
         block = jnp.concatenate([conv[k, pl.ds(first, plan.conv_pad), :] for k in range(4)], axis=0)
@@ -440,6 +520,10 @@
     return [pl.BlockSpec(memory_space=pltpu.VMEM)] * count
 
 
+def cost(mflops, moved):
+    return pl.CostEstimate(flops=mflops << 20, bytes_accessed=moved, transcendentals=0)
+
+
 def limit(size):
     return pltpu.CompilerParams(vmem_limit_bytes=size << 20)
 
@@ -451,17 +535,26 @@
         self.sizes, self.line = sizes, inner_size // 2
         self.conv_len, self.dense_len, self.small_len = conv_len, dense_len, small_len
         self.conv_rows, self.dense_rows = conv_len // C, dense_len // C
-        powers = all(n & (n - 1) == 0 for _, n in sizes) and inner_size > 1
+        powers = inner_size & (inner_size - 1) == 0 and inner_size >= 4 and outer_size == 4
         self.rings = powers and conv_len % C == 0 and dense_len % C == 0 and small_len <= C
-        self.inputs = 2 * outer_size if self.rings else 3
         self.conv_pad = self.padded(self.conv_rows, count)
         self.dense_pad = self.padded(self.dense_rows, count)
-        self.dense_at = 4 * self.conv_pad
-        self.small_at = self.dense_at + self.dense_pad
-        self.own_rows = -(-(self.small_at + 16) // 16) * 16
-        turns = [(core, plane * inner_size + 2 * near + core) for core in (0, 1) for plane in range(outer_size) for near in range(self.line)]
-        self.targets = turns
-        self.sources = [(place % self.line, turn) for place, (_, turn) in enumerate(turns)]
+        self.first_rows = -(-(self.conv_pad + 8) // 16) * 16
+        self.dense_at = 3 * self.conv_pad
+        self.own_rows = self.first_rows + -(-(self.dense_at + self.dense_pad) // 16) * 16
+        near = [2 * k for k in range(self.line)]
+        half = self.line // 2
+        held = [
+            [k ^ turn for turn in (0, inner_size) for k in near[:half]],
+            [k ^ turn for turn in (0, 2 * inner_size) for k in near[half:]],
+        ]
+        held += [[k ^ 2 * inner_size for k in held[0]], [k ^ inner_size for k in held[1]]]
+        held += [[k ^ 1 for k in part] for part in held]
+        self.parts = len(held)
+        self.sources = [(part, place, turn) for part, turns in enumerate(held) for place, turn in enumerate(turns)]
+        self.targets = [
+            (core, plane * inner_size + k + core) for core in (0, 1) for plane in range(outer_size) for k in near
+        ]
         self.half = count // 2
         self.width = 4 * self.conv_pad
 
@@ -472,7 +565,7 @@
         return pl.multiple_of(row // 8 * 8, 8)
 
 
-def run_block(plan, class_ids, x, cot, inputs):
+def run_block(plan, class_ids, x, cot, prepared, fronted, inputs):
     struct = jax.ShapeDtypeStruct
     shapes = [
         struct((H // 2, W // 2, 2 * C), bf16),
@@ -492,46 +585,50 @@
     return pl.pallas_call(
         functools.partial(block_body, plan),
         out_shape=shapes,
-        in_specs=[pl.BlockSpec(memory_space=pltpu.SMEM)] + vmem_specs(2 + len(inputs)),
-        out_specs=vmem_specs(8),
+        in_specs=[pl.BlockSpec(memory_space=pltpu.SMEM)] + vmem_specs(11 + len(inputs)),
+        out_specs=[pl.BlockSpec(memory_space=pltpu.HBM)] * 2 + vmem_specs(6),
         scratch_shapes=[
             windows,
             windows,
-            windows,
             pltpu.VMEM((H + 2, W // 2, 3 * C), bf16),
-            pltpu.VMEM((H // 2 + 1, W // 2, 4 * C), bf16),
-            plane,
-            plane,
             plane,
             plane,
             pltpu.VMEM((12 * C, 2 * C), bf16),
             pltpu.VMEM((4, KERNEL_ROWS + 2 * plan.conv_pad, C), f32),
             pltpu.VMEM((MLP_ROWS + 2 * plan.dense_pad, C), f32),
-            pltpu.VMEM((4, KERNEL_ROWS, C), bf16),
-            pltpu.VMEM((16, C), f32),
+            pltpu.VMEM((3, KERNEL_ROWS, C), bf16),
+            pltpu.VMEM((H // 2, W // 2, 2 * C), bf16),
+            pltpu.VMEM((H, W, C), bf16),
+            pltpu.SemaphoreType.DMA,
+            pltpu.SemaphoreType.DMA((4,)),
         ],
-        compiler_params=limit(48),
+        compiler_params=limit(36),
+        cost_estimate=cost(9000, 16 << 20),
         name="block",
-    )(class_ids, x, cot, *inputs)
-
-
-def pack_body(plan, conv_ref, dense_ref, small_ref, out_ref, rows):
+    )(class_ids, x, cot, *prepared, *fronted, *inputs)
+
+
+def pack_body(plan, conv_hbm, dense_hbm, small_hbm, out_ref, conv_ref, dense_ref, small_ref, rows, sems):
+    pairs = ((conv_hbm.at[0], conv_ref), (dense_hbm, dense_ref), (small_hbm, small_ref))
+    copies = [pltpu.make_async_copy(source, target, sems.at[k]) for k, (source, target) in enumerate(pairs)]
+    for copy in copies:
+        copy.start()
     me = position_of(plan.sizes)
     rows[...] = jnp.zeros(rows.shape, f32)
+    starts = [0] + [plan.first_rows + k * plan.conv_pad for k in range(3)]
     first = me * plan.conv_rows % 8
+    copies[0].wait()
     for r in range(plan.conv_rows):
-        rows[pl.ds(first + r, 4, plan.conv_pad), :] = conv_ref[0, :, r * C : (r + 1) * C]
-    first = plan.dense_at + me * plan.dense_rows % 8
+        for k in range(4):
+            rows[pl.ds(starts[k] + first + r, 1), :] = conv_ref[k : k + 1, r * C : (r + 1) * C]
+    copies[1].wait()
+    first = plan.first_rows + plan.dense_at + me * plan.dense_rows % 8
     for r in range(plan.dense_rows):
         rows[pl.ds(first + r, 1), :] = dense_ref[0:1, r * C : (r + 1) * C]
-    start = me * plan.small_len
+    copies[2].wait()
     own = jnp.concatenate([small_ref[0:1, :], jnp.zeros((1, C - plan.small_len), f32)], axis=1)
-    own = pltpu.roll(jnp.broadcast_to(own, (16, C)), start % C, 1)
-    row = lax.broadcasted_iota(jnp.int32, (16, C), 0)
-    lane = lax.broadcasted_iota(jnp.int32, (16, C), 1)
-    place = row * C + lane
-    mine = (place >= start) & (place < start + plan.small_len)
-    rows[plan.small_at : plan.small_at + 16] = jnp.where(mine, own, 0.0)
+    own = pltpu.roll(jnp.broadcast_to(own, (8, C)), me * plan.small_len % C, 1)
+    rows[plan.conv_pad : plan.conv_pad + 1] = own[0:1]
     out_ref[...] = rows[...].astype(bf16)
 
 
@@ -539,10 +636,16 @@
     return pl.pallas_call(
         functools.partial(pack_body, plan),
         out_shape=jax.ShapeDtypeStruct((plan.own_rows, C), bf16),
-        in_specs=vmem_specs(3),
+        in_specs=[pl.BlockSpec(memory_space=pltpu.HBM)] * 3,
         out_specs=pl.BlockSpec(memory_space=pltpu.VMEM),
-        scratch_shapes=[pltpu.VMEM((plan.own_rows, C), f32)],
-        compiler_params=limit(8),
+        scratch_shapes=[
+            pltpu.VMEM((4, plan.conv_len), f32),
+            pltpu.VMEM((4, plan.dense_len), f32),
+            pltpu.VMEM((4, plan.small_len), f32),
+            pltpu.VMEM((plan.own_rows, C), f32),
+            pltpu.SemaphoreType.DMA((3,)),
+        ],
+        compiler_params=pltpu.CompilerParams(vmem_limit_bytes=(64 << 20) - (160 << 10)),
         name="pack",
     )(conv_state, mlp_state, small_state)
 
@@ -710,11 +813,16 @@
     return lax.ppermute(values, axis, [(i, i ^ turn) for i in range(size)])
 
 
-def gather_ring(plan, own):
+def gather_ring(plan, own, prepare):
     (outer, outer_size), (inner, inner_size) = plan.sizes
-    line = jnp.stack([own] + [swap(own, inner, inner_size, 2 * k) for k in range(1, plan.line)])
-    planes = [line] + [swap(line, outer, outer_size, k) for k in range(1, outer_size)]
-    return planes + [swap(plane, inner, inner_size, 1) for plane in planes]
+    line = [own] + [swap(own, inner, inner_size, 2 * k) for k in range(1, plan.line)]
+    line, prepared = lax.optimization_barrier((line, prepare()))
+    line = jnp.stack(line)
+    held = []
+    for part, turn in ((line[: plan.line // 2], 1), (line[plan.line // 2 :], 2)):
+        held.append(jnp.concatenate([part, swap(part, outer, outer_size, turn)]))
+    held = held + [swap(part, outer, outer_size, 2 - k) for k, part in enumerate(held)]
+    return prepared, held + [swap(part, inner, inner_size, 1) for part in held]
 
 
 def reduce_ring(plan, keep, send):
@@ -751,18 +859,18 @@
 def per_device(sizes, samples, cotangent, class_ids, *states):
     conv_state, mlp_state, small_state = states
     plan = Plan(sizes, conv_state.shape[2], mlp_state.shape[1], small_state.shape[1])
+    x, cot = samples[0], cotangent[0]
     if plan.rings:
-        inputs = gather_ring(plan, run_pack(plan, *states))
+        prepared, firsts = gather_ring(plan, run_pack(plan, *states), lambda: run_prepare(x, cot))
+        rests = firsts
     else:
         conv, dense, small = [state[0].astype(bf16) for state in states]
-        inputs = [
-            lax.all_gather(conv, AXES, axis=1, tiled=True).reshape(4, KERNEL_ROWS, C),
-            lax.all_gather(dense, AXES, axis=0, tiled=True).reshape(MLP_ROWS, C),
-            lax.all_gather(small, AXES, axis=0, tiled=True).reshape(-1, C),
-        ]
-    out, dx, table, m1, m2, hidden, first, second = run_block(
-        plan, class_ids, samples[0], cotangent[0], inputs
-    )
+        conv = lax.all_gather(conv, AXES, axis=1, tiled=True).reshape(4, KERNEL_ROWS, C)
+        firsts = [conv[0], lax.all_gather(small, AXES, axis=0, tiled=True).reshape(-1, C)]
+        rests = [conv[1:], lax.all_gather(dense, AXES, axis=0, tiled=True).reshape(MLP_ROWS, C)]
+        prepared = run_prepare(x, cot)
+    fronted = run_front(plan, x, prepared[0], firsts)
+    out, dx, table, m1, m2, hidden, first, second = run_block(plan, class_ids, x, cot, prepared, fronted, rests)
     mlp = (table, m1, m2, hidden)
     if plan.rings:
         keep, received = reduce_ring(plan, first, second)

time: 90.9 us -> 84.8 us (0.933)
  waiting for transfers between devices: 33.1 us -> 24.5 us
  starting transfers between devices: 17.7 us -> 21 us
  local copies, waits for them, and re-layouts: 4.95 us -> 2.3 us
  other arithmetic: 0.04 us -> 0.97 us
    ppermute x17 -> x18, waiting for transfers between devices: 33.1 us -> 24.5 us  [swap(): return lax.ppermute(values, axis, [(i, i ^ turn) for i in range(size)])]
    pallas_call x1, Pallas kernels: 30.7 us -> 23 us  [run_block(): pl.pallas_call(functools.partial(block_body, plan), out_shape=shapes, in_...]
    pallas_call x0 -> x2, Pallas kernels: none -> 6.91 us  [the longest x1 4.94 us: run_front(): pl.pallas_call(functools.partial(front_body, plan), out_shape=[struct((H...]
    ppermute x17 -> x18, starting transfers between devices: 17.7 us -> 21 us  [swap(): return lax.ppermute(values, axis, [(i, i ^ turn) for i in range(size)])]
    unnamed x18 -> x16, local copies, waits for them, and re-layouts: 4.95 us -> 2.3 us
    pallas_call x1, Pallas kernels: 0.13 us -> 1.74 us  [run_pack(): pl.pallas_call(functools.partial(pack_body, plan), out_shape=jax.ShapeDty...]
  transfers between devices with their start and end apart: 17 -> 18, of which waited for: 12 -> 11; matrix products, arithmetic and copies ran while one was open for 0% -> 0% of each run, Pallas kernels for 0% -> 2%
where the time goes in v3:
time: 84.8 us; the launch traced here: 84.5 us
  Pallas kernels  34.3 us (40%)
  waiting for transfers between devices  24.5 us (29%)
  starting transfers between devices  21 us (25%)
  local copies, waits for them, and re-layouts  2.3 us (3%)
  between operations  1.42 us (2%)
  other arithmetic  0.97 us (1%)
    ppermute x18, waiting for transfers between devices, swap(): return lax.ppermute(values, axis, [(i, i ^ turn) for i in range(size)])  24.5 us
    pallas_call x1, Pallas kernels, run_block(): pl.pallas_call(functools.partial(block_body, plan), out_shape=shapes, in_...  23 us
    ppermute x18, starting transfers between devices, swap(): return lax.ppermute(values, axis, [(i, i ^ turn) for i in range(size)])  21 us
    pallas_call x1, Pallas kernels, run_front(): pl.pallas_call(functools.partial(front_body, plan), out_shape=[struct((H...  4.94 us
    pallas_call x1, Pallas kernels, run_update(): pl.pallas_call(functools.partial(update_body, plan, len(received)), out_s...  2.41 us
    unnamed x16, local copies, waits for them, and re-layouts  2.3 us
    pallas_call x1, Pallas kernels, run_prepare(): pl.pallas_call(prepare_body, out_shape=[struct((16, C), f32), struct((H /...  1.97 us
    pallas_call x1, Pallas kernels, run_pack(): pl.pallas_call(functools.partial(pack_body, plan), out_shape=jax.ShapeDty...  1.74 us
  transfers between devices with their start and end apart: 18, of which 11 were waited for; matrix products, arithmetic and copies ran while one was open for 0% of the time, Pallas kernels for 2%

profile of v3, /device:TPU:0, one launch (start us, length us, event | category | flops | bytes accessed | tf_op | source)
XLA Modules:
  0.0 84.5 jit_solution(7352651407590341340)
XLA Ops:
  0.6 1.7 %pack.1 = bf16[272,128]{1,0:T(8,128)(2,1)} custom-call(f32[4,4,4608]{2,1,0:T(4,128)} %refs_8_.1, f32[4,12544]{1,0:T(4,128)} %refs_9_.1, f32[4,56]{1,0:T(4,128)} %refs_10_.1), custom_call_target="tpu_custom_call" | custom-call | tf_op jit(solution)/shard_map/pack/pallas_call | solution.py:636
  2.4 5.1 %collective-permute-start.2 = (bf16[272,128]{1,0:T(8,128)(2,1)}, bf16[272,128]{1,0:T(8,128)(2,1)S(1)}, u32[]{:S(2)}, u32[]{:S(2)}) collective-permute-start(bf16[272,128]{1,0:T(8,128)(2,1)} %pack.1), channel_id=1, source_target_pairs={{0,6},{1,7},{2,4},{3,5},{4,2},{5,3},{6,0},{7,1},{8,14},{9,15},{10,... | collective-permute-start | bytes 208904 | tf_op jit(solution)/shard_map/ppermute | solution.py:813
  7.5 0.6 collective-permute-start
  8.1 1.2 %copy-done.1 = bf16[1,64,64,128]{3,2,1,0:T(8,128)(2,1)S(1)} copy-done((bf16[1,64,64,128]{3,2,1,0:T(8,128)(2,1)S(1)}, bf16[1,64,64,128]{3,2,1,0:T(8,128)(2,1)}, u32[]{:S(2)}) %copy-start.1) | copy-done | bytes 1048600
  9.4 1.0 %copy-done.4 = bf16[1,32,32,256]{3,2,1,0:T(8,128)(2,1)S(1)} copy-done((bf16[1,32,32,256]{3,2,1,0:T(8,128)(2,1)S(1)}, bf16[1,32,32,256]{3,2,1,0:T(8,128)(2,1)}, u32[]{:S(2)}) %copy-start.4) | copy-done | bytes 524312
  10.4 2.0 %prepare.1 = (f32[16,128]{1,0:T(8,128)S(1)}, bf16[33,32,512]{2,1,0:T(8,128)(2,1)S(1)}, f32[8,256]{1,0:T(8,128)S(1)}) custom-call(bf16[64,64,128]{2,1,0:T(8,128)(2,1)S(1)} %bitcast.10, bf16[32,32,256]{2,1,0:T(8,128)(2,1)S(1)} %bitcast.13), custom_call_target="tpu_custom_call" | custom-call | flops 2097152 | bytes 3145728 | tf_op jit(solution)/shard_map/prepare/pallas_call | solution.py:182
  12.4 1.2 %collective-permute-done.1 = bf16[272,128]{1,0:T(8,128)(2,1)S(1)} collective-permute-done((bf16[272,128]{1,0:T(8,128)(2,1)}, bf16[272,128]{1,0:T(8,128)(2,1)S(1)}, u32[]{:S(2)}, u32[]{:S(2)}) %collective-permute-start.1) | collective-permute-done | bytes 69664 | tf_op jit(solution)/shard_map/ppermute | solution.py:813
  13.6 0.9 %pad_maximum_fusion.2 = bf16[2,272,128]{2,1,0:T(8,128)(2,1)S(1)} fusion(bf16[1,272,128]{2,1,0:T(8,128)(2,1)S(1)} %bitcast.21, bf16[1,272,128]{2,1,0:T(8,128)(2,1)} %bitcast.15), kind=kLoop, calls=%fused_computation.2 | loop fusion | flops 69632 | bytes 278528 | tf_op jit(solution)/shard_map/stack | solution.py:820
  14.5 1.6 %collective-permute-start.3 = (bf16[2,272,128]{2,1,0:T(8,128)(2,1)S(1)}, bf16[2,272,128]{2,1,0:T(8,128)(2,1)S(1)}, u32[]{:S(2)}, u32[]{:S(2)}) collective-permute-start(bf16[2,272,128]{2,1,0:T(8,128)(2,1)S(1)} %pad_maximum_fusion.2), channel_id=1, source_target_pairs={{0,8},{8,0},{16,24},{24,16},{1,9},{9,1},{17,25},{25,17},{2,10},{10... | collective-permute-start | bytes 417800 | tf_op jit(solution)/shard_map/ppermute | solution.py:813
  16.1 1.6 %collective-permute-start.4 = (bf16[2,272,128]{2,1,0:T(8,128)(2,1)S(1)}, bf16[2,272,128]{2,1,0:T(8,128)(2,1)S(1)}, u32[]{:S(2)}, u32[]{:S(2)}) collective-permute-start(bf16[2,272,128]{2,1,0:T(8,128)(2,1)S(1)} %pad_maximum_fusion.3), channel_id=1, source_target_pairs={{0,16},{8,24},{16,0},{24,8},{1,17},{9,25},{17,1},{25,9},{2,18},{10... | collective-permute-start | bytes 417800 | tf_op jit(solution)/shard_map/ppermute | solution.py:813
  17.7 2.0 %collective-permute-done.3 = bf16[2,272,128]{2,1,0:T(8,128)(2,1)S(1)} collective-permute-done((bf16[2,272,128]{2,1,0:T(8,128)(2,1)S(1)}, bf16[2,272,128]{2,1,0:T(8,128)(2,1)S(1)}, u32[]{:S(2)}, u32[]{:S(2)}) %collective-permute-start.3) | collective-permute-done | bytes 139296 | tf_op jit(solution)/shard_map/ppermute | solution.py:813
  19.8 1.8 %collective-permute-start.5 = (bf16[4,272,128]{2,1,0:T(8,128)(2,1)S(1)}, bf16[4,272,128]{2,1,0:T(8,128)(2,1)S(1)}, u32[]{:S(2)}, u32[]{:S(2)}) collective-permute-start(bf16[4,272,128]{2,1,0:T(8,128)(2,1)S(1)} %pad_maximum_fusion.refs_2_.refs_12_), channel_id=1, source_target_pairs={{0,16},{8,24},{16,0},{24,8},{1,17},{9,25},{17,1},{25,9},{2,18},{10... | collective-permute-start | bytes 835592 | tf_op jit(solution)/shard_map/ppermute | solution.py:813
  21.6 1.6 %collective-permute-start.6 = (bf16[4,272,128]{2,1,0:T(8,128)(2,1)S(1)}, bf16[4,272,128]{2,1,0:T(8,128)(2,1)S(1)}, u32[]{:S(2)}, u32[]{:S(2)}) collective-permute-start(bf16[4,272,128]{2,1,0:T(8,128)(2,1)S(1)} %pad_maximum_fusion.1.refs_3_.refs_13_), channel_id=1, source_target_pairs={{0,8},{8,0},{16,24},{24,16},{1,9},{9,1},{17,25},{25,17},{2,10},{10... | collective-permute-start | bytes 835592 | tf_op jit(solution)/shard_map/ppermute | solution.py:813
  23.2 0.5 collective-permute-start.8
  23.7 3.6 %collective-permute-done.5.refs_4_.refs_14_ = bf16[4,272,128]{2,1,0:T(8,128)(2,1)S(1)} collective-permute-done((bf16[4,272,128]{2,1,0:T(8,128)(2,1)S(1)}, bf16[4,272,128]{2,1,0:T(8,128)(2,1)S(1)}, u32[]{:S(2)}, u32[]{:S(2)}) %collective-permute-start.5) | collective-permute-done | bytes 278560 | tf_op jit(solution)/shard_map/ppermute | solution.py:813
  27.3 1.6 %collective-permute-done.6.refs_5_.refs_15_ = bf16[4,272,128]{2,1,0:T(8,128)(2,1)S(1)} collective-permute-done((bf16[4,272,128]{2,1,0:T(8,128)(2,1)S(1)}, bf16[4,272,128]{2,1,0:T(8,128)(2,1)S(1)}, u32[]{:S(2)}, u32[]{:S(2)}) %collective-permute-start.6) | collective-permute-done | bytes 278560 | tf_op jit(solution)/shard_map/ppermute | solution.py:813
  29.6 0.9 %collective-permute-done.10.refs_9_.refs_19_ = bf16[4,272,128]{2,1,0:T(8,128)(2,1)S(1)} collective-permute-done((bf16[4,272,128]{2,1,0:T(8,128)(2,1)S(1)}, bf16[4,272,128]{2,1,0:T(8,128)(2,1)S(1)}, u32[]{:S(2)}, u32[]{:S(2)}) %collective-permute-start.10) | collective-permute-done | bytes 278560 | tf_op jit(solution)/shard_map/ppermute | solution.py:813
  30.5 4.9 %front.1 = (bf16[66,64,384]{2,1,0:T(8,128)(2,1)S(1)}, f32[64,64,128]{2,1,0:T(8,128)S(1)}, f32[64,64,128]{2,1,0:T(8,128)S(1)}, f32[16,128]{1,0:T(8,128)S(1)}, bf1...) custom-call(bf16[64,64,128]{2,1,0:T(8,128)(2,1)S(1)} %bitcast.11, f32[16,128]{1,0:T(8,128)S(1)} %get-tuple-element.49.refs_1_.refs_3_, ...), custom_call_target="tpu_custom_call" | custom-call | flops 1363148800 | bytes 8388608 | tf_op jit(solution)/shard_map/front/pallas_call | solution.py:253
  35.4 23.0 %block.1 = (bf16[32,32,256]{2,1,0:T(8,128)(2,1)}, bf16[64,64,128]{2,1,0:T(8,128)(2,1)}, bf16[16,512]{1,0:T(8,128)(2,1)S(1)}, bf16[512,512]{1,0:T(8,128)(2,1)S(1)...) custom-call(s32[1]{0:T(128)S(6)} %copy.14.refs_0_, ...), custom_call_target="tpu_custom_call" | custom-call | flops 9437184000 | bytes 16777216 | tf_op jit(solution)/shard_map/block/pallas_call | solution.py:585
  58.7 2.0 %collective-permute-done.11.refs_1_ = bf16[2640,128]{1,0:T(8,128)(2,1)S(1)} collective-permute-done((bf16[2640,128]{1,0:T(8,128)(2,1)S(1)}, bf16[2640,128]{1,0:T(8,128)(2,1)S(1)}, u32[]{:S(2)}, u32[]{:S(2)}) %collective-permute-start.11) | collective-permute-done | bytes 675872 | tf_op jit(solution)/shard_map/ppermute | solution.py:813
  60.8 1.6 %collective-permute-start.12 = (bf16[720,128]{1,0:T(8,128)(2,1)S(1)}, bf16[720,128]{1,0:T(8,128)(2,1)S(1)}, u32[]{:S(2)}, u32[]{:S(2)}) collective-permute-start(bf16[720,128]{1,0:T(8,128)(2,1)S(1)} %get-tuple-element.67), channel_id=1, source_target_pairs={{0,8},{8,0},{16,24},{24,16},{1,9},{9,1},{17,25},{25,17},{2,10},{10... | collective-permute-start | bytes 552968 | tf_op jit(solution)/shard_map/ppermute | solution.py:813
  62.4 0.6 collective-permute-start.13
  62.9 1.4 %collective-permute-start.14 = (bf16[720,128]{1,0:T(8,128)(2,1)S(1)}, bf16[720,128]{1,0:T(8,128)(2,1)S(1)}, u32[]{:S(2)}, u32[]{:S(2)}) collective-permute-start(bf16[720,128]{1,0:T(8,128)(2,1)S(1)} %get-tuple-element.69), channel_id=1, source_target_pairs={{0,24},{8,16},{16,8},{24,0},{1,25},{9,17},{17,9},{25,1},{2,26},{10... | collective-permute-start | bytes 552968 | tf_op jit(solution)/shard_map/ppermute | solution.py:813
  64.4 4.0 %collective-permute-done.12.refs_1_ = bf16[720,128]{1,0:T(8,128)(2,1)S(1)} collective-permute-done((bf16[720,128]{1,0:T(8,128)(2,1)S(1)}, bf16[720,128]{1,0:T(8,128)(2,1)S(1)}, u32[]{:S(2)}, u32[]{:S(2)}) %collective-permute-start.12) | collective-permute-done | bytes 184352 | tf_op jit(solution)/shard_map/ppermute | solution.py:813
  68.4 4.4 %collective-permute-done.13.refs_2_ = bf16[720,128]{1,0:T(8,128)(2,1)S(1)} collective-permute-done((bf16[720,128]{1,0:T(8,128)(2,1)S(1)}, bf16[720,128]{1,0:T(8,128)(2,1)S(1)}, u32[]{:S(2)}, u32[]{:S(2)}) %collective-permute-start.13) | collective-permute-done | bytes 184352 | tf_op jit(solution)/shard_map/ppermute | solution.py:813
  72.8 1.1 %collective-permute-start.15 = (bf16[240,128]{1,0:T(8,128)(2,1)S(1)}, bf16[240,128]{1,0:T(8,128)(2,1)S(1)}, u32[]{:S(2)}, u32[]{:S(2)}) collective-permute-start(bf16[240,128]{1,0:T(8,128)(2,1)S(1)} %get-tuple-element.71), channel_id=1, source_target_pairs={{0,2},{1,3},{2,0},{3,1},{4,6},{5,7},{6,4},{7,5},{8,10},{9,11},{10,... | collective-permute-start | bytes 184328 | tf_op jit(solution)/shard_map/ppermute | solution.py:813
  73.9 2.1 %collective-permute-start.16 = (bf16[240,128]{1,0:T(8,128)(2,1)S(1)}, bf16[240,128]{1,0:T(8,128)(2,1)S(1)}, u32[]{:S(2)}, u32[]{:S(2)}) collective-permute-start(bf16[240,128]{1,0:T(8,128)(2,1)S(1)} %get-tuple-element.72), channel_id=1, source_target_pairs={{0,4},{1,5},{2,6},{3,7},{4,0},{5,1},{6,2},{7,3},{8,12},{9,13},{10,... | collective-permute-start | bytes 184328 | tf_op jit(solution)/shard_map/ppermute | solution.py:813
  76.1 1.2 %collective-permute-start.17 = (bf16[240,128]{1,0:T(8,128)(2,1)S(1)}, bf16[240,128]{1,0:T(8,128)(2,1)S(1)}, u32[]{:S(2)}, u32[]{:S(2)}) collective-permute-start(bf16[240,128]{1,0:T(8,128)(2,1)S(1)} %get-tuple-element.73), channel_id=1, source_target_pairs={{0,6},{1,7},{2,4},{3,5},{4,2},{5,3},{6,0},{7,1},{8,14},{9,15},{10,... | collective-permute-start | bytes 184328 | tf_op jit(solution)/shard_map/ppermute | solution.py:813
  77.3 0.5 collective-permute-done.15.refs_1_
  77.8 2.6 %collective-permute-done.16.refs_2_ = bf16[240,128]{1,0:T(8,128)(2,1)S(1)} collective-permute-done((bf16[240,128]{1,0:T(8,128)(2,1)S(1)}, bf16[240,128]{1,0:T(8,128)(2,1)S(1)}, u32[]{:S(2)}, u32[]{:S(2)}) %collective-permute-start.16) | collective-permute-done | bytes 61472 | tf_op jit(solution)/shard_map/ppermute | solution.py:813
  80.4 1.7 %collective-permute-done.17.refs_3_ = bf16[240,128]{1,0:T(8,128)(2,1)S(1)} collective-permute-done((bf16[240,128]{1,0:T(8,128)(2,1)S(1)}, bf16[240,128]{1,0:T(8,128)(2,1)S(1)}, u32[]{:S(2)}, u32[]{:S(2)}) %collective-permute-start.17) | collective-permute-done | bytes 61472 | tf_op jit(solution)/shard_map/ppermute | solution.py:813
  82.1 2.4 %update.1 = (f32[4,4,4608]{2,1,0:T(4,128)}, f32[4,12544]{1,0:T(4,128)}, f32[4,56]{1,0:T(4,128)}, bf16[4,4608]{1,0:T(4,128)(2,1)}, bf16[98,128]{1,0:T(8,128)(2,1)}, /*index=5*/bf16[1,56]{1,0:T(2,128)(2,1)}) custom-call(f32[200,128]{1,0:T(8,128)S(1)} %get-tuple-element.70.refs_0_, bf16[240,128]{1,0:T(8,128)(2,1)S(1)} %collective-permute-done.15.refs_1_, ...), custom_call_target="tpu_custom_call" | custom-call | tf_op jit(solution)/shard_map/update/pallas_call | solution.py:796
  (31 shorter events, 0.6 us)
Async XLA Ops:
  2.4 10.0 %collective-permute-start.2 = (bf16[272,128]{1,0:T(8,128)(2,1)}, bf16[272,128]{1,0:T(8,128)(2,1)S(1)}, u32[]{:S(2)}, u32[]{:S(2)}) collective-permute-start(bf16[272,128]{1,0:T(8,128)(2,1)} %pack.1), channel_id=1, source_target_pairs={{0,6},{1,7},{2,4},{3,5},{4,2},{5,3},{6,0},{7,1},{8,14},{9,15},{10,... | collective-permute-start | bytes 208904 | tf_op jit(solution)/shard_map/ppermute | solution.py:813
  7.5 6.1 %collective-permute-start.1 = (bf16[272,128]{1,0:T(8,128)(2,1)}, bf16[272,128]{1,0:T(8,128)(2,1)S(1)}, u32[]{:S(2)}, u32[]{:S(2)}) collective-permute-start(bf16[272,128]{1,0:T(8,128)(2,1)} %pack.1), channel_id=1, source_target_pairs={{0,4},{1,5},{2,6},{3,7},{4,0},{5,1},{6,2},{7,3},{8,12},{9,13},{10,... | collective-permute-start | bytes 208904 | tf_op jit(solution)/shard_map/ppermute | solution.py:813
  7.5 6.1 %collective-permute-start = (bf16[272,128]{1,0:T(8,128)(2,1)}, bf16[272,128]{1,0:T(8,128)(2,1)S(1)}, u32[]{:S(2)}, u32[]{:S(2)}) collective-permute-start(bf16[272,128]{1,0:T(8,128)(2,1)} %pack.1), channel_id=1, source_target_pairs={{0,2},{1,3},{2,0},{3,1},{4,6},{5,7},{6,4},{7,5},{8,10},{9,11},{10,... | collective-permute-start | bytes 208904 | tf_op jit(solution)/shard_map/ppermute | solution.py:813
  8.1 1.2 %copy-start.1 = (bf16[1,64,64,128]{3,2,1,0:T(8,128)(2,1)S(1)}, bf16[1,64,64,128]{3,2,1,0:T(8,128)(2,1)}, u32[]{:S(2)}) copy-start(bf16[1,64,64,128]{3,2,1,0:T(8,128)(2,1)} %param.6) | copy-start | bytes 3145732
  9.4 1.0 %copy-start.4 = (bf16[1,32,32,256]{3,2,1,0:T(8,128)(2,1)S(1)}, bf16[1,32,32,256]{3,2,1,0:T(8,128)(2,1)}, u32[]{:S(2)}) copy-start(bf16[1,32,32,256]{3,2,1,0:T(8,128)(2,1)} %param.7) | copy-start | bytes 1572868
  10.4 9.3 %copy-start.7 = (bf16[272,128]{1,0:T(8,128)(2,1)S(1)}, bf16[272,128]{1,0:T(8,128)(2,1)}, u32[]{:S(2)}) copy-start(bf16[272,128]{1,0:T(8,128)(2,1)} %pack.1) | copy-start | bytes 208900
  10.4 20.1 %copy-start.2 = (bf16[1,64,64,128]{3,2,1,0:T(8,128)(2,1)S(1)}, bf16[1,64,64,128]{3,2,1,0:T(8,128)(2,1)}, u32[]{:S(2)}) copy-start(bf16[1,64,64,128]{3,2,1,0:T(8,128)(2,1)} %param.6) | copy-start | bytes 3145732
  14.5 5.2 %collective-permute-start.3 = (bf16[2,272,128]{2,1,0:T(8,128)(2,1)S(1)}, bf16[2,272,128]{2,1,0:T(8,128)(2,1)S(1)}, u32[]{:S(2)}, u32[]{:S(2)}) collective-permute-start(bf16[2,272,128]{2,1,0:T(8,128)(2,1)S(1)} %pad_maximum_fusion.2), channel_id=1, source_target_pairs={{0,8},{8,0},{16,24},{24,16},{1,9},{9,1},{17,25},{25,17},{2,10},{10... | collective-permute-start | bytes 417800 | tf_op jit(solution)/shard_map/ppermute | solution.py:813
  16.1 5.5 %collective-permute-start.4 = (bf16[2,272,128]{2,1,0:T(8,128)(2,1)S(1)}, bf16[2,272,128]{2,1,0:T(8,128)(2,1)S(1)}, u32[]{:S(2)}, u32[]{:S(2)}) collective-permute-start(bf16[2,272,128]{2,1,0:T(8,128)(2,1)S(1)} %pad_maximum_fusion.3), channel_id=1, source_target_pairs={{0,16},{8,24},{16,0},{24,8},{1,17},{9,25},{17,1},{25,9},{2,18},{10... | collective-permute-start | bytes 417800 | tf_op jit(solution)/shard_map/ppermute | solution.py:813
  19.8 7.6 %collective-permute-start.5 = (bf16[4,272,128]{2,1,0:T(8,128)(2,1)S(1)}, bf16[4,272,128]{2,1,0:T(8,128)(2,1)S(1)}, u32[]{:S(2)}, u32[]{:S(2)}) collective-permute-start(bf16[4,272,128]{2,1,0:T(8,128)(2,1)S(1)} %pad_maximum_fusion.refs_2_.refs_12_), channel_id=1, source_target_pairs={{0,16},{8,24},{16,0},{24,8},{1,17},{9,25},{17,1},{25,9},{2,18},{10... | collective-permute-start | bytes 835592 | tf_op jit(solution)/shard_map/ppermute | solution.py:813
  21.6 7.3 %collective-permute-start.6 = (bf16[4,272,128]{2,1,0:T(8,128)(2,1)S(1)}, bf16[4,272,128]{2,1,0:T(8,128)(2,1)S(1)}, u32[]{:S(2)}, u32[]{:S(2)}) collective-permute-start(bf16[4,272,128]{2,1,0:T(8,128)(2,1)S(1)} %pad_maximum_fusion.1.refs_3_.refs_13_), channel_id=1, source_target_pairs={{0,8},{8,0},{16,24},{24,16},{1,9},{9,1},{17,25},{25,17},{2,10},{10... | collective-permute-start | bytes 835592 | tf_op jit(solution)/shard_map/ppermute | solution.py:813
  23.2 6.4 %collective-permute-start.7 = (bf16[4,272,128]{2,1,0:T(8,128)(2,1)S(1)}, bf16[4,272,128]{2,1,0:T(8,128)(2,1)S(1)}, u32[]{:S(2)}, u32[]{:S(2)}) collective-permute-start(bf16[4,272,128]{2,1,0:T(8,128)(2,1)S(1)} %pad_maximum_fusion.refs_2_.refs_12_), channel_id=1, source_target_pairs={{0,1},{1,0},{2,3},{3,2},{4,5},{5,4},{6,7},{7,6},{8,9},{9,8},{10,11... | collective-permute-start | bytes 835592 | tf_op jit(solution)/shard_map/ppermute | solution.py:813
  23.2 6.4 %collective-permute-start.8 = (bf16[4,272,128]{2,1,0:T(8,128)(2,1)S(1)}, bf16[4,272,128]{2,1,0:T(8,128)(2,1)S(1)}, u32[]{:S(2)}, u32[]{:S(2)}) collective-permute-start(bf16[4,272,128]{2,1,0:T(8,128)(2,1)S(1)} %pad_maximum_fusion.1.refs_3_.refs_13_), channel_id=1, source_target_pairs={{0,1},{1,0},{2,3},{3,2},{4,5},{5,4},{6,7},{7,6},{8,9},{9,8},{10,11... | collective-permute-start | bytes 835592 | tf_op jit(solution)/shard_map/ppermute | solution.py:813
  27.3 2.3 %collective-permute-start.9 = (bf16[4,272,128]{2,1,0:T(8,128)(2,1)S(1)}, bf16[4,272,128]{2,1,0:T(8,128)(2,1)S(1)}, u32[]{:S(2)}, u32[]{:S(2)}) collective-permute-start(bf16[4,272,128]{2,1,0:T(8,128)(2,1)S(1)} %collective-permute-done.5.refs_4_.refs_14_), channel_id=1, source_target_pairs={{0,1},{1,0},{2,3},{3,2},{4,5},{5,4},{6,7},{7,6},{8,9},{9,8},{10,11... | collective-permute-start | bytes 835592 | tf_op jit(solution)/shard_map/ppermute | solution.py:813
  28.9 1.6 %collective-permute-start.10 = (bf16[4,272,128]{2,1,0:T(8,128)(2,1)S(1)}, bf16[4,272,128]{2,1,0:T(8,128)(2,1)S(1)}, u32[]{:S(2)}, u32[]{:S(2)}) collective-permute-start(bf16[4,272,128]{2,1,0:T(8,128)(2,1)S(1)} %collective-permute-done.6.refs_5_.refs_15_), channel_id=1, source_target_pairs={{0,1},{1,0},{2,3},{3,2},{4,5},{5,4},{6,7},{7,6},{8,9},{9,8},{10,11... | collective-permute-start | bytes 835592 | tf_op jit(solution)/shard_map/ppermute | solution.py:813
  29.6 5.8 %copy-start.5 = (bf16[1,32,32,256]{3,2,1,0:T(8,128)(2,1)S(1)}, bf16[1,32,32,256]{3,2,1,0:T(8,128)(2,1)}, u32[]{:S(2)}) copy-start(bf16[1,32,32,256]{3,2,1,0:T(8,128)(2,1)} %param.7) | copy-start | bytes 1572868
  58.4 23.7 %copy-start = (f32[4,4,4608]{2,1,0:T(4,128)S(1)}, f32[4,4,4608]{2,1,0:T(4,128)}, u32[]{:S(2)}) copy-start(f32[4,4,4608]{2,1,0:T(4,128)} %refs_8_.1) | copy-start | bytes 884740
  58.4 23.7 %copy-start.3 = (f32[4,12544]{1,0:T(4,128)S(1)}, f32[4,12544]{1,0:T(4,128)}, u32[]{:S(2)}) copy-start(f32[4,12544]{1,0:T(4,128)} %refs_9_.1) | copy-start | bytes 602116
  58.4 23.7 %copy-start.6 = (f32[4,56]{1,0:T(4,128)S(1)}, f32[4,56]{1,0:T(4,128)}, u32[]{:S(2)}) copy-start(f32[4,56]{1,0:T(4,128)} %refs_10_.1) | copy-start | bytes 2692
  58.5 2.2 %collective-permute-start.11 = (bf16[2640,128]{1,0:T(8,128)(2,1)S(1)}, bf16[2640,128]{1,0:T(8,128)(2,1)S(1)}, u32[]{:S(2)}, u32[]{:S(2)}) collective-permute-start(bf16[2640,128]{1,0:T(8,128)(2,1)S(1)} %get-tuple-element.65), channel_id=1, source_target_pairs={{0,1},{1,0},{2,3},{3,2},{4,5},{5,4},{6,7},{7,6},{8,9},{9,8},{10,11... | collective-permute-start | bytes 2027528 | tf_op jit(solution)/shard_map/ppermute | solution.py:813
  60.8 7.5 %collective-permute-start.12 = (bf16[720,128]{1,0:T(8,128)(2,1)S(1)}, bf16[720,128]{1,0:T(8,128)(2,1)S(1)}, u32[]{:S(2)}, u32[]{:S(2)}) collective-permute-start(bf16[720,128]{1,0:T(8,128)(2,1)S(1)} %get-tuple-element.67), channel_id=1, source_target_pairs={{0,8},{8,0},{16,24},{24,16},{1,9},{9,1},{17,25},{25,17},{2,10},{10... | collective-permute-start | bytes 552968 | tf_op jit(solution)/shard_map/ppermute | solution.py:813
  62.4 10.4 %collective-permute-start.13 = (bf16[720,128]{1,0:T(8,128)(2,1)S(1)}, bf16[720,128]{1,0:T(8,128)(2,1)S(1)}, u32[]{:S(2)}, u32[]{:S(2)}) collective-permute-start(bf16[720,128]{1,0:T(8,128)(2,1)S(1)} %get-tuple-element.68), channel_id=1, source_target_pairs={{0,16},{8,24},{16,0},{24,8},{1,17},{9,25},{17,1},{25,9},{2,18},{10... | collective-permute-start | bytes 552968 | tf_op jit(solution)/shard_map/ppermute | solution.py:813
  62.9 9.8 %collective-permute-start.14 = (bf16[720,128]{1,0:T(8,128)(2,1)S(1)}, bf16[720,128]{1,0:T(8,128)(2,1)S(1)}, u32[]{:S(2)}, u32[]{:S(2)}) collective-permute-start(bf16[720,128]{1,0:T(8,128)(2,1)S(1)} %get-tuple-element.69), channel_id=1, source_target_pairs={{0,24},{8,16},{16,8},{24,0},{1,25},{9,17},{17,9},{25,1},{2,26},{10... | collective-permute-start | bytes 552968 | tf_op jit(solution)/shard_map/ppermute | solution.py:813
  72.8 4.9 %collective-permute-start.15 = (bf16[240,128]{1,0:T(8,128)(2,1)S(1)}, bf16[240,128]{1,0:T(8,128)(2,1)S(1)}, u32[]{:S(2)}, u32[]{:S(2)}) collective-permute-start(bf16[240,128]{1,0:T(8,128)(2,1)S(1)} %get-tuple-element.71), channel_id=1, source_target_pairs={{0,2},{1,3},{2,0},{3,1},{4,6},{5,7},{6,4},{7,5},{8,10},{9,11},{10,... | collective-permute-start | bytes 184328 | tf_op jit(solution)/shard_map/ppermute | solution.py:813
  73.9 6.4 %collective-permute-start.16 = (bf16[240,128]{1,0:T(8,128)(2,1)S(1)}, bf16[240,128]{1,0:T(8,128)(2,1)S(1)}, u32[]{:S(2)}, u32[]{:S(2)}) collective-permute-start(bf16[240,128]{1,0:T(8,128)(2,1)S(1)} %get-tuple-element.72), channel_id=1, source_target_pairs={{0,4},{1,5},{2,6},{3,7},{4,0},{5,1},{6,2},{7,3},{8,12},{9,13},{10,... | collective-permute-start | bytes 184328 | tf_op jit(solution)/shard_map/ppermute | solution.py:813
  76.1 6.0 %collective-permute-start.17 = (bf16[240,128]{1,0:T(8,128)(2,1)S(1)}, bf16[240,128]{1,0:T(8,128)(2,1)S(1)}, u32[]{:S(2)}, u32[]{:S(2)}) collective-permute-start(bf16[240,128]{1,0:T(8,128)(2,1)S(1)} %get-tuple-element.73), channel_id=1, source_target_pairs={{0,6},{1,7},{2,4},{3,5},{4,2},{5,3},{6,0},{7,1},{8,14},{9,15},{10,... | collective-permute-start | bytes 184328 | tf_op jit(solution)/shard_map/ppermute | solution.py:813

commit v4 on v3

--- a/solution.py
+++ b/solution.py
@@ -42,7 +42,15 @@
 TN = (((0,), (0,)), ((), ()))
 EXTRA = 8 + 2 * NCLASS
 R = 8
-Q = 8
+Q = 4
+STEPS = H // R
+PART = CELLS // STEPS
+
+
+def each(count, step, carry):
+    for index in range(count):
+        carry = step(index, carry)
+    return carry
 
 
 def mm(a, b, dims=NN):
@@ -148,154 +156,137 @@
     return lax.axis_index(outer) * inner_size + lax.axis_index(inner)
 
 
-def prepare_body(x_ref, cot_ref, stats_ref, cw, gdb_ref):
+def prepare_body(x_ref, cot_ref, own_ref, stats_ref, cw, gdb_ref, near_ref):
+    near_ref[...] = own_ref[...]
     zero8 = jnp.zeros((8, C), f32)
 
     def read_x(i):
         return x_ref[pl.ds(i * R, R)].astype(f32)
 
-    total = lax.fori_loop(0, H // R, lambda i, s: s + fold(read_x(i)), zero8)
+    total = each(H // R, lambda i, s: s + fold(read_x(i)), zero8)
     mean = group_sum(total_of(total)) * (1.0 / PER_GROUP)
 
     def square_x(i, s):
         d = read_x(i) - one(mean)
         return s + fold(d * d)
 
-    var = group_sum(total_of(lax.fori_loop(0, H // R, square_x, zero8))) * (1.0 / PER_GROUP)
+    var = group_sum(total_of(each(H // R, square_x, zero8))) * (1.0 / PER_GROUP)
     stats_ref[0:8] = mean
     stats_ref[8:16] = lax.rsqrt(var + norm_eps)
     cw[H // 2 : H // 2 + 1] = jnp.zeros((1, W // 2, 4 * C), bf16)
 
     def cot_windows(i, s):
-        values = cot_ref[pl.ds(i * Q, Q)].astype(f32)
+        values = cot_ref[pl.ds(i * R, R)].astype(f32)
         place = lax.broadcasted_iota(jnp.int32, values.shape, 1)
         after = jnp.where(place == W // 2 - 1, 0.0, pltpu.roll(values, W // 2 - 1, 1))
-        cw[pl.ds(i * Q, Q), :, 0 : 2 * C] = values.astype(bf16)
-        cw[pl.ds(i * Q, Q), :, 2 * C :] = after.astype(bf16)
+        cw[pl.ds(i * R, R), :, 0 : 2 * C] = values.astype(bf16)
+        cw[pl.ds(i * R, R), :, 2 * C :] = after.astype(bf16)
         return s + fold(values)
 
-    gdb_ref[...] = total_of(lax.fori_loop(0, H // 2 // Q, cot_windows, jnp.zeros((8, 2 * C), f32)))
-
-
-def run_prepare(x, cot):
+    gdb_ref[...] = total_of(each(H // 2 // R, cot_windows, jnp.zeros((8, 2 * C), f32)))
+
+
+def run_prepare(x, cot, own):
     struct = jax.ShapeDtypeStruct
     return pl.pallas_call(
         prepare_body,
-        out_shape=[struct((16, C), f32), struct((H // 2 + 1, W // 2, 4 * C), bf16), struct((8, 2 * C), f32)],
-        in_specs=vmem_specs(2),
-        out_specs=vmem_specs(3),
+        out_shape=[struct((16, C), f32), struct((H // 2 + 1, W // 2, 4 * C), bf16), struct((8, 2 * C), f32), struct(own.shape, bf16)],
+        in_specs=vmem_specs(3),
+        out_specs=vmem_specs(4),
         compiler_params=limit(8),
         cost_estimate=cost(2, 3 << 20),
         name="prepare",
-    )(x, cot)
-
-
-def front_body(plan, *refs):
-    count = plan.parts if plan.rings else 2
-    x_ref, stats_ref = refs[:2]
-    inputs = refs[2 : 2 + count]
-    a1w, g1p, c1, moments_ref, k1_ref, smalls, conv, pair = refs[2 + count :]
+    )(x, cot, own)
+
+
+def block_body(plan, *refs):
+    refs = list(refs)
+    count = 8 if plan.rings else 4
+    cls_ref, x_ref, cot_ref, stats_ref, cw, gdb_ref = refs[:6]
+    inputs = refs[6 : 6 + count]
+    out_hbm, slope1_ref, drf, factors_ref, table_ref, m1_ref, m2_ref, hidden_ref = refs[6 + count : 14 + count]
+    results = refs[14 + count : 16 + count]
+    a1w, a2w, t1w, t2w, rw, c1, g1p, g2p, rf, pairs, conv, dense, kernels, smalls, out_ref, out_sem = refs[16 + count :]
+    me = position_of(plan.sizes)
+    k1_ref, k2_ref, kd0_ref, kd1_ref = [kernels.at[k] for k in range(4)]
+    pair1, pair2, back1, back2 = [pairs.at[k] for k in range(4)]
+    zero8 = jnp.zeros((8, C), f32)
+
     if plan.rings:
-        me = position_of(plan.sizes)
+        shards = list(plan.sources(me))
         conv[...] = jnp.zeros(conv.shape, f32)
+        dense[...] = jnp.zeros(dense.shape, f32)
         small = jnp.zeros((16, C), f32)
         row = lax.broadcasted_iota(jnp.int32, (16, C), 0)
         lane = lax.broadcasted_iota(jnp.int32, (16, C), 1)
-        for part, place, turn in plan.sources:
-            owner = me ^ turn
+        for part, place, owner in shards:
             values = inputs[part][place, 0 : plan.first_rows].astype(f32)
             first = plan.tile_of(owner * plan.conv_rows)
-            conv[pl.ds(first, plan.conv_pad), :] += values[: plan.conv_pad]
+            conv[0, pl.ds(first, plan.conv_pad), :] += values[: plan.conv_pad]
             at = row * C + lane - owner * plan.small_len
             own = jnp.broadcast_to(values[plan.conv_pad : plan.conv_pad + 1], (16, C))
             small = jnp.where((at >= 0) & (at < plan.small_len), own, small)
         smalls[...] = small
-        k1_ref[...] = conv[0:KERNEL_ROWS].astype(bf16)
+        k1_ref[...] = conv[0, 0:KERNEL_ROWS].astype(bf16)
     else:
         k1_ref[...] = inputs[0][...]
         smalls[0:14] = inputs[1][...].astype(f32)
-    gain1, bias1, cb1 = [jnp.broadcast_to(smalls[i : i + 1, :], (8, C)) for i in range(3)]
-    mean1 = stats_ref[0:8]
-    slope1 = stats_ref[8:16] * (1.0 + gain1)
-    zero8 = jnp.zeros((8, C), f32)
-    clear_edges(a1w)
-
-    def front1(i, carry):
-        v = (x_ref[pl.ds(i * R, R)].astype(f32) - one(mean1)) * one(slope1) + one(bias1)
-        prob = normal_cdf(v)
-        put_windows(a1w, i * R, v * prob)
-        g1p[pl.ds(i * R, R)] = gelu_slope(v, prob)
-        return carry
-
-    lax.fori_loop(0, H // R, front1, 0)
-    pair_forward(pair, k1_ref)
-
-    def conv1(i, s):
-        got = pair_conv(a1w, pair, i * Q)
-        for parity, place in enumerate(pairs_of(c1, i * Q)):
-            value = got[..., parity * C : (parity + 1) * C] + one(cb1)
-            place[...] = value
-            s = s + fold(value)
-        return s
-
-    centre = total_of(lax.fori_loop(0, H // 2 // Q, conv1, zero8)) * (1.0 / CELLS)
-
-    def square_c(i, s):
-        d = c1[pl.ds(i * R, R)] - one(centre)
-        return s + fold(d * d)
-
-    moments_ref[0:8] = centre
-    moments_ref[8:16] = total_of(lax.fori_loop(0, H // R, square_c, zero8)) * (1.0 / CELLS)
-
-
-def run_front(plan, x, stats, inputs):
-    struct = jax.ShapeDtypeStruct
-    return pl.pallas_call(
-        functools.partial(front_body, plan),
-        out_shape=[
-            struct((H + 2, W, 3 * C), bf16),
-            struct((H, W, C), f32),
-            struct((H, W, C), f32),
-            struct((16, C), f32),
-            struct((KERNEL_ROWS, C), bf16),
-            struct((16, C), f32),
-        ],
-        in_specs=vmem_specs(2 + len(inputs)),
-        out_specs=vmem_specs(6),
-        scratch_shapes=[
-            pltpu.VMEM((KERNEL_ROWS + 2 * plan.conv_pad, C), f32),
-            pltpu.VMEM((12 * C, 2 * C), bf16),
-        ],
-        compiler_params=limit(20),
-        cost_estimate=cost(1300, 8 << 20),
-        name="front",
-    )(x, stats, *inputs)
-
-
-def block_body(plan, *refs):
-    refs = list(refs)
-    cls_ref, x_ref, cot_ref, stats_ref, cw, gdb_ref, a1w, g1p, c1, moments_ref, k1_ref, smalls = refs[:12]
-    count = plan.parts if plan.rings else 2
-    inputs = refs[12 : 12 + count]
-    out_hbm, dx_hbm, table_ref, m1_ref, m2_ref, hidden_ref = refs[12 + count : 18 + count]
-    results = refs[18 + count : 20 + count]
-    a2w, tw, rw, g2p, drf, pair, conv, dense, kernels, out_ref, dx_ref, out_sem, dx_sem = refs[20 + count :]
-    me = position_of(plan.sizes)
-    if plan.rings:
-        conv[1:4] = jnp.zeros((3,) + conv.shape[1:], f32)
-        dense[...] = jnp.zeros(dense.shape, f32)
-        for part, place, turn in plan.sources:
-            owner = me ^ turn
+
+    def take_rest(step, steps):
+        if not plan.rings:
+            return
+        for part, place, owner in shards[step::steps]:
             values = inputs[part][place, plan.first_rows : plan.own_rows].astype(f32)
             first = plan.tile_of(owner * plan.conv_rows)
             for k in range(3):
                 conv[k + 1, pl.ds(first, plan.conv_pad), :] += values[k * plan.conv_pad : (k + 1) * plan.conv_pad]
             first = plan.tile_of(owner * plan.dense_rows)
             dense[pl.ds(first, plan.dense_pad), :] += values[plan.dense_at : plan.dense_at + plan.dense_pad]
-        kernels[...] = conv[1:4, 0:KERNEL_ROWS].astype(bf16)
+
+    def small_row(index):
+        return jnp.broadcast_to(smalls[index : index + 1, :], (8, C))
+
+    def small_run(first, count):
+        return jnp.concatenate([smalls[first + i : first + i + 1, :] for i in range(count)], axis=1)
+
+    gain1, bias1, cb1, gain2, bias2, cb2 = [small_row(i) for i in range(6)]
+    mean1, rs1 = stats_ref[0:8], stats_ref[8:16]
+    slope1 = rs1 * (1.0 + gain1)
+
+    pair_forward(pair1, k1_ref)
+    clear_edges(a1w)
+
+    def front1(i):
+        v = (x_ref[pl.ds(i * R, R)].astype(f32) - one(mean1)) * one(slope1) + one(bias1)
+        prob = normal_cdf(v)
+        put_windows(a1w, i * R, v * prob)
+        g1p[pl.ds(i * R, R)] = gelu_slope(v, prob)
+
+    moments = []
+
+    def conv1(i):
+        got = pair_conv(a1w, pair1, i * Q)
+        values = [got[..., parity * C : (parity + 1) * C] + one(cb1) for parity in range(2)]
+        for place, value in zip(pairs_of(c1, i * Q), values):
+            place[...] = value
+        centre = total_of(fold(values[0]) + fold(values[1])) * (1.0 / PART)
+        off = [value - one(centre) for value in values]
+        moments.append((centre, fold(off[0] * off[0]) + fold(off[1] * off[1])))
+
+    front1(0)
+    for i in range(STEPS):
+        if i + 1 < STEPS:
+            front1(i + 1)
+        conv1(i)
+        take_rest(i, STEPS)
+    centre = sum(part[0] for part in moments) * (1.0 / STEPS)
+    spread = sum(total_of(part[1]) + PART * (part[0] - centre) * (part[0] - centre) for part in moments) * (1.0 / CELLS)
+
+    if plan.rings:
+        kernels[1:4] = conv[1:4, 0:KERNEL_ROWS].astype(bf16)
     else:
-        kernels[...] = inputs[0][...]
-        dense[0:MLP_ROWS] = inputs[1][...].astype(f32)
+        kernels[1:4] = inputs[2][...]
+        dense[0:MLP_ROWS] = inputs[3][...].astype(f32)
 
     def lanes(first, rows, parts):
         pieces = [dense[pl.ds(first + part, rows, parts), :] for part in range(parts)]
@@ -304,21 +295,6 @@
     table_ref[...] = lanes(0, NCLASS, EMB // C)
     m1_ref[...] = lanes(TABLE_ROWS, EMB, EMB // C)
     m2_ref[...] = lanes(TABLE_ROWS + M1_ROWS, EMB, 2)
-    k2_ref, kd0_ref, kd1_ref = [kernels.at[k] for k in range(3)]
-    gk1_ref, gk2_ref, gkd0_ref, gkd1_ref = [conv.at[k] for k in range(4)]
-
-    def small_row(index):
-        return jnp.broadcast_to(smalls[index : index + 1, :], (8, C))
-
-    def small_run(first, count):
-        return jnp.concatenate([smalls[first + i : first + i + 1, :] for i in range(count)], axis=1)
-
-    def alone(step):
-        pl.when(me >= 0)(step)
-
-    gain1, _, _, gain2, bias2, cb2 = [small_row(i) for i in range(6)]
-    zero8 = jnp.zeros((8, C), f32)
-
     hidden = mm(table_ref[...], m1_ref[...]) + small_run(8, 4)
     hidden_ref[...] = hidden
     act = hidden * normal_cdf(hidden)
@@ -327,9 +303,7 @@
     chosen = jnp.sum(jnp.where(mine, ss, 0.0), axis=0, keepdims=True)
     scale = jnp.broadcast_to(1.0 + chosen[:, :C], (8, C))
     shift = jnp.broadcast_to(chosen[:, C:], (8, C))
-
-    mean1, rs1 = stats_ref[0:8], stats_ref[8:16]
-    centre, spread = moments_ref[0:8], moments_ref[8:16]
+    pair_forward(pair2, k2_ref)
 
     centre_s = centre * scale + shift
     mean2 = group_sum(centre_s) * (GROUPS / C)
@@ -342,38 +316,26 @@
 
     clear_edges(a2w)
 
-    def front2(i, carry):
+    def front2(i):
         v = unit2(c1[pl.ds(i * R, R)]) * one(1.0 + gain2) + one(bias2)
         prob = normal_cdf(v)
         put_windows(a2w, i * R, v * prob)
         g2p[pl.ds(i * R, R)] = gelu_slope(v, prob)
-        return carry
-
-    lax.fori_loop(0, H // R, front2, 0)
-
-    pair_forward(pair, k2_ref)
-
-    def conv2(i, carry):
-        got = pair_conv(a2w, pair, i * Q)
-        for parity, (place, source) in enumerate(zip(pairs_of(drf, i * Q), pairs_of(x_ref, i * Q))):
+
+    rw[0:1] = jnp.zeros((1, W // 2, 3 * C), bf16)
+
+    def conv2(i):
+        got = pair_conv(a2w, pair2, i * Q)
+        for parity, (place, source) in enumerate(zip(pairs_of(rf, i * Q), pairs_of(x_ref, i * Q))):
             r = source[...].astype(f32) + (got[..., parity * C : (parity + 1) * C] + one(cb2))
             place[...] = r.astype(bf16).astype(f32)
-        return carry
-
-    lax.fori_loop(0, H // 2 // Q, conv2, 0)
-    rw[0:1] = jnp.zeros((1, W // 2, 3 * C), bf16)
-
-    def split(i, carry):
-        even = drf[pl.ds(i * R, R), pl.ds(0, W // 2, 2), :]
-        odd = drf[pl.ds(i * R, R), pl.ds(1, W // 2, 2), :]
+        even = rf[pl.ds(i * R, R), pl.ds(0, W // 2, 2), :]
+        odd = rf[pl.ds(i * R, R), pl.ds(1, W // 2, 2), :]
         place = lax.broadcasted_iota(jnp.int32, odd.shape, 1)
         before = jnp.where(place == 0, 0.0, pltpu.roll(odd, 1, 1))
         rw[pl.ds(i * R + 1, R), :, 0:C] = before.astype(bf16)
         rw[pl.ds(i * R + 1, R), :, C : 2 * C] = even.astype(bf16)
         rw[pl.ds(i * R + 1, R), :, 2 * C :] = odd.astype(bf16)
-        return carry
-
-    lax.fori_loop(0, H // R, split, 0)
 
     def down_rows(first, rows):
         view = rw.reshape(H // 2 + 1, 2, W // 2, 3 * C)
@@ -383,22 +345,19 @@
     kd = jnp.concatenate([kd0_ref[...], kd1_ref[...]], axis=1)
     bias_down = small_run(6, 2)
 
-    def down(i, carry):
-        got = mm(down_rows(i * Q, Q), kd) + bias_down
-        out_ref[pl.ds(i * Q, Q)] = got.reshape(Q, W // 2, 2 * C).astype(bf16)
-        return carry
-
-    lax.fori_loop(0, H // 2 // Q, down, 0)
+    def down(i):
+        got = mm(down_rows(i * R, R), kd) + bias_down
+        out_ref[pl.ds(i * R, R)] = got.reshape(R, W // 2, 2 * C).astype(bf16)
+
+    front2(0)
+    for i in range(STEPS):
+        if i + 1 < STEPS:
+            front2(i + 1)
+        conv2(i)
+        if i % 2 == 1:
+            down(i // 2)
     out_copy = pltpu.make_async_copy(out_ref, out_hbm, out_sem)
     out_copy.start()
-    @alone
-    def _():
-        gkd = mm(down_rows(0, H // 2), cot_ref[...].reshape(CELLS // 4, 2 * C), TN)
-        gkd0_ref[0:KERNEL_ROWS] = gkd[:, :C]
-        gkd1_ref[0:KERNEL_ROWS] = gkd[:, C:]
-
-
-    gdb = gdb_ref[...]
 
     def tap(i, j):
         return flip(kd[(3 * i + j) * C : (3 * i + j + 1) * C, :])
@@ -412,103 +371,138 @@
         jnp.concatenate([tap(2, 1), none, tap(0, 1), none], axis=0),
         jnp.concatenate([tap(2, 2), tap(2, 0), tap(0, 2), tap(0, 0)], axis=0),
     ], axis=1)
-
-    def back_down(i, s):
-        rows = jnp.concatenate([cw[pl.ds(i * Q, Q)], cw[pl.ds(i * Q + 1, Q)]], axis=-1)
-        rows = rows.reshape(Q * W // 2, 8 * C)
+    clear_edges(t2w)
+
+    def back_down(i):
+        rows = jnp.concatenate([cw[pl.ds(i * R, R)], cw[pl.ds(i * R + 1, R)]], axis=-1)
+        rows = rows.reshape(R * W // 2, 8 * C)
         view = drf.reshape(H // 2, 2, W, C)
         for parity, got in enumerate((mm(rows[:, : 4 * C], even_rows), mm(rows, odd_rows))):
-            got = got.reshape(Q, W // 2, 2 * C)
-            view[pl.ds(i * Q, Q), parity, pl.ds(0, W // 2, 2), :] = got[..., :C]
-            view[pl.ds(i * Q, Q), parity, pl.ds(1, W // 2, 2), :] = got[..., C:]
+            got = got.reshape(R, W // 2, 2 * C)
+            view[pl.ds(i * R, R), parity, pl.ds(0, W // 2, 2), :] = got[..., :C]
+            view[pl.ds(i * R, R), parity, pl.ds(1, W // 2, 2), :] = got[..., C:]
+
+    def t2_windows(i):
+        values = drf[pl.ds(i * R, R)]
+        put_windows(t2w, i * R, values)
+        return fold(values)
+
+    gcb2 = zero8
+    for i in range(H // 2 // R):
+        back_down(i)
+        gcb2 = gcb2 + t2_windows(2 * i) + t2_windows(2 * i + 1)
+    gcb2 = total_of(gcb2)
+
+    gkd = mm(down_rows(0, H // 2), cot_ref[...].reshape(CELLS // 4, 2 * C), TN)
+    conv[2, 0:KERNEL_ROWS] = gkd[:, :C]
+    conv[3, 0:KERNEL_ROWS] = gkd[:, C:]
+
+    def pull(i, s, win_ref, back_ref, slope_ref, out_slope_ref, units):
+        got = pair_conv(win_ref, back_ref, i * Q)
+        places = zip(pairs_of(slope_ref, i * Q), pairs_of(out_slope_ref, i * Q), units)
+        for parity, (place, out_place, unit) in enumerate(places):
+            dn = got[..., parity * C : (parity + 1) * C] * place[...]
+            out_place[...] = dn
+            s = s[0] + fold(dn), s[1] + fold(dn * unit)
         return s
 
-    lax.fori_loop(0, H // 2 // Q, back_down, 0)
-
-    def pull(kernel_ref, slope_ref, units):
-        pair_backward(pair, kernel_ref)
-
-        def step(i, s):
-            got = pair_conv(tw, pair, i * Q)
-            for parity, (place, unit) in enumerate(zip(pairs_of(slope_ref, i * Q), units(i))):
-                dn = got[..., parity * C : (parity + 1) * C] * place[...]
-                place[...] = dn
-                s = s[0] + fold(dn), s[1] + fold(dn * unit)
-            return s
-
-        got = lax.fori_loop(0, H // 2 // Q, step, (zero8, zero8))
-        return total_of(got[0]), total_of(got[1])
-
-    clear_edges(tw)
-
-    def t2_windows(i, s):
-        values = drf[pl.ds(i * R, R)]
-        put_windows(tw, i * R, values)
-        return s + fold(values)
-
-    gcb2 = total_of(lax.fori_loop(0, H // R, t2_windows, zero8))
-    alone(lambda: kernel_grad(a2w, tw, gk2_ref))
-    gb2, gg2 = pull(k2_ref, g2p, lambda i: [unit2(ref[...]) for ref in pairs_of(c1, i * Q)])
+    pair_backward(back2, k2_ref)
+    sums = (zero8, zero8)
+    for i in range(STEPS):
+        sums = pull(i, sums, t2w, back2, g2p, g2p, [unit2(ref[...]) for ref in pairs_of(c1, i * Q)])
+    gb2, gg2 = [total_of(part) for part in sums]
     mean_du2 = group_sum(gb2 * (1.0 + gain2)) * (1.0 / PER_GROUP)
     mean_duu2 = group_sum(gg2 * (1.0 + gain2)) * (1.0 / PER_GROUP)
+    kernel_grad(a2w, t2w, conv.at[1])
+
+    pair_backward(back1, k1_ref)
+    clear_edges(t1w)
 
     def t1_windows(i, s):
         values = c1[pl.ds(i * R, R)]
         du = g2p[pl.ds(i * R, R)] * one(1.0 + gain2)
         ds = (du - one(mean_du2) - unit2(values) * one(mean_duu2)) * one(rs2)
-        put_windows(tw, i * R, ds * one(scale))
+        put_windows(t1w, i * R, ds * one(scale))
         return s[0] + fold(ds * values), s[1] + fold(ds)
-
-    gsc, gsh = lax.fori_loop(0, H // R, t1_windows, (zero8, zero8))
-    gsc, gsh = total_of(gsc), total_of(gsh)
-    alone(lambda: kernel_grad(a1w, tw, gk1_ref))
 
     def unit1(ref):
         return (ref[...].astype(f32) - one(mean1)) * one(rs1)
 
-    gb1, gg1 = pull(k1_ref, g1p, lambda i: [unit1(ref) for ref in pairs_of(x_ref, i * Q)])
+    class_sums = t1_windows(0, (zero8, zero8))
+    sums = (zero8, zero8)
+    for i in range(STEPS):
+        if i + 1 < STEPS:
+            class_sums = t1_windows(i + 1, class_sums)
+        sums = pull(i, sums, t1w, back1, g1p, slope1_ref, [unit1(ref) for ref in pairs_of(x_ref, i * Q)])
+    gsc, gsh = [total_of(part) for part in class_sums]
+    gb1, gg1 = [total_of(part) for part in sums]
     mean_du1 = group_sum(gb1 * (1.0 + gain1)) * (1.0 / PER_GROUP)
     mean_duu1 = group_sum(gg1 * (1.0 + gain1)) * (1.0 / PER_GROUP)
-
-    def finish(i, carry):
-        du = g1p[pl.ds(i * R, R)] * one(1.0 + gain1)
-        unit = unit1(x_ref.at[pl.ds(i * R, R)])
-        dx = (du - one(mean_du1) - unit * one(mean_duu1)) * one(rs1)
-        dx_ref[pl.ds(i * R, R)] = (drf[pl.ds(i * R, R)] + dx).astype(bf16)
-        return carry
-
-    dx_copies = []
-    for part in range(4):
-        lax.fori_loop(part * H // R // 4, (part + 1) * H // R // 4, finish, 0)
-        rows = pl.ds(part * H // 4, H // 4)
-        dx_copies.append(pltpu.make_async_copy(dx_ref.at[rows], dx_hbm.at[rows], dx_sem.at[part]))
-        dx_copies[-1].start()
-
+    for index, row in enumerate((1.0 + gain1, mean_du1, mean_duu1)):
+        factors_ref[8 * index : 8 * index + 8] = row
+    gdb = gdb_ref[...]
     rows = [gg1, gb1, gsh * scale, gg2, gb2, gcb2, gdb[:, :C], gdb[:, C:]]
     rows = [row[0:1] for row in rows]
     rows = rows + [jnp.where(mine[:, :C], row[0:1], 0.0) for row in (gsc, gsh)]
     extra = jnp.concatenate(rows, axis=0)
     if plan.rings:
-        put_results(plan, me, conv, extra, *results)
+        for k in (2, 3, 1):
+            put_results(plan, me, k, conv, *results)
+        kernel_grad(a1w, t1w, conv.at[0])
+        put_results(plan, me, 0, conv, *results)
+        keep_ref, send_ref = results
+        keep_ref[plan.half * plan.width :] = extra
+        send_ref[plan.half * plan.width :] = two_terms(extra)
     else:
+        kernel_grad(a1w, t1w, conv.at[0])
         results[0][...] = conv[:, 0:KERNEL_ROWS]
         results[1][...] = extra
     out_copy.wait()
-    for copy in dx_copies:
+
+
+def finish_body(x_ref, stats_ref, slope_ref, grad_ref, factors_ref, dx_hbm, dx_ref, sems):
+    mean, scale = stats_ref[0:8], stats_ref[8:16]
+    gain, mean_du, mean_duu = [factors_ref[8 * k : 8 * k + 8] for k in range(3)]
+
+    def finish(i, carry):
+        du = slope_ref[pl.ds(i * R, R)] * one(gain)
+        unit = (x_ref[pl.ds(i * R, R)].astype(f32) - one(mean)) * one(scale)
+        dx = (du - one(mean_du) - unit * one(mean_duu)) * one(scale)
+        dx_ref[pl.ds(i * R, R)] = (grad_ref[pl.ds(i * R, R)] + dx).astype(bf16)
+        return carry
+
+    copies = []
+    for part in range(4):
+        lax.fori_loop(part * H // R // 4, (part + 1) * H // R // 4, finish, 0)
+        rows = pl.ds(part * H // 4, H // 4)
+        copies.append(pltpu.make_async_copy(dx_ref.at[rows], dx_hbm.at[rows], sems.at[part]))
+        copies[-1].start()
+    for copy in copies:
         copy.wait()
 
 
-def put_results(plan, me, conv, extra, keep_ref, send_ref):
-    for place, (core, turn) in enumerate(plan.targets):
-        first = plan.tile_of((me ^ turn) * plan.conv_rows)
-        block = jnp.concatenate([conv[k, pl.ds(first, plan.conv_pad), :] for k in range(4)], axis=0)
-        at = place % plan.half * plan.width
-        if core:
-            send_ref[at : at + plan.width] = block.astype(bf16)
-        else:
-            keep_ref[at : at + plan.width] = block
-    keep_ref[plan.half * plan.width :] = extra
-    send_ref[plan.half * plan.width :] = two_terms(extra)
+def run_finish(x, stats, slope, grad, factors):
+    return pl.pallas_call(
+        finish_body,
+        out_shape=jax.ShapeDtypeStruct((H, W, C), bf16),
+        in_specs=vmem_specs(5),
+        out_specs=pl.BlockSpec(memory_space=pltpu.HBM),
+        scratch_shapes=[pltpu.VMEM((H, W, C), bf16), pltpu.SemaphoreType.DMA((4,))],
+        compiler_params=limit(8),
+        cost_estimate=cost(2, 6 << 20),
+        name="finish",
+    )(x, stats, slope, grad, factors)
+
+
+def put_results(plan, me, k, conv, keep_ref, send_ref):
+    pad = plan.conv_pad
+    for core, result in enumerate((keep_ref, send_ref)):
+        owners = plan.targets(me ^ core)
+        parts = [conv[k, pl.ds(plan.tile_of(owner * plan.conv_rows), pad), :] for owner in owners]
+        for place in range(0, len(parts), 2):
+            two = jnp.concatenate(parts[place : place + 2], axis=0)
+            at = (k * plan.half + place) * pad
+            result[at : at + 2 * pad] = two.astype(result.dtype)
 
 
 def two_terms(extra):
@@ -541,23 +535,25 @@
         self.dense_pad = self.padded(self.dense_rows, count)
         self.first_rows = -(-(self.conv_pad + 8) // 16) * 16
         self.dense_at = 3 * self.conv_pad
-        self.own_rows = self.first_rows + -(-(self.dense_at + self.dense_pad) // 16) * 16
-        near = [2 * k for k in range(self.line)]
-        half = self.line // 2
-        held = [
-            [k ^ turn for turn in (0, inner_size) for k in near[:half]],
-            [k ^ turn for turn in (0, 2 * inner_size) for k in near[half:]],
-        ]
-        held += [[k ^ 2 * inner_size for k in held[0]], [k ^ inner_size for k in held[1]]]
-        held += [[k ^ 1 for k in part] for part in held]
-        self.parts = len(held)
-        self.sources = [(part, place, turn) for part, turns in enumerate(held) for place, turn in enumerate(turns)]
-        self.targets = [
-            (core, plane * inner_size + k + core) for core in (0, 1) for plane in range(outer_size) for k in near
-        ]
+        self.rest_rows = -(-(self.dense_at + self.dense_pad) // 16) * 16
+        self.own_rows = self.first_rows + self.rest_rows
+        self.inner = inner_size
         self.half = count // 2
         self.width = 4 * self.conv_pad
 
+    def sources(self, me):
+        near = [2 * k for k in range(self.line)]
+        low, high = near[: self.line // 2], near[self.line // 2 :]
+        held = [low + [k ^ self.inner for k in low], high + [k ^ 2 * self.inner for k in high]]
+        held += [[k ^ 2 * self.inner for k in held[0]], [k ^ self.inner for k in held[1]]]
+        held += [[k ^ 1 for k in part] for part in held]
+        for part, turns in enumerate(held):
+            for place, turn in enumerate(turns):
+                yield part, place, me ^ turn
+
+    def targets(self, own):
+        return [own ^ (plane * self.inner + 2 * k) for plane in range(4) for k in range(self.line)]
+
     def padded(self, rows, count):
         return max(-(-(rows * k % 8 + rows) // 8) * 8 for k in range(count))
 
@@ -565,11 +561,13 @@
         return pl.multiple_of(row // 8 * 8, 8)
 
 
-def run_block(plan, class_ids, x, cot, prepared, fronted, inputs):
+def run_block(plan, class_ids, x, cot, prepared, inputs):
     struct = jax.ShapeDtypeStruct
     shapes = [
         struct((H // 2, W // 2, 2 * C), bf16),
-        struct((H, W, C), bf16),
+        struct((H, W, C), f32),
+        struct((H, W, C), f32),
+        struct((24, C), f32),
         struct((NCLASS, EMB), bf16),
         struct((EMB, EMB), bf16),
         struct((EMB, 2 * C), bf16),
@@ -585,27 +583,30 @@
     return pl.pallas_call(
         functools.partial(block_body, plan),
         out_shape=shapes,
-        in_specs=[pl.BlockSpec(memory_space=pltpu.SMEM)] + vmem_specs(11 + len(inputs)),
-        out_specs=[pl.BlockSpec(memory_space=pltpu.HBM)] * 2 + vmem_specs(6),
+        in_specs=[pl.BlockSpec(memory_space=pltpu.SMEM)] + vmem_specs(5 + len(inputs)),
+        out_specs=[pl.BlockSpec(memory_space=pltpu.HBM)] + vmem_specs(9),
         scratch_shapes=[
+            windows,
+            windows,
             windows,
             windows,
             pltpu.VMEM((H + 2, W // 2, 3 * C), bf16),
             plane,
             plane,
-            pltpu.VMEM((12 * C, 2 * C), bf16),
+            plane,
+            plane,
+            pltpu.VMEM((4, 12 * C, 2 * C), bf16),
             pltpu.VMEM((4, KERNEL_ROWS + 2 * plan.conv_pad, C), f32),
             pltpu.VMEM((MLP_ROWS + 2 * plan.dense_pad, C), f32),
-            pltpu.VMEM((3, KERNEL_ROWS, C), bf16),
+            pltpu.VMEM((4, KERNEL_ROWS, C), bf16),
+            pltpu.VMEM((16, C), f32),
             pltpu.VMEM((H // 2, W // 2, 2 * C), bf16),
-            pltpu.VMEM((H, W, C), bf16),
             pltpu.SemaphoreType.DMA,
-            pltpu.SemaphoreType.DMA((4,)),
         ],
-        compiler_params=limit(36),
+        compiler_params=limit(44),
         cost_estimate=cost(9000, 16 << 20),
         name="block",
-    )(class_ids, x, cot, *prepared, *fronted, *inputs)
+    )(class_ids, x, cot, *prepared, *inputs)
 
 
 def pack_body(plan, conv_hbm, dense_hbm, small_hbm, out_ref, conv_ref, dense_ref, small_ref, rows, sems):
@@ -645,7 +646,7 @@
             pltpu.VMEM((plan.own_rows, C), f32),
             pltpu.SemaphoreType.DMA((3,)),
         ],
-        compiler_params=pltpu.CompilerParams(vmem_limit_bytes=(64 << 20) - (160 << 10)),
+        compiler_params=pltpu.CompilerParams(vmem_limit_bytes=(64 << 20) - (190 << 10)),
         name="pack",
     )(conv_state, mlp_state, small_state)
 
@@ -659,19 +660,21 @@
 def merge_body(plan, blocks, groups, *refs):
     keep_ref, received = refs[0], refs[1 : len(refs) - groups]
     outs = refs[len(refs) - groups :]
-    size = blocks // groups
-    for block in range(blocks):
-        at = block * plan.width
-        total = keep_ref[at : at + plan.width]
-        for ref in received:
-            total = total + ref[at : at + plan.width].astype(f32)
-        group, place = block // size, block % size * plan.width
-        outs[group][place : place + plan.width] = total.astype(outs[group].dtype)
+    size = blocks // groups * plan.conv_pad
+    for group, out in enumerate(outs):
+        parts = []
+        for k in range(4):
+            at = k * blocks * plan.conv_pad + group * size
+            total = keep_ref[at : at + size]
+            for ref in received:
+                total = total + ref[at : at + size].astype(f32)
+            parts.append(total)
+        out[0 : 4 * size] = jnp.concatenate(parts, axis=0).astype(out.dtype)
     at = blocks * plan.width
     extra = sum_extra(keep_ref[at : at + EXTRA], received, at)
-    outs[0][size * plan.width :] = extra
+    outs[0][4 * size :] = extra
     for ref in outs[1:]:
-        ref[size * plan.width :] = two_terms(extra)
+        ref[4 * size :] = two_terms(extra)
 
 
 def run_merge(plan, blocks, groups, keep, received):
@@ -815,11 +818,12 @@
 
 def gather_ring(plan, own, prepare):
     (outer, outer_size), (inner, inner_size) = plan.sizes
-    line = [own] + [swap(own, inner, inner_size, 2 * k) for k in range(1, plan.line)]
-    line, prepared = lax.optimization_barrier((line, prepare()))
-    line = jnp.stack(line)
+    line = [swap(own, inner, inner_size, 2 * k) for k in range(1, plan.line)]
+    line, (*prepared, own) = lax.optimization_barrier((line, prepare(own)))
+    line = [own] + line
+    half = plan.line // 2
     held = []
-    for part, turn in ((line[: plan.line // 2], 1), (line[plan.line // 2 :], 2)):
+    for part, turn in ((jnp.stack(line[:half]), 1), (jnp.stack(line[half:]), 2)):
         held.append(jnp.concatenate([part, swap(part, outer, outer_size, turn)]))
     held = held + [swap(part, outer, outer_size, 2 - k) for k, part in enumerate(held)]
     return prepared, held + [swap(part, inner, inner_size, 1) for part in held]
@@ -828,7 +832,7 @@
 def reduce_ring(plan, keep, send):
     (outer, outer_size), (inner, inner_size) = plan.sizes
     received = [swap(send, inner, inner_size, 1)]
-    keep, *sends = run_merge(plan, plan.half, outer_size, keep, received)
+    keep, *sends = run_merge(plan, outer_size * plan.line, outer_size, keep, received)
     received = [swap(part, outer, outer_size, k + 1) for k, part in enumerate(sends)]
     keep, *sends = run_merge(plan, plan.line, plan.line, keep, received)
     return keep, [swap(part, inner, inner_size, 2 * (k + 1)) for k, part in enumerate(sends)]
@@ -861,16 +865,18 @@
     plan = Plan(sizes, conv_state.shape[2], mlp_state.shape[1], small_state.shape[1])
     x, cot = samples[0], cotangent[0]
     if plan.rings:
-        prepared, firsts = gather_ring(plan, run_pack(plan, *states), lambda: run_prepare(x, cot))
-        rests = firsts
+        prepared, inputs = gather_ring(plan, run_pack(plan, *states), lambda own: run_prepare(x, cot, own))
     else:
         conv, dense, small = [state[0].astype(bf16) for state in states]
         conv = lax.all_gather(conv, AXES, axis=1, tiled=True).reshape(4, KERNEL_ROWS, C)
-        firsts = [conv[0], lax.all_gather(small, AXES, axis=0, tiled=True).reshape(-1, C)]
-        rests = [conv[1:], lax.all_gather(dense, AXES, axis=0, tiled=True).reshape(MLP_ROWS, C)]
-        prepared = run_prepare(x, cot)
-    fronted = run_front(plan, x, prepared[0], firsts)
-    out, dx, table, m1, m2, hidden, first, second = run_block(plan, class_ids, x, cot, prepared, fronted, rests)
+        small = lax.all_gather(small, AXES, axis=0, tiled=True).reshape(-1, C)
+        dense = lax.all_gather(dense, AXES, axis=0, tiled=True).reshape(MLP_ROWS, C)
+        inputs = [conv[0], small, conv[1:], dense]
+        prepared = run_prepare(x, cot, small)[:3]
+    out, slope, grad, factors, table, m1, m2, hidden, first, second = run_block(
+        plan, class_ids, x, cot, prepared, inputs
+    )
+    dx = run_finish(x, prepared[0], slope, grad, factors)
     mlp = (table, m1, m2, hidden)
     if plan.rings:
         keep, received = reduce_ring(plan, first, second)

time: 84.8 us -> 76 us (0.90)
  Pallas kernels: 34.3 us -> 27 us
  waiting for transfers between devices: 24.5 us -> 23 us
  other arithmetic: 0.97 us -> 0.09 us
  local copies, waits for them, and re-layouts: 2.3 us -> 3.17 us
    pallas_call x1, Pallas kernels: 4.94 us -> 1.44 us  [run_finish(): pl.pallas_call(finish_body, out_shape=jax.ShapeDtypeStruct((H, W, C), bf1...]
    pallas_call x1, Pallas kernels: 23 us -> 20 us  [run_block(): pl.pallas_call(functools.partial(block_body, plan), out_shape=shapes, in_...]
    ppermute x18, waiting for transfers between devices: 24.5 us -> 23 us  [swap(): return lax.ppermute(values, axis, [(i, i ^ turn) for i in range(size)])]
    another operation x2, other arithmetic: 0.91 us -> 0.03 us  [the longest x1 0.01 us: gather_ring(): jnp.stack(line[half:])]
    unnamed x16 -> x18, local copies, waits for them, and re-layouts: 2.3 us -> 3.17 us
  transfers between devices with their start and end apart: 18 -> 18, of which waited for: 11 -> 10; matrix products, arithmetic and copies ran while one was open for 0% -> 0% of each run, Pallas kernels for 2% -> 3%
where the time goes in v4:
time: 76 us; the launch traced here: 75.7 us
  Pallas kernels  27 us (36%)
  waiting for transfers between devices  23 us (30%)
  starting transfers between devices  21 us (28%)
  local copies, waits for them, and re-layouts  3.17 us (4%)
  between operations  1.41 us (2%)
    ppermute x18, waiting for transfers between devices, swap(): return lax.ppermute(values, axis, [(i, i ^ turn) for i in range(size)])  23 us
    ppermute x18, starting transfers between devices, swap(): return lax.ppermute(values, axis, [(i, i ^ turn) for i in range(size)])  21 us
    pallas_call x1, Pallas kernels, run_block(): pl.pallas_call(functools.partial(block_body, plan), out_shape=shapes, in_...  20 us
    unnamed x18, local copies, waits for them, and re-layouts  3.17 us
    pallas_call x1, Pallas kernels, run_update(): pl.pallas_call(functools.partial(update_body, plan, len(received)), out_s...  2.4 us
    pallas_call x1, Pallas kernels, run_pack(): pl.pallas_call(functools.partial(pack_body, plan), out_shape=jax.ShapeDty...  1.74 us
  transfers between devices with their start and end apart: 18, of which 10 were waited for; matrix products, arithmetic and copies ran while one was open for 0% of the time, Pallas kernels for 3%

profile of v4, /device:TPU:0, one launch (start us, length us, event | category | flops | bytes accessed | tf_op | source)
XLA Modules:
  0.0 75.7 jit_solution(2047674263330388784)
XLA Ops:
  0.6 1.7 %pack.1.own_ref = bf16[272,128]{1,0:T(8,128)(2,1)} custom-call(f32[4,4,4608]{2,1,0:T(4,128)} %refs_8_.1, f32[4,12544]{1,0:T(4,128)} %refs_9_.1, f32[4,56]{1,0:T(4,128)} %refs_10_.1), custom_call_target="tpu_custom_call" | custom-call | tf_op jit(solution)/shard_map/pack/pallas_call | solution.py:637
  2.4 5.1 %collective-permute-start.2 = (bf16[272,128]{1,0:T(8,128)(2,1)}, bf16[272,128]{1,0:T(8,128)(2,1)S(1)}, u32[]{:S(2)}, u32[]{:S(2)}) collective-permute-start(bf16[272,128]{1,0:T(8,128)(2,1)} %pack.1.own_ref), channel_id=1, source_target_pairs={{0,6},{1,7},{2,4},{3,5},{4,2},{5,3},{6,0},{7,1},{8,14},{9,15},{10,... | collective-permute-start | bytes 208904 | tf_op jit(solution)/shard_map/ppermute | solution.py:816
  7.5 0.6 collective-permute-start
  8.1 1.2 %copy-done = bf16[1,64,64,128]{3,2,1,0:T(8,128)(2,1)S(1)} copy-done((bf16[1,64,64,128]{3,2,1,0:T(8,128)(2,1)S(1)}, bf16[1,64,64,128]{3,2,1,0:T(8,128)(2,1)}, u32[]{:S(2)}) %copy-start) | copy-done | bytes 1048600
  9.4 1.0 %copy-done.5 = bf16[1,32,32,256]{3,2,1,0:T(8,128)(2,1)S(1)} copy-done((bf16[1,32,32,256]{3,2,1,0:T(8,128)(2,1)S(1)}, bf16[1,32,32,256]{3,2,1,0:T(8,128)(2,1)}, u32[]{:S(2)}) %copy-start.5) | copy-done | bytes 524312
  10.4 0.9 %copy-done.7 = bf16[272,128]{1,0:T(8,128)(2,1)S(1)} copy-done((bf16[272,128]{1,0:T(8,128)(2,1)S(1)}, bf16[272,128]{1,0:T(8,128)(2,1)}, u32[]{:S(2)}) %copy-start.7) | copy-done | bytes 69656
  11.3 1.2 %prepare.1 = (f32[16,128]{1,0:T(8,128)S(1)}, bf16[33,32,512]{2,1,0:T(8,128)(2,1)S(1)}, f32[8,256]{1,0:T(8,128)S(1)}, bf16[272,128]{1,0:T(8,128)(2,1)S(1)}) custom-call(bf16[64,64,128]{2,1,0:T(8,128)(2,1)S(1)} %bitcast.10, bf16[32,32,256]{2,1,0:T(8,128)(2,1)S(1)} %bitcast.13, bf16[272,128]{1,0:T(8,128)(2,1)S(1)} %copy-done.7), custom_call_target="tpu_custom_call" | custom-call | flops 2097152 | bytes 3145728 | tf_op jit(solution)/shard_map/prepare/pallas_call | solution.py:191
  12.5 1.1 %collective-permute-done.1 = bf16[272,128]{1,0:T(8,128)(2,1)S(1)} collective-permute-done((bf16[272,128]{1,0:T(8,128)(2,1)}, bf16[272,128]{1,0:T(8,128)(2,1)S(1)}, u32[]{:S(2)}, u32[]{:S(2)}) %collective-permute-start.1) | collective-permute-done | bytes 69664 | tf_op jit(solution)/shard_map/ppermute | solution.py:816
  13.6 1.6 %collective-permute-start.3 = (bf16[2,272,128]{2,1,0:T(8,128)(2,1)S(1)}, bf16[2,272,128]{2,1,0:T(8,128)(2,1)S(1)}, u32[]{:S(2)}, u32[]{:S(2)}) collective-permute-start(bf16[2,272,128]{2,1,0:T(8,128)(2,1)S(1)} %pad_maximum_fusion.2), channel_id=1, source_target_pairs={{0,8},{8,0},{16,24},{24,16},{1,9},{9,1},{17,25},{25,17},{2,10},{10... | collective-permute-start | bytes 417800 | tf_op jit(solution)/shard_map/ppermute | solution.py:816
  15.2 1.6 %collective-permute-start.4 = (bf16[2,272,128]{2,1,0:T(8,128)(2,1)S(1)}, bf16[2,272,128]{2,1,0:T(8,128)(2,1)S(1)}, u32[]{:S(2)}, u32[]{:S(2)}) collective-permute-start(bf16[2,272,128]{2,1,0:T(8,128)(2,1)S(1)} %pad_maximum_fusion.3), channel_id=1, source_target_pairs={{0,16},{8,24},{16,0},{24,8},{1,17},{9,25},{17,1},{25,9},{2,18},{10... | collective-permute-start | bytes 417800 | tf_op jit(solution)/shard_map/ppermute | solution.py:816
  16.8 2.0 %collective-permute-done.3 = bf16[2,272,128]{2,1,0:T(8,128)(2,1)S(1)} collective-permute-done((bf16[2,272,128]{2,1,0:T(8,128)(2,1)S(1)}, bf16[2,272,128]{2,1,0:T(8,128)(2,1)S(1)}, u32[]{:S(2)}, u32[]{:S(2)}) %collective-permute-start.3) | collective-permute-done | bytes 139296 | tf_op jit(solution)/shard_map/ppermute | solution.py:816
  18.9 1.8 %collective-permute-start.5 = (bf16[4,272,128]{2,1,0:T(8,128)(2,1)S(1)}, bf16[4,272,128]{2,1,0:T(8,128)(2,1)S(1)}, u32[]{:S(2)}, u32[]{:S(2)}) collective-permute-start(bf16[4,272,128]{2,1,0:T(8,128)(2,1)S(1)} %pad_maximum_fusion.refs_6_), channel_id=1, source_target_pairs={{0,16},{8,24},{16,0},{24,8},{1,17},{9,25},{17,1},{25,9},{2,18},{10... | collective-permute-start | bytes 835592 | tf_op jit(solution)/shard_map/ppermute | solution.py:816
  20.7 1.6 %collective-permute-start.6 = (bf16[4,272,128]{2,1,0:T(8,128)(2,1)S(1)}, bf16[4,272,128]{2,1,0:T(8,128)(2,1)S(1)}, u32[]{:S(2)}, u32[]{:S(2)}) collective-permute-start(bf16[4,272,128]{2,1,0:T(8,128)(2,1)S(1)} %pad_maximum_fusion.1.refs_7_), channel_id=1, source_target_pairs={{0,8},{8,0},{16,24},{24,16},{1,9},{9,1},{17,25},{25,17},{2,10},{10... | collective-permute-start | bytes 835592 | tf_op jit(solution)/shard_map/ppermute | solution.py:816
  22.3 0.5 collective-permute-start.8
  22.8 3.6 %collective-permute-done.5.refs_8_ = bf16[4,272,128]{2,1,0:T(8,128)(2,1)S(1)} collective-permute-done((bf16[4,272,128]{2,1,0:T(8,128)(2,1)S(1)}, bf16[4,272,128]{2,1,0:T(8,128)(2,1)S(1)}, u32[]{:S(2)}, u32[]{:S(2)}) %collective-permute-start.5) | collective-permute-done | bytes 278560 | tf_op jit(solution)/shard_map/ppermute | solution.py:816
  26.5 1.6 %collective-permute-done.6.refs_9_ = bf16[4,272,128]{2,1,0:T(8,128)(2,1)S(1)} collective-permute-done((bf16[4,272,128]{2,1,0:T(8,128)(2,1)S(1)}, bf16[4,272,128]{2,1,0:T(8,128)(2,1)S(1)}, u32[]{:S(2)}, u32[]{:S(2)}) %collective-permute-start.6) | collective-permute-done | bytes 278560 | tf_op jit(solution)/shard_map/ppermute | solution.py:816
  28.7 0.9 %collective-permute-done.10.refs_13_ = bf16[4,272,128]{2,1,0:T(8,128)(2,1)S(1)} collective-permute-done((bf16[4,272,128]{2,1,0:T(8,128)(2,1)S(1)}, bf16[4,272,128]{2,1,0:T(8,128)(2,1)S(1)}, u32[]{:S(2)}, u32[]{:S(2)}) %collective-permute-start.10) | collective-permute-done | bytes 278560 | tf_op jit(solution)/shard_map/ppermute | solution.py:816
  29.6 20.0 %block.1 = (bf16[32,32,256]{2,1,0:T(8,128)(2,1)}, f32[64,64,128]{2,1,0:T(8,128)S(1)}, f32[64,64,128]{2,1,0:T(8,128)}, f32[24,128]{1,0:T(8,128)S(1)}, bf16[16,512...) custom-call(s32[1]{0:T(128)S(6)} %copy.14.refs_0_, ...), custom_call_target="tpu_custom_call" | custom-call | flops 9437184000 | bytes 16777216 | tf_op jit(solution)/shard_map/block/pallas_call | solution.py:583
  49.6 0.2 collective-permute-start.11
  49.8 2.0 %collective-permute-done.11.refs_1_ = bf16[2640,128]{1,0:T(8,128)(2,1)S(1)} collective-permute-done((bf16[2640,128]{1,0:T(8,128)(2,1)S(1)}, bf16[2640,128]{1,0:T(8,128)(2,1)S(1)}, u32[]{:S(2)}, u32[]{:S(2)}) %collective-permute-start.11) | collective-permute-done | bytes 675872 | tf_op jit(solution)/shard_map/ppermute | solution.py:816
  51.9 1.6 %collective-permute-start.12 = (bf16[720,128]{1,0:T(8,128)(2,1)S(1)}, bf16[720,128]{1,0:T(8,128)(2,1)S(1)}, u32[]{:S(2)}, u32[]{:S(2)}) collective-permute-start(bf16[720,128]{1,0:T(8,128)(2,1)S(1)} %get-tuple-element.61), channel_id=1, source_target_pairs={{0,8},{8,0},{16,24},{24,16},{1,9},{9,1},{17,25},{25,17},{2,10},{10... | collective-permute-start | bytes 552968 | tf_op jit(solution)/shard_map/ppermute | solution.py:816
  53.5 0.6 collective-permute-start.13
  54.1 1.4 %collective-permute-start.14 = (bf16[720,128]{1,0:T(8,128)(2,1)S(1)}, bf16[720,128]{1,0:T(8,128)(2,1)S(1)}, u32[]{:S(2)}, u32[]{:S(2)}) collective-permute-start(bf16[720,128]{1,0:T(8,128)(2,1)S(1)} %get-tuple-element.63), channel_id=1, source_target_pairs={{0,24},{8,16},{16,8},{24,0},{1,25},{9,17},{17,9},{25,1},{2,26},{10... | collective-permute-start | bytes 552968 | tf_op jit(solution)/shard_map/ppermute | solution.py:816
  55.5 4.0 %collective-permute-done.12.refs_1_ = bf16[720,128]{1,0:T(8,128)(2,1)S(1)} collective-permute-done((bf16[720,128]{1,0:T(8,128)(2,1)S(1)}, bf16[720,128]{1,0:T(8,128)(2,1)S(1)}, u32[]{:S(2)}, u32[]{:S(2)}) %collective-permute-start.12) | collective-permute-done | bytes 184352 | tf_op jit(solution)/shard_map/ppermute | solution.py:816
  59.5 4.4 %collective-permute-done.13.refs_2_ = bf16[720,128]{1,0:T(8,128)(2,1)S(1)} collective-permute-done((bf16[720,128]{1,0:T(8,128)(2,1)S(1)}, bf16[720,128]{1,0:T(8,128)(2,1)S(1)}, u32[]{:S(2)}, u32[]{:S(2)}) %collective-permute-start.13) | collective-permute-done | bytes 184352 | tf_op jit(solution)/shard_map/ppermute | solution.py:816
  64.0 1.1 %collective-permute-start.15 = (bf16[240,128]{1,0:T(8,128)(2,1)S(1)}, bf16[240,128]{1,0:T(8,128)(2,1)S(1)}, u32[]{:S(2)}, u32[]{:S(2)}) collective-permute-start(bf16[240,128]{1,0:T(8,128)(2,1)S(1)} %get-tuple-element.65), channel_id=1, source_target_pairs={{0,2},{1,3},{2,0},{3,1},{4,6},{5,7},{6,4},{7,5},{8,10},{9,11},{10,... | collective-permute-start | bytes 184328 | tf_op jit(solution)/shard_map/ppermute | solution.py:816
  65.1 2.1 %collective-permute-start.16 = (bf16[240,128]{1,0:T(8,128)(2,1)S(1)}, bf16[240,128]{1,0:T(8,128)(2,1)S(1)}, u32[]{:S(2)}, u32[]{:S(2)}) collective-permute-start(bf16[240,128]{1,0:T(8,128)(2,1)S(1)} %get-tuple-element.66), channel_id=1, source_target_pairs={{0,4},{1,5},{2,6},{3,7},{4,0},{5,1},{6,2},{7,3},{8,12},{9,13},{10,... | collective-permute-start | bytes 184328 | tf_op jit(solution)/shard_map/ppermute | solution.py:816
  67.2 1.2 %collective-permute-start.17 = (bf16[240,128]{1,0:T(8,128)(2,1)S(1)}, bf16[240,128]{1,0:T(8,128)(2,1)S(1)}, u32[]{:S(2)}, u32[]{:S(2)}) collective-permute-start(bf16[240,128]{1,0:T(8,128)(2,1)S(1)} %get-tuple-element.67), channel_id=1, source_target_pairs={{0,6},{1,7},{2,4},{3,5},{4,2},{5,3},{6,0},{7,1},{8,14},{9,15},{10,... | collective-permute-start | bytes 184328 | tf_op jit(solution)/shard_map/ppermute | solution.py:816
  68.4 1.4 %finish.1 = bf16[64,64,128]{2,1,0:T(8,128)(2,1)} custom-call(bf16[64,64,128]{2,1,0:T(8,128)(2,1)S(1)} %bitcast.12, f32[16,128]{1,0:T(8,128)S(1)} %get-tuple-element.47.refs_3_.stats_ref, f32[64,64,128]{2,1,0:T(8,128)S(1)} %get-tuple-element.55.slope_ref, f32[64,64,128]{2,1,0:T(8,128)S(1)} %copy-done.2, f32[24,128]{1,0:T(8,128)S(1)} %get-tuple-element.57.factors_ref), custom_call_target="tpu_custom_call" | custom-call | flops 2097152 | bytes 6291456 | tf_op jit(solution)/shard_map/finish/pallas_call | solution.py:485
  69.9 1.7 %collective-permute-done.16.refs_2_ = bf16[240,128]{1,0:T(8,128)(2,1)S(1)} collective-permute-done((bf16[240,128]{1,0:T(8,128)(2,1)S(1)}, bf16[240,128]{1,0:T(8,128)(2,1)S(1)}, u32[]{:S(2)}, u32[]{:S(2)}) %collective-permute-start.16) | collective-permute-done | bytes 61472 | tf_op jit(solution)/shard_map/ppermute | solution.py:816
  71.5 1.7 %collective-permute-done.17.refs_3_ = bf16[240,128]{1,0:T(8,128)(2,1)S(1)} collective-permute-done((bf16[240,128]{1,0:T(8,128)(2,1)S(1)}, bf16[240,128]{1,0:T(8,128)(2,1)S(1)}, u32[]{:S(2)}, u32[]{:S(2)}) %collective-permute-start.17) | collective-permute-done | bytes 61472 | tf_op jit(solution)/shard_map/ppermute | solution.py:816
  73.3 2.4 %update.1 = (f32[4,4,4608]{2,1,0:T(4,128)}, f32[4,12544]{1,0:T(4,128)}, f32[4,56]{1,0:T(4,128)}, bf16[4,4608]{1,0:T(4,128)(2,1)}, bf16[98,128]{1,0:T(8,128)(2,1)}, /*index=5*/bf16[1,56]{1,0:T(2,128)(2,1)}) custom-call(f32[200,128]{1,0:T(8,128)S(1)} %get-tuple-element.64.refs_0_, bf16[240,128]{1,0:T(8,128)(2,1)S(1)} %collective-permute-done.15.refs_1_, ...), custom_call_target="tpu_custom_call" | custom-call | tf_op jit(solution)/shard_map/update/pallas_call | solution.py:799
  (33 shorter events, 0.4 us)
Async XLA Ops:
  2.4 10.1 %collective-permute-start.2 = (bf16[272,128]{1,0:T(8,128)(2,1)}, bf16[272,128]{1,0:T(8,128)(2,1)S(1)}, u32[]{:S(2)}, u32[]{:S(2)}) collective-permute-start(bf16[272,128]{1,0:T(8,128)(2,1)} %pack.1.own_ref), channel_id=1, source_target_pairs={{0,6},{1,7},{2,4},{3,5},{4,2},{5,3},{6,0},{7,1},{8,14},{9,15},{10,... | collective-permute-start | bytes 208904 | tf_op jit(solution)/shard_map/ppermute | solution.py:816
  7.5 6.1 %collective-permute-start.1 = (bf16[272,128]{1,0:T(8,128)(2,1)}, bf16[272,128]{1,0:T(8,128)(2,1)S(1)}, u32[]{:S(2)}, u32[]{:S(2)}) collective-permute-start(bf16[272,128]{1,0:T(8,128)(2,1)} %pack.1.own_ref), channel_id=1, source_target_pairs={{0,4},{1,5},{2,6},{3,7},{4,0},{5,1},{6,2},{7,3},{8,12},{9,13},{10,... | collective-permute-start | bytes 208904 | tf_op jit(solution)/shard_map/ppermute | solution.py:816
  7.5 6.1 %collective-permute-start = (bf16[272,128]{1,0:T(8,128)(2,1)}, bf16[272,128]{1,0:T(8,128)(2,1)S(1)}, u32[]{:S(2)}, u32[]{:S(2)}) collective-permute-start(bf16[272,128]{1,0:T(8,128)(2,1)} %pack.1.own_ref), channel_id=1, source_target_pairs={{0,2},{1,3},{2,0},{3,1},{4,6},{5,7},{6,4},{7,5},{8,10},{9,11},{10,... | collective-permute-start | bytes 208904 | tf_op jit(solution)/shard_map/ppermute | solution.py:816
  8.1 1.2 %copy-start = (bf16[1,64,64,128]{3,2,1,0:T(8,128)(2,1)S(1)}, bf16[1,64,64,128]{3,2,1,0:T(8,128)(2,1)}, u32[]{:S(2)}) copy-start(bf16[1,64,64,128]{3,2,1,0:T(8,128)(2,1)} %param.6) | copy-start | bytes 3145732
  9.4 1.0 %copy-start.5 = (bf16[1,32,32,256]{3,2,1,0:T(8,128)(2,1)S(1)}, bf16[1,32,32,256]{3,2,1,0:T(8,128)(2,1)}, u32[]{:S(2)}) copy-start(bf16[1,32,32,256]{3,2,1,0:T(8,128)(2,1)} %param.7) | copy-start | bytes 1572868
  10.4 0.9 %copy-start.7 = (bf16[272,128]{1,0:T(8,128)(2,1)S(1)}, bf16[272,128]{1,0:T(8,128)(2,1)}, u32[]{:S(2)}) copy-start(bf16[272,128]{1,0:T(8,128)(2,1)} %pack.1.own_ref) | copy-start | bytes 208900
  11.3 18.3 %copy-start.1 = (bf16[1,64,64,128]{3,2,1,0:T(8,128)(2,1)S(1)}, bf16[1,64,64,128]{3,2,1,0:T(8,128)(2,1)}, u32[]{:S(2)}) copy-start(bf16[1,64,64,128]{3,2,1,0:T(8,128)(2,1)} %param.6) | copy-start | bytes 3145732
  11.3 18.3 %copy-start.6 = (bf16[1,32,32,256]{3,2,1,0:T(8,128)(2,1)S(1)}, bf16[1,32,32,256]{3,2,1,0:T(8,128)(2,1)}, u32[]{:S(2)}) copy-start(bf16[1,32,32,256]{3,2,1,0:T(8,128)(2,1)} %param.7) | copy-start | bytes 1572868
  13.6 5.2 %collective-permute-start.3 = (bf16[2,272,128]{2,1,0:T(8,128)(2,1)S(1)}, bf16[2,272,128]{2,1,0:T(8,128)(2,1)S(1)}, u32[]{:S(2)}, u32[]{:S(2)}) collective-permute-start(bf16[2,272,128]{2,1,0:T(8,128)(2,1)S(1)} %pad_maximum_fusion.2), channel_id=1, source_target_pairs={{0,8},{8,0},{16,24},{24,16},{1,9},{9,1},{17,25},{25,17},{2,10},{10... | collective-permute-start | bytes 417800 | tf_op jit(solution)/shard_map/ppermute | solution.py:816
  15.2 5.5 %collective-permute-start.4 = (bf16[2,272,128]{2,1,0:T(8,128)(2,1)S(1)}, bf16[2,272,128]{2,1,0:T(8,128)(2,1)S(1)}, u32[]{:S(2)}, u32[]{:S(2)}) collective-permute-start(bf16[2,272,128]{2,1,0:T(8,128)(2,1)S(1)} %pad_maximum_fusion.3), channel_id=1, source_target_pairs={{0,16},{8,24},{16,0},{24,8},{1,17},{9,25},{17,1},{25,9},{2,18},{10... | collective-permute-start | bytes 417800 | tf_op jit(solution)/shard_map/ppermute | solution.py:816
  18.9 7.6 %collective-permute-start.5 = (bf16[4,272,128]{2,1,0:T(8,128)(2,1)S(1)}, bf16[4,272,128]{2,1,0:T(8,128)(2,1)S(1)}, u32[]{:S(2)}, u32[]{:S(2)}) collective-permute-start(bf16[4,272,128]{2,1,0:T(8,128)(2,1)S(1)} %pad_maximum_fusion.refs_6_), channel_id=1, source_target_pairs={{0,16},{8,24},{16,0},{24,8},{1,17},{9,25},{17,1},{25,9},{2,18},{10... | collective-permute-start | bytes 835592 | tf_op jit(solution)/shard_map/ppermute | solution.py:816
  20.7 7.3 %collective-permute-start.6 = (bf16[4,272,128]{2,1,0:T(8,128)(2,1)S(1)}, bf16[4,272,128]{2,1,0:T(8,128)(2,1)S(1)}, u32[]{:S(2)}, u32[]{:S(2)}) collective-permute-start(bf16[4,272,128]{2,1,0:T(8,128)(2,1)S(1)} %pad_maximum_fusion.1.refs_7_), channel_id=1, source_target_pairs={{0,8},{8,0},{16,24},{24,16},{1,9},{9,1},{17,25},{25,17},{2,10},{10... | collective-permute-start | bytes 835592 | tf_op jit(solution)/shard_map/ppermute | solution.py:816
  22.3 6.4 %collective-permute-start.7 = (bf16[4,272,128]{2,1,0:T(8,128)(2,1)S(1)}, bf16[4,272,128]{2,1,0:T(8,128)(2,1)S(1)}, u32[]{:S(2)}, u32[]{:S(2)}) collective-permute-start(bf16[4,272,128]{2,1,0:T(8,128)(2,1)S(1)} %pad_maximum_fusion.refs_6_), channel_id=1, source_target_pairs={{0,1},{1,0},{2,3},{3,2},{4,5},{5,4},{6,7},{7,6},{8,9},{9,8},{10,11... | collective-permute-start | bytes 835592 | tf_op jit(solution)/shard_map/ppermute | solution.py:816
  22.3 6.4 %collective-permute-start.8 = (bf16[4,272,128]{2,1,0:T(8,128)(2,1)S(1)}, bf16[4,272,128]{2,1,0:T(8,128)(2,1)S(1)}, u32[]{:S(2)}, u32[]{:S(2)}) collective-permute-start(bf16[4,272,128]{2,1,0:T(8,128)(2,1)S(1)} %pad_maximum_fusion.1.refs_7_), channel_id=1, source_target_pairs={{0,1},{1,0},{2,3},{3,2},{4,5},{5,4},{6,7},{7,6},{8,9},{9,8},{10,11... | collective-permute-start | bytes 835592 | tf_op jit(solution)/shard_map/ppermute | solution.py:816
  26.5 2.2 %collective-permute-start.9 = (bf16[4,272,128]{2,1,0:T(8,128)(2,1)S(1)}, bf16[4,272,128]{2,1,0:T(8,128)(2,1)S(1)}, u32[]{:S(2)}, u32[]{:S(2)}) collective-permute-start(bf16[4,272,128]{2,1,0:T(8,128)(2,1)S(1)} %collective-permute-done.5.refs_8_), channel_id=1, source_target_pairs={{0,1},{1,0},{2,3},{3,2},{4,5},{5,4},{6,7},{7,6},{8,9},{9,8},{10,11... | collective-permute-start | bytes 835592 | tf_op jit(solution)/shard_map/ppermute | solution.py:816
  28.0 1.6 %collective-permute-start.10 = (bf16[4,272,128]{2,1,0:T(8,128)(2,1)S(1)}, bf16[4,272,128]{2,1,0:T(8,128)(2,1)S(1)}, u32[]{:S(2)}, u32[]{:S(2)}) collective-permute-start(bf16[4,272,128]{2,1,0:T(8,128)(2,1)S(1)} %collective-permute-done.6.refs_9_), channel_id=1, source_target_pairs={{0,1},{1,0},{2,3},{3,2},{4,5},{5,4},{6,7},{7,6},{8,9},{9,8},{10,11... | collective-permute-start | bytes 835592 | tf_op jit(solution)/shard_map/ppermute | solution.py:816
  49.6 18.9 %copy-start.2 = (f32[64,64,128]{2,1,0:T(8,128)S(1)}, f32[64,64,128]{2,1,0:T(8,128)}, u32[]{:S(2)}) copy-start(f32[64,64,128]{2,1,0:T(8,128)} %get-tuple-element.56.grad_ref) | copy-start | bytes 6291460
  49.6 2.2 %collective-permute-start.11 = (bf16[2640,128]{1,0:T(8,128)(2,1)S(1)}, bf16[2640,128]{1,0:T(8,128)(2,1)S(1)}, u32[]{:S(2)}, u32[]{:S(2)}) collective-permute-start(bf16[2640,128]{1,0:T(8,128)(2,1)S(1)} %get-tuple-element.59), channel_id=1, source_target_pairs={{0,1},{1,0},{2,3},{3,2},{4,5},{5,4},{6,7},{7,6},{8,9},{9,8},{10,11... | collective-permute-start | bytes 2027528 | tf_op jit(solution)/shard_map/ppermute | solution.py:816
  51.9 7.5 %collective-permute-start.12 = (bf16[720,128]{1,0:T(8,128)(2,1)S(1)}, bf16[720,128]{1,0:T(8,128)(2,1)S(1)}, u32[]{:S(2)}, u32[]{:S(2)}) collective-permute-start(bf16[720,128]{1,0:T(8,128)(2,1)S(1)} %get-tuple-element.61), channel_id=1, source_target_pairs={{0,8},{8,0},{16,24},{24,16},{1,9},{9,1},{17,25},{25,17},{2,10},{10... | collective-permute-start | bytes 552968 | tf_op jit(solution)/shard_map/ppermute | solution.py:816
  53.5 10.4 %collective-permute-start.13 = (bf16[720,128]{1,0:T(8,128)(2,1)S(1)}, bf16[720,128]{1,0:T(8,128)(2,1)S(1)}, u32[]{:S(2)}, u32[]{:S(2)}) collective-permute-start(bf16[720,128]{1,0:T(8,128)(2,1)S(1)} %get-tuple-element.62), channel_id=1, source_target_pairs={{0,16},{8,24},{16,0},{24,8},{1,17},{9,25},{17,1},{25,9},{2,18},{10... | collective-permute-start | bytes 552968 | tf_op jit(solution)/shard_map/ppermute | solution.py:816
  54.1 9.8 %collective-permute-start.14 = (bf16[720,128]{1,0:T(8,128)(2,1)S(1)}, bf16[720,128]{1,0:T(8,128)(2,1)S(1)}, u32[]{:S(2)}, u32[]{:S(2)}) collective-permute-start(bf16[720,128]{1,0:T(8,128)(2,1)S(1)} %get-tuple-element.63), channel_id=1, source_target_pairs={{0,24},{8,16},{16,8},{24,0},{1,25},{9,17},{17,9},{25,1},{2,26},{10... | collective-permute-start | bytes 552968 | tf_op jit(solution)/shard_map/ppermute | solution.py:816
  64.0 5.9 %collective-permute-start.15 = (bf16[240,128]{1,0:T(8,128)(2,1)S(1)}, bf16[240,128]{1,0:T(8,128)(2,1)S(1)}, u32[]{:S(2)}, u32[]{:S(2)}) collective-permute-start(bf16[240,128]{1,0:T(8,128)(2,1)S(1)} %get-tuple-element.65), channel_id=1, source_target_pairs={{0,2},{1,3},{2,0},{3,1},{4,6},{5,7},{6,4},{7,5},{8,10},{9,11},{10,... | collective-permute-start | bytes 184328 | tf_op jit(solution)/shard_map/ppermute | solution.py:816
  65.1 6.4 %collective-permute-start.16 = (bf16[240,128]{1,0:T(8,128)(2,1)S(1)}, bf16[240,128]{1,0:T(8,128)(2,1)S(1)}, u32[]{:S(2)}, u32[]{:S(2)}) collective-permute-start(bf16[240,128]{1,0:T(8,128)(2,1)S(1)} %get-tuple-element.66), channel_id=1, source_target_pairs={{0,4},{1,5},{2,6},{3,7},{4,0},{5,1},{6,2},{7,3},{8,12},{9,13},{10,... | collective-permute-start | bytes 184328 | tf_op jit(solution)/shard_map/ppermute | solution.py:816
  67.2 6.0 %collective-permute-start.17 = (bf16[240,128]{1,0:T(8,128)(2,1)S(1)}, bf16[240,128]{1,0:T(8,128)(2,1)S(1)}, u32[]{:S(2)}, u32[]{:S(2)}) collective-permute-start(bf16[240,128]{1,0:T(8,128)(2,1)S(1)} %get-tuple-element.67), channel_id=1, source_target_pairs={{0,6},{1,7},{2,4},{3,5},{4,2},{5,3},{6,0},{7,1},{8,14},{9,15},{10,... | collective-permute-start | bytes 184328 | tf_op jit(solution)/shard_map/ppermute | solution.py:816
  68.4 4.9 %copy-start.3 = (f32[4,4,4608]{2,1,0:T(4,128)S(1)}, f32[4,4,4608]{2,1,0:T(4,128)}, u32[]{:S(2)}) copy-start(f32[4,4,4608]{2,1,0:T(4,128)} %refs_8_.1) | copy-start | bytes 884740
  68.4 4.9 %copy-start.4 = (f32[4,12544]{1,0:T(4,128)S(1)}, f32[4,12544]{1,0:T(4,128)}, u32[]{:S(2)}) copy-start(f32[4,12544]{1,0:T(4,128)} %refs_9_.1) | copy-start | bytes 602116
  68.4 4.9 %copy-start.8 = (f32[4,56]{1,0:T(4,128)S(1)}, f32[4,56]{1,0:T(4,128)}, u32[]{:S(2)}) copy-start(f32[4,56]{1,0:T(4,128)} %refs_10_.1) | copy-start | bytes 2692

commit v5 on v4

--- a/solution.py
+++ b/solution.py
@@ -40,9 +40,10 @@
 NN = (((1,), (0,)), ((), ()))
 NT = (((1,), (1,)), ((), ()))
 TN = (((0,), (0,)), ((), ()))
-EXTRA = 8 + 2 * NCLASS
-R = 8
-Q = 4
+EXTRA = -(-(8 + 2 * NCLASS) // 16) * 16
+PAIRS = ((2, 3), (1, 0))
+R = 4
+Q = 2
 STEPS = H // R
 PART = CELLS // STEPS
 
@@ -62,6 +63,12 @@
     rest = v - high.astype(f32)
     mid = rest.astype(bf16)
     return high, mid, (rest - mid.astype(f32)).astype(bf16)
+
+
+def exact(values, weights, dims=NN):
+    rows = values.shape[0]
+    got = mm(jnp.concatenate(three(values), axis=0), weights, dims)
+    return got[:rows] + got[rows : 2 * rows] + got[2 * rows :]
 
 
 def group_sum(rows):
@@ -204,30 +211,42 @@
     count = 8 if plan.rings else 4
     cls_ref, x_ref, cot_ref, stats_ref, cw, gdb_ref = refs[:6]
     inputs = refs[6 : 6 + count]
-    out_hbm, slope1_ref, drf, factors_ref, table_ref, m1_ref, m2_ref, hidden_ref = refs[6 + count : 14 + count]
-    results = refs[14 + count : 16 + count]
-    a1w, a2w, t1w, t2w, rw, c1, g1p, g2p, rf, pairs, conv, dense, kernels, smalls, out_ref, out_sem = refs[16 + count :]
+    rw, kernels, smalls, slope1_ref, drf, factors_ref, table_ref, m1_ref, m2_ref, hidden_ref = refs[6 + count : 16 + count]
+    results = refs[16 + count : 18 + count]
+    a1w, a2w, t1w, t2w, c1, g1p, g2p, rf, pairs, conv, dense = refs[18 + count :]
+    kernels_f = conv
     me = position_of(plan.sizes)
     k1_ref, k2_ref, kd0_ref, kd1_ref = [kernels.at[k] for k in range(4)]
     pair1, pair2, back1, back2 = [pairs.at[k] for k in range(4)]
     zero8 = jnp.zeros((8, C), f32)
 
+    def take(k, part, place, owner):
+        odd = owner & 1
+        first = owner // 2 * plan.pair_rows
+        full = plan.full
+        mine = inputs[part][place, k * full : (k + 1) * full]
+        mate = inputs[part + 4][place, k * full : (k + 1) * full]
+        kernels_f[k, pl.ds(pl.multiple_of(first + (full + 8) * odd, 8), full), :] = mine.astype(f32)
+        kernels_f[k, pl.ds(pl.multiple_of(first + (full + 8) * (1 - odd), 8), full), :] = mate.astype(f32)
+        halves = [inputs[p][place, 4 * full : 4 * full + 16].astype(f32) for p in (part, part + 4)]
+        halves = [v[8 * (k // 2) : 8 * (k // 2) + 8] for v in halves]
+        if k % 2 == 1:
+            halves = [pltpu.roll(v, 4, 0) for v in halves]
+        kernels_f[k, pl.ds(pl.multiple_of(first + full, 8), 8), :] = jnp.where(own_half(odd), *halves)
+
     if plan.rings:
-        shards = list(plan.sources(me))
-        conv[...] = jnp.zeros(conv.shape, f32)
-        dense[...] = jnp.zeros(dense.shape, f32)
+        shards = plan.sources(me)
         small = jnp.zeros((16, C), f32)
         row = lax.broadcasted_iota(jnp.int32, (16, C), 0)
         lane = lax.broadcasted_iota(jnp.int32, (16, C), 1)
         for part, place, owner in shards:
-            values = inputs[part][place, 0 : plan.first_rows].astype(f32)
-            first = plan.tile_of(owner * plan.conv_rows)
-            conv[0, pl.ds(first, plan.conv_pad), :] += values[: plan.conv_pad]
-            at = row * C + lane - owner * plan.small_len
-            own = jnp.broadcast_to(values[plan.conv_pad : plan.conv_pad + 1], (16, C))
-            small = jnp.where((at >= 0) & (at < plan.small_len), own, small)
+            take(0, part, place, owner)
+            for p, device in ((part, owner), (part + 4, owner ^ 1)):
+                at = row * C + lane - device * plan.small_len
+                own = inputs[p][place, plan.small_at - 8 : plan.small_at + 8].astype(f32)[8:9]
+                small = jnp.where((at >= 0) & (at < plan.small_len), jnp.broadcast_to(own, (16, C)), small)
         smalls[...] = small
-        k1_ref[...] = conv[0, 0:KERNEL_ROWS].astype(bf16)
+        k1_ref[...] = kernels_f[0].astype(bf16)
     else:
         k1_ref[...] = inputs[0][...]
         smalls[0:14] = inputs[1][...].astype(f32)
@@ -235,13 +254,15 @@
     def take_rest(step, steps):
         if not plan.rings:
             return
+        if step == 0:
+            dense[...] = jnp.zeros(dense.shape, f32)
         for part, place, owner in shards[step::steps]:
-            values = inputs[part][place, plan.first_rows : plan.own_rows].astype(f32)
-            first = plan.tile_of(owner * plan.conv_rows)
-            for k in range(3):
-                conv[k + 1, pl.ds(first, plan.conv_pad), :] += values[k * plan.conv_pad : (k + 1) * plan.conv_pad]
-            first = plan.tile_of(owner * plan.dense_rows)
-            dense[pl.ds(first, plan.dense_pad), :] += values[plan.dense_at : plan.dense_at + plan.dense_pad]
+            for k in (1, 2, 3):
+                take(k, part, place, owner)
+            for p, device in ((part, owner), (part + 4, owner ^ 1)):
+                values = inputs[p][place, plan.dense_at : plan.small_at + 8].astype(f32)
+                first = plan.tile_of(device * plan.dense_rows)
+                dense[pl.ds(first, plan.dense_pad), :] += values[: plan.dense_pad]
 
     def small_row(index):
         return jnp.broadcast_to(smalls[index : index + 1, :], (8, C))
@@ -283,7 +304,7 @@
     spread = sum(total_of(part[1]) + PART * (part[0] - centre) * (part[0] - centre) for part in moments) * (1.0 / CELLS)
 
     if plan.rings:
-        kernels[1:4] = conv[1:4, 0:KERNEL_ROWS].astype(bf16)
+        kernels[1:4] = conv[1:4].astype(bf16)
     else:
         kernels[1:4] = inputs[2][...]
         dense[0:MLP_ROWS] = inputs[3][...].astype(f32)
@@ -298,12 +319,48 @@
     hidden = mm(table_ref[...], m1_ref[...]) + small_run(8, 4)
     hidden_ref[...] = hidden
     act = hidden * normal_cdf(hidden)
-    ss = sum(mm(part, m2_ref[...]) for part in three(act)) + small_run(12, 2)
+    ss = exact(act, m2_ref[...]) + small_run(12, 2)
     mine = lax.broadcasted_iota(jnp.int32, (NCLASS, 2 * C), 0) == cls_ref[0]
     chosen = jnp.sum(jnp.where(mine, ss, 0.0), axis=0, keepdims=True)
     scale = jnp.broadcast_to(1.0 + chosen[:, :C], (8, C))
     shift = jnp.broadcast_to(chosen[:, C:], (8, C))
     pair_forward(pair2, k2_ref)
+
+    kd = jnp.concatenate([kd0_ref[...], kd1_ref[...]], axis=1)
+
+    def tap(i, j):
+        return flip(kd[(3 * i + j) * C : (3 * i + j + 1) * C, :])
+
+    none = jnp.zeros((2 * C, C), bf16)
+    even_rows = jnp.concatenate([
+        jnp.concatenate([tap(1, 1), none], axis=0),
+        jnp.concatenate([tap(1, 2), tap(1, 0)], axis=0),
+    ], axis=1)
+    odd_rows = jnp.concatenate([
+        jnp.concatenate([tap(2, 1), none, tap(0, 1), none], axis=0),
+        jnp.concatenate([tap(2, 2), tap(2, 0), tap(0, 2), tap(0, 0)], axis=0),
+    ], axis=1)
+    clear_edges(t2w)
+
+    def back_down(i):
+        rows = jnp.concatenate([cw[pl.ds(i * R, R)], cw[pl.ds(i * R + 1, R)]], axis=-1)
+        rows = rows.reshape(R * W // 2, 8 * C)
+        view = drf.reshape(H // 2, 2, W, C)
+        for parity, got in enumerate((mm(rows[:, : 4 * C], even_rows), mm(rows, odd_rows))):
+            got = got.reshape(R, W // 2, 2 * C)
+            view[pl.ds(i * R, R), parity, pl.ds(0, W // 2, 2), :] = got[..., :C]
+            view[pl.ds(i * R, R), parity, pl.ds(1, W // 2, 2), :] = got[..., C:]
+
+    def t2_windows(i):
+        values = drf[pl.ds(i * R, R)]
+        put_windows(t2w, i * R, values)
+        return fold(values)
+
+    gcb2 = zero8
+    for i in range(H // 2 // R):
+        back_down(i)
+        gcb2 = gcb2 + t2_windows(2 * i) + t2_windows(2 * i + 1)
+    gcb2 = total_of(gcb2)
 
     centre_s = centre * scale + shift
     mean2 = group_sum(centre_s) * (GROUPS / C)
@@ -337,65 +394,15 @@
         rw[pl.ds(i * R + 1, R), :, C : 2 * C] = even.astype(bf16)
         rw[pl.ds(i * R + 1, R), :, 2 * C :] = odd.astype(bf16)
 
-    def down_rows(first, rows):
-        view = rw.reshape(H // 2 + 1, 2, W // 2, 3 * C)
-        taken = [view[pl.ds(first + t // 2, rows), t % 2] for t in range(3)]
-        return jnp.concatenate(taken, axis=-1).reshape(rows * W // 2, TAPS * C)
-
-    kd = jnp.concatenate([kd0_ref[...], kd1_ref[...]], axis=1)
-    bias_down = small_run(6, 2)
-
-    def down(i):
-        got = mm(down_rows(i * R, R), kd) + bias_down
-        out_ref[pl.ds(i * R, R)] = got.reshape(R, W // 2, 2 * C).astype(bf16)
-
     front2(0)
     for i in range(STEPS):
         if i + 1 < STEPS:
             front2(i + 1)
         conv2(i)
-        if i % 2 == 1:
-            down(i // 2)
-    out_copy = pltpu.make_async_copy(out_ref, out_hbm, out_sem)
-    out_copy.start()
-
-    def tap(i, j):
-        return flip(kd[(3 * i + j) * C : (3 * i + j + 1) * C, :])
-
-    none = jnp.zeros((2 * C, C), bf16)
-    even_rows = jnp.concatenate([
-        jnp.concatenate([tap(1, 1), none], axis=0),
-        jnp.concatenate([tap(1, 2), tap(1, 0)], axis=0),
-    ], axis=1)
-    odd_rows = jnp.concatenate([
-        jnp.concatenate([tap(2, 1), none, tap(0, 1), none], axis=0),
-        jnp.concatenate([tap(2, 2), tap(2, 0), tap(0, 2), tap(0, 0)], axis=0),
-    ], axis=1)
-    clear_edges(t2w)
-
-    def back_down(i):
-        rows = jnp.concatenate([cw[pl.ds(i * R, R)], cw[pl.ds(i * R + 1, R)]], axis=-1)
-        rows = rows.reshape(R * W // 2, 8 * C)
-        view = drf.reshape(H // 2, 2, W, C)
-        for parity, got in enumerate((mm(rows[:, : 4 * C], even_rows), mm(rows, odd_rows))):
-            got = got.reshape(R, W // 2, 2 * C)
-            view[pl.ds(i * R, R), parity, pl.ds(0, W // 2, 2), :] = got[..., :C]
-            view[pl.ds(i * R, R), parity, pl.ds(1, W // 2, 2), :] = got[..., C:]
-
-    def t2_windows(i):
-        values = drf[pl.ds(i * R, R)]
-        put_windows(t2w, i * R, values)
-        return fold(values)
-
-    gcb2 = zero8
-    for i in range(H // 2 // R):
-        back_down(i)
-        gcb2 = gcb2 + t2_windows(2 * i) + t2_windows(2 * i + 1)
-    gcb2 = total_of(gcb2)
-
-    gkd = mm(down_rows(0, H // 2), cot_ref[...].reshape(CELLS // 4, 2 * C), TN)
-    conv[2, 0:KERNEL_ROWS] = gkd[:, :C]
-    conv[3, 0:KERNEL_ROWS] = gkd[:, C:]
+
+    gkd = mm(down_rows(rw, 0, H // 2), cot_ref[...].reshape(CELLS // 4, 2 * C), TN)
+    conv[2] = gkd[:, :C]
+    conv[3] = gkd[:, C:]
 
     def pull(i, s, win_ref, back_ref, slope_ref, out_slope_ref, units):
         got = pair_conv(win_ref, back_ref, i * Q)
@@ -444,20 +451,51 @@
     rows = [gg1, gb1, gsh * scale, gg2, gb2, gcb2, gdb[:, :C], gdb[:, C:]]
     rows = [row[0:1] for row in rows]
     rows = rows + [jnp.where(mine[:, :C], row[0:1], 0.0) for row in (gsc, gsh)]
-    extra = jnp.concatenate(rows, axis=0)
+    extra = jnp.concatenate(rows + [jnp.zeros((EXTRA - len(rows) - 2 * NCLASS + 2, C), f32)], axis=0)
     if plan.rings:
-        for k in (2, 3, 1):
-            put_results(plan, me, k, conv, *results)
+        put_results(plan, me, 0, conv, *results)
         kernel_grad(a1w, t1w, conv.at[0])
-        put_results(plan, me, 0, conv, *results)
-        keep_ref, send_ref = results
-        keep_ref[plan.half * plan.width :] = extra
-        send_ref[plan.half * plan.width :] = two_terms(extra)
+        put_results(plan, me, 1, conv, *results)
+        for ref in results:
+            ref[plan.half * 2 * plan.pair_rows :] = extra.astype(ref.dtype)
     else:
         kernel_grad(a1w, t1w, conv.at[0])
-        results[0][...] = conv[:, 0:KERNEL_ROWS]
+        results[0][...] = conv[...]
         results[1][...] = extra
-    out_copy.wait()
+
+
+def down_rows(rw, first, rows):
+    view = rw.reshape(H // 2 + 1, 2, W // 2, 3 * C)
+    taken = [view[pl.ds(first + t // 2, rows), t % 2] for t in range(3)]
+    return jnp.concatenate(taken, axis=-1).reshape(rows * W // 2, TAPS * C)
+
+
+def down_body(rw, kernels, smalls, out_hbm, out_ref, sems):
+    kd = jnp.concatenate([kernels[2], kernels[3]], axis=1)
+    bias = jnp.concatenate([smalls[6:7, :], smalls[7:8, :]], axis=1)
+    copies = []
+    for part in range(4):
+        rows = slice(part * H // 8, (part + 1) * H // 8)
+        got = mm(down_rows(rw, part * H // 8, H // 8), kd) + bias
+        out_ref[rows] = got.reshape(H // 8, W // 2, 2 * C).astype(bf16)
+        copies.append(pltpu.make_async_copy(out_ref.at[rows], out_hbm.at[rows], sems.at[part]))
+        copies[-1].start()
+    for copy in copies:
+        copy.wait()
+
+
+def run_down(rw, kernels, smalls):
+    shape = (H // 2, W // 2, 2 * C)
+    return pl.pallas_call(
+        down_body,
+        out_shape=jax.ShapeDtypeStruct(shape, bf16),
+        in_specs=vmem_specs(3),
+        out_specs=pl.BlockSpec(memory_space=pltpu.HBM),
+        scratch_shapes=[pltpu.VMEM(shape, bf16), pltpu.SemaphoreType.DMA((4,))],
+        compiler_params=limit(8),
+        cost_estimate=cost(604, 3 << 20),
+        name="down",
+    )(rw, kernels, smalls)
 
 
 def finish_body(x_ref, stats_ref, slope_ref, grad_ref, factors_ref, dx_hbm, dx_ref, sems):
@@ -494,20 +532,25 @@
     )(x, stats, slope, grad, factors)
 
 
-def put_results(plan, me, k, conv, keep_ref, send_ref):
-    pad = plan.conv_pad
+def own_half(odd):
+    return (lax.broadcasted_iota(jnp.int32, (8, C), 0) < 4) == (odd == 0)
+
+
+def put_results(plan, me, index, conv, keep_ref, send_ref):
+    left, right = PAIRS[index]
     for core, result in enumerate((keep_ref, send_ref)):
-        owners = plan.targets(me ^ core)
-        parts = [conv[k, pl.ds(plan.tile_of(owner * plan.conv_rows), pad), :] for owner in owners]
-        for place in range(0, len(parts), 2):
-            two = jnp.concatenate(parts[place : place + 2], axis=0)
-            at = (k * plan.half + place) * pad
-            result[at : at + 2 * pad] = two.astype(result.dtype)
-
-
-def two_terms(extra):
-    high = extra.astype(bf16)
-    return jnp.concatenate([high.astype(f32), extra - high.astype(f32)], axis=0).astype(bf16)
+        odd = (me ^ core) & 1
+        parts = []
+        for owner in plan.targets(me ^ core):
+            full, half = plan.places(odd, plan.tile_of(owner * plan.conv_rows))
+            parts += [conv[k, pl.ds(full, plan.full), :] for k in (left, right)]
+            halves = [conv[k, pl.ds(half, 8), :] for k in (left, right)]
+            parts.append(jnp.where(own_half(odd), halves[0], pltpu.roll(halves[1], 4, 0)))
+        rows = 2 * plan.pair_rows
+        for place in range(0, plan.half, 2):
+            two = jnp.concatenate(parts[3 * place : 3 * place + 6], axis=0)
+            at = (index * plan.half + place) * plan.pair_rows
+            result[at : at + rows] = two.astype(result.dtype)
 
 
 def vmem_specs(count):
@@ -530,41 +573,40 @@
         self.conv_len, self.dense_len, self.small_len = conv_len, dense_len, small_len
         self.conv_rows, self.dense_rows = conv_len // C, dense_len // C
         powers = inner_size & (inner_size - 1) == 0 and inner_size >= 4 and outer_size == 4
-        self.rings = powers and conv_len % C == 0 and dense_len % C == 0 and small_len <= C
-        self.conv_pad = self.padded(self.conv_rows, count)
-        self.dense_pad = self.padded(self.dense_rows, count)
-        self.first_rows = -(-(self.conv_pad + 8) // 16) * 16
-        self.dense_at = 3 * self.conv_pad
-        self.rest_rows = -(-(self.dense_at + self.dense_pad) // 16) * 16
-        self.own_rows = self.first_rows + self.rest_rows
+        self.rings = powers and conv_len % C == 0 and dense_len % C == 0 and small_len <= C and self.conv_rows % 8 == 4
+        self.dense_pad = max(-(-(self.dense_rows * k % 8 + self.dense_rows) // 8) * 8 for k in range(count))
+        self.full = self.conv_rows - 4
+        self.window = self.conv_rows + 4
+        self.pair_rows = 2 * self.conv_rows
+        self.dense_at = 4 * self.full + 16
+        self.small_at = self.dense_at + self.dense_pad
+        self.own_rows = -(-(self.small_at + 8) // 16) * 16
         self.inner = inner_size
         self.half = count // 2
-        self.width = 4 * self.conv_pad
 
     def sources(self, me):
         near = [2 * k for k in range(self.line)]
         low, high = near[: self.line // 2], near[self.line // 2 :]
         held = [low + [k ^ self.inner for k in low], high + [k ^ 2 * self.inner for k in high]]
         held += [[k ^ 2 * self.inner for k in held[0]], [k ^ self.inner for k in held[1]]]
-        held += [[k ^ 1 for k in part] for part in held]
-        for part, turns in enumerate(held):
-            for place, turn in enumerate(turns):
-                yield part, place, me ^ turn
+        return [(part, place, me ^ turn) for part, turns in enumerate(held) for place, turn in enumerate(turns)]
 
     def targets(self, own):
         return [own ^ (plane * self.inner + 2 * k) for plane in range(4) for k in range(self.line)]
 
-    def padded(self, rows, count):
-        return max(-(-(rows * k % 8 + rows) // 8) * 8 for k in range(count))
-
     def tile_of(self, row):
         return pl.multiple_of(row // 8 * 8, 8)
+
+    def places(self, odd, first=0):
+        return pl.multiple_of(first + 8 * odd, 8), pl.multiple_of(first + self.full * (1 - odd), 8)
 
 
 def run_block(plan, class_ids, x, cot, prepared, inputs):
     struct = jax.ShapeDtypeStruct
     shapes = [
-        struct((H // 2, W // 2, 2 * C), bf16),
+        struct((H + 2, W // 2, 3 * C), bf16),
+        struct((4, KERNEL_ROWS, C), bf16),
+        struct((16, C), f32),
         struct((H, W, C), f32),
         struct((H, W, C), f32),
         struct((24, C), f32),
@@ -574,8 +616,8 @@
         struct((NCLASS, EMB), f32),
     ]
     if plan.rings:
-        rows = plan.half * plan.width
-        shapes += [struct((rows + EXTRA, C), f32), struct((rows + 2 * EXTRA, C), bf16)]
+        rows = plan.half * 2 * plan.pair_rows
+        shapes += [struct((rows + EXTRA, C), f32), struct((rows + EXTRA, C), bf16)]
     else:
         shapes += [struct((4, KERNEL_ROWS, C), f32), struct((EXTRA, C), f32)]
     windows = pltpu.VMEM((H + 2, W, 3 * C), bf16)
@@ -584,52 +626,55 @@
         functools.partial(block_body, plan),
         out_shape=shapes,
         in_specs=[pl.BlockSpec(memory_space=pltpu.SMEM)] + vmem_specs(5 + len(inputs)),
-        out_specs=[pl.BlockSpec(memory_space=pltpu.HBM)] + vmem_specs(9),
+        out_specs=vmem_specs(12),
         scratch_shapes=[
             windows,
             windows,
             windows,
             windows,
-            pltpu.VMEM((H + 2, W // 2, 3 * C), bf16),
             plane,
             plane,
             plane,
             plane,
             pltpu.VMEM((4, 12 * C, 2 * C), bf16),
-            pltpu.VMEM((4, KERNEL_ROWS + 2 * plan.conv_pad, C), f32),
+            pltpu.VMEM((4, KERNEL_ROWS, C), f32),
             pltpu.VMEM((MLP_ROWS + 2 * plan.dense_pad, C), f32),
-            pltpu.VMEM((4, KERNEL_ROWS, C), bf16),
-            pltpu.VMEM((16, C), f32),
-            pltpu.VMEM((H // 2, W // 2, 2 * C), bf16),
-            pltpu.SemaphoreType.DMA,
         ],
-        compiler_params=limit(44),
+        compiler_params=limit(40),
         cost_estimate=cost(9000, 16 << 20),
         name="block",
     )(class_ids, x, cot, *prepared, *inputs)
 
 
-def pack_body(plan, conv_hbm, dense_hbm, small_hbm, out_ref, conv_ref, dense_ref, small_ref, rows, sems):
+def pack_body(plan, conv_hbm, dense_hbm, small_hbm, out_ref, conv_ref, dense_ref, small_ref, windows, rows, sems):
     pairs = ((conv_hbm.at[0], conv_ref), (dense_hbm, dense_ref), (small_hbm, small_ref))
     copies = [pltpu.make_async_copy(source, target, sems.at[k]) for k, (source, target) in enumerate(pairs)]
     for copy in copies:
         copy.start()
     me = position_of(plan.sizes)
+    odd = me & 1
+    windows[...] = jnp.zeros(windows.shape, f32)
     rows[...] = jnp.zeros(rows.shape, f32)
-    starts = [0] + [plan.first_rows + k * plan.conv_pad for k in range(3)]
-    first = me * plan.conv_rows % 8
     copies[0].wait()
     for r in range(plan.conv_rows):
         for k in range(4):
-            rows[pl.ds(starts[k] + first + r, 1), :] = conv_ref[k : k + 1, r * C : (r + 1) * C]
+            windows[pl.ds(k * plan.window + 4 * odd + r, 1), :] = conv_ref[k : k + 1, r * C : (r + 1) * C]
+    halves = []
+    for k in range(4):
+        full, half = plan.places(odd, k * plan.window)
+        rows[k * plan.full : (k + 1) * plan.full] = windows[pl.ds(full, plan.full), :]
+        halves.append(windows[pl.ds(half, 8), :])
+    for k in (0, 2):
+        at = 4 * plan.full + 4 * k
+        rows[at : at + 8] = jnp.where(own_half(odd), halves[k], pltpu.roll(halves[k + 1], 4, 0))
     copies[1].wait()
-    first = plan.first_rows + plan.dense_at + me * plan.dense_rows % 8
+    first = plan.dense_at + me * plan.dense_rows % 8
     for r in range(plan.dense_rows):
         rows[pl.ds(first + r, 1), :] = dense_ref[0:1, r * C : (r + 1) * C]
     copies[2].wait()
     own = jnp.concatenate([small_ref[0:1, :], jnp.zeros((1, C - plan.small_len), f32)], axis=1)
     own = pltpu.roll(jnp.broadcast_to(own, (8, C)), me * plan.small_len % C, 1)
-    rows[plan.conv_pad : plan.conv_pad + 1] = own[0:1]
+    rows[plan.small_at : plan.small_at + 1] = own[0:1]
     out_ref[...] = rows[...].astype(bf16)
 
 
@@ -643,6 +688,7 @@
             pltpu.VMEM((4, plan.conv_len), f32),
             pltpu.VMEM((4, plan.dense_len), f32),
             pltpu.VMEM((4, plan.small_len), f32),
+            pltpu.VMEM((4 * plan.window, C), f32),
             pltpu.VMEM((plan.own_rows, C), f32),
             pltpu.SemaphoreType.DMA((3,)),
         ],
@@ -651,36 +697,26 @@
     )(conv_state, mlp_state, small_state)
 
 
-def sum_extra(extra, received, at):
-    for ref in received:
-        extra = extra + ref[at : at + EXTRA].astype(f32) + ref[at + EXTRA : at + 2 * EXTRA].astype(f32)
-    return extra
-
-
 def merge_body(plan, blocks, groups, *refs):
     keep_ref, received = refs[0], refs[1 : len(refs) - groups]
     outs = refs[len(refs) - groups :]
-    size = blocks // groups * plan.conv_pad
+
+    def sums(at, size):
+        total = keep_ref[at : at + size]
+        for ref in received:
+            total = total + ref[at : at + size].astype(f32)
+        return total
+
+    size = blocks // groups * plan.pair_rows
+    extra = sums(2 * blocks * plan.pair_rows, EXTRA)
     for group, out in enumerate(outs):
-        parts = []
-        for k in range(4):
-            at = k * blocks * plan.conv_pad + group * size
-            total = keep_ref[at : at + size]
-            for ref in received:
-                total = total + ref[at : at + size].astype(f32)
-            parts.append(total)
-        out[0 : 4 * size] = jnp.concatenate(parts, axis=0).astype(out.dtype)
-    at = blocks * plan.width
-    extra = sum_extra(keep_ref[at : at + EXTRA], received, at)
-    outs[0][4 * size :] = extra
-    for ref in outs[1:]:
-        ref[4 * size :] = two_terms(extra)
+        parts = [sums(k * blocks * plan.pair_rows + group * size, size) for k in range(2)]
+        out[...] = jnp.concatenate(parts + [extra], axis=0).astype(out.dtype)
 
 
 def run_merge(plan, blocks, groups, keep, received):
-    rows = blocks // groups * plan.width
-    shapes = [jax.ShapeDtypeStruct((rows + EXTRA, C), f32)]
-    shapes += [jax.ShapeDtypeStruct((rows + 2 * EXTRA, C), bf16)] * (groups - 1)
+    rows = blocks // groups * 2 * plan.pair_rows + EXTRA
+    shapes = [jax.ShapeDtypeStruct((rows, C), f32 if group == 0 else bf16) for group in range(groups)]
     return pl.pallas_call(
         functools.partial(merge_body, plan, blocks, groups),
         out_shape=shapes,
@@ -704,11 +740,8 @@
         rights = [b for k, a in enumerate(left) for b in right[: 3 - k]]
         return mm(jnp.concatenate(lefts, axis=0), jnp.concatenate(rights, axis=0), TN)
 
-    def back(values, weights):
-        return sum(mm(part, weights, NT) for part in three(values))
-
-    dp = back(dss, m2_ref[...]) * gelu_slope(hidden, prob)
-    put(0, back(dp, m1_ref[...]))
+    dp = exact(dss, m2_ref[...], NT) * gelu_slope(hidden, prob)
+    put(0, exact(dp, m1_ref[...], NT))
     put(TABLE_ROWS, outer([table], three(dp)))
     put(TABLE_ROWS + M1_ROWS, outer(three(hidden * prob), three(dss)))
     ge1 = jnp.sum(dp, axis=0, keepdims=True)
@@ -748,21 +781,27 @@
     conv_new, dense_new, small_new, conv_copy, dense_copy, small_copy = refs[8 + received_count : 14 + received_count]
     block, grads, rows, smalls = refs[14 + received_count :]
     me = position_of(plan.sizes)
-    total = keep_ref[0 : plan.width]
+    total = keep_ref[...]
     for ref in received:
-        total = total + ref[0 : plan.width].astype(f32)
-    block[...] = total
-    extra = sum_extra(keep_ref[plan.width : plan.width + EXTRA], received, plan.width)
+        total = total + ref[...].astype(f32)
+    odd = me & 1
+    for index, pair in enumerate(PAIRS):
+        at = index * plan.pair_rows
+        rest = total[at + 2 * plan.full : at + plan.pair_rows]
+        for side, k in enumerate(pair):
+            full, half = plan.places(odd, k * plan.window)
+            block[pl.ds(full, plan.full), :] = total[at + side * plan.full : at + (side + 1) * plan.full]
+            block[pl.ds(half, 8), :] = pltpu.roll(rest, 4, 0) if side else rest
+    extra = total[2 * plan.pair_rows :]
     smalls[0:8] = extra[0:8]
-    dss = jnp.concatenate([extra[8 : 8 + NCLASS], extra[8 + NCLASS :]], axis=1)
+    dss = jnp.concatenate([extra[8 : 8 + NCLASS], extra[8 + NCLASS : 8 + 2 * NCLASS]], axis=1)
     tail = mlp_grads(table_ref[...], m1_ref, m2_ref, hidden_ref[...], dss, grads)
     for i, row in enumerate(tail):
         smalls[8 + i : 9 + i, :] = row
 
-    first = me * plan.conv_rows % 8
     for r in range(plan.conv_rows):
         at = slice(r * C, (r + 1) * C)
-        gradient = block[pl.ds(first + r, 4, plan.conv_pad), :]
+        gradient = block[pl.ds(4 * odd + r, 4, plan.window), :]
         new = adam(*[conv_ref[k, :, at] for k in range(4)], gradient, rate_conv, decay_weights)
         for k in range(4):
             conv_new[k, :, at] = new[k]
@@ -802,7 +841,7 @@
         in_specs=vmem_specs(1 + len(received) + 4 + 3),
         out_specs=vmem_specs(6),
         scratch_shapes=[
-            pltpu.VMEM((plan.width, C), f32),
+            pltpu.VMEM((4 * plan.window, C), f32),
             pltpu.VMEM((MLP_ROWS, C), f32),
             pltpu.VMEM((plan.dense_rows, C), f32),
             pltpu.VMEM((24, C), f32),
@@ -829,20 +868,21 @@
     return prepared, held + [swap(part, inner, inner_size, 1) for part in held]
 
 
-def reduce_ring(plan, keep, send):
+def reduce_ring(plan, keep, send, beside):
     (outer, outer_size), (inner, inner_size) = plan.sizes
     received = [swap(send, inner, inner_size, 1)]
     keep, *sends = run_merge(plan, outer_size * plan.line, outer_size, keep, received)
     received = [swap(part, outer, outer_size, k + 1) for k, part in enumerate(sends)]
+    received, beside = lax.optimization_barrier((received, beside))
     keep, *sends = run_merge(plan, plan.line, plan.line, keep, received)
-    return keep, [swap(part, inner, inner_size, 2 * (k + 1)) for k, part in enumerate(sends)]
+    return beside, keep, [swap(part, inner, inner_size, 2 * (k + 1)) for k, part in enumerate(sends)]
 
 
 def plain_update(plan, position, grads, extra, mlp, states):
     conv_state, mlp_state, small_state = states
     conv_red = lax.psum_scatter(grads.reshape(4, -1), AXES, scatter_dimension=1, tiled=True)
     extra = lax.psum(extra, AXES)
-    dss = jnp.concatenate([extra[8 : 8 + NCLASS], extra[8 + NCLASS :]], axis=1)
+    dss = jnp.concatenate([extra[8 : 8 + NCLASS], extra[8 + NCLASS : 8 + 2 * NCLASS]], axis=1)
     dense_grad, tail = run_mlp(*mlp, dss)
     dense_red = lax.dynamic_slice_in_dim(dense_grad.reshape(-1), position * plan.dense_len, plan.dense_len)
     flat = jnp.concatenate([extra[:8], tail]).reshape(-1)
@@ -873,13 +913,14 @@
         dense = lax.all_gather(dense, AXES, axis=0, tiled=True).reshape(MLP_ROWS, C)
         inputs = [conv[0], small, conv[1:], dense]
         prepared = run_prepare(x, cot, small)[:3]
-    out, slope, grad, factors, table, m1, m2, hidden, first, second = run_block(
+    rw, kernels, smalls, slope, grad, factors, table, m1, m2, hidden, first, second = run_block(
         plan, class_ids, x, cot, prepared, inputs
     )
+    out = run_down(rw, kernels, smalls)
     dx = run_finish(x, prepared[0], slope, grad, factors)
     mlp = (table, m1, m2, hidden)
     if plan.rings:
-        keep, received = reduce_ring(plan, first, second)
+        (out, dx), keep, received = reduce_ring(plan, first, second, (out, dx))
         results = run_update(plan, keep, received, mlp, states)
     else:
         results = plain_update(plan, lax.axis_index(AXES), first, second, mlp, states)

time: 76 us -> 69.8 us (0.918)
  waiting for transfers between devices: 23 us -> 19.6 us
  Pallas kernels: 27 us -> 24.3 us
    pallas_call x1, Pallas kernels: 20 us -> 16.3 us  [run_block(): pl.pallas_call(functools.partial(block_body, plan), out_shape=shapes, in_...]
    ppermute x18, waiting for transfers between devices: 23 us -> 19.6 us  [swap(): return lax.ppermute(values, axis, [(i, i ^ turn) for i in range(size)])]
    pallas_call x0 -> x1, Pallas kernels: none -> 1.58 us  [run_down(): pl.pallas_call(down_body, out_shape=jax.ShapeDtypeStruct(shape, bf16), in...]
    unnamed x18 -> x16, local copies, waits for them, and re-layouts: 3.17 us -> 3.13 us
  transfers between devices with their start and end apart: 18 -> 18, of which waited for: 10 -> 10; matrix products, arithmetic and copies ran while one was open for 0% -> 0% of each run, Pallas kernels for 3% -> 6%
where the time goes in v5:
time: 69.8 us; the launch traced here: 69.5 us
  Pallas kernels  24.3 us (35%)
  starting transfers between devices  20.9 us (30%)
  waiting for transfers between devices  19.6 us (28%)
  local copies, waits for them, and re-layouts  3.13 us (4%)
  between operations  1.43 us (2%)
    ppermute x18, starting transfers between devices, swap(): return lax.ppermute(values, axis, [(i, i ^ turn) for i in range(size)])  20.9 us
    ppermute x18, waiting for transfers between devices, swap(): return lax.ppermute(values, axis, [(i, i ^ turn) for i in range(size)])  19.6 us
    pallas_call x1, Pallas kernels, run_block(): pl.pallas_call(functools.partial(block_body, plan), out_shape=shapes, in_...  16.3 us
    unnamed x16, local copies, waits for them, and re-layouts  3.13 us
    pallas_call x1, Pallas kernels, run_update(): pl.pallas_call(functools.partial(update_body, plan, len(received)), out_s...  1.88 us
    pallas_call x1, Pallas kernels, run_pack(): pl.pallas_call(functools.partial(pack_body, plan), out_shape=jax.ShapeDty...  1.74 us
    pallas_call x1, Pallas kernels, run_down(): pl.pallas_call(down_body, out_shape=jax.ShapeDtypeStruct(shape, bf16), in...  1.58 us
    pallas_call x1, Pallas kernels, run_finish(): pl.pallas_call(finish_body, out_shape=jax.ShapeDtypeStruct((H, W, C), bf1...  1.51 us
  transfers between devices with their start and end apart: 18, of which 10 were waited for; matrix products, arithmetic and copies ran while one was open for 0% of the time, Pallas kernels for 6%

profile of v5, /device:TPU:0, one launch (start us, length us, event | category | flops | bytes accessed | tf_op | source)
XLA Modules:
  0.0 69.5 jit_solution(11446574547244805109)
XLA Ops:
  0.6 1.7 %pack.1.own_ref = bf16[256,128]{1,0:T(8,128)(2,1)} custom-call(f32[4,4,4608]{2,1,0:T(4,128)} %refs_8_.1, f32[4,12544]{1,0:T(4,128)} %refs_9_.1, f32[4,56]{1,0:T(4,128)} %refs_10_.1), custom_call_target="tpu_custom_call" | custom-call | tf_op jit(solution)/shard_map/pack/pallas_call | solution.py:682
  2.4 5.1 %collective-permute-start.2 = (bf16[256,128]{1,0:T(8,128)(2,1)}, bf16[256,128]{1,0:T(8,128)(2,1)S(1)}, u32[]{:S(2)}, u32[]{:S(2)}) collective-permute-start(bf16[256,128]{1,0:T(8,128)(2,1)} %pack.1.own_ref), channel_id=1, source_target_pairs={{0,6},{1,7},{2,4},{3,5},{4,2},{5,3},{6,0},{7,1},{8,14},{9,15},{10,... | collective-permute-start | bytes 196616 | tf_op jit(solution)/shard_map/ppermute | solution.py:855
  7.5 0.6 collective-permute-start
  8.1 1.2 %copy-done = bf16[1,64,64,128]{3,2,1,0:T(8,128)(2,1)S(1)} copy-done((bf16[1,64,64,128]{3,2,1,0:T(8,128)(2,1)S(1)}, bf16[1,64,64,128]{3,2,1,0:T(8,128)(2,1)}, u32[]{:S(2)}) %copy-start) | copy-done | bytes 1048600
  9.4 1.0 %copy-done.4 = bf16[1,32,32,256]{3,2,1,0:T(8,128)(2,1)S(1)} copy-done((bf16[1,32,32,256]{3,2,1,0:T(8,128)(2,1)S(1)}, bf16[1,32,32,256]{3,2,1,0:T(8,128)(2,1)}, u32[]{:S(2)}) %copy-start.4) | copy-done | bytes 524312
  10.4 0.8 %copy-done.6 = bf16[256,128]{1,0:T(8,128)(2,1)S(1)} copy-done((bf16[256,128]{1,0:T(8,128)(2,1)S(1)}, bf16[256,128]{1,0:T(8,128)(2,1)}, u32[]{:S(2)}) %copy-start.6) | copy-done | bytes 65560
  11.2 1.1 %prepare.1 = (f32[16,128]{1,0:T(8,128)S(1)}, bf16[33,32,512]{2,1,0:T(8,128)(2,1)S(1)}, f32[8,256]{1,0:T(8,128)S(1)}, bf16[256,128]{1,0:T(8,128)(2,1)S(1)}) custom-call(bf16[64,64,128]{2,1,0:T(8,128)(2,1)S(1)} %bitcast.10, bf16[32,32,256]{2,1,0:T(8,128)(2,1)S(1)} %bitcast.13, bf16[256,128]{1,0:T(8,128)(2,1)S(1)} %copy-done.6), custom_call_target="tpu_custom_call" | custom-call | flops 2097152 | bytes 3145728 | tf_op jit(solution)/shard_map/prepare/pallas_call | solution.py:198
  12.4 0.9 %collective-permute-done.1 = bf16[256,128]{1,0:T(8,128)(2,1)S(1)} collective-permute-done((bf16[256,128]{1,0:T(8,128)(2,1)}, bf16[256,128]{1,0:T(8,128)(2,1)S(1)}, u32[]{:S(2)}, u32[]{:S(2)}) %collective-permute-start.1) | collective-permute-done | bytes 65568 | tf_op jit(solution)/shard_map/ppermute | solution.py:855
  13.3 1.6 %collective-permute-start.3 = (bf16[2,256,128]{2,1,0:T(8,128)(2,1)S(1)}, bf16[2,256,128]{2,1,0:T(8,128)(2,1)S(1)}, u32[]{:S(2)}, u32[]{:S(2)}) collective-permute-start(bf16[2,256,128]{2,1,0:T(8,128)(2,1)S(1)} %pad_maximum_fusion.2), channel_id=1, source_target_pairs={{0,8},{8,0},{16,24},{24,16},{1,9},{9,1},{17,25},{25,17},{2,10},{10... | collective-permute-start | bytes 393224 | tf_op jit(solution)/shard_map/ppermute | solution.py:855
  14.9 1.6 %collective-permute-start.4 = (bf16[2,256,128]{2,1,0:T(8,128)(2,1)S(1)}, bf16[2,256,128]{2,1,0:T(8,128)(2,1)S(1)}, u32[]{:S(2)}, u32[]{:S(2)}) collective-permute-start(bf16[2,256,128]{2,1,0:T(8,128)(2,1)S(1)} %pad_maximum_fusion.3), channel_id=1, source_target_pairs={{0,16},{8,24},{16,0},{24,8},{1,17},{9,25},{17,1},{25,9},{2,18},{10... | collective-permute-start | bytes 393224 | tf_op jit(solution)/shard_map/ppermute | solution.py:855
  16.5 2.0 %collective-permute-done.3 = bf16[2,256,128]{2,1,0:T(8,128)(2,1)S(1)} collective-permute-done((bf16[2,256,128]{2,1,0:T(8,128)(2,1)S(1)}, bf16[2,256,128]{2,1,0:T(8,128)(2,1)S(1)}, u32[]{:S(2)}, u32[]{:S(2)}) %collective-permute-start.3) | collective-permute-done | bytes 131104 | tf_op jit(solution)/shard_map/ppermute | solution.py:855
  18.5 1.8 %collective-permute-start.5 = (bf16[4,256,128]{2,1,0:T(8,128)(2,1)S(1)}, bf16[4,256,128]{2,1,0:T(8,128)(2,1)S(1)}, u32[]{:S(2)}, u32[]{:S(2)}) collective-permute-start(bf16[4,256,128]{2,1,0:T(8,128)(2,1)S(1)} %pad_maximum_fusion.refs_6_), channel_id=1, source_target_pairs={{0,16},{8,24},{16,0},{24,8},{1,17},{9,25},{17,1},{25,9},{2,18},{10... | collective-permute-start | bytes 786440 | tf_op jit(solution)/shard_map/ppermute | solution.py:855
  20.3 1.6 %collective-permute-start.6 = (bf16[4,256,128]{2,1,0:T(8,128)(2,1)S(1)}, bf16[4,256,128]{2,1,0:T(8,128)(2,1)S(1)}, u32[]{:S(2)}, u32[]{:S(2)}) collective-permute-start(bf16[4,256,128]{2,1,0:T(8,128)(2,1)S(1)} %pad_maximum_fusion.1.refs_7_), channel_id=1, source_target_pairs={{0,8},{8,0},{16,24},{24,16},{1,9},{9,1},{17,25},{25,17},{2,10},{10... | collective-permute-start | bytes 786440 | tf_op jit(solution)/shard_map/ppermute | solution.py:855
  21.9 0.5 collective-permute-start.8
  22.4 3.3 %collective-permute-done.5.refs_8_ = bf16[4,256,128]{2,1,0:T(8,128)(2,1)S(1)} collective-permute-done((bf16[4,256,128]{2,1,0:T(8,128)(2,1)S(1)}, bf16[4,256,128]{2,1,0:T(8,128)(2,1)S(1)}, u32[]{:S(2)}, u32[]{:S(2)}) %collective-permute-start.5) | collective-permute-done | bytes 262176 | tf_op jit(solution)/shard_map/ppermute | solution.py:855
  25.7 1.6 %collective-permute-done.6.refs_9_ = bf16[4,256,128]{2,1,0:T(8,128)(2,1)S(1)} collective-permute-done((bf16[4,256,128]{2,1,0:T(8,128)(2,1)S(1)}, bf16[4,256,128]{2,1,0:T(8,128)(2,1)S(1)}, u32[]{:S(2)}, u32[]{:S(2)}) %collective-permute-start.6) | collective-permute-done | bytes 262176 | tf_op jit(solution)/shard_map/ppermute | solution.py:855
  28.0 0.8 %collective-permute-done.10.refs_13_ = bf16[4,256,128]{2,1,0:T(8,128)(2,1)S(1)} collective-permute-done((bf16[4,256,128]{2,1,0:T(8,128)(2,1)S(1)}, bf16[4,256,128]{2,1,0:T(8,128)(2,1)S(1)}, u32[]{:S(2)}, u32[]{:S(2)}) %collective-permute-start.10) | collective-permute-done | bytes 262176 | tf_op jit(solution)/shard_map/ppermute | solution.py:855
  28.8 16.3 %block.1 = (bf16[66,32,384]{2,1,0:T(8,128)(2,1)S(1)}, bf16[4,1152,128]{2,1,0:T(8,128)(2,1)S(1)}, f32[16,128]{1,0:T(8,128)S(1)}, f32[64,64,128]{2,1,0:T(8,128)S(1...) custom-call(s32[1]{0:T(128)S(6)} %copy.14.refs_0_, ...), custom_call_target="tpu_custom_call" | custom-call | flops 9437184000 | bytes 16777216 | tf_op jit(solution)/shard_map/block/pallas_call | solution.py:625
  45.3 1.9 %collective-permute-done.11.refs_1_ = bf16[2352,128]{1,0:T(8,128)(2,1)S(1)} collective-permute-done((bf16[2352,128]{1,0:T(8,128)(2,1)S(1)}, bf16[2352,128]{1,0:T(8,128)(2,1)S(1)}, u32[]{:S(2)}, u32[]{:S(2)}) %collective-permute-start.11) | collective-permute-done | bytes 602144 | tf_op jit(solution)/shard_map/ppermute | solution.py:855
  47.3 1.6 %collective-permute-start.12 = (bf16[624,128]{1,0:T(8,128)(2,1)S(1)}, bf16[624,128]{1,0:T(8,128)(2,1)S(1)}, u32[]{:S(2)}, u32[]{:S(2)}) collective-permute-start(bf16[624,128]{1,0:T(8,128)(2,1)S(1)} %get-tuple-element.63), channel_id=1, source_target_pairs={{0,8},{8,0},{16,24},{24,16},{1,9},{9,1},{17,25},{25,17},{2,10},{10... | collective-permute-start | bytes 479240 | tf_op jit(solution)/shard_map/ppermute | solution.py:855
  48.9 0.6 collective-permute-start.13
  49.4 1.4 %collective-permute-start.14 = (bf16[624,128]{1,0:T(8,128)(2,1)S(1)}, bf16[624,128]{1,0:T(8,128)(2,1)S(1)}, u32[]{:S(2)}, u32[]{:S(2)}) collective-permute-start(bf16[624,128]{1,0:T(8,128)(2,1)S(1)} %get-tuple-element.65), channel_id=1, source_target_pairs={{0,24},{8,16},{16,8},{24,0},{1,25},{9,17},{17,9},{25,1},{2,26},{10... | collective-permute-start | bytes 479240 | tf_op jit(solution)/shard_map/ppermute | solution.py:855
  50.8 1.5 %finish.1 = bf16[64,64,128]{2,1,0:T(8,128)(2,1)} custom-call(bf16[64,64,128]{2,1,0:T(8,128)(2,1)S(1)} %bitcast.12, f32[16,128]{1,0:T(8,128)S(1)} %get-tuple-element.54.refs_3_.stats_ref, f32[64,64,128]{2,1,0:T(8,128)S(1)} %get-tuple-element.69.slope_ref, f32[64,64,128]{2,1,0:T(8,128)S(1)} %get-tuple-element.70.grad_ref, ...), custom_call_target="tpu_custom_call" | custom-call | flops 2097152 | bytes 6291456 | tf_op jit(solution)/shard_map/finish/pallas_call | solution.py:523
  52.4 1.6 %down.1 = bf16[32,32,256]{2,1,0:T(8,128)(2,1)} custom-call(bf16[66,32,384]{2,1,0:T(8,128)(2,1)S(1)} %get-tuple-element.66.rw, bf16[4,1152,128]{2,1,0:T(8,128)(2,1)S(1)} %get-tuple-element.67.kernels, f32[16,128]{1,0:T(8,128)S(1)} %get-tuple-element.68.smalls), custom_call_target="tpu_custom_call" | custom-call | flops 633339904 | bytes 3145728 | tf_op jit(solution)/shard_map/down/pallas_call | solution.py:489
  54.0 0.3 collective-permute-done.12.refs_1_
  54.3 3.8 %collective-permute-done.13.refs_2_ = bf16[624,128]{1,0:T(8,128)(2,1)S(1)} collective-permute-done((bf16[624,128]{1,0:T(8,128)(2,1)S(1)}, bf16[624,128]{1,0:T(8,128)(2,1)S(1)}, u32[]{:S(2)}, u32[]{:S(2)}) %collective-permute-start.13) | collective-permute-done | bytes 159776 | tf_op jit(solution)/shard_map/ppermute | solution.py:855
  58.2 1.3 %collective-permute-start.15 = (bf16[192,128]{1,0:T(8,128)(2,1)S(1)}, bf16[192,128]{1,0:T(8,128)(2,1)S(1)}, u32[]{:S(2)}, u32[]{:S(2)}) collective-permute-start(bf16[192,128]{1,0:T(8,128)(2,1)S(1)} %get-tuple-element.79), channel_id=1, source_target_pairs={{0,2},{1,3},{2,0},{3,1},{4,6},{5,7},{6,4},{7,5},{8,10},{9,11},{10,... | collective-permute-start | bytes 147464 | tf_op jit(solution)/shard_map/ppermute | solution.py:855
  59.6 2.2 %collective-permute-start.16 = (bf16[192,128]{1,0:T(8,128)(2,1)S(1)}, bf16[192,128]{1,0:T(8,128)(2,1)S(1)}, u32[]{:S(2)}, u32[]{:S(2)}) collective-permute-start(bf16[192,128]{1,0:T(8,128)(2,1)S(1)} %get-tuple-element.80), channel_id=1, source_target_pairs={{0,4},{1,5},{2,6},{3,7},{4,0},{5,1},{6,2},{7,3},{8,12},{9,13},{10,... | collective-permute-start | bytes 147464 | tf_op jit(solution)/shard_map/ppermute | solution.py:855
  61.7 0.9 %collective-permute-start.17 = (bf16[192,128]{1,0:T(8,128)(2,1)S(1)}, bf16[192,128]{1,0:T(8,128)(2,1)S(1)}, u32[]{:S(2)}, u32[]{:S(2)}) collective-permute-start(bf16[192,128]{1,0:T(8,128)(2,1)S(1)} %get-tuple-element.81), channel_id=1, source_target_pairs={{0,6},{1,7},{2,4},{3,5},{4,2},{5,3},{6,0},{7,1},{8,14},{9,15},{10,... | collective-permute-start | bytes 147464 | tf_op jit(solution)/shard_map/ppermute | solution.py:855
  62.7 2.9 %collective-permute-done.16.refs_2_ = bf16[192,128]{1,0:T(8,128)(2,1)S(1)} collective-permute-done((bf16[192,128]{1,0:T(8,128)(2,1)S(1)}, bf16[192,128]{1,0:T(8,128)(2,1)S(1)}, u32[]{:S(2)}, u32[]{:S(2)}) %collective-permute-start.16) | collective-permute-done | bytes 49184 | tf_op jit(solution)/shard_map/ppermute | solution.py:855
  65.6 2.0 %collective-permute-done.17.refs_3_ = bf16[192,128]{1,0:T(8,128)(2,1)S(1)} collective-permute-done((bf16[192,128]{1,0:T(8,128)(2,1)S(1)}, bf16[192,128]{1,0:T(8,128)(2,1)S(1)}, u32[]{:S(2)}, u32[]{:S(2)}) %collective-permute-start.17) | collective-permute-done | bytes 49184 | tf_op jit(solution)/shard_map/ppermute | solution.py:855
  67.6 1.9 %update.1 = (f32[4,4,4608]{2,1,0:T(4,128)}, f32[4,12544]{1,0:T(4,128)}, f32[4,56]{1,0:T(4,128)}, bf16[4,4608]{1,0:T(4,128)(2,1)}, bf16[98,128]{1,0:T(8,128)(2,1)}, /*index=5*/bf16[1,56]{1,0:T(2,128)(2,1)}) custom-call(f32[192,128]{1,0:T(8,128)S(1)} %get-tuple-element.78.refs_0_, bf16[192,128]{1,0:T(8,128)(2,1)S(1)} %collective-permute-done.15.refs_1_, ...), custom_call_target="tpu_custom_call" | custom-call | tf_op jit(solution)/shard_map/update/pallas_call | solution.py:838
  (32 shorter events, 0.5 us)
Async XLA Ops:
  2.4 10.0 %collective-permute-start.2 = (bf16[256,128]{1,0:T(8,128)(2,1)}, bf16[256,128]{1,0:T(8,128)(2,1)S(1)}, u32[]{:S(2)}, u32[]{:S(2)}) collective-permute-start(bf16[256,128]{1,0:T(8,128)(2,1)} %pack.1.own_ref), channel_id=1, source_target_pairs={{0,6},{1,7},{2,4},{3,5},{4,2},{5,3},{6,0},{7,1},{8,14},{9,15},{10,... | collective-permute-start | bytes 196616 | tf_op jit(solution)/shard_map/ppermute | solution.py:855
  7.5 5.8 %collective-permute-start.1 = (bf16[256,128]{1,0:T(8,128)(2,1)}, bf16[256,128]{1,0:T(8,128)(2,1)S(1)}, u32[]{:S(2)}, u32[]{:S(2)}) collective-permute-start(bf16[256,128]{1,0:T(8,128)(2,1)} %pack.1.own_ref), channel_id=1, source_target_pairs={{0,4},{1,5},{2,6},{3,7},{4,0},{5,1},{6,2},{7,3},{8,12},{9,13},{10,... | collective-permute-start | bytes 196616 | tf_op jit(solution)/shard_map/ppermute | solution.py:855
  7.5 5.8 %collective-permute-start = (bf16[256,128]{1,0:T(8,128)(2,1)}, bf16[256,128]{1,0:T(8,128)(2,1)S(1)}, u32[]{:S(2)}, u32[]{:S(2)}) collective-permute-start(bf16[256,128]{1,0:T(8,128)(2,1)} %pack.1.own_ref), channel_id=1, source_target_pairs={{0,2},{1,3},{2,0},{3,1},{4,6},{5,7},{6,4},{7,5},{8,10},{9,11},{10,... | collective-permute-start | bytes 196616 | tf_op jit(solution)/shard_map/ppermute | solution.py:855
  8.1 1.2 %copy-start = (bf16[1,64,64,128]{3,2,1,0:T(8,128)(2,1)S(1)}, bf16[1,64,64,128]{3,2,1,0:T(8,128)(2,1)}, u32[]{:S(2)}) copy-start(bf16[1,64,64,128]{3,2,1,0:T(8,128)(2,1)} %param.6) | copy-start | bytes 3145732
  9.4 1.0 %copy-start.4 = (bf16[1,32,32,256]{3,2,1,0:T(8,128)(2,1)S(1)}, bf16[1,32,32,256]{3,2,1,0:T(8,128)(2,1)}, u32[]{:S(2)}) copy-start(bf16[1,32,32,256]{3,2,1,0:T(8,128)(2,1)} %param.7) | copy-start | bytes 1572868
  10.4 0.8 %copy-start.6 = (bf16[256,128]{1,0:T(8,128)(2,1)S(1)}, bf16[256,128]{1,0:T(8,128)(2,1)}, u32[]{:S(2)}) copy-start(bf16[256,128]{1,0:T(8,128)(2,1)} %pack.1.own_ref) | copy-start | bytes 196612
  11.2 17.6 %copy-start.1 = (bf16[1,64,64,128]{3,2,1,0:T(8,128)(2,1)S(1)}, bf16[1,64,64,128]{3,2,1,0:T(8,128)(2,1)}, u32[]{:S(2)}) copy-start(bf16[1,64,64,128]{3,2,1,0:T(8,128)(2,1)} %param.6) | copy-start | bytes 3145732
  11.2 17.6 %copy-start.5 = (bf16[1,32,32,256]{3,2,1,0:T(8,128)(2,1)S(1)}, bf16[1,32,32,256]{3,2,1,0:T(8,128)(2,1)}, u32[]{:S(2)}) copy-start(bf16[1,32,32,256]{3,2,1,0:T(8,128)(2,1)} %param.7) | copy-start | bytes 1572868
  13.3 5.1 %collective-permute-start.3 = (bf16[2,256,128]{2,1,0:T(8,128)(2,1)S(1)}, bf16[2,256,128]{2,1,0:T(8,128)(2,1)S(1)}, u32[]{:S(2)}, u32[]{:S(2)}) collective-permute-start(bf16[2,256,128]{2,1,0:T(8,128)(2,1)S(1)} %pad_maximum_fusion.2), channel_id=1, source_target_pairs={{0,8},{8,0},{16,24},{24,16},{1,9},{9,1},{17,25},{25,17},{2,10},{10... | collective-permute-start | bytes 393224 | tf_op jit(solution)/shard_map/ppermute | solution.py:855
  14.9 5.4 %collective-permute-start.4 = (bf16[2,256,128]{2,1,0:T(8,128)(2,1)S(1)}, bf16[2,256,128]{2,1,0:T(8,128)(2,1)S(1)}, u32[]{:S(2)}, u32[]{:S(2)}) collective-permute-start(bf16[2,256,128]{2,1,0:T(8,128)(2,1)S(1)} %pad_maximum_fusion.3), channel_id=1, source_target_pairs={{0,16},{8,24},{16,0},{24,8},{1,17},{9,25},{17,1},{25,9},{2,18},{10... | collective-permute-start | bytes 393224 | tf_op jit(solution)/shard_map/ppermute | solution.py:855
  18.5 7.2 %collective-permute-start.5 = (bf16[4,256,128]{2,1,0:T(8,128)(2,1)S(1)}, bf16[4,256,128]{2,1,0:T(8,128)(2,1)S(1)}, u32[]{:S(2)}, u32[]{:S(2)}) collective-permute-start(bf16[4,256,128]{2,1,0:T(8,128)(2,1)S(1)} %pad_maximum_fusion.refs_6_), channel_id=1, source_target_pairs={{0,16},{8,24},{16,0},{24,8},{1,17},{9,25},{17,1},{25,9},{2,18},{10... | collective-permute-start | bytes 786440 | tf_op jit(solution)/shard_map/ppermute | solution.py:855
  20.3 7.0 %collective-permute-start.6 = (bf16[4,256,128]{2,1,0:T(8,128)(2,1)S(1)}, bf16[4,256,128]{2,1,0:T(8,128)(2,1)S(1)}, u32[]{:S(2)}, u32[]{:S(2)}) collective-permute-start(bf16[4,256,128]{2,1,0:T(8,128)(2,1)S(1)} %pad_maximum_fusion.1.refs_7_), channel_id=1, source_target_pairs={{0,8},{8,0},{16,24},{24,16},{1,9},{9,1},{17,25},{25,17},{2,10},{10... | collective-permute-start | bytes 786440 | tf_op jit(solution)/shard_map/ppermute | solution.py:855
  21.8 6.1 %collective-permute-start.7 = (bf16[4,256,128]{2,1,0:T(8,128)(2,1)S(1)}, bf16[4,256,128]{2,1,0:T(8,128)(2,1)S(1)}, u32[]{:S(2)}, u32[]{:S(2)}) collective-permute-start(bf16[4,256,128]{2,1,0:T(8,128)(2,1)S(1)} %pad_maximum_fusion.refs_6_), channel_id=1, source_target_pairs={{0,1},{1,0},{2,3},{3,2},{4,5},{5,4},{6,7},{7,6},{8,9},{9,8},{10,11... | collective-permute-start | bytes 786440 | tf_op jit(solution)/shard_map/ppermute | solution.py:855
  21.9 6.1 %collective-permute-start.8 = (bf16[4,256,128]{2,1,0:T(8,128)(2,1)S(1)}, bf16[4,256,128]{2,1,0:T(8,128)(2,1)S(1)}, u32[]{:S(2)}, u32[]{:S(2)}) collective-permute-start(bf16[4,256,128]{2,1,0:T(8,128)(2,1)S(1)} %pad_maximum_fusion.1.refs_7_), channel_id=1, source_target_pairs={{0,1},{1,0},{2,3},{3,2},{4,5},{5,4},{6,7},{7,6},{8,9},{9,8},{10,11... | collective-permute-start | bytes 786440 | tf_op jit(solution)/shard_map/ppermute | solution.py:855
  25.7 2.2 %collective-permute-start.9 = (bf16[4,256,128]{2,1,0:T(8,128)(2,1)S(1)}, bf16[4,256,128]{2,1,0:T(8,128)(2,1)S(1)}, u32[]{:S(2)}, u32[]{:S(2)}) collective-permute-start(bf16[4,256,128]{2,1,0:T(8,128)(2,1)S(1)} %collective-permute-done.5.refs_8_), channel_id=1, source_target_pairs={{0,1},{1,0},{2,3},{3,2},{4,5},{5,4},{6,7},{7,6},{8,9},{9,8},{10,11... | collective-permute-start | bytes 786440 | tf_op jit(solution)/shard_map/ppermute | solution.py:855
  27.3 1.5 %collective-permute-start.10 = (bf16[4,256,128]{2,1,0:T(8,128)(2,1)S(1)}, bf16[4,256,128]{2,1,0:T(8,128)(2,1)S(1)}, u32[]{:S(2)}, u32[]{:S(2)}) collective-permute-start(bf16[4,256,128]{2,1,0:T(8,128)(2,1)S(1)} %collective-permute-done.6.refs_9_), channel_id=1, source_target_pairs={{0,1},{1,0},{2,3},{3,2},{4,5},{5,4},{6,7},{7,6},{8,9},{9,8},{10,11... | collective-permute-start | bytes 786440 | tf_op jit(solution)/shard_map/ppermute | solution.py:855
  45.1 2.1 %collective-permute-start.11 = (bf16[2352,128]{1,0:T(8,128)(2,1)S(1)}, bf16[2352,128]{1,0:T(8,128)(2,1)S(1)}, u32[]{:S(2)}, u32[]{:S(2)}) collective-permute-start(bf16[2352,128]{1,0:T(8,128)(2,1)S(1)} %get-tuple-element.62), channel_id=1, source_target_pairs={{0,1},{1,0},{2,3},{3,2},{4,5},{5,4},{6,7},{7,6},{8,9},{9,8},{10,11... | collective-permute-start | bytes 1806344 | tf_op jit(solution)/shard_map/ppermute | solution.py:855
  47.3 7.0 %collective-permute-start.12 = (bf16[624,128]{1,0:T(8,128)(2,1)S(1)}, bf16[624,128]{1,0:T(8,128)(2,1)S(1)}, u32[]{:S(2)}, u32[]{:S(2)}) collective-permute-start(bf16[624,128]{1,0:T(8,128)(2,1)S(1)} %get-tuple-element.63), channel_id=1, source_target_pairs={{0,8},{8,0},{16,24},{24,16},{1,9},{9,1},{17,25},{25,17},{2,10},{10... | collective-permute-start | bytes 479240 | tf_op jit(solution)/shard_map/ppermute | solution.py:855
  48.9 9.3 %collective-permute-start.13 = (bf16[624,128]{1,0:T(8,128)(2,1)S(1)}, bf16[624,128]{1,0:T(8,128)(2,1)S(1)}, u32[]{:S(2)}, u32[]{:S(2)}) collective-permute-start(bf16[624,128]{1,0:T(8,128)(2,1)S(1)} %get-tuple-element.64), channel_id=1, source_target_pairs={{0,16},{8,24},{16,0},{24,8},{1,17},{9,25},{17,1},{25,9},{2,18},{10... | collective-permute-start | bytes 479240 | tf_op jit(solution)/shard_map/ppermute | solution.py:855
  49.4 8.7 %collective-permute-start.14 = (bf16[624,128]{1,0:T(8,128)(2,1)S(1)}, bf16[624,128]{1,0:T(8,128)(2,1)S(1)}, u32[]{:S(2)}, u32[]{:S(2)}) collective-permute-start(bf16[624,128]{1,0:T(8,128)(2,1)S(1)} %get-tuple-element.65), channel_id=1, source_target_pairs={{0,24},{8,16},{16,8},{24,0},{1,25},{9,17},{17,9},{25,1},{2,26},{10... | collective-permute-start | bytes 479240 | tf_op jit(solution)/shard_map/ppermute | solution.py:855
  52.4 15.3 %copy-start.2 = (f32[4,4,4608]{2,1,0:T(4,128)S(1)}, f32[4,4,4608]{2,1,0:T(4,128)}, u32[]{:S(2)}) copy-start(f32[4,4,4608]{2,1,0:T(4,128)} %refs_8_.1) | copy-start | bytes 884740
  52.4 15.3 %copy-start.3 = (f32[4,12544]{1,0:T(4,128)S(1)}, f32[4,12544]{1,0:T(4,128)}, u32[]{:S(2)}) copy-start(f32[4,12544]{1,0:T(4,128)} %refs_9_.1) | copy-start | bytes 602116
  52.4 15.3 %copy-start.7 = (f32[4,56]{1,0:T(4,128)S(1)}, f32[4,56]{1,0:T(4,128)}, u32[]{:S(2)}) copy-start(f32[4,56]{1,0:T(4,128)} %refs_10_.1) | copy-start | bytes 2692
  58.2 4.5 %collective-permute-start.15 = (bf16[192,128]{1,0:T(8,128)(2,1)S(1)}, bf16[192,128]{1,0:T(8,128)(2,1)S(1)}, u32[]{:S(2)}, u32[]{:S(2)}) collective-permute-start(bf16[192,128]{1,0:T(8,128)(2,1)S(1)} %get-tuple-element.79), channel_id=1, source_target_pairs={{0,2},{1,3},{2,0},{3,1},{4,6},{5,7},{6,4},{7,5},{8,10},{9,11},{10,... | collective-permute-start | bytes 147464 | tf_op jit(solution)/shard_map/ppermute | solution.py:855
  59.6 6.0 %collective-permute-start.16 = (bf16[192,128]{1,0:T(8,128)(2,1)S(1)}, bf16[192,128]{1,0:T(8,128)(2,1)S(1)}, u32[]{:S(2)}, u32[]{:S(2)}) collective-permute-start(bf16[192,128]{1,0:T(8,128)(2,1)S(1)} %get-tuple-element.80), channel_id=1, source_target_pairs={{0,4},{1,5},{2,6},{3,7},{4,0},{5,1},{6,2},{7,3},{8,12},{9,13},{10,... | collective-permute-start | bytes 147464 | tf_op jit(solution)/shard_map/ppermute | solution.py:855
  61.7 5.9 %collective-permute-start.17 = (bf16[192,128]{1,0:T(8,128)(2,1)S(1)}, bf16[192,128]{1,0:T(8,128)(2,1)S(1)}, u32[]{:S(2)}, u32[]{:S(2)}) collective-permute-start(bf16[192,128]{1,0:T(8,128)(2,1)S(1)} %get-tuple-element.81), channel_id=1, source_target_pairs={{0,6},{1,7},{2,4},{3,5},{4,2},{5,3},{6,0},{7,1},{8,14},{9,15},{10,... | collective-permute-start | bytes 147464 | tf_op jit(solution)/shard_map/ppermute | solution.py:855

commit v6 on v5

--- a/solution.py
+++ b/solution.py
@@ -872,10 +872,10 @@
     (outer, outer_size), (inner, inner_size) = plan.sizes
     received = [swap(send, inner, inner_size, 1)]
     keep, *sends = run_merge(plan, outer_size * plan.line, outer_size, keep, received)
-    received = [swap(part, outer, outer_size, k + 1) for k, part in enumerate(sends)]
+    received = [swap(sends[k], outer, outer_size, k + 1) for k in range(outer_size - 1)]
     received, beside = lax.optimization_barrier((received, beside))
     keep, *sends = run_merge(plan, plan.line, plan.line, keep, received)
-    return beside, keep, [swap(part, inner, inner_size, 2 * (k + 1)) for k, part in enumerate(sends)]
+    return beside, keep, [swap(sends[k], inner, inner_size, 2 * (k + 1)) for k in reversed(range(plan.line - 1))]
 
 
 def plain_update(plan, position, grads, extra, mlp, states):

time: 69.8 us -> 68.4 us (0.980)
  waiting for transfers between devices: 19.6 us -> 18.2 us
    ppermute x18, waiting for transfers between devices: 19.6 us -> 18.2 us  [swap(): return lax.ppermute(values, axis, [(i, i ^ turn) for i in range(size)])]
where the time goes in v6:
time: 68.4 us; the launch traced here: 68.1 us
  Pallas kernels  24.3 us (36%)
  starting transfers between devices  20.9 us (31%)
  waiting for transfers between devices  18.2 us (27%)
  local copies, waits for them, and re-layouts  3.13 us (5%)
  between operations  1.43 us (2%)
    ppermute x18, starting transfers between devices, swap(): return lax.ppermute(values, axis, [(i, i ^ turn) for i in range(size)])  20.9 us
    ppermute x18, waiting for transfers between devices, swap(): return lax.ppermute(values, axis, [(i, i ^ turn) for i in range(size)])  18.2 us
    pallas_call x1, Pallas kernels, run_block(): pl.pallas_call(functools.partial(block_body, plan), out_shape=shapes, in_...  16.3 us
    unnamed x16, local copies, waits for them, and re-layouts  3.13 us
    pallas_call x1, Pallas kernels, run_update(): pl.pallas_call(functools.partial(update_body, plan, len(received)), out_s...  1.88 us
    pallas_call x1, Pallas kernels, run_pack(): pl.pallas_call(functools.partial(pack_body, plan), out_shape=jax.ShapeDty...  1.74 us
    pallas_call x1, Pallas kernels, run_down(): pl.pallas_call(down_body, out_shape=jax.ShapeDtypeStruct(shape, bf16), in...  1.58 us
    pallas_call x1, Pallas kernels, run_finish(): pl.pallas_call(finish_body, out_shape=jax.ShapeDtypeStruct((H, W, C), bf1...  1.51 us
  transfers between devices with their start and end apart: 18, of which 10 were waited for; matrix products, arithmetic and copies ran while one was open for 0% of the time, Pallas kernels for 6%

profile of v6, /device:TPU:0, one launch (start us, length us, event | category | flops | bytes accessed | tf_op | source)
XLA Modules:
  0.0 68.1 jit_solution(2928725554668865796)
XLA Ops:
  0.6 1.7 %pack.1.own_ref = bf16[256,128]{1,0:T(8,128)(2,1)} custom-call(f32[4,4,4608]{2,1,0:T(4,128)} %refs_8_.1, f32[4,12544]{1,0:T(4,128)} %refs_9_.1, f32[4,56]{1,0:T(4,128)} %refs_10_.1), custom_call_target="tpu_custom_call" | custom-call | tf_op jit(solution)/shard_map/pack/pallas_call | solution.py:682
  2.4 5.1 %collective-permute-start.2 = (bf16[256,128]{1,0:T(8,128)(2,1)}, bf16[256,128]{1,0:T(8,128)(2,1)S(1)}, u32[]{:S(2)}, u32[]{:S(2)}) collective-permute-start(bf16[256,128]{1,0:T(8,128)(2,1)} %pack.1.own_ref), channel_id=1, source_target_pairs={{0,6},{1,7},{2,4},{3,5},{4,2},{5,3},{6,0},{7,1},{8,14},{9,15},{10,... | collective-permute-start | bytes 196616 | tf_op jit(solution)/shard_map/ppermute | solution.py:855
  7.5 0.6 collective-permute-start
  8.1 1.2 %copy-done = bf16[1,64,64,128]{3,2,1,0:T(8,128)(2,1)S(1)} copy-done((bf16[1,64,64,128]{3,2,1,0:T(8,128)(2,1)S(1)}, bf16[1,64,64,128]{3,2,1,0:T(8,128)(2,1)}, u32[]{:S(2)}) %copy-start) | copy-done | bytes 1048600
  9.4 1.0 %copy-done.4 = bf16[1,32,32,256]{3,2,1,0:T(8,128)(2,1)S(1)} copy-done((bf16[1,32,32,256]{3,2,1,0:T(8,128)(2,1)S(1)}, bf16[1,32,32,256]{3,2,1,0:T(8,128)(2,1)}, u32[]{:S(2)}) %copy-start.4) | copy-done | bytes 524312
  10.4 0.8 %copy-done.6 = bf16[256,128]{1,0:T(8,128)(2,1)S(1)} copy-done((bf16[256,128]{1,0:T(8,128)(2,1)S(1)}, bf16[256,128]{1,0:T(8,128)(2,1)}, u32[]{:S(2)}) %copy-start.6) | copy-done | bytes 65560
  11.2 1.1 %prepare.1 = (f32[16,128]{1,0:T(8,128)S(1)}, bf16[33,32,512]{2,1,0:T(8,128)(2,1)S(1)}, f32[8,256]{1,0:T(8,128)S(1)}, bf16[256,128]{1,0:T(8,128)(2,1)S(1)}) custom-call(bf16[64,64,128]{2,1,0:T(8,128)(2,1)S(1)} %bitcast.10, bf16[32,32,256]{2,1,0:T(8,128)(2,1)S(1)} %bitcast.13, bf16[256,128]{1,0:T(8,128)(2,1)S(1)} %copy-done.6), custom_call_target="tpu_custom_call" | custom-call | flops 2097152 | bytes 3145728 | tf_op jit(solution)/shard_map/prepare/pallas_call | solution.py:198
  12.4 0.9 %collective-permute-done.1 = bf16[256,128]{1,0:T(8,128)(2,1)S(1)} collective-permute-done((bf16[256,128]{1,0:T(8,128)(2,1)}, bf16[256,128]{1,0:T(8,128)(2,1)S(1)}, u32[]{:S(2)}, u32[]{:S(2)}) %collective-permute-start.1) | collective-permute-done | bytes 65568 | tf_op jit(solution)/shard_map/ppermute | solution.py:855
  13.3 1.6 %collective-permute-start.3 = (bf16[2,256,128]{2,1,0:T(8,128)(2,1)S(1)}, bf16[2,256,128]{2,1,0:T(8,128)(2,1)S(1)}, u32[]{:S(2)}, u32[]{:S(2)}) collective-permute-start(bf16[2,256,128]{2,1,0:T(8,128)(2,1)S(1)} %pad_maximum_fusion.2), channel_id=1, source_target_pairs={{0,8},{8,0},{16,24},{24,16},{1,9},{9,1},{17,25},{25,17},{2,10},{10... | collective-permute-start | bytes 393224 | tf_op jit(solution)/shard_map/ppermute | solution.py:855
  14.9 1.6 %collective-permute-start.4 = (bf16[2,256,128]{2,1,0:T(8,128)(2,1)S(1)}, bf16[2,256,128]{2,1,0:T(8,128)(2,1)S(1)}, u32[]{:S(2)}, u32[]{:S(2)}) collective-permute-start(bf16[2,256,128]{2,1,0:T(8,128)(2,1)S(1)} %pad_maximum_fusion.3), channel_id=1, source_target_pairs={{0,16},{8,24},{16,0},{24,8},{1,17},{9,25},{17,1},{25,9},{2,18},{10... | collective-permute-start | bytes 393224 | tf_op jit(solution)/shard_map/ppermute | solution.py:855
  16.5 2.0 %collective-permute-done.3 = bf16[2,256,128]{2,1,0:T(8,128)(2,1)S(1)} collective-permute-done((bf16[2,256,128]{2,1,0:T(8,128)(2,1)S(1)}, bf16[2,256,128]{2,1,0:T(8,128)(2,1)S(1)}, u32[]{:S(2)}, u32[]{:S(2)}) %collective-permute-start.3) | collective-permute-done | bytes 131104 | tf_op jit(solution)/shard_map/ppermute | solution.py:855
  18.5 1.8 %collective-permute-start.5 = (bf16[4,256,128]{2,1,0:T(8,128)(2,1)S(1)}, bf16[4,256,128]{2,1,0:T(8,128)(2,1)S(1)}, u32[]{:S(2)}, u32[]{:S(2)}) collective-permute-start(bf16[4,256,128]{2,1,0:T(8,128)(2,1)S(1)} %pad_maximum_fusion.refs_6_), channel_id=1, source_target_pairs={{0,16},{8,24},{16,0},{24,8},{1,17},{9,25},{17,1},{25,9},{2,18},{10... | collective-permute-start | bytes 786440 | tf_op jit(solution)/shard_map/ppermute | solution.py:855
  20.3 1.6 %collective-permute-start.6 = (bf16[4,256,128]{2,1,0:T(8,128)(2,1)S(1)}, bf16[4,256,128]{2,1,0:T(8,128)(2,1)S(1)}, u32[]{:S(2)}, u32[]{:S(2)}) collective-permute-start(bf16[4,256,128]{2,1,0:T(8,128)(2,1)S(1)} %pad_maximum_fusion.1.refs_7_), channel_id=1, source_target_pairs={{0,8},{8,0},{16,24},{24,16},{1,9},{9,1},{17,25},{25,17},{2,10},{10... | collective-permute-start | bytes 786440 | tf_op jit(solution)/shard_map/ppermute | solution.py:855
  21.9 0.5 collective-permute-start.8
  22.4 3.3 %collective-permute-done.5.refs_8_ = bf16[4,256,128]{2,1,0:T(8,128)(2,1)S(1)} collective-permute-done((bf16[4,256,128]{2,1,0:T(8,128)(2,1)S(1)}, bf16[4,256,128]{2,1,0:T(8,128)(2,1)S(1)}, u32[]{:S(2)}, u32[]{:S(2)}) %collective-permute-start.5) | collective-permute-done | bytes 262176 | tf_op jit(solution)/shard_map/ppermute | solution.py:855
  25.7 1.6 %collective-permute-done.6.refs_9_ = bf16[4,256,128]{2,1,0:T(8,128)(2,1)S(1)} collective-permute-done((bf16[4,256,128]{2,1,0:T(8,128)(2,1)S(1)}, bf16[4,256,128]{2,1,0:T(8,128)(2,1)S(1)}, u32[]{:S(2)}, u32[]{:S(2)}) %collective-permute-start.6) | collective-permute-done | bytes 262176 | tf_op jit(solution)/shard_map/ppermute | solution.py:855
  28.0 0.8 %collective-permute-done.10.refs_13_ = bf16[4,256,128]{2,1,0:T(8,128)(2,1)S(1)} collective-permute-done((bf16[4,256,128]{2,1,0:T(8,128)(2,1)S(1)}, bf16[4,256,128]{2,1,0:T(8,128)(2,1)S(1)}, u32[]{:S(2)}, u32[]{:S(2)}) %collective-permute-start.10) | collective-permute-done | bytes 262176 | tf_op jit(solution)/shard_map/ppermute | solution.py:855
  28.8 16.3 %block.1 = (bf16[66,32,384]{2,1,0:T(8,128)(2,1)S(1)}, bf16[4,1152,128]{2,1,0:T(8,128)(2,1)S(1)}, f32[16,128]{1,0:T(8,128)S(1)}, f32[64,64,128]{2,1,0:T(8,128)S(1...) custom-call(s32[1]{0:T(128)S(6)} %copy.14.refs_0_, ...), custom_call_target="tpu_custom_call" | custom-call | flops 9437184000 | bytes 16777216 | tf_op jit(solution)/shard_map/block/pallas_call | solution.py:625
  45.1 0.2 collective-permute-start.11
  45.3 1.9 %collective-permute-done.11.refs_1_ = bf16[2352,128]{1,0:T(8,128)(2,1)S(1)} collective-permute-done((bf16[2352,128]{1,0:T(8,128)(2,1)S(1)}, bf16[2352,128]{1,0:T(8,128)(2,1)S(1)}, u32[]{:S(2)}, u32[]{:S(2)}) %collective-permute-start.11) | collective-permute-done | bytes 602144 | tf_op jit(solution)/shard_map/ppermute | solution.py:855
  47.3 1.6 %collective-permute-start.12 = (bf16[624,128]{1,0:T(8,128)(2,1)S(1)}, bf16[624,128]{1,0:T(8,128)(2,1)S(1)}, u32[]{:S(2)}, u32[]{:S(2)}) collective-permute-start(bf16[624,128]{1,0:T(8,128)(2,1)S(1)} %get-tuple-element.63), channel_id=1, source_target_pairs={{0,8},{8,0},{16,24},{24,16},{1,9},{9,1},{17,25},{25,17},{2,10},{10... | collective-permute-start | bytes 479240 | tf_op jit(solution)/shard_map/ppermute | solution.py:855
  48.9 0.6 collective-permute-start.13
  49.4 1.4 %collective-permute-start.14 = (bf16[624,128]{1,0:T(8,128)(2,1)S(1)}, bf16[624,128]{1,0:T(8,128)(2,1)S(1)}, u32[]{:S(2)}, u32[]{:S(2)}) collective-permute-start(bf16[624,128]{1,0:T(8,128)(2,1)S(1)} %get-tuple-element.65), channel_id=1, source_target_pairs={{0,24},{8,16},{16,8},{24,0},{1,25},{9,17},{17,9},{25,1},{2,26},{10... | collective-permute-start | bytes 479240 | tf_op jit(solution)/shard_map/ppermute | solution.py:855
  50.8 1.5 %finish.1 = bf16[64,64,128]{2,1,0:T(8,128)(2,1)} custom-call(bf16[64,64,128]{2,1,0:T(8,128)(2,1)S(1)} %bitcast.12, f32[16,128]{1,0:T(8,128)S(1)} %get-tuple-element.54.refs_3_.stats_ref, f32[64,64,128]{2,1,0:T(8,128)S(1)} %get-tuple-element.69.slope_ref, f32[64,64,128]{2,1,0:T(8,128)S(1)} %get-tuple-element.70.grad_ref, ...), custom_call_target="tpu_custom_call" | custom-call | flops 2097152 | bytes 6291456 | tf_op jit(solution)/shard_map/finish/pallas_call | solution.py:523
  52.4 1.6 %down.1 = bf16[32,32,256]{2,1,0:T(8,128)(2,1)} custom-call(bf16[66,32,384]{2,1,0:T(8,128)(2,1)S(1)} %get-tuple-element.66.rw, bf16[4,1152,128]{2,1,0:T(8,128)(2,1)S(1)} %get-tuple-element.67.kernels, f32[16,128]{1,0:T(8,128)S(1)} %get-tuple-element.68.smalls), custom_call_target="tpu_custom_call" | custom-call | flops 633339904 | bytes 3145728 | tf_op jit(solution)/shard_map/down/pallas_call | solution.py:489
  54.0 0.3 collective-permute-done.12.refs_1_
  54.3 3.8 %collective-permute-done.13.refs_2_ = bf16[624,128]{1,0:T(8,128)(2,1)S(1)} collective-permute-done((bf16[624,128]{1,0:T(8,128)(2,1)S(1)}, bf16[624,128]{1,0:T(8,128)(2,1)S(1)}, u32[]{:S(2)}, u32[]{:S(2)}) %collective-permute-start.13) | collective-permute-done | bytes 159776 | tf_op jit(solution)/shard_map/ppermute | solution.py:855
  58.2 2.9 %collective-permute-start.15 = (bf16[192,128]{1,0:T(8,128)(2,1)S(1)}, bf16[192,128]{1,0:T(8,128)(2,1)S(1)}, u32[]{:S(2)}, u32[]{:S(2)}) collective-permute-start(bf16[192,128]{1,0:T(8,128)(2,1)S(1)} %get-tuple-element.79), channel_id=1, source_target_pairs={{0,6},{1,7},{2,4},{3,5},{4,2},{5,3},{6,0},{7,1},{8,14},{9,15},{10,... | collective-permute-start | bytes 147464 | tf_op jit(solution)/shard_map/ppermute | solution.py:855
  61.2 1.5 %collective-permute-start.17 = (bf16[192,128]{1,0:T(8,128)(2,1)S(1)}, bf16[192,128]{1,0:T(8,128)(2,1)S(1)}, u32[]{:S(2)}, u32[]{:S(2)}) collective-permute-start(bf16[192,128]{1,0:T(8,128)(2,1)S(1)} %get-tuple-element.81), channel_id=1, source_target_pairs={{0,2},{1,3},{2,0},{3,1},{4,6},{5,7},{6,4},{7,5},{8,10},{9,11},{10,... | collective-permute-start | bytes 147464 | tf_op jit(solution)/shard_map/ppermute | solution.py:855
  62.7 1.5 %collective-permute-done.15.refs_1_ = bf16[192,128]{1,0:T(8,128)(2,1)S(1)} collective-permute-done((bf16[192,128]{1,0:T(8,128)(2,1)S(1)}, bf16[192,128]{1,0:T(8,128)(2,1)S(1)}, u32[]{:S(2)}, u32[]{:S(2)}) %collective-permute-start.15) | collective-permute-done | bytes 49184 | tf_op jit(solution)/shard_map/ppermute | solution.py:855
  64.2 2.0 %collective-permute-done.16.refs_2_ = bf16[192,128]{1,0:T(8,128)(2,1)S(1)} collective-permute-done((bf16[192,128]{1,0:T(8,128)(2,1)S(1)}, bf16[192,128]{1,0:T(8,128)(2,1)S(1)}, u32[]{:S(2)}, u32[]{:S(2)}) %collective-permute-start.16) | collective-permute-done | bytes 49184 | tf_op jit(solution)/shard_map/ppermute | solution.py:855
  66.3 1.9 %update.1 = (f32[4,4,4608]{2,1,0:T(4,128)}, f32[4,12544]{1,0:T(4,128)}, f32[4,56]{1,0:T(4,128)}, bf16[4,4608]{1,0:T(4,128)(2,1)}, bf16[98,128]{1,0:T(8,128)(2,1)}, /*index=5*/bf16[1,56]{1,0:T(2,128)(2,1)}) custom-call(f32[192,128]{1,0:T(8,128)S(1)} %get-tuple-element.78.refs_0_, bf16[192,128]{1,0:T(8,128)(2,1)S(1)} %collective-permute-done.15.refs_1_, ...), custom_call_target="tpu_custom_call" | custom-call | tf_op jit(solution)/shard_map/update/pallas_call | solution.py:838
  (32 shorter events, 0.4 us)
Async XLA Ops:
  2.4 10.0 %collective-permute-start.2 = (bf16[256,128]{1,0:T(8,128)(2,1)}, bf16[256,128]{1,0:T(8,128)(2,1)S(1)}, u32[]{:S(2)}, u32[]{:S(2)}) collective-permute-start(bf16[256,128]{1,0:T(8,128)(2,1)} %pack.1.own_ref), channel_id=1, source_target_pairs={{0,6},{1,7},{2,4},{3,5},{4,2},{5,3},{6,0},{7,1},{8,14},{9,15},{10,... | collective-permute-start | bytes 196616 | tf_op jit(solution)/shard_map/ppermute | solution.py:855
  7.5 5.8 %collective-permute-start.1 = (bf16[256,128]{1,0:T(8,128)(2,1)}, bf16[256,128]{1,0:T(8,128)(2,1)S(1)}, u32[]{:S(2)}, u32[]{:S(2)}) collective-permute-start(bf16[256,128]{1,0:T(8,128)(2,1)} %pack.1.own_ref), channel_id=1, source_target_pairs={{0,4},{1,5},{2,6},{3,7},{4,0},{5,1},{6,2},{7,3},{8,12},{9,13},{10,... | collective-permute-start | bytes 196616 | tf_op jit(solution)/shard_map/ppermute | solution.py:855
  7.5 5.8 %collective-permute-start = (bf16[256,128]{1,0:T(8,128)(2,1)}, bf16[256,128]{1,0:T(8,128)(2,1)S(1)}, u32[]{:S(2)}, u32[]{:S(2)}) collective-permute-start(bf16[256,128]{1,0:T(8,128)(2,1)} %pack.1.own_ref), channel_id=1, source_target_pairs={{0,2},{1,3},{2,0},{3,1},{4,6},{5,7},{6,4},{7,5},{8,10},{9,11},{10,... | collective-permute-start | bytes 196616 | tf_op jit(solution)/shard_map/ppermute | solution.py:855
  8.1 1.2 %copy-start = (bf16[1,64,64,128]{3,2,1,0:T(8,128)(2,1)S(1)}, bf16[1,64,64,128]{3,2,1,0:T(8,128)(2,1)}, u32[]{:S(2)}) copy-start(bf16[1,64,64,128]{3,2,1,0:T(8,128)(2,1)} %param.6) | copy-start | bytes 3145732
  9.4 1.0 %copy-start.4 = (bf16[1,32,32,256]{3,2,1,0:T(8,128)(2,1)S(1)}, bf16[1,32,32,256]{3,2,1,0:T(8,128)(2,1)}, u32[]{:S(2)}) copy-start(bf16[1,32,32,256]{3,2,1,0:T(8,128)(2,1)} %param.7) | copy-start | bytes 1572868
  10.4 0.8 %copy-start.6 = (bf16[256,128]{1,0:T(8,128)(2,1)S(1)}, bf16[256,128]{1,0:T(8,128)(2,1)}, u32[]{:S(2)}) copy-start(bf16[256,128]{1,0:T(8,128)(2,1)} %pack.1.own_ref) | copy-start | bytes 196612
  11.2 17.6 %copy-start.1 = (bf16[1,64,64,128]{3,2,1,0:T(8,128)(2,1)S(1)}, bf16[1,64,64,128]{3,2,1,0:T(8,128)(2,1)}, u32[]{:S(2)}) copy-start(bf16[1,64,64,128]{3,2,1,0:T(8,128)(2,1)} %param.6) | copy-start | bytes 3145732
  11.2 17.6 %copy-start.5 = (bf16[1,32,32,256]{3,2,1,0:T(8,128)(2,1)S(1)}, bf16[1,32,32,256]{3,2,1,0:T(8,128)(2,1)}, u32[]{:S(2)}) copy-start(bf16[1,32,32,256]{3,2,1,0:T(8,128)(2,1)} %param.7) | copy-start | bytes 1572868
  13.3 5.1 %collective-permute-start.3 = (bf16[2,256,128]{2,1,0:T(8,128)(2,1)S(1)}, bf16[2,256,128]{2,1,0:T(8,128)(2,1)S(1)}, u32[]{:S(2)}, u32[]{:S(2)}) collective-permute-start(bf16[2,256,128]{2,1,0:T(8,128)(2,1)S(1)} %pad_maximum_fusion.2), channel_id=1, source_target_pairs={{0,8},{8,0},{16,24},{24,16},{1,9},{9,1},{17,25},{25,17},{2,10},{10... | collective-permute-start | bytes 393224 | tf_op jit(solution)/shard_map/ppermute | solution.py:855
  14.9 5.4 %collective-permute-start.4 = (bf16[2,256,128]{2,1,0:T(8,128)(2,1)S(1)}, bf16[2,256,128]{2,1,0:T(8,128)(2,1)S(1)}, u32[]{:S(2)}, u32[]{:S(2)}) collective-permute-start(bf16[2,256,128]{2,1,0:T(8,128)(2,1)S(1)} %pad_maximum_fusion.3), channel_id=1, source_target_pairs={{0,16},{8,24},{16,0},{24,8},{1,17},{9,25},{17,1},{25,9},{2,18},{10... | collective-permute-start | bytes 393224 | tf_op jit(solution)/shard_map/ppermute | solution.py:855
  18.5 7.2 %collective-permute-start.5 = (bf16[4,256,128]{2,1,0:T(8,128)(2,1)S(1)}, bf16[4,256,128]{2,1,0:T(8,128)(2,1)S(1)}, u32[]{:S(2)}, u32[]{:S(2)}) collective-permute-start(bf16[4,256,128]{2,1,0:T(8,128)(2,1)S(1)} %pad_maximum_fusion.refs_6_), channel_id=1, source_target_pairs={{0,16},{8,24},{16,0},{24,8},{1,17},{9,25},{17,1},{25,9},{2,18},{10... | collective-permute-start | bytes 786440 | tf_op jit(solution)/shard_map/ppermute | solution.py:855
  20.3 7.0 %collective-permute-start.6 = (bf16[4,256,128]{2,1,0:T(8,128)(2,1)S(1)}, bf16[4,256,128]{2,1,0:T(8,128)(2,1)S(1)}, u32[]{:S(2)}, u32[]{:S(2)}) collective-permute-start(bf16[4,256,128]{2,1,0:T(8,128)(2,1)S(1)} %pad_maximum_fusion.1.refs_7_), channel_id=1, source_target_pairs={{0,8},{8,0},{16,24},{24,16},{1,9},{9,1},{17,25},{25,17},{2,10},{10... | collective-permute-start | bytes 786440 | tf_op jit(solution)/shard_map/ppermute | solution.py:855
  21.8 6.1 %collective-permute-start.7 = (bf16[4,256,128]{2,1,0:T(8,128)(2,1)S(1)}, bf16[4,256,128]{2,1,0:T(8,128)(2,1)S(1)}, u32[]{:S(2)}, u32[]{:S(2)}) collective-permute-start(bf16[4,256,128]{2,1,0:T(8,128)(2,1)S(1)} %pad_maximum_fusion.refs_6_), channel_id=1, source_target_pairs={{0,1},{1,0},{2,3},{3,2},{4,5},{5,4},{6,7},{7,6},{8,9},{9,8},{10,11... | collective-permute-start | bytes 786440 | tf_op jit(solution)/shard_map/ppermute | solution.py:855
  21.9 6.1 %collective-permute-start.8 = (bf16[4,256,128]{2,1,0:T(8,128)(2,1)S(1)}, bf16[4,256,128]{2,1,0:T(8,128)(2,1)S(1)}, u32[]{:S(2)}, u32[]{:S(2)}) collective-permute-start(bf16[4,256,128]{2,1,0:T(8,128)(2,1)S(1)} %pad_maximum_fusion.1.refs_7_), channel_id=1, source_target_pairs={{0,1},{1,0},{2,3},{3,2},{4,5},{5,4},{6,7},{7,6},{8,9},{9,8},{10,11... | collective-permute-start | bytes 786440 | tf_op jit(solution)/shard_map/ppermute | solution.py:855
  25.7 2.2 %collective-permute-start.9 = (bf16[4,256,128]{2,1,0:T(8,128)(2,1)S(1)}, bf16[4,256,128]{2,1,0:T(8,128)(2,1)S(1)}, u32[]{:S(2)}, u32[]{:S(2)}) collective-permute-start(bf16[4,256,128]{2,1,0:T(8,128)(2,1)S(1)} %collective-permute-done.5.refs_8_), channel_id=1, source_target_pairs={{0,1},{1,0},{2,3},{3,2},{4,5},{5,4},{6,7},{7,6},{8,9},{9,8},{10,11... | collective-permute-start | bytes 786440 | tf_op jit(solution)/shard_map/ppermute | solution.py:855
  27.3 1.5 %collective-permute-start.10 = (bf16[4,256,128]{2,1,0:T(8,128)(2,1)S(1)}, bf16[4,256,128]{2,1,0:T(8,128)(2,1)S(1)}, u32[]{:S(2)}, u32[]{:S(2)}) collective-permute-start(bf16[4,256,128]{2,1,0:T(8,128)(2,1)S(1)} %collective-permute-done.6.refs_9_), channel_id=1, source_target_pairs={{0,1},{1,0},{2,3},{3,2},{4,5},{5,4},{6,7},{7,6},{8,9},{9,8},{10,11... | collective-permute-start | bytes 786440 | tf_op jit(solution)/shard_map/ppermute | solution.py:855
  45.1 2.1 %collective-permute-start.11 = (bf16[2352,128]{1,0:T(8,128)(2,1)S(1)}, bf16[2352,128]{1,0:T(8,128)(2,1)S(1)}, u32[]{:S(2)}, u32[]{:S(2)}) collective-permute-start(bf16[2352,128]{1,0:T(8,128)(2,1)S(1)} %get-tuple-element.62), channel_id=1, source_target_pairs={{0,1},{1,0},{2,3},{3,2},{4,5},{5,4},{6,7},{7,6},{8,9},{9,8},{10,11... | collective-permute-start | bytes 1806344 | tf_op jit(solution)/shard_map/ppermute | solution.py:855
  47.3 7.0 %collective-permute-start.12 = (bf16[624,128]{1,0:T(8,128)(2,1)S(1)}, bf16[624,128]{1,0:T(8,128)(2,1)S(1)}, u32[]{:S(2)}, u32[]{:S(2)}) collective-permute-start(bf16[624,128]{1,0:T(8,128)(2,1)S(1)} %get-tuple-element.63), channel_id=1, source_target_pairs={{0,8},{8,0},{16,24},{24,16},{1,9},{9,1},{17,25},{25,17},{2,10},{10... | collective-permute-start | bytes 479240 | tf_op jit(solution)/shard_map/ppermute | solution.py:855
  48.9 9.3 %collective-permute-start.13 = (bf16[624,128]{1,0:T(8,128)(2,1)S(1)}, bf16[624,128]{1,0:T(8,128)(2,1)S(1)}, u32[]{:S(2)}, u32[]{:S(2)}) collective-permute-start(bf16[624,128]{1,0:T(8,128)(2,1)S(1)} %get-tuple-element.64), channel_id=1, source_target_pairs={{0,16},{8,24},{16,0},{24,8},{1,17},{9,25},{17,1},{25,9},{2,18},{10... | collective-permute-start | bytes 479240 | tf_op jit(solution)/shard_map/ppermute | solution.py:855
  49.4 8.7 %collective-permute-start.14 = (bf16[624,128]{1,0:T(8,128)(2,1)S(1)}, bf16[624,128]{1,0:T(8,128)(2,1)S(1)}, u32[]{:S(2)}, u32[]{:S(2)}) collective-permute-start(bf16[624,128]{1,0:T(8,128)(2,1)S(1)} %get-tuple-element.65), channel_id=1, source_target_pairs={{0,24},{8,16},{16,8},{24,0},{1,25},{9,17},{17,9},{25,1},{2,26},{10... | collective-permute-start | bytes 479240 | tf_op jit(solution)/shard_map/ppermute | solution.py:855
  52.4 13.9 %copy-start.2 = (f32[4,4,4608]{2,1,0:T(4,128)S(1)}, f32[4,4,4608]{2,1,0:T(4,128)}, u32[]{:S(2)}) copy-start(f32[4,4,4608]{2,1,0:T(4,128)} %refs_8_.1) | copy-start | bytes 884740
  52.4 13.9 %copy-start.3 = (f32[4,12544]{1,0:T(4,128)S(1)}, f32[4,12544]{1,0:T(4,128)}, u32[]{:S(2)}) copy-start(f32[4,12544]{1,0:T(4,128)} %refs_9_.1) | copy-start | bytes 602116
  52.4 13.9 %copy-start.7 = (f32[4,56]{1,0:T(4,128)S(1)}, f32[4,56]{1,0:T(4,128)}, u32[]{:S(2)}) copy-start(f32[4,56]{1,0:T(4,128)} %refs_10_.1) | copy-start | bytes 2692
  58.2 6.0 %collective-permute-start.15 = (bf16[192,128]{1,0:T(8,128)(2,1)S(1)}, bf16[192,128]{1,0:T(8,128)(2,1)S(1)}, u32[]{:S(2)}, u32[]{:S(2)}) collective-permute-start(bf16[192,128]{1,0:T(8,128)(2,1)S(1)} %get-tuple-element.79), channel_id=1, source_target_pairs={{0,6},{1,7},{2,4},{3,5},{4,2},{5,3},{6,0},{7,1},{8,14},{9,15},{10,... | collective-permute-start | bytes 147464 | tf_op jit(solution)/shard_map/ppermute | solution.py:855
  61.2 5.0 %collective-permute-start.16 = (bf16[192,128]{1,0:T(8,128)(2,1)S(1)}, bf16[192,128]{1,0:T(8,128)(2,1)S(1)}, u32[]{:S(2)}, u32[]{:S(2)}) collective-permute-start(bf16[192,128]{1,0:T(8,128)(2,1)S(1)} %get-tuple-element.80), channel_id=1, source_target_pairs={{0,4},{1,5},{2,6},{3,7},{4,0},{5,1},{6,2},{7,3},{8,12},{9,13},{10,... | collective-permute-start | bytes 147464 | tf_op jit(solution)/shard_map/ppermute | solution.py:855
  61.2 5.0 %collective-permute-start.17 = (bf16[192,128]{1,0:T(8,128)(2,1)S(1)}, bf16[192,128]{1,0:T(8,128)(2,1)S(1)}, u32[]{:S(2)}, u32[]{:S(2)}) collective-permute-start(bf16[192,128]{1,0:T(8,128)(2,1)S(1)} %get-tuple-element.81), channel_id=1, source_target_pairs={{0,2},{1,3},{2,0},{3,1},{4,6},{5,7},{6,4},{7,5},{8,10},{9,11},{10,... | collective-permute-start | bytes 147464 | tf_op jit(solution)/shard_map/ppermute | solution.py:855

commit v7 on v6

--- a/solution.py
+++ b/solution.py
@@ -163,8 +163,7 @@
     return lax.axis_index(outer) * inner_size + lax.axis_index(inner)
 
 
-def prepare_body(x_ref, cot_ref, own_ref, stats_ref, cw, gdb_ref, near_ref):
-    near_ref[...] = own_ref[...]
+def prepare_body(x_ref, cot_ref, stats_ref, cw, gdb_ref):
     zero8 = jnp.zeros((8, C), f32)
 
     def read_x(i):
@@ -193,17 +192,33 @@
     gdb_ref[...] = total_of(each(H // 2 // R, cot_windows, jnp.zeros((8, 2 * C), f32)))
 
 
-def run_prepare(x, cot, own):
+def copy_body(own_ref, near_ref):
+    near_ref[...] = own_ref[...]
+
+
+def run_copy(own):
+    return pl.pallas_call(
+        copy_body,
+        out_shape=jax.ShapeDtypeStruct(own.shape, own.dtype),
+        in_specs=vmem_specs(1),
+        out_specs=pl.BlockSpec(memory_space=pltpu.VMEM),
+        compiler_params=limit(4),
+        cost_estimate=cost(0, 1 << 17),
+        name="copy_own",
+    )(own)
+
+
+def run_prepare(x, cot):
     struct = jax.ShapeDtypeStruct
     return pl.pallas_call(
         prepare_body,
-        out_shape=[struct((16, C), f32), struct((H // 2 + 1, W // 2, 4 * C), bf16), struct((8, 2 * C), f32), struct(own.shape, bf16)],
-        in_specs=vmem_specs(3),
-        out_specs=vmem_specs(4),
+        out_shape=[struct((16, C), f32), struct((H // 2 + 1, W // 2, 4 * C), bf16), struct((8, 2 * C), f32)],
+        in_specs=vmem_specs(2),
+        out_specs=vmem_specs(3),
         compiler_params=limit(8),
         cost_estimate=cost(2, 3 << 20),
         name="prepare",
-    )(x, cot, own)
+    )(x, cot)
 
 
 def block_body(plan, *refs):
@@ -212,8 +227,9 @@
     cls_ref, x_ref, cot_ref, stats_ref, cw, gdb_ref = refs[:6]
     inputs = refs[6 : 6 + count]
     rw, kernels, smalls, slope1_ref, drf, factors_ref, table_ref, m1_ref, m2_ref, hidden_ref = refs[6 + count : 16 + count]
-    results = refs[16 + count : 18 + count]
-    a1w, a2w, t1w, t2w, c1, g1p, g2p, rf, pairs, conv, dense = refs[18 + count :]
+    made = 24 + count if plan.rings else 18 + count
+    results = refs[16 + count : made]
+    a1w, a2w, t1w, t2w, c1, g1p, g2p, rf, pairs, conv, dense = refs[made:]
     kernels_f = conv
     me = position_of(plan.sizes)
     k1_ref, k2_ref, kd0_ref, kd1_ref = [kernels.at[k] for k in range(4)]
@@ -453,11 +469,11 @@
     rows = rows + [jnp.where(mine[:, :C], row[0:1], 0.0) for row in (gsc, gsh)]
     extra = jnp.concatenate(rows + [jnp.zeros((EXTRA - len(rows) - 2 * NCLASS + 2, C), f32)], axis=0)
     if plan.rings:
-        put_results(plan, me, 0, conv, *results)
+        put_results(plan, me, 0, conv, results)
         kernel_grad(a1w, t1w, conv.at[0])
-        put_results(plan, me, 1, conv, *results)
+        put_results(plan, me, 1, conv, results)
         for ref in results:
-            ref[plan.half * 2 * plan.pair_rows :] = extra.astype(ref.dtype)
+            ref[plan.line * 2 * plan.pair_rows :] = extra.astype(ref.dtype)
     else:
         kernel_grad(a1w, t1w, conv.at[0])
         results[0][...] = conv[...]
@@ -536,21 +552,23 @@
     return (lax.broadcasted_iota(jnp.int32, (8, C), 0) < 4) == (odd == 0)
 
 
-def put_results(plan, me, index, conv, keep_ref, send_ref):
+def put_results(plan, me, index, conv, results):
     left, right = PAIRS[index]
-    for core, result in enumerate((keep_ref, send_ref)):
+    for core in (0, 1):
         odd = (me ^ core) & 1
-        parts = []
-        for owner in plan.targets(me ^ core):
-            full, half = plan.places(odd, plan.tile_of(owner * plan.conv_rows))
-            parts += [conv[k, pl.ds(full, plan.full), :] for k in (left, right)]
-            halves = [conv[k, pl.ds(half, 8), :] for k in (left, right)]
-            parts.append(jnp.where(own_half(odd), halves[0], pltpu.roll(halves[1], 4, 0)))
-        rows = 2 * plan.pair_rows
-        for place in range(0, plan.half, 2):
-            two = jnp.concatenate(parts[3 * place : 3 * place + 6], axis=0)
-            at = (index * plan.half + place) * plan.pair_rows
-            result[at : at + rows] = two.astype(result.dtype)
+        owners = plan.targets(me ^ core)
+        for group, result in enumerate(results[4 * core : 4 * core + 4]):
+            parts = []
+            for owner in owners[group * plan.line : (group + 1) * plan.line]:
+                full, half = plan.places(odd, plan.tile_of(owner * plan.conv_rows))
+                parts += [conv[k, pl.ds(full, plan.full), :] for k in (left, right)]
+                halves = [conv[k, pl.ds(half, 8), :] for k in (left, right)]
+                parts.append(jnp.where(own_half(odd), halves[0], pltpu.roll(halves[1], 4, 0)))
+            rows = 2 * plan.pair_rows
+            for place in range(0, plan.line, 2):
+                two = jnp.concatenate(parts[3 * place : 3 * place + 6], axis=0)
+                at = (index * plan.line + place) * plan.pair_rows
+                result[at : at + rows] = two.astype(result.dtype)
 
 
 def vmem_specs(count):
@@ -585,7 +603,7 @@
         self.half = count // 2
 
     def sources(self, me):
-        near = [2 * k for k in range(self.line)]
+        near = [0] + [2 * k for k in reversed(range(1, self.line))]
         low, high = near[: self.line // 2], near[self.line // 2 :]
         held = [low + [k ^ self.inner for k in low], high + [k ^ 2 * self.inner for k in high]]
         held += [[k ^ 2 * self.inner for k in held[0]], [k ^ self.inner for k in held[1]]]
@@ -616,8 +634,8 @@
         struct((NCLASS, EMB), f32),
     ]
     if plan.rings:
-        rows = plan.half * 2 * plan.pair_rows
-        shapes += [struct((rows + EXTRA, C), f32), struct((rows + EXTRA, C), bf16)]
+        rows = plan.line * 2 * plan.pair_rows + EXTRA
+        shapes += [struct((rows, C), f32)] * 4 + [struct((rows, C), bf16)] * 4
     else:
         shapes += [struct((4, KERNEL_ROWS, C), f32), struct((EXTRA, C), f32)]
     windows = pltpu.VMEM((H + 2, W, 3 * C), bf16)
@@ -626,7 +644,7 @@
         functools.partial(block_body, plan),
         out_shape=shapes,
         in_specs=[pl.BlockSpec(memory_space=pltpu.SMEM)] + vmem_specs(5 + len(inputs)),
-        out_specs=vmem_specs(12),
+        out_specs=vmem_specs(len(shapes)),
         scratch_shapes=[
             windows,
             windows,
@@ -857,25 +875,29 @@
 
 def gather_ring(plan, own, prepare):
     (outer, outer_size), (inner, inner_size) = plan.sizes
-    line = [swap(own, inner, inner_size, 2 * k) for k in range(1, plan.line)]
-    line, (*prepared, own) = lax.optimization_barrier((line, prepare(own)))
-    line = [own] + line
     half = plan.line // 2
+    line = [swap(own, inner, inner_size, 2 * k) for k in reversed(range(1, plan.line))]
+    low, own = lax.optimization_barrier((line[: half - 1], run_copy(own)))
     held = []
-    for part, turn in ((jnp.stack(line[:half]), 1), (jnp.stack(line[half:]), 2)):
+    for part, turn in (([own] + low, 1), (line[half - 1 :], 2)):
+        part = jnp.stack(part)
         held.append(jnp.concatenate([part, swap(part, outer, outer_size, turn)]))
-    held = held + [swap(part, outer, outer_size, 2 - k) for k, part in enumerate(held)]
+    late = [swap(part, outer, outer_size, 2 - k) for k, part in enumerate(held)]
+    late, prepared = lax.optimization_barrier((late, prepare()))
+    held = held + late
     return prepared, held + [swap(part, inner, inner_size, 1) for part in held]
 
 
-def reduce_ring(plan, keep, send, beside):
+def reduce_ring(plan, keeps, sends, beside):
     (outer, outer_size), (inner, inner_size) = plan.sizes
-    received = [swap(send, inner, inner_size, 1)]
-    keep, *sends = run_merge(plan, outer_size * plan.line, outer_size, keep, received)
-    received = [swap(sends[k], outer, outer_size, k + 1) for k in range(outer_size - 1)]
+    mates = [swap(part, inner, inner_size, 1) for part in sends]
+    received = []
+    for turn in range(1, outer_size):
+        part = keeps[turn] + mates[turn].astype(f32)
+        received.append(swap(part.astype(bf16), outer, outer_size, turn))
     received, beside = lax.optimization_barrier((received, beside))
-    keep, *sends = run_merge(plan, plan.line, plan.line, keep, received)
-    return beside, keep, [swap(sends[k], inner, inner_size, 2 * (k + 1)) for k in reversed(range(plan.line - 1))]
+    keep, *parts = run_merge(plan, plan.line, plan.line, keeps[0], [mates[0], *received])
+    return beside, keep, [swap(parts[k], inner, inner_size, 2 * (k + 1)) for k in reversed(range(plan.line - 1))]
 
 
 def plain_update(plan, position, grads, extra, mlp, states):
@@ -905,25 +927,25 @@
     plan = Plan(sizes, conv_state.shape[2], mlp_state.shape[1], small_state.shape[1])
     x, cot = samples[0], cotangent[0]
     if plan.rings:
-        prepared, inputs = gather_ring(plan, run_pack(plan, *states), lambda own: run_prepare(x, cot, own))
+        prepared, inputs = gather_ring(plan, run_pack(plan, *states), lambda: run_prepare(x, cot))
     else:
         conv, dense, small = [state[0].astype(bf16) for state in states]
         conv = lax.all_gather(conv, AXES, axis=1, tiled=True).reshape(4, KERNEL_ROWS, C)
         small = lax.all_gather(small, AXES, axis=0, tiled=True).reshape(-1, C)
         dense = lax.all_gather(dense, AXES, axis=0, tiled=True).reshape(MLP_ROWS, C)
         inputs = [conv[0], small, conv[1:], dense]
-        prepared = run_prepare(x, cot, small)[:3]
-    rw, kernels, smalls, slope, grad, factors, table, m1, m2, hidden, first, second = run_block(
+        prepared = run_prepare(x, cot)
+    rw, kernels, smalls, slope, grad, factors, table, m1, m2, hidden, *sums = run_block(
         plan, class_ids, x, cot, prepared, inputs
     )
     out = run_down(rw, kernels, smalls)
     dx = run_finish(x, prepared[0], slope, grad, factors)
     mlp = (table, m1, m2, hidden)
     if plan.rings:
-        (out, dx), keep, received = reduce_ring(plan, first, second, (out, dx))
+        (out, dx), keep, received = reduce_ring(plan, sums[:4], sums[4:], (out, dx))
         results = run_update(plan, keep, received, mlp, states)
     else:
-        results = plain_update(plan, lax.axis_index(AXES), first, second, mlp, states)
+        results = plain_update(plan, lax.axis_index(AXES), *sums, mlp, states)
     conv_new, mlp_new, small_new, conv_copy, mlp_copy, small_copy = results
     return out[None], dx[None], conv_new, mlp_new, small_new, conv_copy, mlp_copy.reshape(-1), small_copy.reshape(-1)
 

time: 68.4 us -> 66.9 us (0.978)
  local copies, waits for them, and re-layouts: 3.13 us -> 0.9 us
  starting transfers between devices: 20.9 us -> 22.1 us
    unnamed x16 -> x12, local copies, waits for them, and re-layouts: 3.13 us -> 0.9 us
    ppermute x18 -> x21, starting transfers between devices: 20.9 us -> 22.1 us  [swap(): return lax.ppermute(values, axis, [(i, i ^ turn) for i in range(size)])]
    ppermute x18 -> x21, waiting for transfers between devices: 18.2 us -> 17.8 us  [swap(): return lax.ppermute(values, axis, [(i, i ^ turn) for i in range(size)])]
  transfers between devices with their start and end apart: 18 -> 21, of which waited for: 10 -> 12; matrix products, arithmetic and copies ran while one was open for 0% -> 0% of each run, Pallas kernels for 6% -> 6%
where the time goes in v7:
time: 66.9 us; the launch traced here: 66.7 us
  Pallas kernels  24.3 us (36%)
  starting transfers between devices  22.1 us (33%)
  waiting for transfers between devices  17.8 us (27%)
  between operations  1.45 us (2%)
  local copies, waits for them, and re-layouts  0.9 us (1%)
    ppermute x21, starting transfers between devices, swap(): return lax.ppermute(values, axis, [(i, i ^ turn) for i in range(size)])  22.1 us
    ppermute x21, waiting for transfers between devices, swap(): return lax.ppermute(values, axis, [(i, i ^ turn) for i in range(size)])  17.8 us
    pallas_call x1, Pallas kernels, run_block(): pl.pallas_call(functools.partial(block_body, plan), out_shape=shapes, in_...  16.3 us
    pallas_call x1, Pallas kernels, run_update(): pl.pallas_call(functools.partial(update_body, plan, len(received)), out_s...  1.87 us
    pallas_call x1, Pallas kernels, run_pack(): pl.pallas_call(functools.partial(pack_body, plan), out_shape=jax.ShapeDty...  1.74 us
    pallas_call x1, Pallas kernels, run_down(): pl.pallas_call(down_body, out_shape=jax.ShapeDtypeStruct(shape, bf16), in...  1.58 us
    pallas_call x1, Pallas kernels, run_finish(): pl.pallas_call(finish_body, out_shape=jax.ShapeDtypeStruct((H, W, C), bf1...  1.51 us
  transfers between devices with their start and end apart: 21, of which 12 were waited for; matrix products, arithmetic and copies ran while one was open for 0% of the time, Pallas kernels for 6%

profile of v7, /device:TPU:0, one launch (start us, length us, event | category | flops | bytes accessed | tf_op | source)
XLA Modules:
  0.0 66.7 jit_solution(2717759698747509448)
XLA Ops:
  0.6 1.7 %pack.1.own_ref = bf16[256,128]{1,0:T(8,128)(2,1)} custom-call(f32[4,4,4608]{2,1,0:T(4,128)} %refs_8_.1, f32[4,12544]{1,0:T(4,128)} %refs_9_.1, f32[4,56]{1,0:T(4,128)} %refs_10_.1), custom_call_target="tpu_custom_call" | custom-call | tf_op jit(solution)/shard_map/pack/pallas_call | solution.py:700
  2.4 5.1 %collective-permute-start = (bf16[256,128]{1,0:T(8,128)(2,1)}, bf16[256,128]{1,0:T(8,128)(2,1)S(1)}, u32[]{:S(2)}, u32[]{:S(2)}) collective-permute-start(bf16[256,128]{1,0:T(8,128)(2,1)} %pack.1.own_ref), channel_id=1, source_target_pairs={{0,6},{1,7},{2,4},{3,5},{4,2},{5,3},{6,0},{7,1},{8,14},{9,15},{10,... | collective-permute-start | bytes 196616 | tf_op jit(solution)/shard_map/ppermute | solution.py:873
  7.5 0.6 collective-permute-start.3
  8.2 0.9 %copy-done.4 = bf16[256,128]{1,0:T(8,128)(2,1)S(1)} copy-done((bf16[256,128]{1,0:T(8,128)(2,1)S(1)}, bf16[256,128]{1,0:T(8,128)(2,1)}, u32[]{:S(2)}) %copy-start.4) | copy-done | bytes 65560
  9.0 1.6 %collective-permute-done = bf16[256,128]{1,0:T(8,128)(2,1)S(1)} collective-permute-done((bf16[256,128]{1,0:T(8,128)(2,1)}, bf16[256,128]{1,0:T(8,128)(2,1)S(1)}, u32[]{:S(2)}, u32[]{:S(2)}) %collective-permute-start) | collective-permute-done | bytes 65568 | tf_op jit(solution)/shard_map/ppermute | solution.py:873
  10.6 1.6 %collective-permute-start.1 = (bf16[2,256,128]{2,1,0:T(8,128)(2,1)S(1)}, bf16[2,256,128]{2,1,0:T(8,128)(2,1)S(1)}, u32[]{:S(2)}, u32[]{:S(2)}) collective-permute-start(bf16[2,256,128]{2,1,0:T(8,128)(2,1)S(1)} %pad_maximum_fusion.2), channel_id=1, source_target_pairs={{0,8},{8,0},{16,24},{24,16},{1,9},{9,1},{17,25},{25,17},{2,10},{10... | collective-permute-start | bytes 393224 | tf_op jit(solution)/shard_map/ppermute | solution.py:873
  12.4 1.0 %collective-permute-done.3 = bf16[256,128]{1,0:T(8,128)(2,1)S(1)} collective-permute-done((bf16[256,128]{1,0:T(8,128)(2,1)}, bf16[256,128]{1,0:T(8,128)(2,1)S(1)}, u32[]{:S(2)}, u32[]{:S(2)}) %collective-permute-start.3) | collective-permute-done | bytes 65568 | tf_op jit(solution)/shard_map/ppermute | solution.py:873
  13.4 1.6 %collective-permute-start.5 = (bf16[2,256,128]{2,1,0:T(8,128)(2,1)S(1)}, bf16[2,256,128]{2,1,0:T(8,128)(2,1)S(1)}, u32[]{:S(2)}, u32[]{:S(2)}) collective-permute-start(bf16[2,256,128]{2,1,0:T(8,128)(2,1)S(1)} %pad_maximum_fusion.3), channel_id=1, source_target_pairs={{0,16},{8,24},{16,0},{24,8},{1,17},{9,25},{17,1},{25,9},{2,18},{10... | collective-permute-start | bytes 393224 | tf_op jit(solution)/shard_map/ppermute | solution.py:873
  15.0 0.7 %collective-permute-done.1 = bf16[2,256,128]{2,1,0:T(8,128)(2,1)S(1)} collective-permute-done((bf16[2,256,128]{2,1,0:T(8,128)(2,1)S(1)}, bf16[2,256,128]{2,1,0:T(8,128)(2,1)S(1)}, u32[]{:S(2)}, u32[]{:S(2)}) %collective-permute-start.1) | collective-permute-done | bytes 131104 | tf_op jit(solution)/shard_map/ppermute | solution.py:873
  15.7 1.6 %collective-permute-start.2 = (bf16[4,256,128]{2,1,0:T(8,128)(2,1)S(1)}, bf16[4,256,128]{2,1,0:T(8,128)(2,1)S(1)}, u32[]{:S(2)}, u32[]{:S(2)}) collective-permute-start(bf16[4,256,128]{2,1,0:T(8,128)(2,1)S(1)} %pad_maximum_fusion.refs_6_), channel_id=1, source_target_pairs={{0,16},{8,24},{16,0},{24,8},{1,17},{9,25},{17,1},{25,9},{2,18},{10... | collective-permute-start | bytes 786440 | tf_op jit(solution)/shard_map/ppermute | solution.py:873
  17.3 2.5 %collective-permute-done.5 = bf16[2,256,128]{2,1,0:T(8,128)(2,1)S(1)} collective-permute-done((bf16[2,256,128]{2,1,0:T(8,128)(2,1)S(1)}, bf16[2,256,128]{2,1,0:T(8,128)(2,1)S(1)}, u32[]{:S(2)}, u32[]{:S(2)}) %collective-permute-start.5) | collective-permute-done | bytes 131104 | tf_op jit(solution)/shard_map/ppermute | solution.py:873
  19.8 1.6 %collective-permute-start.6 = (bf16[4,256,128]{2,1,0:T(8,128)(2,1)S(1)}, bf16[4,256,128]{2,1,0:T(8,128)(2,1)S(1)}, u32[]{:S(2)}, u32[]{:S(2)}) collective-permute-start(bf16[4,256,128]{2,1,0:T(8,128)(2,1)S(1)} %pad_maximum_fusion.1.refs_7_), channel_id=1, source_target_pairs={{0,8},{8,0},{16,24},{24,16},{1,9},{9,1},{17,25},{25,17},{2,10},{10... | collective-permute-start | bytes 786440 | tf_op jit(solution)/shard_map/ppermute | solution.py:873
  21.5 1.1 %prepare.1 = (f32[16,128]{1,0:T(8,128)S(1)}, bf16[33,32,512]{2,1,0:T(8,128)(2,1)S(1)}, f32[8,256]{1,0:T(8,128)S(1)}) custom-call(bf16[64,64,128]{2,1,0:T(8,128)(2,1)S(1)} %bitcast.10, bf16[32,32,256]{2,1,0:T(8,128)(2,1)S(1)} %bitcast.15), custom_call_target="tpu_custom_call" | custom-call | flops 2097152 | bytes 3145728 | tf_op jit(solution)/shard_map/prepare/pallas_call | solution.py:213
  22.7 0.5 collective-permute-start.8
  23.2 3.1 %collective-permute-done.6.refs_9_ = bf16[4,256,128]{2,1,0:T(8,128)(2,1)S(1)} collective-permute-done((bf16[4,256,128]{2,1,0:T(8,128)(2,1)S(1)}, bf16[4,256,128]{2,1,0:T(8,128)(2,1)S(1)}, u32[]{:S(2)}, u32[]{:S(2)}) %collective-permute-start.6) | collective-permute-done | bytes 262176 | tf_op jit(solution)/shard_map/ppermute | solution.py:873
  26.3 0.5 collective-permute-start.10
  27.8 0.4 collective-permute-done.10.refs_13_
  28.2 16.3 %block.1 = (bf16[66,32,384]{2,1,0:T(8,128)(2,1)S(1)}, bf16[4,1152,128]{2,1,0:T(8,128)(2,1)S(1)}, f32[16,128]{1,0:T(8,128)S(1)}, f32[64,64,128]{2,1,0:T(8,128)S(1...) custom-call(s32[1]{0:T(128)S(6)} %copy.14.refs_0_, ...), custom_call_target="tpu_custom_call" | custom-call | flops 9437184000 | bytes 16777216 | tf_op jit(solution)/shard_map/block/pallas_call | solution.py:643
  44.7 0.4 collective-permute-start.13
  45.2 0.7 %collective-permute-done.11 = bf16[624,128]{1,0:T(8,128)(2,1)S(1)} collective-permute-done((bf16[624,128]{1,0:T(8,128)(2,1)S(1)}, bf16[624,128]{1,0:T(8,128)(2,1)S(1)}, u32[]{:S(2)}, u32[]{:S(2)}) %collective-permute-start.11) | collective-permute-done | bytes 159776 | tf_op jit(solution)/shard_map/ppermute | solution.py:873
  46.0 1.6 %collective-permute-start.12 = (bf16[624,128]{1,0:T(8,128)(2,1)S(1)}, bf16[624,128]{1,0:T(8,128)(2,1)S(1)}, u32[]{:S(2)}, u32[]{:S(2)}) collective-permute-start(bf16[624,128]{1,0:T(8,128)(2,1)S(1)} %add_convert_fusion.2), channel_id=1, source_target_pairs={{0,8},{8,0},{16,24},{24,16},{1,9},{9,1},{17,25},{25,17},{2,10},{10... | collective-permute-start | bytes 479240 | tf_op jit(solution)/shard_map/ppermute | solution.py:873
  47.7 1.6 %collective-permute-start.14 = (bf16[624,128]{1,0:T(8,128)(2,1)S(1)}, bf16[624,128]{1,0:T(8,128)(2,1)S(1)}, u32[]{:S(2)}, u32[]{:S(2)}) collective-permute-start(bf16[624,128]{1,0:T(8,128)(2,1)S(1)} %add_convert_fusion.1), channel_id=1, source_target_pairs={{0,16},{8,24},{16,0},{24,8},{1,17},{9,25},{17,1},{25,9},{2,18},{10... | collective-permute-start | bytes 479240 | tf_op jit(solution)/shard_map/ppermute | solution.py:873
  49.3 0.5 collective-permute-start.16
  49.8 1.5 %finish.1 = bf16[64,64,128]{2,1,0:T(8,128)(2,1)} custom-call(bf16[64,64,128]{2,1,0:T(8,128)(2,1)S(1)} %bitcast.12, f32[16,128]{1,0:T(8,128)S(1)} %get-tuple-element.56.refs_3_.stats_ref, f32[64,64,128]{2,1,0:T(8,128)S(1)} %get-tuple-element.70.slope_ref, f32[64,64,128]{2,1,0:T(8,128)S(1)} %get-tuple-element.71.grad_ref, ...), custom_call_target="tpu_custom_call" | custom-call | flops 2097152 | bytes 6291456 | tf_op jit(solution)/shard_map/finish/pallas_call | solution.py:539
  51.3 1.6 %down.1 = bf16[32,32,256]{2,1,0:T(8,128)(2,1)} custom-call(bf16[66,32,384]{2,1,0:T(8,128)(2,1)S(1)} %get-tuple-element.67.rw, bf16[4,1152,128]{2,1,0:T(8,128)(2,1)S(1)} %get-tuple-element.68.kernels, f32[16,128]{1,0:T(8,128)S(1)} %get-tuple-element.69.smalls), custom_call_target="tpu_custom_call" | custom-call | flops 633339904 | bytes 3145728 | tf_op jit(solution)/shard_map/down/pallas_call | solution.py:505
  52.9 4.1 %collective-permute-done.14.refs_3_ = bf16[624,128]{1,0:T(8,128)(2,1)S(1)} collective-permute-done((bf16[624,128]{1,0:T(8,128)(2,1)S(1)}, bf16[624,128]{1,0:T(8,128)(2,1)S(1)}, u32[]{:S(2)}, u32[]{:S(2)}) %collective-permute-start.14) | collective-permute-done | bytes 159776 | tf_op jit(solution)/shard_map/ppermute | solution.py:873
  57.2 2.3 %collective-permute-start.18 = (bf16[192,128]{1,0:T(8,128)(2,1)S(1)}, bf16[192,128]{1,0:T(8,128)(2,1)S(1)}, u32[]{:S(2)}, u32[]{:S(2)}) collective-permute-start(bf16[192,128]{1,0:T(8,128)(2,1)S(1)} %get-tuple-element.81), channel_id=1, source_target_pairs={{0,6},{1,7},{2,4},{3,5},{4,2},{5,3},{6,0},{7,1},{8,14},{9,15},{10,... | collective-permute-start | bytes 147464 | tf_op jit(solution)/shard_map/ppermute | solution.py:873
  59.5 0.7 %collective-permute-start.19 = (bf16[192,128]{1,0:T(8,128)(2,1)S(1)}, bf16[192,128]{1,0:T(8,128)(2,1)S(1)}, u32[]{:S(2)}, u32[]{:S(2)}) collective-permute-start(bf16[192,128]{1,0:T(8,128)(2,1)S(1)} %get-tuple-element.82), channel_id=1, source_target_pairs={{0,4},{1,5},{2,6},{3,7},{4,0},{5,1},{6,2},{7,3},{8,12},{9,13},{10,... | collective-permute-start | bytes 147464 | tf_op jit(solution)/shard_map/ppermute | solution.py:873
  60.2 1.4 %collective-permute-start.20 = (bf16[192,128]{1,0:T(8,128)(2,1)S(1)}, bf16[192,128]{1,0:T(8,128)(2,1)S(1)}, u32[]{:S(2)}, u32[]{:S(2)}) collective-permute-start(bf16[192,128]{1,0:T(8,128)(2,1)S(1)} %get-tuple-element.83), channel_id=1, source_target_pairs={{0,2},{1,3},{2,0},{3,1},{4,6},{5,7},{6,4},{7,5},{8,10},{9,11},{10,... | collective-permute-start | bytes 147464 | tf_op jit(solution)/shard_map/ppermute | solution.py:873
  61.6 1.6 %collective-permute-done.18.refs_1_ = bf16[192,128]{1,0:T(8,128)(2,1)S(1)} collective-permute-done((bf16[192,128]{1,0:T(8,128)(2,1)S(1)}, bf16[192,128]{1,0:T(8,128)(2,1)S(1)}, u32[]{:S(2)}, u32[]{:S(2)}) %collective-permute-start.18) | collective-permute-done | bytes 49184 | tf_op jit(solution)/shard_map/ppermute | solution.py:873
  63.2 1.6 %collective-permute-done.19.refs_2_ = bf16[192,128]{1,0:T(8,128)(2,1)S(1)} collective-permute-done((bf16[192,128]{1,0:T(8,128)(2,1)S(1)}, bf16[192,128]{1,0:T(8,128)(2,1)S(1)}, u32[]{:S(2)}, u32[]{:S(2)}) %collective-permute-start.19) | collective-permute-done | bytes 49184 | tf_op jit(solution)/shard_map/ppermute | solution.py:873
  64.9 1.9 %update.1 = (f32[4,4,4608]{2,1,0:T(4,128)}, f32[4,12544]{1,0:T(4,128)}, f32[4,56]{1,0:T(4,128)}, bf16[4,4608]{1,0:T(4,128)(2,1)}, bf16[98,128]{1,0:T(8,128)(2,1)}, /*index=5*/bf16[1,56]{1,0:T(2,128)(2,1)}) custom-call(f32[192,128]{1,0:T(8,128)S(1)} %get-tuple-element.80.refs_0_, bf16[192,128]{1,0:T(8,128)(2,1)S(1)} %collective-permute-done.18.refs_1_, ...), custom_call_target="tpu_custom_call" | custom-call | tf_op jit(solution)/shard_map/update/pallas_call | solution.py:856
  (37 shorter events, 1.3 us)
Async XLA Ops:
  2.4 19.1 %copy-start = (bf16[1,64,64,128]{3,2,1,0:T(8,128)(2,1)S(1)}, bf16[1,64,64,128]{3,2,1,0:T(8,128)(2,1)}, u32[]{:S(2)}) copy-start(bf16[1,64,64,128]{3,2,1,0:T(8,128)(2,1)} %param.6) | copy-start | bytes 3145732
  2.4 19.1 %copy-start.3 = (bf16[1,32,32,256]{3,2,1,0:T(8,128)(2,1)S(1)}, bf16[1,32,32,256]{3,2,1,0:T(8,128)(2,1)}, u32[]{:S(2)}) copy-start(bf16[1,32,32,256]{3,2,1,0:T(8,128)(2,1)} %param.7) | copy-start | bytes 1572868
  2.4 8.2 %collective-permute-start = (bf16[256,128]{1,0:T(8,128)(2,1)}, bf16[256,128]{1,0:T(8,128)(2,1)S(1)}, u32[]{:S(2)}, u32[]{:S(2)}) collective-permute-start(bf16[256,128]{1,0:T(8,128)(2,1)} %pack.1.own_ref), channel_id=1, source_target_pairs={{0,6},{1,7},{2,4},{3,5},{4,2},{5,3},{6,0},{7,1},{8,14},{9,15},{10,... | collective-permute-start | bytes 196616 | tf_op jit(solution)/shard_map/ppermute | solution.py:873
  7.5 4.9 %collective-permute-start.4 = (bf16[256,128]{1,0:T(8,128)(2,1)}, bf16[256,128]{1,0:T(8,128)(2,1)S(1)}, u32[]{:S(2)}, u32[]{:S(2)}) collective-permute-start(bf16[256,128]{1,0:T(8,128)(2,1)} %pack.1.own_ref), channel_id=1, source_target_pairs={{0,2},{1,3},{2,0},{3,1},{4,6},{5,7},{6,4},{7,5},{8,10},{9,11},{10,... | collective-permute-start | bytes 196616 | tf_op jit(solution)/shard_map/ppermute | solution.py:873
  7.5 5.8 %collective-permute-start.3 = (bf16[256,128]{1,0:T(8,128)(2,1)}, bf16[256,128]{1,0:T(8,128)(2,1)S(1)}, u32[]{:S(2)}, u32[]{:S(2)}) collective-permute-start(bf16[256,128]{1,0:T(8,128)(2,1)} %pack.1.own_ref), channel_id=1, source_target_pairs={{0,4},{1,5},{2,6},{3,7},{4,0},{5,1},{6,2},{7,3},{8,12},{9,13},{10,... | collective-permute-start | bytes 196616 | tf_op jit(solution)/shard_map/ppermute | solution.py:873
  8.2 0.9 %copy-start.4 = (bf16[256,128]{1,0:T(8,128)(2,1)S(1)}, bf16[256,128]{1,0:T(8,128)(2,1)}, u32[]{:S(2)}) copy-start(bf16[256,128]{1,0:T(8,128)(2,1)} %pack.1.own_ref) | copy-start | bytes 196612
  10.6 5.0 %collective-permute-start.1 = (bf16[2,256,128]{2,1,0:T(8,128)(2,1)S(1)}, bf16[2,256,128]{2,1,0:T(8,128)(2,1)S(1)}, u32[]{:S(2)}, u32[]{:S(2)}) collective-permute-start(bf16[2,256,128]{2,1,0:T(8,128)(2,1)S(1)} %pad_maximum_fusion.2), channel_id=1, source_target_pairs={{0,8},{8,0},{16,24},{24,16},{1,9},{9,1},{17,25},{25,17},{2,10},{10... | collective-permute-start | bytes 393224 | tf_op jit(solution)/shard_map/ppermute | solution.py:873
  13.4 6.4 %collective-permute-start.5 = (bf16[2,256,128]{2,1,0:T(8,128)(2,1)S(1)}, bf16[2,256,128]{2,1,0:T(8,128)(2,1)S(1)}, u32[]{:S(2)}, u32[]{:S(2)}) collective-permute-start(bf16[2,256,128]{2,1,0:T(8,128)(2,1)S(1)} %pad_maximum_fusion.3), channel_id=1, source_target_pairs={{0,16},{8,24},{16,0},{24,8},{1,17},{9,25},{17,1},{25,9},{2,18},{10... | collective-permute-start | bytes 393224 | tf_op jit(solution)/shard_map/ppermute | solution.py:873
  15.7 7.5 %collective-permute-start.2 = (bf16[4,256,128]{2,1,0:T(8,128)(2,1)S(1)}, bf16[4,256,128]{2,1,0:T(8,128)(2,1)S(1)}, u32[]{:S(2)}, u32[]{:S(2)}) collective-permute-start(bf16[4,256,128]{2,1,0:T(8,128)(2,1)S(1)} %pad_maximum_fusion.refs_6_), channel_id=1, source_target_pairs={{0,16},{8,24},{16,0},{24,8},{1,17},{9,25},{17,1},{25,9},{2,18},{10... | collective-permute-start | bytes 786440 | tf_op jit(solution)/shard_map/ppermute | solution.py:873
  19.8 6.4 %collective-permute-start.6 = (bf16[4,256,128]{2,1,0:T(8,128)(2,1)S(1)}, bf16[4,256,128]{2,1,0:T(8,128)(2,1)S(1)}, u32[]{:S(2)}, u32[]{:S(2)}) collective-permute-start(bf16[4,256,128]{2,1,0:T(8,128)(2,1)S(1)} %pad_maximum_fusion.1.refs_7_), channel_id=1, source_target_pairs={{0,8},{8,0},{16,24},{24,16},{1,9},{9,1},{17,25},{25,17},{2,10},{10... | collective-permute-start | bytes 786440 | tf_op jit(solution)/shard_map/ppermute | solution.py:873
  22.6 4.8 %collective-permute-start.7 = (bf16[4,256,128]{2,1,0:T(8,128)(2,1)S(1)}, bf16[4,256,128]{2,1,0:T(8,128)(2,1)S(1)}, u32[]{:S(2)}, u32[]{:S(2)}) collective-permute-start(bf16[4,256,128]{2,1,0:T(8,128)(2,1)S(1)} %pad_maximum_fusion.refs_6_), channel_id=1, source_target_pairs={{0,1},{1,0},{2,3},{3,2},{4,5},{5,4},{6,7},{7,6},{8,9},{9,8},{10,11... | collective-permute-start | bytes 786440 | tf_op jit(solution)/shard_map/ppermute | solution.py:873
  22.7 4.7 %collective-permute-start.8 = (bf16[4,256,128]{2,1,0:T(8,128)(2,1)S(1)}, bf16[4,256,128]{2,1,0:T(8,128)(2,1)S(1)}, u32[]{:S(2)}, u32[]{:S(2)}) collective-permute-start(bf16[4,256,128]{2,1,0:T(8,128)(2,1)S(1)} %pad_maximum_fusion.1.refs_7_), channel_id=1, source_target_pairs={{0,1},{1,0},{2,3},{3,2},{4,5},{5,4},{6,7},{7,6},{8,9},{9,8},{10,11... | collective-permute-start | bytes 786440 | tf_op jit(solution)/shard_map/ppermute | solution.py:873
  26.3 1.5 %collective-permute-start.9 = (bf16[4,256,128]{2,1,0:T(8,128)(2,1)S(1)}, bf16[4,256,128]{2,1,0:T(8,128)(2,1)S(1)}, u32[]{:S(2)}, u32[]{:S(2)}) collective-permute-start(bf16[4,256,128]{2,1,0:T(8,128)(2,1)S(1)} %collective-permute-done.2.refs_8_), channel_id=1, source_target_pairs={{0,1},{1,0},{2,3},{3,2},{4,5},{5,4},{6,7},{7,6},{8,9},{9,8},{10,11... | collective-permute-start | bytes 786440 | tf_op jit(solution)/shard_map/ppermute | solution.py:873
  26.3 1.9 %collective-permute-start.10 = (bf16[4,256,128]{2,1,0:T(8,128)(2,1)S(1)}, bf16[4,256,128]{2,1,0:T(8,128)(2,1)S(1)}, u32[]{:S(2)}, u32[]{:S(2)}) collective-permute-start(bf16[4,256,128]{2,1,0:T(8,128)(2,1)S(1)} %collective-permute-done.6.refs_9_), channel_id=1, source_target_pairs={{0,1},{1,0},{2,3},{3,2},{4,5},{5,4},{6,7},{7,6},{8,9},{9,8},{10,11... | collective-permute-start | bytes 786440 | tf_op jit(solution)/shard_map/ppermute | solution.py:873
  44.5 1.5 %collective-permute-start.11 = (bf16[624,128]{1,0:T(8,128)(2,1)S(1)}, bf16[624,128]{1,0:T(8,128)(2,1)S(1)}, u32[]{:S(2)}, u32[]{:S(2)}) collective-permute-start(bf16[624,128]{1,0:T(8,128)(2,1)S(1)} %get-tuple-element.62), channel_id=1, source_target_pairs={{0,1},{1,0},{2,3},{3,2},{4,5},{5,4},{6,7},{7,6},{8,9},{9,8},{10,11... | collective-permute-start | bytes 479240 | tf_op jit(solution)/shard_map/ppermute | solution.py:873
  44.7 2.9 %collective-permute-start.13 = (bf16[624,128]{1,0:T(8,128)(2,1)S(1)}, bf16[624,128]{1,0:T(8,128)(2,1)S(1)}, u32[]{:S(2)}, u32[]{:S(2)}) collective-permute-start(bf16[624,128]{1,0:T(8,128)(2,1)S(1)} %get-tuple-element.64), channel_id=1, source_target_pairs={{0,1},{1,0},{2,3},{3,2},{4,5},{5,4},{6,7},{7,6},{8,9},{9,8},{10,11... | collective-permute-start | bytes 479240 | tf_op jit(solution)/shard_map/ppermute | solution.py:873
  45.1 4.2 %collective-permute-start.15 = (bf16[624,128]{1,0:T(8,128)(2,1)S(1)}, bf16[624,128]{1,0:T(8,128)(2,1)S(1)}, u32[]{:S(2)}, u32[]{:S(2)}) collective-permute-start(bf16[624,128]{1,0:T(8,128)(2,1)S(1)} %get-tuple-element.66), channel_id=1, source_target_pairs={{0,1},{1,0},{2,3},{3,2},{4,5},{5,4},{6,7},{7,6},{8,9},{9,8},{10,11... | collective-permute-start | bytes 479240 | tf_op jit(solution)/shard_map/ppermute | solution.py:873
  46.0 6.9 %collective-permute-start.12 = (bf16[624,128]{1,0:T(8,128)(2,1)S(1)}, bf16[624,128]{1,0:T(8,128)(2,1)S(1)}, u32[]{:S(2)}, u32[]{:S(2)}) collective-permute-start(bf16[624,128]{1,0:T(8,128)(2,1)S(1)} %add_convert_fusion.2), channel_id=1, source_target_pairs={{0,8},{8,0},{16,24},{24,16},{1,9},{9,1},{17,25},{25,17},{2,10},{10... | collective-permute-start | bytes 479240 | tf_op jit(solution)/shard_map/ppermute | solution.py:873
  47.7 9.4 %collective-permute-start.14 = (bf16[624,128]{1,0:T(8,128)(2,1)S(1)}, bf16[624,128]{1,0:T(8,128)(2,1)S(1)}, u32[]{:S(2)}, u32[]{:S(2)}) collective-permute-start(bf16[624,128]{1,0:T(8,128)(2,1)S(1)} %add_convert_fusion.1), channel_id=1, source_target_pairs={{0,16},{8,24},{16,0},{24,8},{1,17},{9,25},{17,1},{25,9},{2,18},{10... | collective-permute-start | bytes 479240 | tf_op jit(solution)/shard_map/ppermute | solution.py:873
  49.3 7.7 %collective-permute-start.16 = (bf16[624,128]{1,0:T(8,128)(2,1)S(1)}, bf16[624,128]{1,0:T(8,128)(2,1)S(1)}, u32[]{:S(2)}, u32[]{:S(2)}) collective-permute-start(bf16[624,128]{1,0:T(8,128)(2,1)S(1)} %add_convert_fusion), channel_id=1, source_target_pairs={{0,24},{8,16},{16,8},{24,0},{1,25},{9,17},{17,9},{25,1},{2,26},{10... | collective-permute-start | bytes 479240 | tf_op jit(solution)/shard_map/ppermute | solution.py:873
  49.8 7.3 %collective-permute-start.17 = (bf16[624,128]{1,0:T(8,128)(2,1)S(1)}, bf16[624,128]{1,0:T(8,128)(2,1)S(1)}, u32[]{:S(2)}, u32[]{:S(2)}) collective-permute-start(bf16[624,128]{1,0:T(8,128)(2,1)S(1)} %get-tuple-element.76), channel_id=1, source_target_pairs={{0,1},{1,0},{2,3},{3,2},{4,5},{5,4},{6,7},{7,6},{8,9},{9,8},{10,11... | collective-permute-start | bytes 479240 | tf_op jit(solution)/shard_map/ppermute | solution.py:873
  51.3 13.5 %copy-start.1 = (f32[4,4,4608]{2,1,0:T(4,128)S(1)}, f32[4,4,4608]{2,1,0:T(4,128)}, u32[]{:S(2)}) copy-start(f32[4,4,4608]{2,1,0:T(4,128)} %refs_8_.1) | copy-start | bytes 884740
  51.3 13.5 %copy-start.2 = (f32[4,12544]{1,0:T(4,128)S(1)}, f32[4,12544]{1,0:T(4,128)}, u32[]{:S(2)}) copy-start(f32[4,12544]{1,0:T(4,128)} %refs_9_.1) | copy-start | bytes 602116
  51.3 13.5 %copy-start.5 = (f32[4,56]{1,0:T(4,128)S(1)}, f32[4,56]{1,0:T(4,128)}, u32[]{:S(2)}) copy-start(f32[4,56]{1,0:T(4,128)} %refs_10_.1) | copy-start | bytes 2692
  57.2 6.1 %collective-permute-start.18 = (bf16[192,128]{1,0:T(8,128)(2,1)S(1)}, bf16[192,128]{1,0:T(8,128)(2,1)S(1)}, u32[]{:S(2)}, u32[]{:S(2)}) collective-permute-start(bf16[192,128]{1,0:T(8,128)(2,1)S(1)} %get-tuple-element.81), channel_id=1, source_target_pairs={{0,6},{1,7},{2,4},{3,5},{4,2},{5,3},{6,0},{7,1},{8,14},{9,15},{10,... | collective-permute-start | bytes 147464 | tf_op jit(solution)/shard_map/ppermute | solution.py:873
  59.5 5.3 %collective-permute-start.19 = (bf16[192,128]{1,0:T(8,128)(2,1)S(1)}, bf16[192,128]{1,0:T(8,128)(2,1)S(1)}, u32[]{:S(2)}, u32[]{:S(2)}) collective-permute-start(bf16[192,128]{1,0:T(8,128)(2,1)S(1)} %get-tuple-element.82), channel_id=1, source_target_pairs={{0,4},{1,5},{2,6},{3,7},{4,0},{5,1},{6,2},{7,3},{8,12},{9,13},{10,... | collective-permute-start | bytes 147464 | tf_op jit(solution)/shard_map/ppermute | solution.py:873
  60.2 4.6 %collective-permute-start.20 = (bf16[192,128]{1,0:T(8,128)(2,1)S(1)}, bf16[192,128]{1,0:T(8,128)(2,1)S(1)}, u32[]{:S(2)}, u32[]{:S(2)}) collective-permute-start(bf16[192,128]{1,0:T(8,128)(2,1)S(1)} %get-tuple-element.83), channel_id=1, source_target_pairs={{0,2},{1,3},{2,0},{3,1},{4,6},{5,7},{6,4},{7,5},{8,10},{9,11},{10,... | collective-permute-start | bytes 147464 | tf_op jit(solution)/shard_map/ppermute | solution.py:873

commit v8 on v7

--- a/solution.py
+++ b/solution.py
@@ -44,6 +44,7 @@
 PAIRS = ((2, 3), (1, 0))
 R = 4
 Q = 2
+WIDE = 8
 STEPS = H // R
 PART = CELLS // STEPS
 
@@ -138,16 +139,16 @@
         pair_ref[(tap + 3) * C : (tap + 4) * C, C:] = block
 
 
-def pair_conv(win_ref, pair_ref, first):
+def pair_conv(win_ref, pair_ref, first, q=Q):
     view = win_ref.reshape(H // 2 + 1, 2, W, 3 * C)
-    taken = [view[pl.ds(first + t // 2, Q), t % 2] for t in range(4)]
-    stacked = jnp.concatenate(taken, axis=-1).reshape(Q * W, 12 * C)
-    return mm(stacked, pair_ref[...]).reshape(Q, W, 2 * C)
-
-
-def pairs_of(ref, first):
+    taken = [view[pl.ds(first + t // 2, q), t % 2] for t in range(4)]
+    stacked = jnp.concatenate(taken, axis=-1).reshape(q * W, 12 * C)
+    return mm(stacked, pair_ref[...]).reshape(q, W, 2 * C)
+
+
+def pairs_of(ref, first, q=Q):
     view = ref.reshape(H // 2, 2, W, C)
-    return [view.at[pl.ds(first, Q), parity] for parity in range(2)]
+    return [view.at[pl.ds(first, q), parity] for parity in range(2)]
 
 
 def kernel_grad(act_ref, win_ref, out_ref):
@@ -163,7 +164,8 @@
     return lax.axis_index(outer) * inner_size + lax.axis_index(inner)
 
 
-def prepare_body(x_ref, cot_ref, stats_ref, cw, gdb_ref):
+def prepare_body(cls_ref, x_ref, cot_ref, stats_ref, cw, gdb_ref, hot_ref):
+    hot_ref[...] = (lax.broadcasted_iota(jnp.int32, hot_ref.shape, 0) == cls_ref[0]).astype(f32)
     zero8 = jnp.zeros((8, C), f32)
 
     def read_x(i):
@@ -208,23 +210,23 @@
     )(own)
 
 
-def run_prepare(x, cot):
+def run_prepare(class_ids, x, cot):
     struct = jax.ShapeDtypeStruct
     return pl.pallas_call(
         prepare_body,
-        out_shape=[struct((16, C), f32), struct((H // 2 + 1, W // 2, 4 * C), bf16), struct((8, 2 * C), f32)],
-        in_specs=vmem_specs(2),
-        out_specs=vmem_specs(3),
+        out_shape=[struct((16, C), f32), struct((H // 2 + 1, W // 2, 4 * C), bf16), struct((8, 2 * C), f32), struct((NCLASS, 2 * C), f32)],
+        in_specs=[pl.BlockSpec(memory_space=pltpu.SMEM)] + vmem_specs(2),
+        out_specs=vmem_specs(4),
         compiler_params=limit(8),
         cost_estimate=cost(2, 3 << 20),
         name="prepare",
-    )(x, cot)
+    )(class_ids, x, cot)
 
 
 def block_body(plan, *refs):
     refs = list(refs)
     count = 8 if plan.rings else 4
-    cls_ref, x_ref, cot_ref, stats_ref, cw, gdb_ref = refs[:6]
+    x_ref, cot_ref, stats_ref, cw, gdb_ref, hot_ref = refs[:6]
     inputs = refs[6 : 6 + count]
     rw, kernels, smalls, slope1_ref, drf, factors_ref, table_ref, m1_ref, m2_ref, hidden_ref = refs[6 + count : 16 + count]
     made = 24 + count if plan.rings else 18 + count
@@ -336,7 +338,7 @@
     hidden_ref[...] = hidden
     act = hidden * normal_cdf(hidden)
     ss = exact(act, m2_ref[...]) + small_run(12, 2)
-    mine = lax.broadcasted_iota(jnp.int32, (NCLASS, 2 * C), 0) == cls_ref[0]
+    mine = hot_ref[...] > 0.5
     chosen = jnp.sum(jnp.where(mine, ss, 0.0), axis=0, keepdims=True)
     scale = jnp.broadcast_to(1.0 + chosen[:, :C], (8, C))
     shift = jnp.broadcast_to(chosen[:, C:], (8, C))
@@ -420,9 +422,9 @@
     conv[2] = gkd[:, :C]
     conv[3] = gkd[:, C:]
 
-    def pull(i, s, win_ref, back_ref, slope_ref, out_slope_ref, units):
-        got = pair_conv(win_ref, back_ref, i * Q)
-        places = zip(pairs_of(slope_ref, i * Q), pairs_of(out_slope_ref, i * Q), units)
+    def pull(i, s, win_ref, back_ref, slope_ref, out_slope_ref, units, q=Q):
+        got = pair_conv(win_ref, back_ref, i * q, q)
+        places = zip(pairs_of(slope_ref, i * q, q), pairs_of(out_slope_ref, i * q, q), units)
         for parity, (place, out_place, unit) in enumerate(places):
             dn = got[..., parity * C : (parity + 1) * C] * place[...]
             out_place[...] = dn
@@ -431,8 +433,9 @@
 
     pair_backward(back2, k2_ref)
     sums = (zero8, zero8)
-    for i in range(STEPS):
-        sums = pull(i, sums, t2w, back2, g2p, g2p, [unit2(ref[...]) for ref in pairs_of(c1, i * Q)])
+    for i in range(H // 2 // WIDE):
+        units = [unit2(ref[...]) for ref in pairs_of(c1, i * WIDE, WIDE)]
+        sums = pull(i, sums, t2w, back2, g2p, g2p, units, WIDE)
     gb2, gg2 = [total_of(part) for part in sums]
     mean_du2 = group_sum(gb2 * (1.0 + gain2)) * (1.0 / PER_GROUP)
     mean_duu2 = group_sum(gg2 * (1.0 + gain2)) * (1.0 / PER_GROUP)
@@ -619,7 +622,7 @@
         return pl.multiple_of(first + 8 * odd, 8), pl.multiple_of(first + self.full * (1 - odd), 8)
 
 
-def run_block(plan, class_ids, x, cot, prepared, inputs):
+def run_block(plan, x, cot, prepared, inputs):
     struct = jax.ShapeDtypeStruct
     shapes = [
         struct((H + 2, W // 2, 3 * C), bf16),
@@ -643,7 +646,7 @@
     return pl.pallas_call(
         functools.partial(block_body, plan),
         out_shape=shapes,
-        in_specs=[pl.BlockSpec(memory_space=pltpu.SMEM)] + vmem_specs(5 + len(inputs)),
+        in_specs=vmem_specs(6 + len(inputs)),
         out_specs=vmem_specs(len(shapes)),
         scratch_shapes=[
             windows,
@@ -661,7 +664,7 @@
         compiler_params=limit(40),
         cost_estimate=cost(9000, 16 << 20),
         name="block",
-    )(class_ids, x, cot, *prepared, *inputs)
+    )(x, cot, *prepared, *inputs)
 
 
 def pack_body(plan, conv_hbm, dense_hbm, small_hbm, out_ref, conv_ref, dense_ref, small_ref, windows, rows, sems):
@@ -675,8 +678,7 @@
     rows[...] = jnp.zeros(rows.shape, f32)
     copies[0].wait()
     for r in range(plan.conv_rows):
-        for k in range(4):
-            windows[pl.ds(k * plan.window + 4 * odd + r, 1), :] = conv_ref[k : k + 1, r * C : (r + 1) * C]
+        windows[pl.ds(4 * odd + r, 4, plan.window), :] = conv_ref[:, r * C : (r + 1) * C]
     halves = []
     for k in range(4):
         full, half = plan.places(odd, k * plan.window)
@@ -927,16 +929,16 @@
     plan = Plan(sizes, conv_state.shape[2], mlp_state.shape[1], small_state.shape[1])
     x, cot = samples[0], cotangent[0]
     if plan.rings:
-        prepared, inputs = gather_ring(plan, run_pack(plan, *states), lambda: run_prepare(x, cot))
+        prepared, inputs = gather_ring(plan, run_pack(plan, *states), lambda: run_prepare(class_ids, x, cot))
     else:
         conv, dense, small = [state[0].astype(bf16) for state in states]
         conv = lax.all_gather(conv, AXES, axis=1, tiled=True).reshape(4, KERNEL_ROWS, C)
         small = lax.all_gather(small, AXES, axis=0, tiled=True).reshape(-1, C)
         dense = lax.all_gather(dense, AXES, axis=0, tiled=True).reshape(MLP_ROWS, C)
         inputs = [conv[0], small, conv[1:], dense]
-        prepared = run_prepare(x, cot)
+        prepared = run_prepare(class_ids, x, cot)
     rw, kernels, smalls, slope, grad, factors, table, m1, m2, hidden, *sums = run_block(
-        plan, class_ids, x, cot, prepared, inputs
+        plan, x, cot, prepared, inputs
     )
     out = run_down(rw, kernels, smalls)
     dx = run_finish(x, prepared[0], slope, grad, factors)

time: 66.9 us -> 66.5 us (level)
  no operation moved by 1% of the time
where the time goes in v8:
time: 66.5 us; the launch traced here: 66.3 us
  Pallas kernels  23.8 us (36%)
  starting transfers between devices  22.1 us (33%)
  waiting for transfers between devices  17.8 us (27%)
  between operations  1.45 us (2%)
  local copies, waits for them, and re-layouts  0.9 us (1%)
    ppermute x21, starting transfers between devices, swap(): return lax.ppermute(values, axis, [(i, i ^ turn) for i in range(size)])  22.1 us
    ppermute x21, waiting for transfers between devices, swap(): return lax.ppermute(values, axis, [(i, i ^ turn) for i in range(size)])  17.8 us
    pallas_call x1, Pallas kernels, run_block(): pl.pallas_call(functools.partial(block_body, plan), out_shape=shapes, in_...  15.9 us
    pallas_call x1, Pallas kernels, run_update(): pl.pallas_call(functools.partial(update_body, plan, len(received)), out_s...  1.88 us
    pallas_call x1, Pallas kernels, run_pack(): pl.pallas_call(functools.partial(pack_body, plan), out_shape=jax.ShapeDty...  1.74 us
    pallas_call x1, Pallas kernels, run_down(): pl.pallas_call(down_body, out_shape=jax.ShapeDtypeStruct(shape, bf16), in...  1.58 us
    pallas_call x1, Pallas kernels, run_finish(): pl.pallas_call(finish_body, out_shape=jax.ShapeDtypeStruct((H, W, C), bf1...  1.5 us
  transfers between devices with their start and end apart: 21, of which 12 were waited for; matrix products, arithmetic and copies ran while one was open for 0% of the time, Pallas kernels for 6%

profile of v8, /device:TPU:0, one launch (start us, length us, event | category | flops | bytes accessed | tf_op | source)
XLA Modules:
  0.0 66.3 jit_solution(1244884149184327455)
XLA Ops:
  0.6 1.7 %pack.1.own_ref = bf16[256,128]{1,0:T(8,128)(2,1)} custom-call(f32[4,4,4608]{2,1,0:T(4,128)} %refs_8_.1, f32[4,12544]{1,0:T(4,128)} %refs_9_.1, f32[4,56]{1,0:T(4,128)} %refs_10_.1), custom_call_target="tpu_custom_call" | custom-call | tf_op jit(solution)/shard_map/pack/pallas_call | solution.py:702
  2.4 5.1 %collective-permute-start = (bf16[256,128]{1,0:T(8,128)(2,1)}, bf16[256,128]{1,0:T(8,128)(2,1)S(1)}, u32[]{:S(2)}, u32[]{:S(2)}) collective-permute-start(bf16[256,128]{1,0:T(8,128)(2,1)} %pack.1.own_ref), channel_id=1, source_target_pairs={{0,6},{1,7},{2,4},{3,5},{4,2},{5,3},{6,0},{7,1},{8,14},{9,15},{10,... | collective-permute-start | bytes 196616 | tf_op jit(solution)/shard_map/ppermute | solution.py:875
  7.5 0.6 collective-permute-start.3
  8.2 0.9 %copy-done.4 = bf16[256,128]{1,0:T(8,128)(2,1)S(1)} copy-done((bf16[256,128]{1,0:T(8,128)(2,1)S(1)}, bf16[256,128]{1,0:T(8,128)(2,1)}, u32[]{:S(2)}) %copy-start.4) | copy-done | bytes 65560
  9.0 1.6 %collective-permute-done = bf16[256,128]{1,0:T(8,128)(2,1)S(1)} collective-permute-done((bf16[256,128]{1,0:T(8,128)(2,1)}, bf16[256,128]{1,0:T(8,128)(2,1)S(1)}, u32[]{:S(2)}, u32[]{:S(2)}) %collective-permute-start) | collective-permute-done | bytes 65568 | tf_op jit(solution)/shard_map/ppermute | solution.py:875
  10.6 1.6 %collective-permute-start.1 = (bf16[2,256,128]{2,1,0:T(8,128)(2,1)S(1)}, bf16[2,256,128]{2,1,0:T(8,128)(2,1)S(1)}, u32[]{:S(2)}, u32[]{:S(2)}) collective-permute-start(bf16[2,256,128]{2,1,0:T(8,128)(2,1)S(1)} %pad_maximum_fusion.2), channel_id=1, source_target_pairs={{0,8},{8,0},{16,24},{24,16},{1,9},{9,1},{17,25},{25,17},{2,10},{10... | collective-permute-start | bytes 393224 | tf_op jit(solution)/shard_map/ppermute | solution.py:875
  12.4 1.0 %collective-permute-done.3 = bf16[256,128]{1,0:T(8,128)(2,1)S(1)} collective-permute-done((bf16[256,128]{1,0:T(8,128)(2,1)}, bf16[256,128]{1,0:T(8,128)(2,1)S(1)}, u32[]{:S(2)}, u32[]{:S(2)}) %collective-permute-start.3) | collective-permute-done | bytes 65568 | tf_op jit(solution)/shard_map/ppermute | solution.py:875
  13.4 1.6 %collective-permute-start.5 = (bf16[2,256,128]{2,1,0:T(8,128)(2,1)S(1)}, bf16[2,256,128]{2,1,0:T(8,128)(2,1)S(1)}, u32[]{:S(2)}, u32[]{:S(2)}) collective-permute-start(bf16[2,256,128]{2,1,0:T(8,128)(2,1)S(1)} %pad_maximum_fusion.3), channel_id=1, source_target_pairs={{0,16},{8,24},{16,0},{24,8},{1,17},{9,25},{17,1},{25,9},{2,18},{10... | collective-permute-start | bytes 393224 | tf_op jit(solution)/shard_map/ppermute | solution.py:875
  15.0 0.7 %collective-permute-done.1 = bf16[2,256,128]{2,1,0:T(8,128)(2,1)S(1)} collective-permute-done((bf16[2,256,128]{2,1,0:T(8,128)(2,1)S(1)}, bf16[2,256,128]{2,1,0:T(8,128)(2,1)S(1)}, u32[]{:S(2)}, u32[]{:S(2)}) %collective-permute-start.1) | collective-permute-done | bytes 131104 | tf_op jit(solution)/shard_map/ppermute | solution.py:875
  15.7 1.6 %collective-permute-start.2 = (bf16[4,256,128]{2,1,0:T(8,128)(2,1)S(1)}, bf16[4,256,128]{2,1,0:T(8,128)(2,1)S(1)}, u32[]{:S(2)}, u32[]{:S(2)}) collective-permute-start(bf16[4,256,128]{2,1,0:T(8,128)(2,1)S(1)} %pad_maximum_fusion.refs_6_), channel_id=1, source_target_pairs={{0,16},{8,24},{16,0},{24,8},{1,17},{9,25},{17,1},{25,9},{2,18},{10... | collective-permute-start | bytes 786440 | tf_op jit(solution)/shard_map/ppermute | solution.py:875
  17.3 2.5 %collective-permute-done.5 = bf16[2,256,128]{2,1,0:T(8,128)(2,1)S(1)} collective-permute-done((bf16[2,256,128]{2,1,0:T(8,128)(2,1)S(1)}, bf16[2,256,128]{2,1,0:T(8,128)(2,1)S(1)}, u32[]{:S(2)}, u32[]{:S(2)}) %collective-permute-start.5) | collective-permute-done | bytes 131104 | tf_op jit(solution)/shard_map/ppermute | solution.py:875
  19.8 1.6 %collective-permute-start.6 = (bf16[4,256,128]{2,1,0:T(8,128)(2,1)S(1)}, bf16[4,256,128]{2,1,0:T(8,128)(2,1)S(1)}, u32[]{:S(2)}, u32[]{:S(2)}) collective-permute-start(bf16[4,256,128]{2,1,0:T(8,128)(2,1)S(1)} %pad_maximum_fusion.1.refs_7_), channel_id=1, source_target_pairs={{0,8},{8,0},{16,24},{24,16},{1,9},{9,1},{17,25},{25,17},{2,10},{10... | collective-permute-start | bytes 786440 | tf_op jit(solution)/shard_map/ppermute | solution.py:875
  22.1 1.1 %prepare.1 = (f32[16,128]{1,0:T(8,128)S(1)}, bf16[33,32,512]{2,1,0:T(8,128)(2,1)S(1)}, f32[8,256]{1,0:T(8,128)S(1)}, f32[16,256]{1,0:T(8,128)S(1)}) custom-call(s32[1]{0:T(128)S(6)} %copy.14.cls_ref, bf16[64,64,128]{2,1,0:T(8,128)(2,1)S(1)} %bitcast.10, bf16[32,32,256]{2,1,0:T(8,128)(2,1)S(1)} %bitcast.15), custom_call_target="tpu_custom_call" | custom-call | flops 2097152 | bytes 3145728 | tf_op jit(solution)/shard_map/prepare/pallas_call | solution.py:215
  23.4 0.5 collective-permute-start.8
  23.9 2.4 %collective-permute-done.6.refs_9_ = bf16[4,256,128]{2,1,0:T(8,128)(2,1)S(1)} collective-permute-done((bf16[4,256,128]{2,1,0:T(8,128)(2,1)S(1)}, bf16[4,256,128]{2,1,0:T(8,128)(2,1)S(1)}, u32[]{:S(2)}, u32[]{:S(2)}) %collective-permute-start.6) | collective-permute-done | bytes 262176 | tf_op jit(solution)/shard_map/ppermute | solution.py:875
  26.3 0.5 collective-permute-start.10
  26.8 1.0 %collective-permute-done.9.refs_12_ = bf16[4,256,128]{2,1,0:T(8,128)(2,1)S(1)} collective-permute-done((bf16[4,256,128]{2,1,0:T(8,128)(2,1)S(1)}, bf16[4,256,128]{2,1,0:T(8,128)(2,1)S(1)}, u32[]{:S(2)}, u32[]{:S(2)}) %collective-permute-start.9) | collective-permute-done | bytes 262176 | tf_op jit(solution)/shard_map/ppermute | solution.py:875
  27.8 0.4 collective-permute-done.10.refs_13_
  28.2 15.9 %block.1 = (bf16[66,32,384]{2,1,0:T(8,128)(2,1)S(1)}, bf16[4,1152,128]{2,1,0:T(8,128)(2,1)S(1)}, f32[16,128]{1,0:T(8,128)S(1)}, f32[64,64,128]{2,1,0:T(8,128)S(1...) custom-call(bf16[64,64,128]{2,1,0:T(8,128)(2,1)S(1)} %bitcast.11, ...), custom_call_target="tpu_custom_call" | custom-call | flops 9437184000 | bytes 16777216 | tf_op jit(solution)/shard_map/block/pallas_call | solution.py:646
  44.8 0.7 %collective-permute-done.11 = bf16[624,128]{1,0:T(8,128)(2,1)S(1)} collective-permute-done((bf16[624,128]{1,0:T(8,128)(2,1)S(1)}, bf16[624,128]{1,0:T(8,128)(2,1)S(1)}, u32[]{:S(2)}, u32[]{:S(2)}) %collective-permute-start.11) | collective-permute-done | bytes 159776 | tf_op jit(solution)/shard_map/ppermute | solution.py:875
  45.6 1.6 %collective-permute-start.12 = (bf16[624,128]{1,0:T(8,128)(2,1)S(1)}, bf16[624,128]{1,0:T(8,128)(2,1)S(1)}, u32[]{:S(2)}, u32[]{:S(2)}) collective-permute-start(bf16[624,128]{1,0:T(8,128)(2,1)S(1)} %add_convert_fusion.2), channel_id=1, source_target_pairs={{0,8},{8,0},{16,24},{24,16},{1,9},{9,1},{17,25},{25,17},{2,10},{10... | collective-permute-start | bytes 479240 | tf_op jit(solution)/shard_map/ppermute | solution.py:875
  47.3 1.6 %collective-permute-start.14 = (bf16[624,128]{1,0:T(8,128)(2,1)S(1)}, bf16[624,128]{1,0:T(8,128)(2,1)S(1)}, u32[]{:S(2)}, u32[]{:S(2)}) collective-permute-start(bf16[624,128]{1,0:T(8,128)(2,1)S(1)} %add_convert_fusion.1), channel_id=1, source_target_pairs={{0,16},{8,24},{16,0},{24,8},{1,17},{9,25},{17,1},{25,9},{2,18},{10... | collective-permute-start | bytes 479240 | tf_op jit(solution)/shard_map/ppermute | solution.py:875
  48.9 0.5 collective-permute-start.16
  49.4 1.5 %finish.1 = bf16[64,64,128]{2,1,0:T(8,128)(2,1)} custom-call(bf16[64,64,128]{2,1,0:T(8,128)(2,1)S(1)} %bitcast.12, f32[16,128]{1,0:T(8,128)S(1)} %get-tuple-element.59.refs_2_.stats_ref, f32[64,64,128]{2,1,0:T(8,128)S(1)} %get-tuple-element.74.slope_ref, f32[64,64,128]{2,1,0:T(8,128)S(1)} %get-tuple-element.75.grad_ref, ...), custom_call_target="tpu_custom_call" | custom-call | flops 2097152 | bytes 6291456 | tf_op jit(solution)/shard_map/finish/pallas_call | solution.py:542
  50.9 1.6 %down.1 = bf16[32,32,256]{2,1,0:T(8,128)(2,1)} custom-call(bf16[66,32,384]{2,1,0:T(8,128)(2,1)S(1)} %get-tuple-element.71.rw, bf16[4,1152,128]{2,1,0:T(8,128)(2,1)S(1)} %get-tuple-element.72.kernels, f32[16,128]{1,0:T(8,128)S(1)} %get-tuple-element.73.smalls), custom_call_target="tpu_custom_call" | custom-call | flops 633339904 | bytes 3145728 | tf_op jit(solution)/shard_map/down/pallas_call | solution.py:508
  52.5 4.1 %collective-permute-done.14.refs_3_ = bf16[624,128]{1,0:T(8,128)(2,1)S(1)} collective-permute-done((bf16[624,128]{1,0:T(8,128)(2,1)S(1)}, bf16[624,128]{1,0:T(8,128)(2,1)S(1)}, u32[]{:S(2)}, u32[]{:S(2)}) %collective-permute-start.14) | collective-permute-done | bytes 159776 | tf_op jit(solution)/shard_map/ppermute | solution.py:875
  56.7 2.3 %collective-permute-start.18 = (bf16[192,128]{1,0:T(8,128)(2,1)S(1)}, bf16[192,128]{1,0:T(8,128)(2,1)S(1)}, u32[]{:S(2)}, u32[]{:S(2)}) collective-permute-start(bf16[192,128]{1,0:T(8,128)(2,1)S(1)} %get-tuple-element.85), channel_id=1, source_target_pairs={{0,6},{1,7},{2,4},{3,5},{4,2},{5,3},{6,0},{7,1},{8,14},{9,15},{10,... | collective-permute-start | bytes 147464 | tf_op jit(solution)/shard_map/ppermute | solution.py:875
  59.0 0.7 %collective-permute-start.19 = (bf16[192,128]{1,0:T(8,128)(2,1)S(1)}, bf16[192,128]{1,0:T(8,128)(2,1)S(1)}, u32[]{:S(2)}, u32[]{:S(2)}) collective-permute-start(bf16[192,128]{1,0:T(8,128)(2,1)S(1)} %get-tuple-element.86), channel_id=1, source_target_pairs={{0,4},{1,5},{2,6},{3,7},{4,0},{5,1},{6,2},{7,3},{8,12},{9,13},{10,... | collective-permute-start | bytes 147464 | tf_op jit(solution)/shard_map/ppermute | solution.py:875
  59.8 1.4 %collective-permute-start.20 = (bf16[192,128]{1,0:T(8,128)(2,1)S(1)}, bf16[192,128]{1,0:T(8,128)(2,1)S(1)}, u32[]{:S(2)}, u32[]{:S(2)}) collective-permute-start(bf16[192,128]{1,0:T(8,128)(2,1)S(1)} %get-tuple-element.87), channel_id=1, source_target_pairs={{0,2},{1,3},{2,0},{3,1},{4,6},{5,7},{6,4},{7,5},{8,10},{9,11},{10,... | collective-permute-start | bytes 147464 | tf_op jit(solution)/shard_map/ppermute | solution.py:875
  61.2 1.6 %collective-permute-done.18.refs_1_ = bf16[192,128]{1,0:T(8,128)(2,1)S(1)} collective-permute-done((bf16[192,128]{1,0:T(8,128)(2,1)S(1)}, bf16[192,128]{1,0:T(8,128)(2,1)S(1)}, u32[]{:S(2)}, u32[]{:S(2)}) %collective-permute-start.18) | collective-permute-done | bytes 49184 | tf_op jit(solution)/shard_map/ppermute | solution.py:875
  62.8 1.6 %collective-permute-done.19.refs_2_ = bf16[192,128]{1,0:T(8,128)(2,1)S(1)} collective-permute-done((bf16[192,128]{1,0:T(8,128)(2,1)S(1)}, bf16[192,128]{1,0:T(8,128)(2,1)S(1)}, u32[]{:S(2)}, u32[]{:S(2)}) %collective-permute-start.19) | collective-permute-done | bytes 49184 | tf_op jit(solution)/shard_map/ppermute | solution.py:875
  64.4 1.9 %update.1 = (f32[4,4,4608]{2,1,0:T(4,128)}, f32[4,12544]{1,0:T(4,128)}, f32[4,56]{1,0:T(4,128)}, bf16[4,4608]{1,0:T(4,128)(2,1)}, bf16[98,128]{1,0:T(8,128)(2,1)}, /*index=5*/bf16[1,56]{1,0:T(2,128)(2,1)}) custom-call(f32[192,128]{1,0:T(8,128)S(1)} %get-tuple-element.84.refs_0_, bf16[192,128]{1,0:T(8,128)(2,1)S(1)} %collective-permute-done.18.refs_1_, ...), custom_call_target="tpu_custom_call" | custom-call | tf_op jit(solution)/shard_map/update/pallas_call | solution.py:858
  (37 shorter events, 1.4 us)
Async XLA Ops:
  2.4 19.7 %copy-start = (bf16[1,64,64,128]{3,2,1,0:T(8,128)(2,1)S(1)}, bf16[1,64,64,128]{3,2,1,0:T(8,128)(2,1)}, u32[]{:S(2)}) copy-start(bf16[1,64,64,128]{3,2,1,0:T(8,128)(2,1)} %param.6) | copy-start | bytes 3145732
  2.4 19.7 %copy-start.3 = (bf16[1,32,32,256]{3,2,1,0:T(8,128)(2,1)S(1)}, bf16[1,32,32,256]{3,2,1,0:T(8,128)(2,1)}, u32[]{:S(2)}) copy-start(bf16[1,32,32,256]{3,2,1,0:T(8,128)(2,1)} %param.7) | copy-start | bytes 1572868
  2.4 8.2 %collective-permute-start = (bf16[256,128]{1,0:T(8,128)(2,1)}, bf16[256,128]{1,0:T(8,128)(2,1)S(1)}, u32[]{:S(2)}, u32[]{:S(2)}) collective-permute-start(bf16[256,128]{1,0:T(8,128)(2,1)} %pack.1.own_ref), channel_id=1, source_target_pairs={{0,6},{1,7},{2,4},{3,5},{4,2},{5,3},{6,0},{7,1},{8,14},{9,15},{10,... | collective-permute-start | bytes 196616 | tf_op jit(solution)/shard_map/ppermute | solution.py:875
  7.5 4.9 %collective-permute-start.4 = (bf16[256,128]{1,0:T(8,128)(2,1)}, bf16[256,128]{1,0:T(8,128)(2,1)S(1)}, u32[]{:S(2)}, u32[]{:S(2)}) collective-permute-start(bf16[256,128]{1,0:T(8,128)(2,1)} %pack.1.own_ref), channel_id=1, source_target_pairs={{0,2},{1,3},{2,0},{3,1},{4,6},{5,7},{6,4},{7,5},{8,10},{9,11},{10,... | collective-permute-start | bytes 196616 | tf_op jit(solution)/shard_map/ppermute | solution.py:875
  7.5 5.8 %collective-permute-start.3 = (bf16[256,128]{1,0:T(8,128)(2,1)}, bf16[256,128]{1,0:T(8,128)(2,1)S(1)}, u32[]{:S(2)}, u32[]{:S(2)}) collective-permute-start(bf16[256,128]{1,0:T(8,128)(2,1)} %pack.1.own_ref), channel_id=1, source_target_pairs={{0,4},{1,5},{2,6},{3,7},{4,0},{5,1},{6,2},{7,3},{8,12},{9,13},{10,... | collective-permute-start | bytes 196616 | tf_op jit(solution)/shard_map/ppermute | solution.py:875
  8.2 0.9 %copy-start.4 = (bf16[256,128]{1,0:T(8,128)(2,1)S(1)}, bf16[256,128]{1,0:T(8,128)(2,1)}, u32[]{:S(2)}) copy-start(bf16[256,128]{1,0:T(8,128)(2,1)} %pack.1.own_ref) | copy-start | bytes 196612
  10.6 5.0 %collective-permute-start.1 = (bf16[2,256,128]{2,1,0:T(8,128)(2,1)S(1)}, bf16[2,256,128]{2,1,0:T(8,128)(2,1)S(1)}, u32[]{:S(2)}, u32[]{:S(2)}) collective-permute-start(bf16[2,256,128]{2,1,0:T(8,128)(2,1)S(1)} %pad_maximum_fusion.2), channel_id=1, source_target_pairs={{0,8},{8,0},{16,24},{24,16},{1,9},{9,1},{17,25},{25,17},{2,10},{10... | collective-permute-start | bytes 393224 | tf_op jit(solution)/shard_map/ppermute | solution.py:875
  13.4 6.4 %collective-permute-start.5 = (bf16[2,256,128]{2,1,0:T(8,128)(2,1)S(1)}, bf16[2,256,128]{2,1,0:T(8,128)(2,1)S(1)}, u32[]{:S(2)}, u32[]{:S(2)}) collective-permute-start(bf16[2,256,128]{2,1,0:T(8,128)(2,1)S(1)} %pad_maximum_fusion.3), channel_id=1, source_target_pairs={{0,16},{8,24},{16,0},{24,8},{1,17},{9,25},{17,1},{25,9},{2,18},{10... | collective-permute-start | bytes 393224 | tf_op jit(solution)/shard_map/ppermute | solution.py:875
  15.7 8.2 %collective-permute-start.2 = (bf16[4,256,128]{2,1,0:T(8,128)(2,1)S(1)}, bf16[4,256,128]{2,1,0:T(8,128)(2,1)S(1)}, u32[]{:S(2)}, u32[]{:S(2)}) collective-permute-start(bf16[4,256,128]{2,1,0:T(8,128)(2,1)S(1)} %pad_maximum_fusion.refs_6_), channel_id=1, source_target_pairs={{0,16},{8,24},{16,0},{24,8},{1,17},{9,25},{17,1},{25,9},{2,18},{10... | collective-permute-start | bytes 786440 | tf_op jit(solution)/shard_map/ppermute | solution.py:875
  19.8 6.4 %collective-permute-start.6 = (bf16[4,256,128]{2,1,0:T(8,128)(2,1)S(1)}, bf16[4,256,128]{2,1,0:T(8,128)(2,1)S(1)}, u32[]{:S(2)}, u32[]{:S(2)}) collective-permute-start(bf16[4,256,128]{2,1,0:T(8,128)(2,1)S(1)} %pad_maximum_fusion.1.refs_7_), channel_id=1, source_target_pairs={{0,8},{8,0},{16,24},{24,16},{1,9},{9,1},{17,25},{25,17},{2,10},{10... | collective-permute-start | bytes 786440 | tf_op jit(solution)/shard_map/ppermute | solution.py:875
  23.3 3.5 %collective-permute-start.7 = (bf16[4,256,128]{2,1,0:T(8,128)(2,1)S(1)}, bf16[4,256,128]{2,1,0:T(8,128)(2,1)S(1)}, u32[]{:S(2)}, u32[]{:S(2)}) collective-permute-start(bf16[4,256,128]{2,1,0:T(8,128)(2,1)S(1)} %pad_maximum_fusion.refs_6_), channel_id=1, source_target_pairs={{0,1},{1,0},{2,3},{3,2},{4,5},{5,4},{6,7},{7,6},{8,9},{9,8},{10,11... | collective-permute-start | bytes 786440 | tf_op jit(solution)/shard_map/ppermute | solution.py:875
  23.4 3.4 %collective-permute-start.8 = (bf16[4,256,128]{2,1,0:T(8,128)(2,1)S(1)}, bf16[4,256,128]{2,1,0:T(8,128)(2,1)S(1)}, u32[]{:S(2)}, u32[]{:S(2)}) collective-permute-start(bf16[4,256,128]{2,1,0:T(8,128)(2,1)S(1)} %pad_maximum_fusion.1.refs_7_), channel_id=1, source_target_pairs={{0,1},{1,0},{2,3},{3,2},{4,5},{5,4},{6,7},{7,6},{8,9},{9,8},{10,11... | collective-permute-start | bytes 786440 | tf_op jit(solution)/shard_map/ppermute | solution.py:875
  26.3 1.5 %collective-permute-start.9 = (bf16[4,256,128]{2,1,0:T(8,128)(2,1)S(1)}, bf16[4,256,128]{2,1,0:T(8,128)(2,1)S(1)}, u32[]{:S(2)}, u32[]{:S(2)}) collective-permute-start(bf16[4,256,128]{2,1,0:T(8,128)(2,1)S(1)} %collective-permute-done.2.refs_8_), channel_id=1, source_target_pairs={{0,1},{1,0},{2,3},{3,2},{4,5},{5,4},{6,7},{7,6},{8,9},{9,8},{10,11... | collective-permute-start | bytes 786440 | tf_op jit(solution)/shard_map/ppermute | solution.py:875
  26.3 1.9 %collective-permute-start.10 = (bf16[4,256,128]{2,1,0:T(8,128)(2,1)S(1)}, bf16[4,256,128]{2,1,0:T(8,128)(2,1)S(1)}, u32[]{:S(2)}, u32[]{:S(2)}) collective-permute-start(bf16[4,256,128]{2,1,0:T(8,128)(2,1)S(1)} %collective-permute-done.6.refs_9_), channel_id=1, source_target_pairs={{0,1},{1,0},{2,3},{3,2},{4,5},{5,4},{6,7},{7,6},{8,9},{9,8},{10,11... | collective-permute-start | bytes 786440 | tf_op jit(solution)/shard_map/ppermute | solution.py:875
  44.1 1.5 %collective-permute-start.11 = (bf16[624,128]{1,0:T(8,128)(2,1)S(1)}, bf16[624,128]{1,0:T(8,128)(2,1)S(1)}, u32[]{:S(2)}, u32[]{:S(2)}) collective-permute-start(bf16[624,128]{1,0:T(8,128)(2,1)S(1)} %get-tuple-element.66), channel_id=1, source_target_pairs={{0,1},{1,0},{2,3},{3,2},{4,5},{5,4},{6,7},{7,6},{8,9},{9,8},{10,11... | collective-permute-start | bytes 479240 | tf_op jit(solution)/shard_map/ppermute | solution.py:875
  44.3 2.9 %collective-permute-start.13 = (bf16[624,128]{1,0:T(8,128)(2,1)S(1)}, bf16[624,128]{1,0:T(8,128)(2,1)S(1)}, u32[]{:S(2)}, u32[]{:S(2)}) collective-permute-start(bf16[624,128]{1,0:T(8,128)(2,1)S(1)} %get-tuple-element.68), channel_id=1, source_target_pairs={{0,1},{1,0},{2,3},{3,2},{4,5},{5,4},{6,7},{7,6},{8,9},{9,8},{10,11... | collective-permute-start | bytes 479240 | tf_op jit(solution)/shard_map/ppermute | solution.py:875
  44.6 4.2 %collective-permute-start.15 = (bf16[624,128]{1,0:T(8,128)(2,1)S(1)}, bf16[624,128]{1,0:T(8,128)(2,1)S(1)}, u32[]{:S(2)}, u32[]{:S(2)}) collective-permute-start(bf16[624,128]{1,0:T(8,128)(2,1)S(1)} %get-tuple-element.70), channel_id=1, source_target_pairs={{0,1},{1,0},{2,3},{3,2},{4,5},{5,4},{6,7},{7,6},{8,9},{9,8},{10,11... | collective-permute-start | bytes 479240 | tf_op jit(solution)/shard_map/ppermute | solution.py:875
  45.6 6.9 %collective-permute-start.12 = (bf16[624,128]{1,0:T(8,128)(2,1)S(1)}, bf16[624,128]{1,0:T(8,128)(2,1)S(1)}, u32[]{:S(2)}, u32[]{:S(2)}) collective-permute-start(bf16[624,128]{1,0:T(8,128)(2,1)S(1)} %add_convert_fusion.2), channel_id=1, source_target_pairs={{0,8},{8,0},{16,24},{24,16},{1,9},{9,1},{17,25},{25,17},{2,10},{10... | collective-permute-start | bytes 479240 | tf_op jit(solution)/shard_map/ppermute | solution.py:875
  47.3 9.4 %collective-permute-start.14 = (bf16[624,128]{1,0:T(8,128)(2,1)S(1)}, bf16[624,128]{1,0:T(8,128)(2,1)S(1)}, u32[]{:S(2)}, u32[]{:S(2)}) collective-permute-start(bf16[624,128]{1,0:T(8,128)(2,1)S(1)} %add_convert_fusion.1), channel_id=1, source_target_pairs={{0,16},{8,24},{16,0},{24,8},{1,17},{9,25},{17,1},{25,9},{2,18},{10... | collective-permute-start | bytes 479240 | tf_op jit(solution)/shard_map/ppermute | solution.py:875
  48.9 7.7 %collective-permute-start.16 = (bf16[624,128]{1,0:T(8,128)(2,1)S(1)}, bf16[624,128]{1,0:T(8,128)(2,1)S(1)}, u32[]{:S(2)}, u32[]{:S(2)}) collective-permute-start(bf16[624,128]{1,0:T(8,128)(2,1)S(1)} %add_convert_fusion), channel_id=1, source_target_pairs={{0,24},{8,16},{16,8},{24,0},{1,25},{9,17},{17,9},{25,1},{2,26},{10... | collective-permute-start | bytes 479240 | tf_op jit(solution)/shard_map/ppermute | solution.py:875
  49.4 7.3 %collective-permute-start.17 = (bf16[624,128]{1,0:T(8,128)(2,1)S(1)}, bf16[624,128]{1,0:T(8,128)(2,1)S(1)}, u32[]{:S(2)}, u32[]{:S(2)}) collective-permute-start(bf16[624,128]{1,0:T(8,128)(2,1)S(1)} %get-tuple-element.80), channel_id=1, source_target_pairs={{0,1},{1,0},{2,3},{3,2},{4,5},{5,4},{6,7},{7,6},{8,9},{9,8},{10,11... | collective-permute-start | bytes 479240 | tf_op jit(solution)/shard_map/ppermute | solution.py:875
  50.9 13.5 %copy-start.1 = (f32[4,4,4608]{2,1,0:T(4,128)S(1)}, f32[4,4,4608]{2,1,0:T(4,128)}, u32[]{:S(2)}) copy-start(f32[4,4,4608]{2,1,0:T(4,128)} %refs_8_.1) | copy-start | bytes 884740
  50.9 13.5 %copy-start.2 = (f32[4,12544]{1,0:T(4,128)S(1)}, f32[4,12544]{1,0:T(4,128)}, u32[]{:S(2)}) copy-start(f32[4,12544]{1,0:T(4,128)} %refs_9_.1) | copy-start | bytes 602116
  50.9 13.5 %copy-start.5 = (f32[4,56]{1,0:T(4,128)S(1)}, f32[4,56]{1,0:T(4,128)}, u32[]{:S(2)}) copy-start(f32[4,56]{1,0:T(4,128)} %refs_10_.1) | copy-start | bytes 2692
  56.7 6.1 %collective-permute-start.18 = (bf16[192,128]{1,0:T(8,128)(2,1)S(1)}, bf16[192,128]{1,0:T(8,128)(2,1)S(1)}, u32[]{:S(2)}, u32[]{:S(2)}) collective-permute-start(bf16[192,128]{1,0:T(8,128)(2,1)S(1)} %get-tuple-element.85), channel_id=1, source_target_pairs={{0,6},{1,7},{2,4},{3,5},{4,2},{5,3},{6,0},{7,1},{8,14},{9,15},{10,... | collective-permute-start | bytes 147464 | tf_op jit(solution)/shard_map/ppermute | solution.py:875
  59.0 5.4 %collective-permute-start.19 = (bf16[192,128]{1,0:T(8,128)(2,1)S(1)}, bf16[192,128]{1,0:T(8,128)(2,1)S(1)}, u32[]{:S(2)}, u32[]{:S(2)}) collective-permute-start(bf16[192,128]{1,0:T(8,128)(2,1)S(1)} %get-tuple-element.86), channel_id=1, source_target_pairs={{0,4},{1,5},{2,6},{3,7},{4,0},{5,1},{6,2},{7,3},{8,12},{9,13},{10,... | collective-permute-start | bytes 147464 | tf_op jit(solution)/shard_map/ppermute | solution.py:875
  59.8 4.6 %collective-permute-start.20 = (bf16[192,128]{1,0:T(8,128)(2,1)S(1)}, bf16[192,128]{1,0:T(8,128)(2,1)S(1)}, u32[]{:S(2)}, u32[]{:S(2)}) collective-permute-start(bf16[192,128]{1,0:T(8,128)(2,1)S(1)} %get-tuple-element.87), channel_id=1, source_target_pairs={{0,2},{1,3},{2,0},{3,1},{4,6},{5,7},{6,4},{7,5},{8,10},{9,11},{10,... | collective-permute-start | bytes 147464 | tf_op jit(solution)/shard_map/ppermute | solution.py:875

commit v9 on v8

--- a/solution.py
+++ b/solution.py
@@ -708,7 +708,7 @@
             pltpu.VMEM((4, plan.conv_len), f32),
             pltpu.VMEM((4, plan.dense_len), f32),
             pltpu.VMEM((4, plan.small_len), f32),
-            pltpu.VMEM((4 * plan.window, C), f32),
+            pltpu.VMEM((5 * plan.window, C), f32),
             pltpu.VMEM((plan.own_rows, C), f32),
             pltpu.SemaphoreType.DMA((3,)),
         ],
@@ -861,8 +861,8 @@
         in_specs=vmem_specs(1 + len(received) + 4 + 3),
         out_specs=vmem_specs(6),
         scratch_shapes=[
-            pltpu.VMEM((4 * plan.window, C), f32),
-            pltpu.VMEM((MLP_ROWS, C), f32),
+            pltpu.VMEM((5 * plan.window, C), f32),
+            pltpu.VMEM((MLP_ROWS + 8, C), f32),
             pltpu.VMEM((plan.dense_rows, C), f32),
             pltpu.VMEM((24, C), f32),
         ],

time: 66.5 us -> 66.5 us (level)
  no operation moved by 1% of the time
where the time goes in v9:
time: 66.5 us; the launch traced here: 66.3 us
  Pallas kernels  23.8 us (36%)
  starting transfers between devices  22.1 us (33%)
  waiting for transfers between devices  17.8 us (27%)
  between operations  1.45 us (2%)
  local copies, waits for them, and re-layouts  0.9 us (1%)
    ppermute x21, starting transfers between devices, swap(): return lax.ppermute(values, axis, [(i, i ^ turn) for i in range(size)])  22.1 us
    ppermute x21, waiting for transfers between devices, swap(): return lax.ppermute(values, axis, [(i, i ^ turn) for i in range(size)])  17.8 us
    pallas_call x1, Pallas kernels, run_block(): pl.pallas_call(functools.partial(block_body, plan), out_shape=shapes, in_...  15.9 us
    pallas_call x1, Pallas kernels, run_update(): pl.pallas_call(functools.partial(update_body, plan, len(received)), out_s...  1.88 us
    pallas_call x1, Pallas kernels, run_pack(): pl.pallas_call(functools.partial(pack_body, plan), out_shape=jax.ShapeDty...  1.74 us
    pallas_call x1, Pallas kernels, run_down(): pl.pallas_call(down_body, out_shape=jax.ShapeDtypeStruct(shape, bf16), in...  1.58 us
    pallas_call x1, Pallas kernels, run_finish(): pl.pallas_call(finish_body, out_shape=jax.ShapeDtypeStruct((H, W, C), bf1...  1.5 us
  transfers between devices with their start and end apart: 21, of which 12 were waited for; matrix products, arithmetic and copies ran while one was open for 0% of the time, Pallas kernels for 6%

profile of v9, /device:TPU:0, one launch (start us, length us, event | category | flops | bytes accessed | tf_op | source)
XLA Modules:
  0.0 66.3 jit_solution(3638021613227572079)
XLA Ops:
  0.6 1.7 %pack.1.own_ref = bf16[256,128]{1,0:T(8,128)(2,1)} custom-call(f32[4,4,4608]{2,1,0:T(4,128)} %refs_8_.1, f32[4,12544]{1,0:T(4,128)} %refs_9_.1, f32[4,56]{1,0:T(4,128)} %refs_10_.1), custom_call_target="tpu_custom_call" | custom-call | tf_op jit(solution)/shard_map/pack/pallas_call | solution.py:702
  2.4 5.1 %collective-permute-start = (bf16[256,128]{1,0:T(8,128)(2,1)}, bf16[256,128]{1,0:T(8,128)(2,1)S(1)}, u32[]{:S(2)}, u32[]{:S(2)}) collective-permute-start(bf16[256,128]{1,0:T(8,128)(2,1)} %pack.1.own_ref), channel_id=1, source_target_pairs={{0,6},{1,7},{2,4},{3,5},{4,2},{5,3},{6,0},{7,1},{8,14},{9,15},{10,... | collective-permute-start | bytes 196616 | tf_op jit(solution)/shard_map/ppermute | solution.py:875
  7.5 0.6 collective-permute-start.3
  8.2 0.9 %copy-done.4 = bf16[256,128]{1,0:T(8,128)(2,1)S(1)} copy-done((bf16[256,128]{1,0:T(8,128)(2,1)S(1)}, bf16[256,128]{1,0:T(8,128)(2,1)}, u32[]{:S(2)}) %copy-start.4) | copy-done | bytes 65560
  9.0 1.6 %collective-permute-done = bf16[256,128]{1,0:T(8,128)(2,1)S(1)} collective-permute-done((bf16[256,128]{1,0:T(8,128)(2,1)}, bf16[256,128]{1,0:T(8,128)(2,1)S(1)}, u32[]{:S(2)}, u32[]{:S(2)}) %collective-permute-start) | collective-permute-done | bytes 65568 | tf_op jit(solution)/shard_map/ppermute | solution.py:875
  10.6 1.6 %collective-permute-start.1 = (bf16[2,256,128]{2,1,0:T(8,128)(2,1)S(1)}, bf16[2,256,128]{2,1,0:T(8,128)(2,1)S(1)}, u32[]{:S(2)}, u32[]{:S(2)}) collective-permute-start(bf16[2,256,128]{2,1,0:T(8,128)(2,1)S(1)} %pad_maximum_fusion.2), channel_id=1, source_target_pairs={{0,8},{8,0},{16,24},{24,16},{1,9},{9,1},{17,25},{25,17},{2,10},{10... | collective-permute-start | bytes 393224 | tf_op jit(solution)/shard_map/ppermute | solution.py:875
  12.4 1.0 %collective-permute-done.3 = bf16[256,128]{1,0:T(8,128)(2,1)S(1)} collective-permute-done((bf16[256,128]{1,0:T(8,128)(2,1)}, bf16[256,128]{1,0:T(8,128)(2,1)S(1)}, u32[]{:S(2)}, u32[]{:S(2)}) %collective-permute-start.3) | collective-permute-done | bytes 65568 | tf_op jit(solution)/shard_map/ppermute | solution.py:875
  13.4 1.6 %collective-permute-start.5 = (bf16[2,256,128]{2,1,0:T(8,128)(2,1)S(1)}, bf16[2,256,128]{2,1,0:T(8,128)(2,1)S(1)}, u32[]{:S(2)}, u32[]{:S(2)}) collective-permute-start(bf16[2,256,128]{2,1,0:T(8,128)(2,1)S(1)} %pad_maximum_fusion.3), channel_id=1, source_target_pairs={{0,16},{8,24},{16,0},{24,8},{1,17},{9,25},{17,1},{25,9},{2,18},{10... | collective-permute-start | bytes 393224 | tf_op jit(solution)/shard_map/ppermute | solution.py:875
  15.0 0.7 %collective-permute-done.1 = bf16[2,256,128]{2,1,0:T(8,128)(2,1)S(1)} collective-permute-done((bf16[2,256,128]{2,1,0:T(8,128)(2,1)S(1)}, bf16[2,256,128]{2,1,0:T(8,128)(2,1)S(1)}, u32[]{:S(2)}, u32[]{:S(2)}) %collective-permute-start.1) | collective-permute-done | bytes 131104 | tf_op jit(solution)/shard_map/ppermute | solution.py:875
  15.7 1.6 %collective-permute-start.2 = (bf16[4,256,128]{2,1,0:T(8,128)(2,1)S(1)}, bf16[4,256,128]{2,1,0:T(8,128)(2,1)S(1)}, u32[]{:S(2)}, u32[]{:S(2)}) collective-permute-start(bf16[4,256,128]{2,1,0:T(8,128)(2,1)S(1)} %pad_maximum_fusion.refs_6_), channel_id=1, source_target_pairs={{0,16},{8,24},{16,0},{24,8},{1,17},{9,25},{17,1},{25,9},{2,18},{10... | collective-permute-start | bytes 786440 | tf_op jit(solution)/shard_map/ppermute | solution.py:875
  17.3 2.5 %collective-permute-done.5 = bf16[2,256,128]{2,1,0:T(8,128)(2,1)S(1)} collective-permute-done((bf16[2,256,128]{2,1,0:T(8,128)(2,1)S(1)}, bf16[2,256,128]{2,1,0:T(8,128)(2,1)S(1)}, u32[]{:S(2)}, u32[]{:S(2)}) %collective-permute-start.5) | collective-permute-done | bytes 131104 | tf_op jit(solution)/shard_map/ppermute | solution.py:875
  19.8 1.6 %collective-permute-start.6 = (bf16[4,256,128]{2,1,0:T(8,128)(2,1)S(1)}, bf16[4,256,128]{2,1,0:T(8,128)(2,1)S(1)}, u32[]{:S(2)}, u32[]{:S(2)}) collective-permute-start(bf16[4,256,128]{2,1,0:T(8,128)(2,1)S(1)} %pad_maximum_fusion.1.refs_7_), channel_id=1, source_target_pairs={{0,8},{8,0},{16,24},{24,16},{1,9},{9,1},{17,25},{25,17},{2,10},{10... | collective-permute-start | bytes 786440 | tf_op jit(solution)/shard_map/ppermute | solution.py:875
  22.1 1.1 %prepare.1 = (f32[16,128]{1,0:T(8,128)S(1)}, bf16[33,32,512]{2,1,0:T(8,128)(2,1)S(1)}, f32[8,256]{1,0:T(8,128)S(1)}, f32[16,256]{1,0:T(8,128)S(1)}) custom-call(s32[1]{0:T(128)S(6)} %copy.14.cls_ref, bf16[64,64,128]{2,1,0:T(8,128)(2,1)S(1)} %bitcast.10, bf16[32,32,256]{2,1,0:T(8,128)(2,1)S(1)} %bitcast.15), custom_call_target="tpu_custom_call" | custom-call | flops 2097152 | bytes 3145728 | tf_op jit(solution)/shard_map/prepare/pallas_call | solution.py:215
  23.4 0.5 collective-permute-start.8
  23.9 2.4 %collective-permute-done.6.refs_9_ = bf16[4,256,128]{2,1,0:T(8,128)(2,1)S(1)} collective-permute-done((bf16[4,256,128]{2,1,0:T(8,128)(2,1)S(1)}, bf16[4,256,128]{2,1,0:T(8,128)(2,1)S(1)}, u32[]{:S(2)}, u32[]{:S(2)}) %collective-permute-start.6) | collective-permute-done | bytes 262176 | tf_op jit(solution)/shard_map/ppermute | solution.py:875
  26.3 0.5 collective-permute-start.10
  26.8 1.0 %collective-permute-done.9.refs_12_ = bf16[4,256,128]{2,1,0:T(8,128)(2,1)S(1)} collective-permute-done((bf16[4,256,128]{2,1,0:T(8,128)(2,1)S(1)}, bf16[4,256,128]{2,1,0:T(8,128)(2,1)S(1)}, u32[]{:S(2)}, u32[]{:S(2)}) %collective-permute-start.9) | collective-permute-done | bytes 262176 | tf_op jit(solution)/shard_map/ppermute | solution.py:875
  27.8 0.4 collective-permute-done.10.refs_13_
  28.2 15.9 %block.1 = (bf16[66,32,384]{2,1,0:T(8,128)(2,1)S(1)}, bf16[4,1152,128]{2,1,0:T(8,128)(2,1)S(1)}, f32[16,128]{1,0:T(8,128)S(1)}, f32[64,64,128]{2,1,0:T(8,128)S(1...) custom-call(bf16[64,64,128]{2,1,0:T(8,128)(2,1)S(1)} %bitcast.11, ...), custom_call_target="tpu_custom_call" | custom-call | flops 9437184000 | bytes 16777216 | tf_op jit(solution)/shard_map/block/pallas_call | solution.py:646
  44.8 0.7 %collective-permute-done.11 = bf16[624,128]{1,0:T(8,128)(2,1)S(1)} collective-permute-done((bf16[624,128]{1,0:T(8,128)(2,1)S(1)}, bf16[624,128]{1,0:T(8,128)(2,1)S(1)}, u32[]{:S(2)}, u32[]{:S(2)}) %collective-permute-start.11) | collective-permute-done | bytes 159776 | tf_op jit(solution)/shard_map/ppermute | solution.py:875
  45.6 1.6 %collective-permute-start.12 = (bf16[624,128]{1,0:T(8,128)(2,1)S(1)}, bf16[624,128]{1,0:T(8,128)(2,1)S(1)}, u32[]{:S(2)}, u32[]{:S(2)}) collective-permute-start(bf16[624,128]{1,0:T(8,128)(2,1)S(1)} %add_convert_fusion.2), channel_id=1, source_target_pairs={{0,8},{8,0},{16,24},{24,16},{1,9},{9,1},{17,25},{25,17},{2,10},{10... | collective-permute-start | bytes 479240 | tf_op jit(solution)/shard_map/ppermute | solution.py:875
  47.3 1.6 %collective-permute-start.14 = (bf16[624,128]{1,0:T(8,128)(2,1)S(1)}, bf16[624,128]{1,0:T(8,128)(2,1)S(1)}, u32[]{:S(2)}, u32[]{:S(2)}) collective-permute-start(bf16[624,128]{1,0:T(8,128)(2,1)S(1)} %add_convert_fusion.1), channel_id=1, source_target_pairs={{0,16},{8,24},{16,0},{24,8},{1,17},{9,25},{17,1},{25,9},{2,18},{10... | collective-permute-start | bytes 479240 | tf_op jit(solution)/shard_map/ppermute | solution.py:875
  48.9 0.5 collective-permute-start.16
  49.4 1.5 %finish.1 = bf16[64,64,128]{2,1,0:T(8,128)(2,1)} custom-call(bf16[64,64,128]{2,1,0:T(8,128)(2,1)S(1)} %bitcast.12, f32[16,128]{1,0:T(8,128)S(1)} %get-tuple-element.59.refs_2_.stats_ref, f32[64,64,128]{2,1,0:T(8,128)S(1)} %get-tuple-element.74.slope_ref, f32[64,64,128]{2,1,0:T(8,128)S(1)} %get-tuple-element.75.grad_ref, ...), custom_call_target="tpu_custom_call" | custom-call | flops 2097152 | bytes 6291456 | tf_op jit(solution)/shard_map/finish/pallas_call | solution.py:542
  50.9 1.6 %down.1 = bf16[32,32,256]{2,1,0:T(8,128)(2,1)} custom-call(bf16[66,32,384]{2,1,0:T(8,128)(2,1)S(1)} %get-tuple-element.71.rw, bf16[4,1152,128]{2,1,0:T(8,128)(2,1)S(1)} %get-tuple-element.72.kernels, f32[16,128]{1,0:T(8,128)S(1)} %get-tuple-element.73.smalls), custom_call_target="tpu_custom_call" | custom-call | flops 633339904 | bytes 3145728 | tf_op jit(solution)/shard_map/down/pallas_call | solution.py:508
  52.5 4.1 %collective-permute-done.14.refs_3_ = bf16[624,128]{1,0:T(8,128)(2,1)S(1)} collective-permute-done((bf16[624,128]{1,0:T(8,128)(2,1)S(1)}, bf16[624,128]{1,0:T(8,128)(2,1)S(1)}, u32[]{:S(2)}, u32[]{:S(2)}) %collective-permute-start.14) | collective-permute-done | bytes 159776 | tf_op jit(solution)/shard_map/ppermute | solution.py:875
  56.7 2.3 %collective-permute-start.18 = (bf16[192,128]{1,0:T(8,128)(2,1)S(1)}, bf16[192,128]{1,0:T(8,128)(2,1)S(1)}, u32[]{:S(2)}, u32[]{:S(2)}) collective-permute-start(bf16[192,128]{1,0:T(8,128)(2,1)S(1)} %get-tuple-element.85), channel_id=1, source_target_pairs={{0,6},{1,7},{2,4},{3,5},{4,2},{5,3},{6,0},{7,1},{8,14},{9,15},{10,... | collective-permute-start | bytes 147464 | tf_op jit(solution)/shard_map/ppermute | solution.py:875
  59.0 0.7 %collective-permute-start.19 = (bf16[192,128]{1,0:T(8,128)(2,1)S(1)}, bf16[192,128]{1,0:T(8,128)(2,1)S(1)}, u32[]{:S(2)}, u32[]{:S(2)}) collective-permute-start(bf16[192,128]{1,0:T(8,128)(2,1)S(1)} %get-tuple-element.86), channel_id=1, source_target_pairs={{0,4},{1,5},{2,6},{3,7},{4,0},{5,1},{6,2},{7,3},{8,12},{9,13},{10,... | collective-permute-start | bytes 147464 | tf_op jit(solution)/shard_map/ppermute | solution.py:875
  59.8 1.4 %collective-permute-start.20 = (bf16[192,128]{1,0:T(8,128)(2,1)S(1)}, bf16[192,128]{1,0:T(8,128)(2,1)S(1)}, u32[]{:S(2)}, u32[]{:S(2)}) collective-permute-start(bf16[192,128]{1,0:T(8,128)(2,1)S(1)} %get-tuple-element.87), channel_id=1, source_target_pairs={{0,2},{1,3},{2,0},{3,1},{4,6},{5,7},{6,4},{7,5},{8,10},{9,11},{10,... | collective-permute-start | bytes 147464 | tf_op jit(solution)/shard_map/ppermute | solution.py:875
  61.2 1.6 %collective-permute-done.18.refs_1_ = bf16[192,128]{1,0:T(8,128)(2,1)S(1)} collective-permute-done((bf16[192,128]{1,0:T(8,128)(2,1)S(1)}, bf16[192,128]{1,0:T(8,128)(2,1)S(1)}, u32[]{:S(2)}, u32[]{:S(2)}) %collective-permute-start.18) | collective-permute-done | bytes 49184 | tf_op jit(solution)/shard_map/ppermute | solution.py:875
  62.8 1.6 %collective-permute-done.19.refs_2_ = bf16[192,128]{1,0:T(8,128)(2,1)S(1)} collective-permute-done((bf16[192,128]{1,0:T(8,128)(2,1)S(1)}, bf16[192,128]{1,0:T(8,128)(2,1)S(1)}, u32[]{:S(2)}, u32[]{:S(2)}) %collective-permute-start.19) | collective-permute-done | bytes 49184 | tf_op jit(solution)/shard_map/ppermute | solution.py:875
  64.4 1.9 %update.1 = (f32[4,4,4608]{2,1,0:T(4,128)}, f32[4,12544]{1,0:T(4,128)}, f32[4,56]{1,0:T(4,128)}, bf16[4,4608]{1,0:T(4,128)(2,1)}, bf16[98,128]{1,0:T(8,128)(2,1)}, /*index=5*/bf16[1,56]{1,0:T(2,128)(2,1)}) custom-call(f32[192,128]{1,0:T(8,128)S(1)} %get-tuple-element.84.refs_0_, bf16[192,128]{1,0:T(8,128)(2,1)S(1)} %collective-permute-done.18.refs_1_, ...), custom_call_target="tpu_custom_call" | custom-call | tf_op jit(solution)/shard_map/update/pallas_call | solution.py:858
  (37 shorter events, 1.3 us)
Async XLA Ops:
  2.4 19.7 %copy-start = (bf16[1,64,64,128]{3,2,1,0:T(8,128)(2,1)S(1)}, bf16[1,64,64,128]{3,2,1,0:T(8,128)(2,1)}, u32[]{:S(2)}) copy-start(bf16[1,64,64,128]{3,2,1,0:T(8,128)(2,1)} %param.6) | copy-start | bytes 3145732
  2.4 19.7 %copy-start.3 = (bf16[1,32,32,256]{3,2,1,0:T(8,128)(2,1)S(1)}, bf16[1,32,32,256]{3,2,1,0:T(8,128)(2,1)}, u32[]{:S(2)}) copy-start(bf16[1,32,32,256]{3,2,1,0:T(8,128)(2,1)} %param.7) | copy-start | bytes 1572868
  2.4 8.2 %collective-permute-start = (bf16[256,128]{1,0:T(8,128)(2,1)}, bf16[256,128]{1,0:T(8,128)(2,1)S(1)}, u32[]{:S(2)}, u32[]{:S(2)}) collective-permute-start(bf16[256,128]{1,0:T(8,128)(2,1)} %pack.1.own_ref), channel_id=1, source_target_pairs={{0,6},{1,7},{2,4},{3,5},{4,2},{5,3},{6,0},{7,1},{8,14},{9,15},{10,... | collective-permute-start | bytes 196616 | tf_op jit(solution)/shard_map/ppermute | solution.py:875
  7.5 4.9 %collective-permute-start.4 = (bf16[256,128]{1,0:T(8,128)(2,1)}, bf16[256,128]{1,0:T(8,128)(2,1)S(1)}, u32[]{:S(2)}, u32[]{:S(2)}) collective-permute-start(bf16[256,128]{1,0:T(8,128)(2,1)} %pack.1.own_ref), channel_id=1, source_target_pairs={{0,2},{1,3},{2,0},{3,1},{4,6},{5,7},{6,4},{7,5},{8,10},{9,11},{10,... | collective-permute-start | bytes 196616 | tf_op jit(solution)/shard_map/ppermute | solution.py:875
  7.5 5.8 %collective-permute-start.3 = (bf16[256,128]{1,0:T(8,128)(2,1)}, bf16[256,128]{1,0:T(8,128)(2,1)S(1)}, u32[]{:S(2)}, u32[]{:S(2)}) collective-permute-start(bf16[256,128]{1,0:T(8,128)(2,1)} %pack.1.own_ref), channel_id=1, source_target_pairs={{0,4},{1,5},{2,6},{3,7},{4,0},{5,1},{6,2},{7,3},{8,12},{9,13},{10,... | collective-permute-start | bytes 196616 | tf_op jit(solution)/shard_map/ppermute | solution.py:875
  8.2 0.9 %copy-start.4 = (bf16[256,128]{1,0:T(8,128)(2,1)S(1)}, bf16[256,128]{1,0:T(8,128)(2,1)}, u32[]{:S(2)}) copy-start(bf16[256,128]{1,0:T(8,128)(2,1)} %pack.1.own_ref) | copy-start | bytes 196612
  10.6 5.0 %collective-permute-start.1 = (bf16[2,256,128]{2,1,0:T(8,128)(2,1)S(1)}, bf16[2,256,128]{2,1,0:T(8,128)(2,1)S(1)}, u32[]{:S(2)}, u32[]{:S(2)}) collective-permute-start(bf16[2,256,128]{2,1,0:T(8,128)(2,1)S(1)} %pad_maximum_fusion.2), channel_id=1, source_target_pairs={{0,8},{8,0},{16,24},{24,16},{1,9},{9,1},{17,25},{25,17},{2,10},{10... | collective-permute-start | bytes 393224 | tf_op jit(solution)/shard_map/ppermute | solution.py:875
  13.4 6.4 %collective-permute-start.5 = (bf16[2,256,128]{2,1,0:T(8,128)(2,1)S(1)}, bf16[2,256,128]{2,1,0:T(8,128)(2,1)S(1)}, u32[]{:S(2)}, u32[]{:S(2)}) collective-permute-start(bf16[2,256,128]{2,1,0:T(8,128)(2,1)S(1)} %pad_maximum_fusion.3), channel_id=1, source_target_pairs={{0,16},{8,24},{16,0},{24,8},{1,17},{9,25},{17,1},{25,9},{2,18},{10... | collective-permute-start | bytes 393224 | tf_op jit(solution)/shard_map/ppermute | solution.py:875
  15.7 8.2 %collective-permute-start.2 = (bf16[4,256,128]{2,1,0:T(8,128)(2,1)S(1)}, bf16[4,256,128]{2,1,0:T(8,128)(2,1)S(1)}, u32[]{:S(2)}, u32[]{:S(2)}) collective-permute-start(bf16[4,256,128]{2,1,0:T(8,128)(2,1)S(1)} %pad_maximum_fusion.refs_6_), channel_id=1, source_target_pairs={{0,16},{8,24},{16,0},{24,8},{1,17},{9,25},{17,1},{25,9},{2,18},{10... | collective-permute-start | bytes 786440 | tf_op jit(solution)/shard_map/ppermute | solution.py:875
  19.8 6.4 %collective-permute-start.6 = (bf16[4,256,128]{2,1,0:T(8,128)(2,1)S(1)}, bf16[4,256,128]{2,1,0:T(8,128)(2,1)S(1)}, u32[]{:S(2)}, u32[]{:S(2)}) collective-permute-start(bf16[4,256,128]{2,1,0:T(8,128)(2,1)S(1)} %pad_maximum_fusion.1.refs_7_), channel_id=1, source_target_pairs={{0,8},{8,0},{16,24},{24,16},{1,9},{9,1},{17,25},{25,17},{2,10},{10... | collective-permute-start | bytes 786440 | tf_op jit(solution)/shard_map/ppermute | solution.py:875
  23.3 3.5 %collective-permute-start.7 = (bf16[4,256,128]{2,1,0:T(8,128)(2,1)S(1)}, bf16[4,256,128]{2,1,0:T(8,128)(2,1)S(1)}, u32[]{:S(2)}, u32[]{:S(2)}) collective-permute-start(bf16[4,256,128]{2,1,0:T(8,128)(2,1)S(1)} %pad_maximum_fusion.refs_6_), channel_id=1, source_target_pairs={{0,1},{1,0},{2,3},{3,2},{4,5},{5,4},{6,7},{7,6},{8,9},{9,8},{10,11... | collective-permute-start | bytes 786440 | tf_op jit(solution)/shard_map/ppermute | solution.py:875
  23.4 3.4 %collective-permute-start.8 = (bf16[4,256,128]{2,1,0:T(8,128)(2,1)S(1)}, bf16[4,256,128]{2,1,0:T(8,128)(2,1)S(1)}, u32[]{:S(2)}, u32[]{:S(2)}) collective-permute-start(bf16[4,256,128]{2,1,0:T(8,128)(2,1)S(1)} %pad_maximum_fusion.1.refs_7_), channel_id=1, source_target_pairs={{0,1},{1,0},{2,3},{3,2},{4,5},{5,4},{6,7},{7,6},{8,9},{9,8},{10,11... | collective-permute-start | bytes 786440 | tf_op jit(solution)/shard_map/ppermute | solution.py:875
  26.3 1.5 %collective-permute-start.9 = (bf16[4,256,128]{2,1,0:T(8,128)(2,1)S(1)}, bf16[4,256,128]{2,1,0:T(8,128)(2,1)S(1)}, u32[]{:S(2)}, u32[]{:S(2)}) collective-permute-start(bf16[4,256,128]{2,1,0:T(8,128)(2,1)S(1)} %collective-permute-done.2.refs_8_), channel_id=1, source_target_pairs={{0,1},{1,0},{2,3},{3,2},{4,5},{5,4},{6,7},{7,6},{8,9},{9,8},{10,11... | collective-permute-start | bytes 786440 | tf_op jit(solution)/shard_map/ppermute | solution.py:875
  26.3 1.9 %collective-permute-start.10 = (bf16[4,256,128]{2,1,0:T(8,128)(2,1)S(1)}, bf16[4,256,128]{2,1,0:T(8,128)(2,1)S(1)}, u32[]{:S(2)}, u32[]{:S(2)}) collective-permute-start(bf16[4,256,128]{2,1,0:T(8,128)(2,1)S(1)} %collective-permute-done.6.refs_9_), channel_id=1, source_target_pairs={{0,1},{1,0},{2,3},{3,2},{4,5},{5,4},{6,7},{7,6},{8,9},{9,8},{10,11... | collective-permute-start | bytes 786440 | tf_op jit(solution)/shard_map/ppermute | solution.py:875
  44.1 1.5 %collective-permute-start.11 = (bf16[624,128]{1,0:T(8,128)(2,1)S(1)}, bf16[624,128]{1,0:T(8,128)(2,1)S(1)}, u32[]{:S(2)}, u32[]{:S(2)}) collective-permute-start(bf16[624,128]{1,0:T(8,128)(2,1)S(1)} %get-tuple-element.66), channel_id=1, source_target_pairs={{0,1},{1,0},{2,3},{3,2},{4,5},{5,4},{6,7},{7,6},{8,9},{9,8},{10,11... | collective-permute-start | bytes 479240 | tf_op jit(solution)/shard_map/ppermute | solution.py:875
  44.3 2.9 %collective-permute-start.13 = (bf16[624,128]{1,0:T(8,128)(2,1)S(1)}, bf16[624,128]{1,0:T(8,128)(2,1)S(1)}, u32[]{:S(2)}, u32[]{:S(2)}) collective-permute-start(bf16[624,128]{1,0:T(8,128)(2,1)S(1)} %get-tuple-element.68), channel_id=1, source_target_pairs={{0,1},{1,0},{2,3},{3,2},{4,5},{5,4},{6,7},{7,6},{8,9},{9,8},{10,11... | collective-permute-start | bytes 479240 | tf_op jit(solution)/shard_map/ppermute | solution.py:875
  44.6 4.2 %collective-permute-start.15 = (bf16[624,128]{1,0:T(8,128)(2,1)S(1)}, bf16[624,128]{1,0:T(8,128)(2,1)S(1)}, u32[]{:S(2)}, u32[]{:S(2)}) collective-permute-start(bf16[624,128]{1,0:T(8,128)(2,1)S(1)} %get-tuple-element.70), channel_id=1, source_target_pairs={{0,1},{1,0},{2,3},{3,2},{4,5},{5,4},{6,7},{7,6},{8,9},{9,8},{10,11... | collective-permute-start | bytes 479240 | tf_op jit(solution)/shard_map/ppermute | solution.py:875
  45.6 6.9 %collective-permute-start.12 = (bf16[624,128]{1,0:T(8,128)(2,1)S(1)}, bf16[624,128]{1,0:T(8,128)(2,1)S(1)}, u32[]{:S(2)}, u32[]{:S(2)}) collective-permute-start(bf16[624,128]{1,0:T(8,128)(2,1)S(1)} %add_convert_fusion.2), channel_id=1, source_target_pairs={{0,8},{8,0},{16,24},{24,16},{1,9},{9,1},{17,25},{25,17},{2,10},{10... | collective-permute-start | bytes 479240 | tf_op jit(solution)/shard_map/ppermute | solution.py:875
  47.3 9.4 %collective-permute-start.14 = (bf16[624,128]{1,0:T(8,128)(2,1)S(1)}, bf16[624,128]{1,0:T(8,128)(2,1)S(1)}, u32[]{:S(2)}, u32[]{:S(2)}) collective-permute-start(bf16[624,128]{1,0:T(8,128)(2,1)S(1)} %add_convert_fusion.1), channel_id=1, source_target_pairs={{0,16},{8,24},{16,0},{24,8},{1,17},{9,25},{17,1},{25,9},{2,18},{10... | collective-permute-start | bytes 479240 | tf_op jit(solution)/shard_map/ppermute | solution.py:875
  48.9 7.7 %collective-permute-start.16 = (bf16[624,128]{1,0:T(8,128)(2,1)S(1)}, bf16[624,128]{1,0:T(8,128)(2,1)S(1)}, u32[]{:S(2)}, u32[]{:S(2)}) collective-permute-start(bf16[624,128]{1,0:T(8,128)(2,1)S(1)} %add_convert_fusion), channel_id=1, source_target_pairs={{0,24},{8,16},{16,8},{24,0},{1,25},{9,17},{17,9},{25,1},{2,26},{10... | collective-permute-start | bytes 479240 | tf_op jit(solution)/shard_map/ppermute | solution.py:875
  49.4 7.3 %collective-permute-start.17 = (bf16[624,128]{1,0:T(8,128)(2,1)S(1)}, bf16[624,128]{1,0:T(8,128)(2,1)S(1)}, u32[]{:S(2)}, u32[]{:S(2)}) collective-permute-start(bf16[624,128]{1,0:T(8,128)(2,1)S(1)} %get-tuple-element.80), channel_id=1, source_target_pairs={{0,1},{1,0},{2,3},{3,2},{4,5},{5,4},{6,7},{7,6},{8,9},{9,8},{10,11... | collective-permute-start | bytes 479240 | tf_op jit(solution)/shard_map/ppermute | solution.py:875
  50.9 13.5 %copy-start.1 = (f32[4,4,4608]{2,1,0:T(4,128)S(1)}, f32[4,4,4608]{2,1,0:T(4,128)}, u32[]{:S(2)}) copy-start(f32[4,4,4608]{2,1,0:T(4,128)} %refs_8_.1) | copy-start | bytes 884740
  50.9 13.5 %copy-start.2 = (f32[4,12544]{1,0:T(4,128)S(1)}, f32[4,12544]{1,0:T(4,128)}, u32[]{:S(2)}) copy-start(f32[4,12544]{1,0:T(4,128)} %refs_9_.1) | copy-start | bytes 602116
  50.9 13.5 %copy-start.5 = (f32[4,56]{1,0:T(4,128)S(1)}, f32[4,56]{1,0:T(4,128)}, u32[]{:S(2)}) copy-start(f32[4,56]{1,0:T(4,128)} %refs_10_.1) | copy-start | bytes 2692
  56.7 6.1 %collective-permute-start.18 = (bf16[192,128]{1,0:T(8,128)(2,1)S(1)}, bf16[192,128]{1,0:T(8,128)(2,1)S(1)}, u32[]{:S(2)}, u32[]{:S(2)}) collective-permute-start(bf16[192,128]{1,0:T(8,128)(2,1)S(1)} %get-tuple-element.85), channel_id=1, source_target_pairs={{0,6},{1,7},{2,4},{3,5},{4,2},{5,3},{6,0},{7,1},{8,14},{9,15},{10,... | collective-permute-start | bytes 147464 | tf_op jit(solution)/shard_map/ppermute | solution.py:875
  59.0 5.4 %collective-permute-start.19 = (bf16[192,128]{1,0:T(8,128)(2,1)S(1)}, bf16[192,128]{1,0:T(8,128)(2,1)S(1)}, u32[]{:S(2)}, u32[]{:S(2)}) collective-permute-start(bf16[192,128]{1,0:T(8,128)(2,1)S(1)} %get-tuple-element.86), channel_id=1, source_target_pairs={{0,4},{1,5},{2,6},{3,7},{4,0},{5,1},{6,2},{7,3},{8,12},{9,13},{10,... | collective-permute-start | bytes 147464 | tf_op jit(solution)/shard_map/ppermute | solution.py:875
  59.8 4.6 %collective-permute-start.20 = (bf16[192,128]{1,0:T(8,128)(2,1)S(1)}, bf16[192,128]{1,0:T(8,128)(2,1)S(1)}, u32[]{:S(2)}, u32[]{:S(2)}) collective-permute-start(bf16[192,128]{1,0:T(8,128)(2,1)S(1)} %get-tuple-element.87), channel_id=1, source_target_pairs={{0,2},{1,3},{2,0},{3,1},{4,6},{5,7},{6,4},{7,5},{8,10},{9,11},{10,... | collective-permute-start | bytes 147464 | tf_op jit(solution)/shard_map/ppermute | solution.py:875
